TPU v7x, 32 devices: a whole 2x2x4 slice. The times are simulated.
32 devices in a mesh: cube: 4 (over z), row: 4 (over y, core), col: 2 (over x).
Axes of the slice: x: 2, y: 2, z: 4, core: 2. Of those that a mesh axis runs over, the one named last changes fastest.
Arguments:
- diag_block: float32 [4, 256, 256], P('cube', ('row', 'col'))
- pivot_order: int32 [4, 256], P('cube'), may hold values from 0 to 255, as said below
- lower_in: bfloat16 [4, 4096, 256], P('cube', 'row', 'col'), may hold values from -0.14941406 to 0.14941406
- upper_in: bfloat16 [4, 256, 30720], P('cube', 'row', 'col'), may hold values from -6 to 6
- trailing: bfloat16 [4, 4096, 30720], P('cube', 'row', 'col'), may hold values from -6 to 6
- block_mask: int32 [4, 32, 4], P('cube', 'row', 'col'), may hold values 0 or 1
- row_map: int32 [4, 4096], P('cube', 'row'), may hold values from 0 to 1023, as said below
Outputs:
- merged: bfloat16 [4, 4096, 15360], P('cube', 'row', 'col')
Inputs may be any that keep to these rules, and one draw needn't show every extreme that they name: `pivot_order`: each front's row is a permutation of 0 to 255. `row_map`: in each aligned block of 1024 rows of a front the entries are a permutation of 0 to 1023.
All inputs are finite; a program needn't handle non-finite values. No bound on the sum of `block_mask` on one device may be relied on, other than what follows from the above.
Results may differ from a plain program's by a relative error of at most 0.0056.
Values may be sent and summed in bfloat16 or wider, within the bound.
No kernel may reach another device: no remote copies, remote signals or barrier semaphores. Data moves between devices by JAX's collectives and lax.ppermute only.
A program may use at most 320 MiB of HBM per device.

v0:
```python
import jax
import jax.numpy as jnp
from jax import lax
from jax.sharding import PartitionSpec as P


def swapped(block, axis, bit):
    count = lax.axis_size(axis)
    route = []
    for low in range(count):
        high = low | 1 << bit
        if high != low and high < count:
            route += [(low, high), (high, low)]
    return lax.ppermute(block, axis, route)


def exact_product(left, right):
    return jnp.dot(left, right, precision=lax.Precision.HIGHEST, preferred_element_type=left.dtype)


def small_inverses(block):
    size = block.shape[0]
    work = block
    for step in range(size - 1):
        column = work[step + 1 :, step] / work[step, step]
        work = work.at[step + 1 :, step + 1 :].add(
            -column[:, None] * work[step, step + 1 :][None, :]
        )
        work = work.at[step + 1 :, step].set(column)
    identity = jnp.eye(size, dtype=block.dtype)
    lower = jnp.tril(work, -1) + identity
    upper = jnp.triu(work)
    lower_rows = []
    for step in range(size):
        fresh = identity[step]
        for inner in range(step):
            fresh = fresh - lower[step, inner] * lower_rows[inner]
        lower_rows.append(fresh)
    upper_rows = [None] * size
    for step in range(size - 1, -1, -1):
        fresh = identity[step]
        for inner in range(step + 1, size):
            fresh = fresh - upper[step, inner] * upper_rows[inner]
        upper_rows[step] = fresh / upper[step, step]
    return (jnp.stack(lower_rows), jnp.stack(upper_rows))


def block_inverses(block):
    size = block.shape[0]
    if size <= 8:
        return small_inverses(block)
    half = size // 2
    lower_one, upper_one = block_inverses(block[:half, :half])
    lower_side = exact_product(block[half:, :half], upper_one)
    upper_side = exact_product(lower_one, block[:half, half:])
    schur = block[half:, half:] - exact_product(lower_side, upper_side)
    lower_two, upper_two = block_inverses(schur)
    zero = jnp.zeros((half, half), block.dtype)
    corner_lower = -exact_product(lower_two, exact_product(lower_side, lower_one))
    corner_upper = -exact_product(upper_one, exact_product(upper_side, upper_two))
    lower_inv = jnp.concatenate(
        [
            jnp.concatenate([lower_one, zero], axis=1),
            jnp.concatenate([corner_lower, lower_two], axis=1),
        ],
        axis=0,
    )
    upper_inv = jnp.concatenate(
        [
            jnp.concatenate([upper_one, corner_upper], axis=1),
            jnp.concatenate([zero, upper_two], axis=1),
        ],
        axis=0,
    )
    return (lower_inv, upper_inv)


def exact_dot(left, right):
    return jnp.dot(
        left, right, precision=lax.Precision.HIGHEST, preferred_element_type=jnp.float32
    ).astype(jnp.bfloat16)


def local(diag_block, pivot_order, lower_in, upper_in, trailing, block_mask, row_map):
    whole_block = lax.all_gather(diag_block, ("row", "col"), axis=1, tiled=True)[0]
    order = pivot_order[0]
    lower_inv, upper_inv = block_inverses(jnp.take(whole_block, order, axis=0))
    full_rows = lax.all_gather(lower_in, "col", axis=2, tiled=True)[0]
    lower_panel = exact_dot(full_rows.astype(jnp.float32), upper_inv)
    full_cols = lax.all_gather(upper_in, "row", axis=1, tiled=True)[0]
    upper_panel = exact_dot(lower_inv, jnp.take(full_cols, order, axis=0).astype(jnp.float32))
    block = trailing[0]
    flags = block_mask[0].astype(jnp.float32)
    blocks = flags.shape[0]
    half = block.shape[1] // 2
    parity = lax.axis_index("cube") % 2
    product = jnp.dot(lower_panel, upper_panel, preferred_element_type=jnp.float32)
    masked = (product.reshape(blocks, -1, 2, half) * flags[:, None, :, None]).reshape(product.shape)
    updated = (block.astype(jnp.float32) - masked).astype(jnp.bfloat16)
    kept = lax.dynamic_slice_in_dim(updated, parity * half, half, 1)
    outgoing = lax.dynamic_slice_in_dim(updated, (1 - parity) * half, half, 1)
    received = swapped(outgoing, "cube", 0)
    taken = jnp.take(received, row_map[0], axis=0)
    merged = (kept.astype(jnp.float32) + taken.astype(jnp.float32)).astype(jnp.bfloat16)
    return merged[None]


def solution(mesh):
    return jax.shard_map(
        local,
        mesh=mesh,
        in_specs=(
            P("cube", ("row", "col"), None),
            P("cube", None),
            P("cube", "row", "col"),
            P("cube", "row", "col"),
            P("cube", "row", "col"),
            P("cube", "row", "col"),
            P("cube", "row"),
        ),
        out_specs=P("cube", "row", "col"),
        check_vma=False,
    )
```

profile of v0, /device:TPU:0, one launch (start us, length us, event | category | flops | bytes accessed | tf_op | source)
XLA Modules:
  0.0 2553.4 jit_solution(10221518637763910950)
XLA Ops:
  47.5 22.6 subtract_divide_fusion.217
  108.1 22.6 subtract_divide_fusion.210
  169.0 22.6 subtract_divide_fusion.203
  228.1 22.6 subtract_divide_fusion.196
  291.7 22.6 subtract_divide_fusion.189
  351.0 22.6 subtract_divide_fusion.182
  413.7 22.6 subtract_divide_fusion.175
  472.7 22.6 subtract_divide_fusion.168
  537.2 22.6 subtract_divide_fusion.161
  596.2 22.6 subtract_divide_fusion.154
  658.9 22.6 subtract_divide_fusion.147
  718.2 22.6 subtract_divide_fusion.140
  781.7 22.6 subtract_divide_fusion.133
  840.8 22.6 subtract_divide_fusion.126
  903.5 22.6 subtract_divide_fusion.119
  962.6 22.6 subtract_divide_fusion.112
  1028.0 22.6 subtract_divide_fusion.105
  1087.2 22.6 subtract_divide_fusion.98
  1150.0 22.6 subtract_divide_fusion.91
  1209.0 22.6 subtract_divide_fusion.84
  1272.5 22.6 subtract_divide_fusion.77
  1331.6 22.6 subtract_divide_fusion.70
  1394.3 22.6 subtract_divide_fusion.63
  1453.6 22.6 subtract_divide_fusion.56
  1518.0 22.6 subtract_divide_fusion.49
  1577.0 22.6 subtract_divide_fusion.42
  1639.7 22.6 subtract_divide_fusion.35
  1698.8 22.6 subtract_divide_fusion.28
  1923.1 42.5 %copy.10 = f32[128,8,2,7680]{3,1,2,0:T(8,128)} copy(f32[128,8,2,7680]{3,2,1,0:T(2,128)} %bitcast.2978) | data formatting | bytes 125829120
  2097.1 43.7 %fusion = bf16[1024,15360]{1,0:T(8,128)(2,1)} fusion(f32[1024,15360]{1,0:T(8,128)} %bitcast.2977, bf16[256,1024]{1,0:T(8,128)(2,1)S(1)} %convolution_convert_fusion.1, bf16[256,15360]{1,0:T(8,128)(2,1)} %convolution_convert_fusion, bf16[1,1024,15360]{2,1,0:T(8,128)(2,1)} %param.907), kind=kOutput, calls=%fused_computation.4 | convolution fusion | flops 8115978240 | bytes 134217728 | tf_op jit(solution)/shard_map/dot_general | solution.py:97
  2154.8 339.4 %collective-permute-done = bf16[1024,7680]{1,0:T(8,128)(2,1)} collective-permute-done((bf16[1024,7680]{1,0:T(8,128)(2,1)}, bf16[1024,7680]{1,0:T(8,128)(2,1)}, u32[]{:S(2)}, u32[]{:S(2)}) %collective-permute-start) | collective-permute-done | bytes 15728672 | tf_op jit(solution)/shard_map/ppermute | solution.py:14
  2494.2 34.0 %gather_fusion.2 = bf16[1024,7680]{1,0:T(8,128)(2,1)} fusion(bf16[1024,7680]{1,0:T(8,128)(2,1)} %collective-permute-done, s32[1024]{0:T(1024)S(1)} %broadcast_clamp_fusion), kind=kCustom, calls=%fused_computation.2 | custom fusion | bytes 31461376 | tf_op jit(solution)/shard_map/jit(_take)/gather | solution.py:103
  (1832 shorter events, 1362.4 us)
Async XLA Ops:
  6.5 2057.8 %all-gather.2.cloned.1.call-start = ((), (), s32[]{:S(2)}) async-start(), calls=%async_computation | async-start | bytes 9830400 | tf_op jit(solution)/shard_map/all_gather | solution.py:90
  7.3 1893.1 %copy-start.2 = (s32[1,8,2]{1,2,0:T(2,128)S(1)}, s32[1,8,2]{1,2,0:T(2,128)}, u32[]{:S(2)}) copy-start(s32[1,8,2]{1,2,0:T(2,128)} %param.908) | copy-start | bytes 196
  1923.1 128.2 %copy-start = (bf16[1,1024,128]{2,1,0:T(8,128)(2,1)S(1)}, bf16[1,1024,128]{2,1,0:T(8,128)(2,1)}, u32[]{:S(2)}) copy-start(bf16[1,1024,128]{2,1,0:T(8,128)(2,1)} %param.905) | copy-start | bytes 786436
  2140.8 13.9 copy-start.1
  2154.0 340.1 %collective-permute-start = (bf16[1024,7680]{1,0:T(8,128)(2,1)}, bf16[1024,7680]{1,0:T(8,128)(2,1)}, u32[]{:S(2)}, u32[]{:S(2)}) collective-permute-start(bf16[1024,7680]{1,0:T(8,128)(2,1)} %constant_dynamic-slice_fusion), channel_id=1, source_target_pairs={{0,8},{8,0},{16,24},{24,16},{1,9},{9,1},{17,25},{25,17},{2,10},{10... | collective-permute-start | bytes 47185928 | tf_op jit(solution)/shard_map/ppermute | solution.py:14
Sparse Core Ops, SparseCore 0:
  8.9 58.5 all-gather.1
where the time goes:
time: 2580 us; the launch traced here: 2550 us
  other arithmetic  1470 us (57%)
  local copies, waits for them, and re-layouts  521 us (20%)
  waiting for transfers between devices  340 us (13%)
  between operations  98.8 us (4%)
  matrix products  91.1 us (4%)
  blocking collectives  27.6 us (1%)
    div x32, other arithmetic, small_inverses(): upper_rows[step] = fresh / upper[step, step]  723 us
    sub x32, other arithmetic, small_inverses(): fresh = fresh - lower[step, inner] * lower_rows[inner]  556 us
    ppermute x1, waiting for transfers between devices, swapped(): return lax.ppermute(block, axis, route)  339 us
    neg x192, other arithmetic, small_inverses(): -column[:, None] * work[step, step + 1:][None, :]  156 us
    slice x192, local copies, waits for them, and re-layouts, small_inverses(): column = work[step + 1:, step] / work[step, step]  111 us
    scatter-add x224, local copies, waits for them, and re-layouts, small_inverses(): work.at[step + 1:, step + 1:]  90.6 us
    scatter x224, local copies, waits for them, and re-layouts, small_inverses(): work = work.at[step + 1:, step].set(column)  56.4 us
  transfers between devices with their start and end apart: 2, of which 1 were waited for; matrix products, arithmetic and copies ran while one was open for 76% of the time, Pallas kernels for 0%

commit v1 on v0

v1 whole, which is shorter than its diff:
```python
import functools

import jax
import jax.numpy as jnp
from jax import lax
from jax.experimental import pallas as pl
from jax.experimental.pallas import tpu as pltpu
from jax.sharding import PartitionSpec as P

CHUNKS = 15
ROW_STEPS = 4
HIGH = lax.Precision.HIGHEST
VMEM_LIMIT = 48 * 1024 * 1024


def partner(block, axis, bits):
    count = lax.axis_size(axis)
    return lax.ppermute(block, axis, [(i, i ^ bits) for i in range(count)])


def exact(left, right):
    return jnp.dot(left, right, precision=HIGH, preferred_element_type=jnp.float32)


def fast(left, right):
    return jnp.dot(left, right, preferred_element_type=jnp.float32)


def split(value):
    high = value.astype(jnp.bfloat16)
    return high, (value - high.astype(jnp.float32)).astype(jnp.bfloat16)


def eliminate(block):
    size = block.shape[0]
    row = lax.broadcasted_iota(jnp.int32, (size, size), 0)
    lane = lax.broadcasted_iota(jnp.int32, (size, size), 1)

    def eight(turn, work):
        left = size - 8 * turn
        for step in range(8):
            column = work[:, step : step + 1]
            pivot_row = work[step : step + 1, :]
            inverse = 1.0 / work[step : step + 1, step : step + 1]
            scaled = pivot_row * inverse
            lane_one = lane[:1]
            at = lane_one == step
            passed = (lane_one < step) | (lane_one >= left)
            for_later = jnp.where(at, inverse, scaled)
            for_passed = jnp.where(passed | at, 0.0, scaled)
            row_passed = (row < step) | (row >= left)
            base = jnp.where((lane == step) & jnp.logical_not(row_passed), 0.0, work)
            fresh = base - column * jnp.where(row_passed, for_passed, for_later)
            own = jnp.where(at, inverse, jnp.where(passed, pivot_row, -scaled))
            work = jnp.where(row == step, own, fresh)
        work = jnp.concatenate([work[8:], work[:8]], axis=0)
        return pltpu.roll(work, size - 8, 1)

    return lax.fori_loop(0, size // 8, eight, block)


def inverses(block):
    size = block.shape[0]
    work = eliminate(block)
    row = lax.broadcasted_iota(jnp.int32, (size, size), 0)
    lane = lax.broadcasted_iota(jnp.int32, (size, size), 1)
    diagonal = jnp.sum(jnp.where(row == lane, work, 0.0), axis=0, keepdims=True)
    lower = jnp.where(row > lane, work, jnp.where(row == lane, 1.0, 0.0))
    upper = jnp.where(row < lane, work * diagonal, jnp.where(row == lane, work, 0.0))
    return lower, upper


def factor_kernel(block, order_of_diag, order_of_upper, order_of_lower, panel, mask, hi, lo, sent, kept):
    size = block.shape[0]
    half = size // 2
    lane = lax.broadcasted_iota(jnp.int32, (size, size), 1)

    def chosen(order):
        return jnp.where(order[...] == lane, 1.0, 0.0)

    pivoted = exact(chosen(order_of_diag), block[...])
    lower_one, upper_one = inverses(pivoted[:half, :half])
    lower_side = exact(pivoted[half:, :half], upper_one)
    upper_side = exact(lower_one, pivoted[:half, half:])
    schur = pivoted[half:, half:] - exact(lower_side, upper_side)
    lower_two, upper_two = inverses(schur)
    zero = jnp.zeros((half, half), jnp.float32)
    corner_lower = -exact(lower_two, exact(lower_side, lower_one))
    corner_upper = -exact(upper_one, exact(upper_side, upper_two))
    lower_inv = jnp.concatenate(
        [jnp.concatenate([lower_one, zero], 1), jnp.concatenate([corner_lower, lower_two], 1)], 0
    )
    upper_inv = jnp.concatenate(
        [jnp.concatenate([upper_one, corner_upper], 1), jnp.concatenate([zero, upper_two], 1)], 0
    )
    hi[...], lo[...] = split(exact(lower_inv, chosen(order_of_upper)))
    upper_hi, upper_lo = split(exact(chosen(order_of_lower), upper_inv))
    for start in range(0, panel.shape[0], size):
        rows = slice(start, start + size)
        part = panel[rows, :]
        result = fast(part, upper_hi) + fast(part, upper_lo)
        result = result.astype(jnp.bfloat16).astype(jnp.float32)
        sent[rows, :] = (result * mask[rows, 0:1]).astype(jnp.bfloat16)
        kept[rows, :] = (result * mask[rows, 1:2]).astype(jnp.bfloat16)


def factor(block, orders, panel, mask):
    size = block.shape[0]
    rows = panel.shape[0]
    half_type = jnp.bfloat16
    return pl.pallas_call(
        factor_kernel,
        out_shape=(
            jax.ShapeDtypeStruct((size, size), half_type),
            jax.ShapeDtypeStruct((size, size), half_type),
            jax.ShapeDtypeStruct((rows, size), half_type),
            jax.ShapeDtypeStruct((rows, size), half_type),
        ),
        compiler_params=pltpu.CompilerParams(vmem_limit_bytes=VMEM_LIMIT),
        cost_estimate=pl.CostEstimate(flops=30_000_000_000, bytes_accessed=3_000_000, transcendentals=0),
        name="factor",
    )(block, *orders, panel, mask)


def panel_tile(hi, lo, pieces):
    columns = jnp.concatenate([piece[...] for piece in pieces], axis=0)
    return (fast(hi[...], columns) + fast(lo[...], columns)).astype(jnp.bfloat16)


def send_kernel(place, hi, lo, left, trailing, *rest):
    *pieces, out, right = rest

    @pl.when(pl.program_id(0) == 0)
    def _():
        right[...] = panel_tile(hi, lo, pieces)

    out[...] = (trailing[...].astype(jnp.float32) - fast(left[...], right[...])).astype(jnp.bfloat16)


def merge_kernel(place, hi, lo, left, trailing, chosen, received, *rest):
    *pieces, out, right = rest

    @pl.when(pl.program_id(0) == 0)
    def _():
        right[...] = panel_tile(hi, lo, pieces)

    own = (trailing[...].astype(jnp.float32) - fast(left[...], right[...])).astype(jnp.bfloat16)
    out[...] = (own.astype(jnp.float32) + fast(chosen[...], received[...])).astype(jnp.bfloat16)


def merge_kernel_into(place, hi, lo, left, trailing, chosen, received, *rest):
    *pieces, _, out, right = rest
    merge_kernel(place, hi, lo, left, trailing, chosen, received, *pieces, out, right)


def specs_for(hi, left, width, steps, half_blocks, chunk, pieces, starts):
    size = hi.shape[0]
    rows = left.shape[0] // steps
    whole = pl.BlockSpec((size, size), lambda i, place: (0, 0))
    specs = [
        whole,
        whole,
        pl.BlockSpec((rows, size), lambda i, place: (i, 0)),
        pl.BlockSpec((rows, width), lambda i, place: (i, place[0] * half_blocks + chunk)),
    ]
    piece_specs = []
    for number, (piece, start) in enumerate(zip(pieces, starts)):
        depth = piece.shape[0]
        if number == 0:
            piece_specs.append(pl.BlockSpec((depth, width), lambda i, place: (0, place[0] * half_blocks + chunk)))
        else:
            piece_specs.append(pl.BlockSpec((depth, width), lambda i, place, at=chunk - start: (0, at)))
    return specs, piece_specs


def send_chunk(place, hi, lo, left, trailing, pieces, starts, width, chunk):
    rows, columns = trailing.shape
    half_blocks = columns // 2 // width
    specs, piece_specs = specs_for(hi, left, width, ROW_STEPS, half_blocks, chunk, pieces, starts)
    return pl.pallas_call(
        send_kernel,
        grid_spec=pltpu.PrefetchScalarGridSpec(
            num_scalar_prefetch=1,
            grid=(ROW_STEPS,),
            in_specs=specs + piece_specs,
            out_specs=pl.BlockSpec((rows // ROW_STEPS, width), lambda i, place: (i, 0)),
            scratch_shapes=[pltpu.VMEM((hi.shape[0], width), jnp.bfloat16)],
        ),
        out_shape=jax.ShapeDtypeStruct((rows, width), jnp.bfloat16),
        compiler_params=pltpu.CompilerParams(vmem_limit_bytes=VMEM_LIMIT),
        cost_estimate=pl.CostEstimate(flops=2 * rows * 256 * width, bytes_accessed=5 * rows * width, transcendentals=0),
        name="send_part",
    )(place, hi, lo, left, trailing, *pieces)


def merge_chunk(place, hi, lo, left, trailing, chosen, received, pieces, starts, width, chunk, merged):
    rows, columns = trailing.shape
    half_blocks = columns // 2 // width
    step_rows = rows // ROW_STEPS
    specs, piece_specs = specs_for(hi, left, width, ROW_STEPS, half_blocks, chunk, pieces, starts)
    specs += [
        pl.BlockSpec((step_rows, rows), lambda i, place: (i, 0)),
        pl.BlockSpec((rows, width), lambda i, place: (0, 0)),
    ] + piece_specs
    operands = [place, hi, lo, left, trailing, chosen, received, *pieces]
    aliases = {}
    body = merge_kernel
    if merged is not None:
        aliases = {len(operands): 0}
        operands.append(merged)
        specs.append(pl.BlockSpec(memory_space=pl.ANY))
        body = merge_kernel_into
    return pl.pallas_call(
        body,
        grid_spec=pltpu.PrefetchScalarGridSpec(
            num_scalar_prefetch=1,
            grid=(ROW_STEPS,),
            in_specs=specs,
            out_specs=pl.BlockSpec((step_rows, width), lambda i, place: (i, chunk)),
            scratch_shapes=[pltpu.VMEM((hi.shape[0], width), jnp.bfloat16)],
        ),
        out_shape=jax.ShapeDtypeStruct((rows, columns // 2), jnp.bfloat16),
        input_output_aliases=aliases,
        compiler_params=pltpu.CompilerParams(vmem_limit_bytes=VMEM_LIMIT),
        cost_estimate=pl.CostEstimate(flops=2 * rows * (rows + 256) * width, bytes_accessed=8 * rows * width, transcendentals=0),
        name="merge_part",
    )(*operands)


def doubled(block, axis, dimension):
    bits = 1
    while bits < lax.axis_size(axis):
        block = jnp.concatenate([block, partner(block, axis, bits)], axis=dimension)
        bits *= 2
    return block


def relative(index, part, me):
    return ((index // part) ^ me) * part + index % part


def local(diag_block, pivot_order, lower_in, upper_in, trailing, block_mask, row_map):
    diag_block, lower_in, upper_in, trailing = diag_block[0], lower_in[0], upper_in[0], trailing[0]
    size = diag_block.shape[1]
    rows, columns = trailing.shape
    half = columns // 2
    width = half // CHUNKS
    group = lax.axis_index(("row", "col"))
    row, col = lax.axis_index("row"), lax.axis_index("col")
    parity = lax.axis_index("cube") % 2
    sent_place = (1 - parity).astype(jnp.int32).reshape(1)
    kept_place = parity.astype(jnp.int32).reshape(1)

    whole_block = doubled(diag_block, ("row", "col"), 0)
    panel = doubled(lower_in, "col", 1)
    order = pivot_order[0][:, None]
    orders = (
        relative(order, diag_block.shape[0], group),
        relative(order, upper_in.shape[0], row),
        relative(jnp.arange(size, dtype=jnp.int32)[:, None], lower_in.shape[1], col),
    )
    flags = jnp.repeat(block_mask[0].astype(jnp.float32), rows // block_mask.shape[1], axis=0)
    flags = jnp.where(parity == 0, flags[:, ::-1], flags)
    chosen = (row_map[0][:, None] == jnp.arange(rows, dtype=jnp.int32)[None, :]).astype(jnp.bfloat16)

    def gathered(place, first, last):
        own = lax.dynamic_slice_in_dim(upper_in, place * half + first * width, (last - first) * width, 1)
        return [partner(own, "row", bits) for bits in range(1, lax.axis_size("row"))]

    cuts = (0, 2, 7, CHUNKS)
    sent_groups = [(a, b, gathered(1 - parity, a, b)) for a, b in zip(cuts, cuts[1:])]
    kept_groups = [(0, CHUNKS, gathered(parity, 0, CHUNKS))]

    def pieces_of(groups, chunk):
        for first, last, arrays in groups:
            if first <= chunk < last:
                return [upper_in, *arrays], [0] + [first] * len(arrays)

    hi, lo, sent_left, kept_left = factor(whole_block, orders, panel, flags)

    received = []
    for chunk in range(CHUNKS):
        pieces, starts = pieces_of(sent_groups, chunk)
        outgoing = send_chunk(sent_place, hi, lo, sent_left, trailing, pieces, starts, width, chunk)
        received.append(partner(outgoing, "cube", 1))
    merged = None
    for chunk in range(CHUNKS):
        pieces, starts = pieces_of(kept_groups, chunk)
        merged = merge_chunk(
            kept_place, hi, lo, kept_left, trailing, chosen, received[chunk], pieces, starts, width, chunk, merged
        )
    return merged[None]


def solution(mesh):
    return jax.shard_map(
        local,
        mesh=mesh,
        in_specs=(
            P("cube", ("row", "col"), None),
            P("cube", None),
            P("cube", "row", "col"),
            P("cube", "row", "col"),
            P("cube", "row", "col"),
            P("cube", "row", "col"),
            P("cube", "row"),
        ),
        out_specs=P("cube", "row", "col"),
        check_vma=False,
    )
```

time: 2580 us -> 439 us (0.17)
  other arithmetic: 1470 us -> 6.31 us
  local copies, waits for them, and re-layouts: 521 us -> 8.65 us
  Pallas kernels: 0 us -> 167 us
  waiting for transfers between devices: 340 us -> 220 us
  between operations: 98.8 us -> 0.2 us
  matrix products: 91.1 us -> 0 us
  starting transfers between devices: 0.7 us -> 34 us
  blocking collectives: 27.6 us -> 0 us
    div x32 -> x0, other arithmetic: 723 us -> none  [small_inverses(): upper_rows[step] = fresh / upper[step, step]]
    sub x32 -> x0, other arithmetic: 556 us -> none  [small_inverses(): fresh = fresh - lower[step, inner] * lower_rows[inner]]
    slice x369 -> x0, local copies, waits for them, and re-layouts: 224 us -> none  [the longest x192 111 us: small_inverses(): column = work[step + 1:, step] / work[step, step]]
    pallas_call x0 -> x31, Pallas kernels: none -> 167 us  [the longest x15 79.4 us: merge_chunk(): pl.pallas_call(body, grid_spec=pltpu.PrefetchScalarGridSpec(num_scalar_pr...]
    neg x192 -> x0, other arithmetic: 156 us -> none  [small_inverses(): -column[:, None] * work[step, step + 1:][None, :]]
    ppermute x1 -> x31, waiting for transfers between devices: 339 us -> 220 us  [partner(): return lax.ppermute(block, axis, [(i, i ^ bits) for i in range(count)])]
    dot_general x220 -> x0, matrix products: 91.1 us -> none  [the longest x1 43.7 us: local(): jnp.dot(lower_panel, upper_panel, preferred_element_type=jnp.float32)]
    scatter-add x224 -> x0, local copies, waits for them, and re-layouts: 90.6 us -> none  [small_inverses(): work.at[step + 1:, step + 1:]]
  transfers between devices with their start and end apart: 2 -> 31, of which waited for: 1 -> 16; matrix products, arithmetic and copies ran while one was open for 76% -> 3% of each run, Pallas kernels for 0% -> 37%
where the time goes in v1:
time: 439 us; the launch traced here: 436 us
  waiting for transfers between devices  220 us (50%)
  Pallas kernels  167 us (38%)
  starting transfers between devices  34 us (8%)
  local copies, waits for them, and re-layouts  8.65 us (2%)
  other arithmetic  6.31 us (1%)
    ppermute x31, waiting for transfers between devices, partner(): return lax.ppermute(block, axis, [(i, i ^ bits) for i in range(count)])  220 us
    pallas_call x15, Pallas kernels, merge_chunk(): pl.pallas_call(body, grid_spec=pltpu.PrefetchScalarGridSpec(num_scalar_pr...  79.4 us
    pallas_call x15, Pallas kernels, send_chunk(): pl.pallas_call(send_kernel, grid_spec=pltpu.PrefetchScalarGridSpec(num_sc...  61.3 us
    ppermute x31, starting transfers between devices, partner(): return lax.ppermute(block, axis, [(i, i ^ bits) for i in range(count)])  34 us
    pallas_call x1, Pallas kernels, factor(): pl.pallas_call(factor_kernel, out_shape=(jax.ShapeDtypeStruct((size, size...  26.7 us
  transfers between devices with their start and end apart: 31, of which 16 were waited for; matrix products, arithmetic and copies ran while one was open for 3% of the time, Pallas kernels for 37%

profile of v1, /device:TPU:0, one launch (start us, length us, event | category | flops | bytes accessed | tf_op | source)
XLA Modules:
  0.0 436.5 jit_solution(4445003024821355890)
XLA Ops:
  26.0 9.4 %collective-permute-done.28.rest_3_ = bf16[64,1024]{1,0:T(8,128)(2,1)S(1)} collective-permute-done((bf16[64,1024]{1,0:T(8,128)(2,1)}, bf16[64,1024]{1,0:T(8,128)(2,1)S(1)}, u32[]{:S(2)}, u32[]{:S(2)}) %collective-permute-start.28) | collective-permute-done | bytes 131104 | tf_op jit(solution)/shard_map/ppermute | solution.py:18
  39.4 26.7 %factor.1 = (bf16[256,256]{1,0:T(8,128)(2,1)S(1)}, bf16[256,256]{1,0:T(8,128)(2,1)S(1)}, bf16[1024,256]{1,0:T(8,128)(2,1)S(1)}, bf16[1024,256]{1,0:T(8,128)(2,1)S(1)}) custom-call(f32[256,256]{1,0:T(8,128)S(1)} %pad_maximum_fusion.1.block, s32[256,1]{1,0:T(8,128)S(1)} %get-tuple-element.14.order_of_diag, s32[256,1]{1,0:T(8,128)S(1)} %get-tuple-element.13.order_of_upper, ...), custom_call_target="tpu_custom_call" | custom-call | flops 30000001024 | bytes 3000000 | tf_op jit(solution)/shard_map/factor/pallas_call | solution.py:111
  66.2 4.1 send_part.29
  70.3 22.7 %collective-permute-done.5.rest_2_ = bf16[64,4096]{1,0:T(8,128)(2,1)S(1)} collective-permute-done((bf16[64,4096]{1,0:T(8,128)(2,1)}, bf16[64,4096]{1,0:T(8,128)(2,1)S(1)}, u32[]{:S(2)}, u32[]{:S(2)}) %collective-permute-start.5) | collective-permute-done | bytes 524320 | tf_op jit(solution)/shard_map/ppermute | solution.py:18
  129.3 12.5 %collective-permute-done.29.received = bf16[1024,512]{1,0:T(8,128)(2,1)} collective-permute-done((bf16[1024,512]{1,0:T(8,128)(2,1)}, bf16[1024,512]{1,0:T(8,128)(2,1)}, u32[]{:S(2)}, u32[]{:S(2)}) %collective-permute-start.29) | collective-permute-done | bytes 1048608 | tf_op jit(solution)/shard_map/ppermute | solution.py:18
  147.5 16.8 %collective-permute-done.25.received = bf16[1024,512]{1,0:T(8,128)(2,1)} collective-permute-done((bf16[1024,512]{1,0:T(8,128)(2,1)}, bf16[1024,512]{1,0:T(8,128)(2,1)}, u32[]{:S(2)}, u32[]{:S(2)}) %collective-permute-start.25) | collective-permute-done | bytes 1048608 | tf_op jit(solution)/shard_map/ppermute | solution.py:18
  169.9 16.7 %collective-permute-done.24.received = bf16[1024,512]{1,0:T(8,128)(2,1)S(1)} collective-permute-done((bf16[1024,512]{1,0:T(8,128)(2,1)}, bf16[1024,512]{1,0:T(8,128)(2,1)S(1)}, u32[]{:S(2)}, u32[]{:S(2)}) %collective-permute-start.24) | collective-permute-done | bytes 1048608 | tf_op jit(solution)/shard_map/ppermute | solution.py:18
  192.3 16.8 %collective-permute-done.23.received = bf16[1024,512]{1,0:T(8,128)(2,1)S(1)} collective-permute-done((bf16[1024,512]{1,0:T(8,128)(2,1)}, bf16[1024,512]{1,0:T(8,128)(2,1)S(1)}, u32[]{:S(2)}, u32[]{:S(2)}) %collective-permute-start.23) | collective-permute-done | bytes 1048608 | tf_op jit(solution)/shard_map/ppermute | solution.py:18
  228.8 4.2 send_part.15
  233.0 5.1 %merge_part.15.rest_4_ = bf16[1024,7680]{1,0:T(8,128)(2,1)} custom-call(s32[1]{0:T(128)} %bitcast.place, bf16[256,256]{1,0:T(8,128)(2,1)S(1)} %get-tuple-element.9.hi, bf16[256,256]{1,0:T(8,128)(2,1)S(1)} %get-tuple-element.10.lo, bf16[1024,256]{1,0:T(8,128)(2,1)S(1)} %get-tuple-element.11.left, bf16[1024,15360]{1,0:T(8,128)(2,1)} %bitcast.66, ...), custom_call_target="tpu_custom_call" | custom-call | flops 1342177280 | bytes 4194304 | tf_op jit(solution)/shard_map/merge_part/pallas_call | solution.py:213
  238.5 5.4 %merge_part.16.rest_4_ = bf16[1024,7680]{1,0:T(8,128)(2,1)} custom-call(s32[1]{0:T(128)} %bitcast.place, bf16[256,256]{1,0:T(8,128)(2,1)S(1)} %get-tuple-element.9.hi, bf16[256,256]{1,0:T(8,128)(2,1)S(1)} %get-tuple-element.10.lo, bf16[1024,256]{1,0:T(8,128)(2,1)S(1)} %get-tuple-element.11.left, ...), custom_call_target="tpu_custom_call", output_to_operand_aliasing={{}: (11, {})} | custom-call | flops 1342177280 | bytes 4194304 | tf_op jit(solution)/shard_map/merge_part/pallas_call | solution.py:213
  243.9 10.3 %collective-permute-done.21.received = bf16[1024,512]{1,0:T(8,128)(2,1)} collective-permute-done((bf16[1024,512]{1,0:T(8,128)(2,1)}, bf16[1024,512]{1,0:T(8,128)(2,1)}, u32[]{:S(2)}, u32[]{:S(2)}) %collective-permute-start.21) | collective-permute-done | bytes 1048608 | tf_op jit(solution)/shard_map/ppermute | solution.py:18
  255.8 5.4 %merge_part.17.rest_4_ = bf16[1024,7680]{1,0:T(8,128)(2,1)} custom-call(s32[1]{0:T(128)} %bitcast.place, bf16[256,256]{1,0:T(8,128)(2,1)S(1)} %get-tuple-element.9.hi, bf16[256,256]{1,0:T(8,128)(2,1)S(1)} %get-tuple-element.10.lo, bf16[1024,256]{1,0:T(8,128)(2,1)S(1)} %get-tuple-element.11.left, ...), custom_call_target="tpu_custom_call", output_to_operand_aliasing={{}: (11, {})} | custom-call | flops 1342177280 | bytes 4194304 | tf_op jit(solution)/shard_map/merge_part/pallas_call | solution.py:213
  261.1 15.5 %collective-permute-done.17.received = bf16[1024,512]{1,0:T(8,128)(2,1)} collective-permute-done((bf16[1024,512]{1,0:T(8,128)(2,1)}, bf16[1024,512]{1,0:T(8,128)(2,1)}, u32[]{:S(2)}, u32[]{:S(2)}) %collective-permute-start.17) | collective-permute-done | bytes 1048608 | tf_op jit(solution)/shard_map/ppermute | solution.py:18
  278.2 5.0 %merge_part.18.rest_4_ = bf16[1024,7680]{1,0:T(8,128)(2,1)} custom-call(s32[1]{0:T(128)} %bitcast.place, bf16[256,256]{1,0:T(8,128)(2,1)S(1)} %get-tuple-element.9.hi, bf16[256,256]{1,0:T(8,128)(2,1)S(1)} %get-tuple-element.10.lo, bf16[1024,256]{1,0:T(8,128)(2,1)S(1)} %get-tuple-element.11.left, ...), custom_call_target="tpu_custom_call", output_to_operand_aliasing={{}: (11, {})} | custom-call | flops 1342177280 | bytes 4194304 | tf_op jit(solution)/shard_map/merge_part/pallas_call | solution.py:213
  283.3 15.9 %collective-permute-done.16.received = bf16[1024,512]{1,0:T(8,128)(2,1)} collective-permute-done((bf16[1024,512]{1,0:T(8,128)(2,1)}, bf16[1024,512]{1,0:T(8,128)(2,1)}, u32[]{:S(2)}, u32[]{:S(2)}) %collective-permute-start.16) | collective-permute-done | bytes 1048608 | tf_op jit(solution)/shard_map/ppermute | solution.py:18
  300.7 5.0 %merge_part.19.rest_4_ = bf16[1024,7680]{1,0:T(8,128)(2,1)} custom-call(s32[1]{0:T(128)} %bitcast.place, bf16[256,256]{1,0:T(8,128)(2,1)S(1)} %get-tuple-element.9.hi, bf16[256,256]{1,0:T(8,128)(2,1)S(1)} %get-tuple-element.10.lo, bf16[1024,256]{1,0:T(8,128)(2,1)S(1)} %get-tuple-element.11.left, ...), custom_call_target="tpu_custom_call", output_to_operand_aliasing={{}: (11, {})} | custom-call | flops 1342177280 | bytes 4194304 | tf_op jit(solution)/shard_map/merge_part/pallas_call | solution.py:213
  305.7 15.9 %collective-permute-done.15.received = bf16[1024,512]{1,0:T(8,128)(2,1)} collective-permute-done((bf16[1024,512]{1,0:T(8,128)(2,1)}, bf16[1024,512]{1,0:T(8,128)(2,1)}, u32[]{:S(2)}, u32[]{:S(2)}) %collective-permute-start.15) | collective-permute-done | bytes 1048608 | tf_op jit(solution)/shard_map/ppermute | solution.py:18
  323.2 5.0 %merge_part.20.rest_4_ = bf16[1024,7680]{1,0:T(8,128)(2,1)} custom-call(s32[1]{0:T(128)} %bitcast.place, bf16[256,256]{1,0:T(8,128)(2,1)S(1)} %get-tuple-element.9.hi, bf16[256,256]{1,0:T(8,128)(2,1)S(1)} %get-tuple-element.10.lo, bf16[1024,256]{1,0:T(8,128)(2,1)S(1)} %get-tuple-element.11.left, ...), custom_call_target="tpu_custom_call", output_to_operand_aliasing={{}: (11, {})} | custom-call | flops 1342177280 | bytes 4194304 | tf_op jit(solution)/shard_map/merge_part/pallas_call | solution.py:213
  328.2 5.4 %merge_part.21.rest_4_ = bf16[1024,7680]{1,0:T(8,128)(2,1)} custom-call(s32[1]{0:T(128)} %bitcast.place, bf16[256,256]{1,0:T(8,128)(2,1)S(1)} %get-tuple-element.9.hi, bf16[256,256]{1,0:T(8,128)(2,1)S(1)} %get-tuple-element.10.lo, bf16[1024,256]{1,0:T(8,128)(2,1)S(1)} %get-tuple-element.11.left, ...), custom_call_target="tpu_custom_call", output_to_operand_aliasing={{}: (11, {})} | custom-call | flops 1342177280 | bytes 4194304 | tf_op jit(solution)/shard_map/merge_part/pallas_call | solution.py:213
  333.6 5.4 %merge_part.22.rest_4_ = bf16[1024,7680]{1,0:T(8,128)(2,1)} custom-call(s32[1]{0:T(128)} %bitcast.place, bf16[256,256]{1,0:T(8,128)(2,1)S(1)} %get-tuple-element.9.hi, bf16[256,256]{1,0:T(8,128)(2,1)S(1)} %get-tuple-element.10.lo, bf16[1024,256]{1,0:T(8,128)(2,1)S(1)} %get-tuple-element.11.left, ...), custom_call_target="tpu_custom_call", output_to_operand_aliasing={{}: (11, {})} | custom-call | flops 1342177280 | bytes 4194304 | tf_op jit(solution)/shard_map/merge_part/pallas_call | solution.py:213
  339.0 5.4 %merge_part.23.rest_4_ = bf16[1024,7680]{1,0:T(8,128)(2,1)} custom-call(s32[1]{0:T(128)} %bitcast.place, bf16[256,256]{1,0:T(8,128)(2,1)S(1)} %get-tuple-element.9.hi, bf16[256,256]{1,0:T(8,128)(2,1)S(1)} %get-tuple-element.10.lo, bf16[1024,256]{1,0:T(8,128)(2,1)S(1)} %get-tuple-element.11.left, ...), custom_call_target="tpu_custom_call", output_to_operand_aliasing={{}: (11, {})} | custom-call | flops 1342177280 | bytes 4194304 | tf_op jit(solution)/shard_map/merge_part/pallas_call | solution.py:213
  344.4 5.4 %merge_part.24.rest_4_ = bf16[1024,7680]{1,0:T(8,128)(2,1)} custom-call(s32[1]{0:T(128)} %bitcast.place, bf16[256,256]{1,0:T(8,128)(2,1)S(1)} %get-tuple-element.9.hi, bf16[256,256]{1,0:T(8,128)(2,1)S(1)} %get-tuple-element.10.lo, bf16[1024,256]{1,0:T(8,128)(2,1)S(1)} %get-tuple-element.11.left, ...), custom_call_target="tpu_custom_call", output_to_operand_aliasing={{}: (11, {})} | custom-call | flops 1342177280 | bytes 4194304 | tf_op jit(solution)/shard_map/merge_part/pallas_call | solution.py:213
  349.8 5.4 %merge_part.25.rest_4_ = bf16[1024,7680]{1,0:T(8,128)(2,1)} custom-call(s32[1]{0:T(128)} %bitcast.place, bf16[256,256]{1,0:T(8,128)(2,1)S(1)} %get-tuple-element.9.hi, bf16[256,256]{1,0:T(8,128)(2,1)S(1)} %get-tuple-element.10.lo, bf16[1024,256]{1,0:T(8,128)(2,1)S(1)} %get-tuple-element.11.left, ...), custom_call_target="tpu_custom_call", output_to_operand_aliasing={{}: (11, {})} | custom-call | flops 1342177280 | bytes 4194304 | tf_op jit(solution)/shard_map/merge_part/pallas_call | solution.py:213
  355.2 11.3 %collective-permute-done.13.received = bf16[1024,512]{1,0:T(8,128)(2,1)} collective-permute-done((bf16[1024,512]{1,0:T(8,128)(2,1)}, bf16[1024,512]{1,0:T(8,128)(2,1)}, u32[]{:S(2)}, u32[]{:S(2)}) %collective-permute-start.13) | collective-permute-done | bytes 1048608 | tf_op jit(solution)/shard_map/ppermute | solution.py:18
  366.5 5.4 %merge_part.26.rest_4_ = bf16[1024,7680]{1,0:T(8,128)(2,1)} custom-call(s32[1]{0:T(128)} %bitcast.place, bf16[256,256]{1,0:T(8,128)(2,1)S(1)} %get-tuple-element.9.hi, bf16[256,256]{1,0:T(8,128)(2,1)S(1)} %get-tuple-element.10.lo, bf16[1024,256]{1,0:T(8,128)(2,1)S(1)} %get-tuple-element.11.left, ...), custom_call_target="tpu_custom_call", output_to_operand_aliasing={{}: (11, {})} | custom-call | flops 1342177280 | bytes 4194304 | tf_op jit(solution)/shard_map/merge_part/pallas_call | solution.py:213
  371.9 17.1 %collective-permute-done.12.received = bf16[1024,512]{1,0:T(8,128)(2,1)} collective-permute-done((bf16[1024,512]{1,0:T(8,128)(2,1)}, bf16[1024,512]{1,0:T(8,128)(2,1)}, u32[]{:S(2)}, u32[]{:S(2)}) %collective-permute-start.12) | collective-permute-done | bytes 1048608 | tf_op jit(solution)/shard_map/ppermute | solution.py:18
  389.0 5.4 %merge_part.27.rest_4_ = bf16[1024,7680]{1,0:T(8,128)(2,1)} custom-call(s32[1]{0:T(128)} %bitcast.place, bf16[256,256]{1,0:T(8,128)(2,1)S(1)} %get-tuple-element.9.hi, bf16[256,256]{1,0:T(8,128)(2,1)S(1)} %get-tuple-element.10.lo, bf16[1024,256]{1,0:T(8,128)(2,1)S(1)} %get-tuple-element.11.left, ...), custom_call_target="tpu_custom_call", output_to_operand_aliasing={{}: (11, {})} | custom-call | flops 1342177280 | bytes 4194304 | tf_op jit(solution)/shard_map/merge_part/pallas_call | solution.py:213
  394.4 17.1 %collective-permute-done.11.received = bf16[1024,512]{1,0:T(8,128)(2,1)} collective-permute-done((bf16[1024,512]{1,0:T(8,128)(2,1)}, bf16[1024,512]{1,0:T(8,128)(2,1)}, u32[]{:S(2)}, u32[]{:S(2)}) %collective-permute-start.11) | collective-permute-done | bytes 1048608 | tf_op jit(solution)/shard_map/ppermute | solution.py:18
  411.5 5.4 %merge_part.28.rest_4_ = bf16[1024,7680]{1,0:T(8,128)(2,1)} custom-call(s32[1]{0:T(128)} %bitcast.place, bf16[256,256]{1,0:T(8,128)(2,1)S(1)} %get-tuple-element.9.hi, bf16[256,256]{1,0:T(8,128)(2,1)S(1)} %get-tuple-element.10.lo, bf16[1024,256]{1,0:T(8,128)(2,1)S(1)} %get-tuple-element.11.left, ...), custom_call_target="tpu_custom_call", output_to_operand_aliasing={{}: (11, {})} | custom-call | flops 1342177280 | bytes 4194304 | tf_op jit(solution)/shard_map/merge_part/pallas_call | solution.py:213
  416.9 14.3 %collective-permute-done.7.received = bf16[1024,512]{1,0:T(8,128)(2,1)} collective-permute-done((bf16[1024,512]{1,0:T(8,128)(2,1)}, bf16[1024,512]{1,0:T(8,128)(2,1)}, u32[]{:S(2)}, u32[]{:S(2)}) %collective-permute-start.7) | collective-permute-done | bytes 1048608 | tf_op jit(solution)/shard_map/ppermute | solution.py:18
  431.1 5.4 %merge_part.29 = bf16[1024,7680]{1,0:T(8,128)(2,1)} custom-call(s32[1]{0:T(128)} %bitcast.place, bf16[256,256]{1,0:T(8,128)(2,1)S(1)} %get-tuple-element.9.hi, bf16[256,256]{1,0:T(8,128)(2,1)S(1)} %get-tuple-element.10.lo, bf16[1024,256]{1,0:T(8,128)(2,1)S(1)} %get-tuple-element.11.left, ...), custom_call_target="tpu_custom_call", output_to_operand_aliasing={{}: (11, {})} | custom-call | flops 1342177280 | bytes 4194304 | tf_op jit(solution)/shard_map/merge_part/pallas_call | solution.py:213
  (95 shorter events, 109.7 us)
Async XLA Ops:
  0.9 13.5 %collective-permute-start.26 = (bf16[64,1024]{1,0:T(8,128)(2,1)S(1)}, bf16[64,1024]{1,0:T(8,128)(2,1)S(1)}, u32[]{:S(2)}, u32[]{:S(2)}) collective-permute-start(bf16[64,1024]{1,0:T(8,128)(2,1)S(1)} %dynamic-slice_bitcast_fusion.3), channel_id=1, source_target_pairs={{0,2},{2,0},{4,6},{6,4},{1,3},{3,1},{5,7},{7,5},{8,10},{10,8},{12,... | collective-permute-start | bytes 393224 | tf_op jit(solution)/shard_map/ppermute | solution.py:18
  1.4 13.1 %collective-permute-start.27 = (bf16[64,1024]{1,0:T(8,128)(2,1)S(1)}, bf16[64,1024]{1,0:T(8,128)(2,1)S(1)}, u32[]{:S(2)}, u32[]{:S(2)}) collective-permute-start(bf16[64,1024]{1,0:T(8,128)(2,1)S(1)} %dynamic-slice_bitcast_fusion.3), channel_id=1, source_target_pairs={{0,4},{2,6},{4,0},{6,2},{1,5},{3,7},{5,1},{7,3},{8,12},{10,14},{12... | collective-permute-start | bytes 393224 | tf_op jit(solution)/shard_map/ppermute | solution.py:18
  4.0 6.1 %collective-permute-start = (f32[32,256]{1,0:T(8,128)}, f32[32,256]{1,0:T(8,128)S(1)}, u32[]{:S(2)}, u32[]{:S(2)}) collective-permute-start(f32[32,256]{1,0:T(8,128)} %bitcast.82), channel_id=1, source_target_pairs={{0,1},{1,0},{2,3},{3,2},{4,5},{5,4},{6,7},{7,6},{8,9},{9,8},{10,11... | collective-permute-start | bytes 98312 | tf_op jit(solution)/shard_map/ppermute | solution.py:18
  5.5 16.7 %collective-permute-start.3 = (bf16[1024,128]{1,0:T(8,128)(2,1)}, bf16[1024,128]{1,0:T(8,128)(2,1)}, u32[]{:S(2)}, u32[]{:S(2)}) collective-permute-start(bf16[1024,128]{1,0:T(8,128)(2,1)} %bitcast.86), channel_id=1, source_target_pairs={{0,1},{1,0},{2,3},{3,2},{4,5},{5,4},{6,7},{7,6},{8,9},{9,8},{10,11... | collective-permute-start | bytes 786440 | tf_op jit(solution)/shard_map/ppermute | solution.py:18
  7.9 30.6 %collective-permute-start.4 = (bf16[64,4096]{1,0:T(8,128)(2,1)}, bf16[64,4096]{1,0:T(8,128)(2,1)S(1)}, u32[]{:S(2)}, u32[]{:S(2)}) collective-permute-start(bf16[64,4096]{1,0:T(8,128)(2,1)} %dynamic-slice_bitcast_fusion.1), channel_id=1, source_target_pairs={{0,2},{2,0},{4,6},{6,4},{1,3},{3,1},{5,7},{7,5},{8,10},{10,8},{12,... | collective-permute-start | bytes 1572872 | tf_op jit(solution)/shard_map/ppermute | solution.py:18
  10.9 2.3 collective-permute-start.1
  14.1 6.5 %collective-permute-start.2 = (f32[128,256]{1,0:T(8,128)S(1)}, f32[128,256]{1,0:T(8,128)}, u32[]{:S(2)}, u32[]{:S(2)}) collective-permute-start(f32[128,256]{1,0:T(8,128)S(1)} %pad_maximum_fusion.2), channel_id=1, source_target_pairs={{0,4},{1,5},{2,6},{3,7},{4,0},{5,1},{6,2},{7,3},{8,12},{9,13},{10,... | collective-permute-start | bytes 393224 | tf_op jit(solution)/shard_map/ppermute | solution.py:18
  14.5 21.6 %collective-permute-start.18 = (bf16[64,2560]{1,0:T(8,128)(2,1)S(1)}, bf16[64,2560]{1,0:T(8,128)(2,1)S(1)}, u32[]{:S(2)}, u32[]{:S(2)}) collective-permute-start(bf16[64,2560]{1,0:T(8,128)(2,1)S(1)} %dynamic-slice_bitcast_fusion.2), channel_id=1, source_target_pairs={{0,2},{2,0},{4,6},{6,4},{1,3},{3,1},{5,7},{7,5},{8,10},{10,8},{12,... | collective-permute-start | bytes 983048 | tf_op jit(solution)/shard_map/ppermute | solution.py:18
  14.6 21.9 %collective-permute-start.19 = (bf16[64,2560]{1,0:T(8,128)(2,1)S(1)}, bf16[64,2560]{1,0:T(8,128)(2,1)S(1)}, u32[]{:S(2)}, u32[]{:S(2)}) collective-permute-start(bf16[64,2560]{1,0:T(8,128)(2,1)S(1)} %dynamic-slice_bitcast_fusion.2), channel_id=1, source_target_pairs={{0,4},{2,6},{4,0},{6,2},{1,5},{3,7},{5,1},{7,3},{8,12},{10,14},{12... | collective-permute-start | bytes 983048 | tf_op jit(solution)/shard_map/ppermute | solution.py:18
  20.6 17.3 %collective-permute-start.20 = (bf16[64,2560]{1,0:T(8,128)(2,1)S(1)}, bf16[64,2560]{1,0:T(8,128)(2,1)S(1)}, u32[]{:S(2)}, u32[]{:S(2)}) collective-permute-start(bf16[64,2560]{1,0:T(8,128)(2,1)S(1)} %dynamic-slice_bitcast_fusion.2), channel_id=1, source_target_pairs={{0,6},{2,4},{4,2},{6,0},{1,7},{3,5},{5,3},{7,1},{8,14},{10,12},{12... | collective-permute-start | bytes 983048 | tf_op jit(solution)/shard_map/ppermute | solution.py:18
  22.2 13.2 %collective-permute-start.28 = (bf16[64,1024]{1,0:T(8,128)(2,1)}, bf16[64,1024]{1,0:T(8,128)(2,1)S(1)}, u32[]{:S(2)}, u32[]{:S(2)}) collective-permute-start(bf16[64,1024]{1,0:T(8,128)(2,1)} %copy-done.7), channel_id=1, source_target_pairs={{0,6},{2,4},{4,2},{6,0},{1,7},{3,5},{5,3},{7,1},{8,14},{10,12},{12... | collective-permute-start | bytes 393224 | tf_op jit(solution)/shard_map/ppermute | solution.py:18
  35.4 72.5 %collective-permute-start.10 = (bf16[64,7680]{1,0:T(8,128)(2,1)}, bf16[64,7680]{1,0:T(8,128)(2,1)S(1)}, u32[]{:S(2)}, u32[]{:S(2)}) collective-permute-start(bf16[64,7680]{1,0:T(8,128)(2,1)} %dynamic-slice_bitcast_fusion), channel_id=1, source_target_pairs={{0,6},{2,4},{4,2},{6,0},{1,7},{3,5},{5,3},{7,1},{8,14},{10,12},{12... | collective-permute-start | bytes 2949128 | tf_op jit(solution)/shard_map/ppermute | solution.py:18
  36.1 76.3 %collective-permute-start.8 = (bf16[64,7680]{1,0:T(8,128)(2,1)}, bf16[64,7680]{1,0:T(8,128)(2,1)S(1)}, u32[]{:S(2)}, u32[]{:S(2)}) collective-permute-start(bf16[64,7680]{1,0:T(8,128)(2,1)} %dynamic-slice_bitcast_fusion), channel_id=1, source_target_pairs={{0,2},{2,0},{4,6},{6,4},{1,3},{3,1},{5,7},{7,5},{8,10},{10,8},{12,... | collective-permute-start | bytes 2949128 | tf_op jit(solution)/shard_map/ppermute | solution.py:18
  36.5 81.7 %collective-permute-start.9 = (bf16[64,7680]{1,0:T(8,128)(2,1)}, bf16[64,7680]{1,0:T(8,128)(2,1)S(1)}, u32[]{:S(2)}, u32[]{:S(2)}) collective-permute-start(bf16[64,7680]{1,0:T(8,128)(2,1)} %dynamic-slice_bitcast_fusion), channel_id=1, source_target_pairs={{0,4},{2,6},{4,0},{6,2},{1,5},{3,7},{5,1},{7,3},{8,12},{10,14},{12... | collective-permute-start | bytes 2949128 | tf_op jit(solution)/shard_map/ppermute | solution.py:18
  37.9 55.0 %collective-permute-start.5 = (bf16[64,4096]{1,0:T(8,128)(2,1)}, bf16[64,4096]{1,0:T(8,128)(2,1)S(1)}, u32[]{:S(2)}, u32[]{:S(2)}) collective-permute-start(bf16[64,4096]{1,0:T(8,128)(2,1)} %dynamic-slice_bitcast_fusion.1), channel_id=1, source_target_pairs={{0,4},{2,6},{4,0},{6,2},{1,5},{3,7},{5,1},{7,3},{8,12},{10,14},{12... | collective-permute-start | bytes 1572872 | tf_op jit(solution)/shard_map/ppermute | solution.py:18
  38.5 63.8 %collective-permute-start.6 = (bf16[64,4096]{1,0:T(8,128)(2,1)}, bf16[64,4096]{1,0:T(8,128)(2,1)S(1)}, u32[]{:S(2)}, u32[]{:S(2)}) collective-permute-start(bf16[64,4096]{1,0:T(8,128)(2,1)} %dynamic-slice_bitcast_fusion.1), channel_id=1, source_target_pairs={{0,6},{2,4},{4,2},{6,0},{1,7},{3,5},{5,3},{7,1},{8,14},{10,12},{12... | collective-permute-start | bytes 1572872 | tf_op jit(solution)/shard_map/ppermute | solution.py:18
  92.9 29.7 %collective-permute-start.30 = (bf16[1024,512]{1,0:T(8,128)(2,1)}, bf16[1024,512]{1,0:T(8,128)(2,1)S(1)}, u32[]{:S(2)}, u32[]{:S(2)}) collective-permute-start(bf16[1024,512]{1,0:T(8,128)(2,1)} %send_part.29), channel_id=1, source_target_pairs={{0,8},{8,0},{16,24},{24,16},{1,9},{9,1},{17,25},{25,17},{2,10},{10... | collective-permute-start | bytes 3145736 | tf_op jit(solution)/shard_map/ppermute | solution.py:18
  102.3 39.6 %collective-permute-start.29 = (bf16[1024,512]{1,0:T(8,128)(2,1)}, bf16[1024,512]{1,0:T(8,128)(2,1)}, u32[]{:S(2)}, u32[]{:S(2)}) collective-permute-start(bf16[1024,512]{1,0:T(8,128)(2,1)} %send_part.28), channel_id=1, source_target_pairs={{0,8},{8,0},{16,24},{24,16},{1,9},{9,1},{17,25},{25,17},{2,10},{10... | collective-permute-start | bytes 3145736 | tf_op jit(solution)/shard_map/ppermute | solution.py:18
  107.9 56.4 %collective-permute-start.25 = (bf16[1024,512]{1,0:T(8,128)(2,1)}, bf16[1024,512]{1,0:T(8,128)(2,1)}, u32[]{:S(2)}, u32[]{:S(2)}) collective-permute-start(bf16[1024,512]{1,0:T(8,128)(2,1)} %send_part.27), channel_id=1, source_target_pairs={{0,8},{8,0},{16,24},{24,16},{1,9},{9,1},{17,25},{25,17},{2,10},{10... | collective-permute-start | bytes 3145736 | tf_op jit(solution)/shard_map/ppermute | solution.py:18
  112.4 74.2 %collective-permute-start.24 = (bf16[1024,512]{1,0:T(8,128)(2,1)}, bf16[1024,512]{1,0:T(8,128)(2,1)S(1)}, u32[]{:S(2)}, u32[]{:S(2)}) collective-permute-start(bf16[1024,512]{1,0:T(8,128)(2,1)} %send_part.26), channel_id=1, source_target_pairs={{0,8},{8,0},{16,24},{24,16},{1,9},{9,1},{17,25},{25,17},{2,10},{10... | collective-permute-start | bytes 3145736 | tf_op jit(solution)/shard_map/ppermute | solution.py:18
  118.1 91.0 %collective-permute-start.23 = (bf16[1024,512]{1,0:T(8,128)(2,1)}, bf16[1024,512]{1,0:T(8,128)(2,1)S(1)}, u32[]{:S(2)}, u32[]{:S(2)}) collective-permute-start(bf16[1024,512]{1,0:T(8,128)(2,1)} %send_part.25), channel_id=1, source_target_pairs={{0,8},{8,0},{16,24},{24,16},{1,9},{9,1},{17,25},{25,17},{2,10},{10... | collective-permute-start | bytes 3145736 | tf_op jit(solution)/shard_map/ppermute | solution.py:18
  123.6 114.4 %collective-permute-start.22 = (bf16[1024,512]{1,0:T(8,128)(2,1)}, bf16[1024,512]{1,0:T(8,128)(2,1)S(1)}, u32[]{:S(2)}, u32[]{:S(2)}) collective-permute-start(bf16[1024,512]{1,0:T(8,128)(2,1)} %send_part.24), channel_id=1, source_target_pairs={{0,8},{8,0},{16,24},{24,16},{1,9},{9,1},{17,25},{25,17},{2,10},{10... | collective-permute-start | bytes 3145736 | tf_op jit(solution)/shard_map/ppermute | solution.py:18
  141.8 112.4 %collective-permute-start.21 = (bf16[1024,512]{1,0:T(8,128)(2,1)}, bf16[1024,512]{1,0:T(8,128)(2,1)}, u32[]{:S(2)}, u32[]{:S(2)}) collective-permute-start(bf16[1024,512]{1,0:T(8,128)(2,1)} %send_part.23), channel_id=1, source_target_pairs={{0,8},{8,0},{16,24},{24,16},{1,9},{9,1},{17,25},{25,17},{2,10},{10... | collective-permute-start | bytes 3145736 | tf_op jit(solution)/shard_map/ppermute | solution.py:18
  164.3 112.4 %collective-permute-start.17 = (bf16[1024,512]{1,0:T(8,128)(2,1)}, bf16[1024,512]{1,0:T(8,128)(2,1)}, u32[]{:S(2)}, u32[]{:S(2)}) collective-permute-start(bf16[1024,512]{1,0:T(8,128)(2,1)} %send_part.22), channel_id=1, source_target_pairs={{0,8},{8,0},{16,24},{24,16},{1,9},{9,1},{17,25},{25,17},{2,10},{10... | collective-permute-start | bytes 3145736 | tf_op jit(solution)/shard_map/ppermute | solution.py:18
  169.9 40.8 %copy-start.8 = (s32[1,1024]{1,0:T(1,128)S(1)}, s32[1,1024]{1,0:T(1,128)}, u32[]{:S(2)}) copy-start(s32[1,1024]{1,0:T(1,128)} %param.13) | copy-start | bytes 12292
  186.7 112.5 %collective-permute-start.16 = (bf16[1024,512]{1,0:T(8,128)(2,1)}, bf16[1024,512]{1,0:T(8,128)(2,1)}, u32[]{:S(2)}, u32[]{:S(2)}) collective-permute-start(bf16[1024,512]{1,0:T(8,128)(2,1)} %send_part.21), channel_id=1, source_target_pairs={{0,8},{8,0},{16,24},{24,16},{1,9},{9,1},{17,25},{25,17},{2,10},{10... | collective-permute-start | bytes 3145736 | tf_op jit(solution)/shard_map/ppermute | solution.py:18
  209.1 112.5 %collective-permute-start.15 = (bf16[1024,512]{1,0:T(8,128)(2,1)}, bf16[1024,512]{1,0:T(8,128)(2,1)}, u32[]{:S(2)}, u32[]{:S(2)}) collective-permute-start(bf16[1024,512]{1,0:T(8,128)(2,1)} %send_part.20), channel_id=1, source_target_pairs={{0,8},{8,0},{16,24},{24,16},{1,9},{9,1},{17,25},{25,17},{2,10},{10... | collective-permute-start | bytes 3145736 | tf_op jit(solution)/shard_map/ppermute | solution.py:18
  238.1 111.8 %collective-permute-start.14 = (bf16[1024,512]{1,0:T(8,128)(2,1)}, bf16[1024,512]{1,0:T(8,128)(2,1)}, u32[]{:S(2)}, u32[]{:S(2)}) collective-permute-start(bf16[1024,512]{1,0:T(8,128)(2,1)} %send_part.19), channel_id=1, source_target_pairs={{0,8},{8,0},{16,24},{24,16},{1,9},{9,1},{17,25},{25,17},{2,10},{10... | collective-permute-start | bytes 3145736 | tf_op jit(solution)/shard_map/ppermute | solution.py:18
  254.2 112.4 %collective-permute-start.13 = (bf16[1024,512]{1,0:T(8,128)(2,1)}, bf16[1024,512]{1,0:T(8,128)(2,1)}, u32[]{:S(2)}, u32[]{:S(2)}) collective-permute-start(bf16[1024,512]{1,0:T(8,128)(2,1)} %send_part.18), channel_id=1, source_target_pairs={{0,8},{8,0},{16,24},{24,16},{1,9},{9,1},{17,25},{25,17},{2,10},{10... | collective-permute-start | bytes 3145736 | tf_op jit(solution)/shard_map/ppermute | solution.py:18
  276.6 112.4 %collective-permute-start.12 = (bf16[1024,512]{1,0:T(8,128)(2,1)}, bf16[1024,512]{1,0:T(8,128)(2,1)}, u32[]{:S(2)}, u32[]{:S(2)}) collective-permute-start(bf16[1024,512]{1,0:T(8,128)(2,1)} %send_part.17), channel_id=1, source_target_pairs={{0,8},{8,0},{16,24},{24,16},{1,9},{9,1},{17,25},{25,17},{2,10},{10... | collective-permute-start | bytes 3145736 | tf_op jit(solution)/shard_map/ppermute | solution.py:18
  299.1 112.4 %collective-permute-start.11 = (bf16[1024,512]{1,0:T(8,128)(2,1)}, bf16[1024,512]{1,0:T(8,128)(2,1)}, u32[]{:S(2)}, u32[]{:S(2)}) collective-permute-start(bf16[1024,512]{1,0:T(8,128)(2,1)} %send_part.16), channel_id=1, source_target_pairs={{0,8},{8,0},{16,24},{24,16},{1,9},{9,1},{17,25},{25,17},{2,10},{10... | collective-permute-start | bytes 3145736 | tf_op jit(solution)/shard_map/ppermute | solution.py:18
  321.6 109.5 %collective-permute-start.7 = (bf16[1024,512]{1,0:T(8,128)(2,1)}, bf16[1024,512]{1,0:T(8,128)(2,1)}, u32[]{:S(2)}, u32[]{:S(2)}) collective-permute-start(bf16[1024,512]{1,0:T(8,128)(2,1)} %send_part.15), channel_id=1, source_target_pairs={{0,8},{8,0},{16,24},{24,16},{1,9},{9,1},{17,25},{25,17},{2,10},{10... | collective-permute-start | bytes 3145736 | tf_op jit(solution)/shard_map/ppermute | solution.py:18
  (8 other events, 91.0 us)

commit v2 on v1

--- a/solution.py
+++ b/solution.py
@@ -8,6 +8,10 @@
 from jax.sharding import PartitionSpec as P
 
 CHUNKS = 15
+RAW = 2
+EARLY = 2
+AHEAD = 3
+BEHIND = 6
 ROW_STEPS = 4
 HIGH = lax.Precision.HIGHEST
 VMEM_LIMIT = 48 * 1024 * 1024
@@ -70,7 +74,7 @@
     return lower, upper
 
 
-def factor_kernel(block, order_of_diag, order_of_upper, order_of_lower, panel, mask, hi, lo, sent, kept):
+def factor_kernel(block, order_of_diag, order_of_upper, order_of_lower, panel, mask, hi, lo, plain, sent, kept):
     size = block.shape[0]
     half = size // 2
     lane = lax.broadcasted_iota(jnp.int32, (size, size), 1)
@@ -94,11 +98,14 @@
         [jnp.concatenate([upper_one, corner_upper], 1), jnp.concatenate([zero, upper_two], 1)], 0
     )
     hi[...], lo[...] = split(exact(lower_inv, chosen(order_of_upper)))
-    upper_hi, upper_lo = split(exact(chosen(order_of_lower), upper_inv))
+    row = lax.broadcasted_iota(jnp.int32, (size, size), 0)
+    in_order = jnp.where(order_of_lower[...] == row, 1.0, 0.0)
+    upper_hi, upper_lo = split(exact(in_order, upper_inv))
     for start in range(0, panel.shape[0], size):
         rows = slice(start, start + size)
         part = panel[rows, :]
         result = fast(part, upper_hi) + fast(part, upper_lo)
+        plain[rows, :] = result.astype(jnp.bfloat16)
         result = result.astype(jnp.bfloat16).astype(jnp.float32)
         sent[rows, :] = (result * mask[rows, 0:1]).astype(jnp.bfloat16)
         kept[rows, :] = (result * mask[rows, 1:2]).astype(jnp.bfloat16)
@@ -115,6 +122,7 @@
             jax.ShapeDtypeStruct((size, size), half_type),
             jax.ShapeDtypeStruct((rows, size), half_type),
             jax.ShapeDtypeStruct((rows, size), half_type),
+            jax.ShapeDtypeStruct((rows, size), half_type),
         ),
         compiler_params=pltpu.CompilerParams(vmem_limit_bytes=VMEM_LIMIT),
         cost_estimate=pl.CostEstimate(flops=30_000_000_000, bytes_accessed=3_000_000, transcendentals=0),
@@ -153,9 +161,28 @@
     merge_kernel(place, hi, lo, left, trailing, chosen, received, *pieces, out, right)
 
 
-def specs_for(hi, left, width, steps, half_blocks, chunk, pieces, starts):
+def merge_raw_kernel(place, hi, lo, left, trailing, chosen, received, other_left, other_right, *rest):
+    *pieces, out, right, updated = rest
+
+    @pl.when(pl.program_id(0) == 0)
+    def _():
+        size = out.shape[0]
+        for first in range(0, received.shape[0], size):
+            rows = slice(first, first + size)
+            update = fast(other_left[rows, :], other_right[...])
+            updated[rows, :] = (received[rows, :].astype(jnp.float32) - update).astype(jnp.bfloat16)
+
+    merge_kernel(place, hi, lo, left, trailing, chosen, updated, *pieces, out, right)
+
+
+def merge_raw_kernel_into(*refs):
+    merge_raw_kernel(*refs[:-4], *refs[-3:])
+
+
+def specs_for(hi, left, columns, width, start, pieces, starts):
     size = hi.shape[0]
-    rows = left.shape[0] // steps
+    rows = left.shape[0] // ROW_STEPS
+    half_blocks, chunk = columns // 2 // width, start // width
     whole = pl.BlockSpec((size, size), lambda i, place: (0, 0))
     specs = [
         whole,
@@ -164,19 +191,18 @@
         pl.BlockSpec((rows, width), lambda i, place: (i, place[0] * half_blocks + chunk)),
     ]
     piece_specs = []
-    for number, (piece, start) in enumerate(zip(pieces, starts)):
-        depth = piece.shape[0]
-        if number == 0:
-            piece_specs.append(pl.BlockSpec((depth, width), lambda i, place: (0, place[0] * half_blocks + chunk)))
+    for piece, first in zip(pieces, starts):
+        block = (piece.shape[0], width)
+        if first is None:
+            piece_specs.append(pl.BlockSpec(block, lambda i, place: (0, place[0] * half_blocks + chunk)))
         else:
-            piece_specs.append(pl.BlockSpec((depth, width), lambda i, place, at=chunk - start: (0, at)))
+            piece_specs.append(pl.BlockSpec(block, lambda i, place, at=(start - first) // width: (0, at)))
     return specs, piece_specs
 
 
-def send_chunk(place, hi, lo, left, trailing, pieces, starts, width, chunk):
+def send_chunk(place, hi, lo, left, trailing, pieces, starts, start, width):
     rows, columns = trailing.shape
-    half_blocks = columns // 2 // width
-    specs, piece_specs = specs_for(hi, left, width, ROW_STEPS, half_blocks, chunk, pieces, starts)
+    specs, piece_specs = specs_for(hi, left, columns, width, start, pieces, starts)
     return pl.pallas_call(
         send_kernel,
         grid_spec=pltpu.PrefetchScalarGridSpec(
@@ -193,23 +219,34 @@
     )(place, hi, lo, left, trailing, *pieces)
 
 
-def merge_chunk(place, hi, lo, left, trailing, chosen, received, pieces, starts, width, chunk, merged):
+def merge_chunk(place, hi, lo, left, trailing, chosen, received, pieces, starts, start, width, merged, raw=None):
     rows, columns = trailing.shape
-    half_blocks = columns // 2 // width
     step_rows = rows // ROW_STEPS
-    specs, piece_specs = specs_for(hi, left, width, ROW_STEPS, half_blocks, chunk, pieces, starts)
-    specs += [
-        pl.BlockSpec((step_rows, rows), lambda i, place: (i, 0)),
-        pl.BlockSpec((rows, width), lambda i, place: (0, 0)),
-    ] + piece_specs
-    operands = [place, hi, lo, left, trailing, chosen, received, *pieces]
+    specs, piece_specs = specs_for(hi, left, columns, width, start, pieces, starts)
+    specs.append(pl.BlockSpec((step_rows, rows), lambda i, place: (i, 0)))
+    operands = [place, hi, lo, left, trailing, chosen, received]
+    scratch = [pltpu.VMEM((hi.shape[0], width), jnp.bfloat16)]
+    body, body_into = merge_kernel, merge_kernel_into
+    if raw is None:
+        specs.append(pl.BlockSpec((rows, width), lambda i, place: (0, 0)))
+    else:
+        first, other_left, other_right = raw
+        at = (start - first) // width
+        specs.append(pl.BlockSpec((rows, width), lambda i, place: (0, at)))
+        specs.append(pl.BlockSpec(other_left.shape, lambda i, place: (0, 0)))
+        specs.append(pl.BlockSpec((other_right.shape[0], width), lambda i, place: (0, at)))
+        operands += [other_left, other_right]
+        scratch.append(pltpu.VMEM((rows, width), jnp.bfloat16))
+        body, body_into = merge_raw_kernel, merge_raw_kernel_into
+    specs += piece_specs
+    operands += pieces
     aliases = {}
-    body = merge_kernel
     if merged is not None:
         aliases = {len(operands): 0}
         operands.append(merged)
         specs.append(pl.BlockSpec(memory_space=pl.ANY))
-        body = merge_kernel_into
+        body = body_into
+    chunk = start // width
     return pl.pallas_call(
         body,
         grid_spec=pltpu.PrefetchScalarGridSpec(
@@ -217,7 +254,7 @@
             grid=(ROW_STEPS,),
             in_specs=specs,
             out_specs=pl.BlockSpec((step_rows, width), lambda i, place: (i, chunk)),
-            scratch_shapes=[pltpu.VMEM((hi.shape[0], width), jnp.bfloat16)],
+            scratch_shapes=scratch,
         ),
         out_shape=jax.ShapeDtypeStruct((rows, columns // 2), jnp.bfloat16),
         input_output_aliases=aliases,
@@ -227,16 +264,30 @@
     )(*operands)
 
 
+def bits_of(axis):
+    return [1 << bit for bit in reversed(range((lax.axis_size(axis) - 1).bit_length()))]
+
+
 def doubled(block, axis, dimension):
-    bits = 1
-    while bits < lax.axis_size(axis):
-        block = jnp.concatenate([block, partner(block, axis, bits)], axis=dimension)
-        bits *= 2
+    for step in range(len(bits_of(axis))):
+        block = next_doubled(block, axis, dimension, step)
     return block
 
 
-def relative(index, part, me):
-    return ((index // part) ^ me) * part + index % part
+def next_doubled(block, axis, dimension, step):
+    return jnp.concatenate([block, partner(block, axis, bits_of(axis)[step])], axis=dimension)
+
+
+def place_of(index, part, axis):
+    apart = (index // part) ^ lax.axis_index(axis)
+    place = jnp.zeros_like(index)
+    for number, bits in enumerate(bits_of(axis)):
+        place = place + jnp.where(apart & bits != 0, 1 << number, 0)
+    return place * part + index % part
+
+
+def after(value, *others):
+    return lax.optimization_barrier((value, *others))[0]
 
 
 def local(diag_block, pivot_order, lower_in, upper_in, trailing, block_mask, row_map):
@@ -245,50 +296,111 @@
     rows, columns = trailing.shape
     half = columns // 2
     width = half // CHUNKS
-    group = lax.axis_index(("row", "col"))
     row, col = lax.axis_index("row"), lax.axis_index("col")
     parity = lax.axis_index("cube") % 2
     sent_place = (1 - parity).astype(jnp.int32).reshape(1)
     kept_place = parity.astype(jnp.int32).reshape(1)
-
-    whole_block = doubled(diag_block, ("row", "col"), 0)
+    raw_end = RAW * width
+
+    raw = lax.dynamic_slice_in_dim(trailing, (1 - parity) * half, raw_end, 1)
+    raw_received = partner(raw, "cube", 1)
+
+    whole_block = doubled(after(diag_block, raw), ("row", "col"), 0)
     panel = doubled(lower_in, "col", 1)
     order = pivot_order[0][:, None]
+    every = jnp.arange(size, dtype=jnp.int32)
+    in_row_order = place_of(every, upper_in.shape[0], "row")
+    in_col_order = place_of(every, lower_in.shape[1], "col")
     orders = (
-        relative(order, diag_block.shape[0], group),
-        relative(order, upper_in.shape[0], row),
-        relative(jnp.arange(size, dtype=jnp.int32)[:, None], lower_in.shape[1], col),
+        place_of(order, diag_block.shape[0], ("row", "col")),
+        place_of(order, upper_in.shape[0], "row"),
+        in_col_order[None, :],
     )
-    flags = jnp.repeat(block_mask[0].astype(jnp.float32), rows // block_mask.shape[1], axis=0)
+    block_rows = rows // block_mask.shape[1]
+    flags = block_mask[0].astype(jnp.float32)
+    other_flags = partner(flags, "cube", 1)
+    other_flags = jnp.where(parity == 0, other_flags[:, :1], other_flags[:, 1:])
+    other_flags = jnp.repeat(other_flags, block_rows, axis=0)
+    flags = jnp.repeat(flags, block_rows, axis=0)
     flags = jnp.where(parity == 0, flags[:, ::-1], flags)
     chosen = (row_map[0][:, None] == jnp.arange(rows, dtype=jnp.int32)[None, :]).astype(jnp.bfloat16)
 
-    def gathered(place, first, last):
-        own = lax.dynamic_slice_in_dim(upper_in, place * half + first * width, (last - first) * width, 1)
-        return [partner(own, "row", bits) for bits in range(1, lax.axis_size("row"))]
-
-    cuts = (0, 2, 7, CHUNKS)
-    sent_groups = [(a, b, gathered(1 - parity, a, b)) for a, b in zip(cuts, cuts[1:])]
-    kept_groups = [(0, CHUNKS, gathered(parity, 0, CHUNKS))]
-
-    def pieces_of(groups, chunk):
-        for first, last, arrays in groups:
-            if first <= chunk < last:
-                return [upper_in, *arrays], [0] + [first] * len(arrays)
-
-    hi, lo, sent_left, kept_left = factor(whole_block, orders, panel, flags)
-
-    received = []
-    for chunk in range(CHUNKS):
-        pieces, starts = pieces_of(sent_groups, chunk)
-        outgoing = send_chunk(sent_place, hi, lo, sent_left, trailing, pieces, starts, width, chunk)
-        received.append(partner(outgoing, "cube", 1))
+    def columns_of(place, first, last):
+        return lax.dynamic_slice_in_dim(upper_in, place * half + first, last - first, 1)
+
+    cut = raw_end + EARLY * width
+    early = doubled(columns_of(1 - parity, 0, cut), "row", 0)
+    late = columns_of(1 - parity, cut, half)
+    late = next_doubled(late, "row", 0, 0)
+
+    hi, lo, plain_left, sent_left, kept_left = factor(whole_block, orders, panel, flags)
+
+    left_share = lax.dynamic_slice_in_dim(plain_left, col * lower_in.shape[1], lower_in.shape[1], 1)
+    left_received = partner(left_share, "cube", 1)
+    share = upper_in.shape[0]
+    share_hi = lax.dynamic_slice_in_dim(hi, row * share, share, 0)
+    share_lo = lax.dynamic_slice_in_dim(lo, row * share, share, 0)
+    same = (in_col_order[:, None, None] == jnp.arange(size)[None, :, None]) & (
+        in_row_order[:, None, None] == jnp.arange(size)[None, None, :]
+    )
+    same = jnp.any(same, axis=0).astype(jnp.bfloat16)
+
+    bounds = [width * chunk for chunk in range(RAW, CHUNKS + 1)]
+    if width % 256 == 0:
+        bounds.insert(-1, half - width // 2)
+    spans = list(zip(bounds, bounds[1:]))
+    sent, received, merged_after = [], [], []
     merged = None
-    for chunk in range(CHUNKS):
-        pieces, starts = pieces_of(kept_groups, chunk)
+
+    def merge(number):
+        start, end = spans[number]
+        return merge_chunk(
+            kept_place, hi, lo, kept_left, trailing, chosen, received[number], [kept_upper], [0], start, end - start,
+            merged,
+        )
+
+    for number, (start, end) in enumerate(spans):
+        before = []
+        if number >= AHEAD - 1:
+            before += [([raw_received] + received)[number - AHEAD + 1], sent[-1]]
+        if number == 1:
+            for step in range(1, len(bits_of("row"))):
+                late = next_doubled(after(late, sent[0]), "row", 0, step)
+        if number == 2:
+            kept_upper = next_doubled(after(columns_of(parity, 0, half), raw_received), "row", 0, 0)
+        if number == 3:
+            before += [left_received]
+            raw_upper = after(early[:, :raw_end], received[0])
+            right_share = (fast(share_hi, raw_upper) + fast(share_lo, raw_upper)).astype(jnp.bfloat16)
+            right_received = partner(right_share, "cube", 1)
+        if number == 4:
+            before += [kept_upper]
+            for step in range(1, len(bits_of("row"))):
+                kept_upper = next_doubled(after(kept_upper, received[1]), "row", 0, step)
+        if number == 5:
+            before += [right_received]
+            other_left = doubled(after(left_received, received[2]), "col", 1)
+            other_left = (fast(other_left, same) * other_flags).astype(jnp.bfloat16)
+        if number == 6:
+            before += [kept_upper]
+            other_right = doubled(after(right_received, received[3]), "row", 0)
+        if number == 7:
+            before += [other_left, other_right]
+        if number >= BEHIND:
+            merged = merge(number - BEHIND)
+            before += [merged]
+        place = after(sent_place, *before) if before else sent_place
+        piece, first = (early, 0) if end <= cut else (late, cut)
+        sent.append(send_chunk(place, hi, lo, sent_left, trailing, [piece], [first], start, end - start))
+        received.append(partner(sent[-1], "cube", 1))
+
+    for start in range(0, raw_end, width):
         merged = merge_chunk(
-            kept_place, hi, lo, kept_left, trailing, chosen, received[chunk], pieces, starts, width, chunk, merged
+            kept_place, hi, lo, kept_left, trailing, chosen, raw_received, [kept_upper], [0], start, width, merged,
+            (0, other_left, other_right),
         )
+    for number in range(len(spans) - BEHIND, len(spans)):
+        merged = merge(number)
     return merged[None]
 
 

time: 439 us -> 397 us (0.904)
  waiting for transfers between devices: 220 us -> 174 us
  Pallas kernels: 167 us -> 152 us
  other arithmetic: 6.31 us -> 14.8 us
  starting transfers between devices: 34 us -> 39.3 us
    ppermute x31, waiting for transfers between devices: 220 us -> 174 us  [partner(): return lax.ppermute(block, axis, [(i, i ^ bits) for i in range(count)])]
    pallas_call x15 -> x14, Pallas kernels: 61.3 us -> 48.9 us  [send_chunk(): pl.pallas_call(send_kernel, grid_spec=pltpu.PrefetchScalarGridSpec(num_sc...]
    reduce_or x0 -> x1, other arithmetic: none -> 11.1 us  [local(): same = jnp.any(same, axis=0).astype(jnp.bfloat16)]
    ppermute x31, starting transfers between devices: 34 us -> 39.3 us  [partner(): return lax.ppermute(block, axis, [(i, i ^ bits) for i in range(count)])]
    pallas_call x15 -> x16, Pallas kernels: 79.4 us -> 76.3 us  [merge_chunk(): pl.pallas_call(body, grid_spec=pltpu.PrefetchScalarGridSpec(num_scalar_pr...]
  transfers between devices with their start and end apart: 31 -> 31, of which waited for: 16 -> 14; matrix products, arithmetic and copies ran while one was open for 3% -> 7% of each run, Pallas kernels for 37% -> 37%
where the time goes in v2:
time: 397 us; the launch traced here: 395 us
  waiting for transfers between devices  174 us (44%)
  Pallas kernels  152 us (38%)
  starting transfers between devices  39.3 us (10%)
  other arithmetic  14.8 us (4%)
  local copies, waits for them, and re-layouts  12.7 us (3%)
    ppermute x31, waiting for transfers between devices, partner(): return lax.ppermute(block, axis, [(i, i ^ bits) for i in range(count)])  174 us
    pallas_call x16, Pallas kernels, merge_chunk(): pl.pallas_call(body, grid_spec=pltpu.PrefetchScalarGridSpec(num_scalar_pr...  76.3 us
    pallas_call x14, Pallas kernels, send_chunk(): pl.pallas_call(send_kernel, grid_spec=pltpu.PrefetchScalarGridSpec(num_sc...  48.9 us
    ppermute x31, starting transfers between devices, partner(): return lax.ppermute(block, axis, [(i, i ^ bits) for i in range(count)])  39.3 us
    pallas_call x1, Pallas kernels, factor(): pl.pallas_call(factor_kernel, out_shape=(jax.ShapeDtypeStruct((size, size...  26.7 us
    reduce_or x1, other arithmetic, local(): same = jnp.any(same, axis=0).astype(jnp.bfloat16)  11.1 us
  transfers between devices with their start and end apart: 31, of which 14 were waited for; matrix products, arithmetic and copies ran while one was open for 7% of the time, Pallas kernels for 37%

profile of v2, /device:TPU:0, one launch (start us, length us, event | category | flops | bytes accessed | tf_op | source)
XLA Modules:
  0.0 395.2 jit_solution(3113439630479602887)
XLA Ops:
  13.9 11.1 %and_reduce_fusion = pred[256,256]{1,0:T(8,128)(4,1)S(1)} fusion(pred[256,256]{1,0:T(8,128)(4,1)S(1)} %iota_compare_fusion.1, pred[256,256]{1,0:T(8,128)(4,1)S(1)} %iota_compare_fusion.2), kind=kLoop, calls=%fused_computation | loop fusion | flops 33488896 | bytes 196608 | tf_op jit(solution)/shard_map/reduce_or | solution.py:346
  27.6 24.7 %collective-permute-done.19 = f32[8,2]{0,1:T(2,128)S(1)} collective-permute-done((f32[8,2]{0,1:T(2,128)S(1)}, f32[8,2]{0,1:T(2,128)S(1)}, u32[]{:S(2)}, u32[]{:S(2)}) %collective-permute-start.19) | collective-permute-done | bytes 96 | tf_op jit(solution)/shard_map/ppermute | solution.py:22
  60.4 26.7 %factor.1 = (bf16[256,256]{1,0:T(8,128)(2,1)S(1)}, bf16[256,256]{1,0:T(8,128)(2,1)S(1)}, bf16[1024,256]{1,0:T(8,128)(2,1)S(1)}, bf16[1024,256]{1,0:T(8,128)(2,1)S(1)}, bf16[1024,256]{1,0:T(8,128)(2,1)S(1)}) custom-call(f32[256,256]{1,0:T(8,128)S(1)} %pad_maximum_fusion.4.block, s32[256,1]{1,0:T(8,128)S(1)} %get-tuple-element.54.order_of_diag, ...), custom_call_target="tpu_custom_call" | custom-call | flops 30000001024 | bytes 3000000 | tf_op jit(solution)/shard_map/factor/pallas_call | solution.py:118
  97.6 21.3 %collective-permute-done.7.received = bf16[1024,512]{1,0:T(8,128)(2,1)S(1)} collective-permute-done((bf16[1024,512]{1,0:T(8,128)(2,1)S(1)}, bf16[1024,512]{1,0:T(8,128)(2,1)S(1)}, u32[]{:S(2)}, u32[]{:S(2)}) %collective-permute-start.7) | collective-permute-done | bytes 1048608 | tf_op jit(solution)/shard_map/ppermute | solution.py:22
  126.9 15.6 %collective-permute-done.12 = bf16[64,7680]{1,0:T(8,128)(2,1)} collective-permute-done((bf16[64,7680]{1,0:T(8,128)(2,1)}, bf16[64,7680]{1,0:T(8,128)(2,1)}, u32[]{:S(2)}, u32[]{:S(2)}) %collective-permute-start.12) | collective-permute-done | bytes 983072 | tf_op jit(solution)/shard_map/ppermute | solution.py:22
  156.4 32.7 %collective-permute-done.16 = bf16[64,1024]{1,0:T(8,128)(2,1)S(1)} collective-permute-done((bf16[64,1024]{1,0:T(8,128)(2,1)S(1)}, bf16[64,1024]{1,0:T(8,128)(2,1)S(1)}, u32[]{:S(2)}, u32[]{:S(2)}) %collective-permute-start.16) | collective-permute-done | bytes 131104 | tf_op jit(solution)/shard_map/ppermute | solution.py:22
  192.3 4.1 %send_part.19 = bf16[1024,512]{1,0:T(8,128)(2,1)} custom-call(s32[1]{0:T(128)} %bitcast.9.place, bf16[256,256]{1,0:T(8,128)(2,1)S(1)} %get-tuple-element.30.hi.refs_1_, bf16[256,256]{1,0:T(8,128)(2,1)S(1)} %get-tuple-element.31.lo.refs_2_, bf16[1024,256]{1,0:T(8,128)(2,1)S(1)} %get-tuple-element.33.left, bf16[1024,15360]{1,0:T(8,128)(2,1)} %bitcast.32, ...), custom_call_target="tpu_custom_call" | custom-call | flops 268435456 | bytes 2621440 | tf_op jit(solution)/shard_map/send_part/pallas_call | solution.py:206
  202.6 4.7 %merge_part.16.rest_1_ = bf16[1024,7680]{1,0:T(8,128)(2,1)} custom-call(s32[1]{0:T(128)} %bitcast.place.refs_0_, bf16[256,256]{1,0:T(8,128)(2,1)S(1)} %get-tuple-element.30.hi.refs_1_, bf16[256,256]{1,0:T(8,128)(2,1)S(1)} %get-tuple-element.31.lo.refs_2_, bf16[1024,256]{1,0:T(8,128)(2,1)S(1)} %get-tuple-element.32.left.refs_3_, ...), custom_call_target="tpu_custom_call" | custom-call | flops 1342177280 | bytes 4194304 | tf_op jit(solution)/shard_map/merge_part/pallas_call | solution.py:250
  207.3 4.1 %send_part.20 = bf16[1024,512]{1,0:T(8,128)(2,1)} custom-call(s32[1]{0:T(128)} %bitcast.9.place, bf16[256,256]{1,0:T(8,128)(2,1)S(1)} %get-tuple-element.30.hi.refs_1_, bf16[256,256]{1,0:T(8,128)(2,1)S(1)} %get-tuple-element.31.lo.refs_2_, bf16[1024,256]{1,0:T(8,128)(2,1)S(1)} %get-tuple-element.33.left, bf16[1024,15360]{1,0:T(8,128)(2,1)} %bitcast.34, ...), custom_call_target="tpu_custom_call" | custom-call | flops 268435456 | bytes 2621440 | tf_op jit(solution)/shard_map/send_part/pallas_call | solution.py:206
  212.8 4.7 %merge_part.17.rest_1_ = bf16[1024,7680]{1,0:T(8,128)(2,1)} custom-call(s32[1]{0:T(128)} %bitcast.place.refs_0_, bf16[256,256]{1,0:T(8,128)(2,1)S(1)} %get-tuple-element.30.hi.refs_1_, bf16[256,256]{1,0:T(8,128)(2,1)S(1)} %get-tuple-element.31.lo.refs_2_, bf16[1024,256]{1,0:T(8,128)(2,1)S(1)} %get-tuple-element.32.left.refs_3_, ...), custom_call_target="tpu_custom_call", output_to_operand_aliasing={{}: (8, {})} | custom-call | flops 1342177280 | bytes 4194304 | tf_op jit(solution)/shard_map/merge_part/pallas_call | solution.py:250
  222.3 4.7 %merge_part.18.rest_1_ = bf16[1024,7680]{1,0:T(8,128)(2,1)} custom-call(s32[1]{0:T(128)} %bitcast.place.refs_0_, bf16[256,256]{1,0:T(8,128)(2,1)S(1)} %get-tuple-element.30.hi.refs_1_, bf16[256,256]{1,0:T(8,128)(2,1)S(1)} %get-tuple-element.31.lo.refs_2_, bf16[1024,256]{1,0:T(8,128)(2,1)S(1)} %get-tuple-element.32.left.refs_3_, ...), custom_call_target="tpu_custom_call", output_to_operand_aliasing={{}: (8, {})} | custom-call | flops 1342177280 | bytes 4194304 | tf_op jit(solution)/shard_map/merge_part/pallas_call | solution.py:250
  227.0 7.0 %collective-permute-done.24.received = bf16[1024,512]{1,0:T(8,128)(2,1)S(1)} collective-permute-done((bf16[1024,512]{1,0:T(8,128)(2,1)}, bf16[1024,512]{1,0:T(8,128)(2,1)S(1)}, u32[]{:S(2)}, u32[]{:S(2)}) %collective-permute-start.24) | collective-permute-done | bytes 1048608 | tf_op jit(solution)/shard_map/ppermute | solution.py:22
  239.9 4.7 %merge_part.19.rest_1_ = bf16[1024,7680]{1,0:T(8,128)(2,1)} custom-call(s32[1]{0:T(128)} %bitcast.place.refs_0_, bf16[256,256]{1,0:T(8,128)(2,1)S(1)} %get-tuple-element.30.hi.refs_1_, bf16[256,256]{1,0:T(8,128)(2,1)S(1)} %get-tuple-element.31.lo.refs_2_, bf16[1024,256]{1,0:T(8,128)(2,1)S(1)} %get-tuple-element.32.left.refs_3_, ...), custom_call_target="tpu_custom_call", output_to_operand_aliasing={{}: (8, {})} | custom-call | flops 1342177280 | bytes 4194304 | tf_op jit(solution)/shard_map/merge_part/pallas_call | solution.py:250
  244.6 11.9 %collective-permute-done.23.received = bf16[1024,512]{1,0:T(8,128)(2,1)S(1)} collective-permute-done((bf16[1024,512]{1,0:T(8,128)(2,1)}, bf16[1024,512]{1,0:T(8,128)(2,1)S(1)}, u32[]{:S(2)}, u32[]{:S(2)}) %collective-permute-start.23) | collective-permute-done | bytes 1048608 | tf_op jit(solution)/shard_map/ppermute | solution.py:22
  256.5 4.1 %send_part.23 = bf16[1024,512]{1,0:T(8,128)(2,1)} custom-call(s32[1]{0:T(128)} %bitcast.9.place, bf16[256,256]{1,0:T(8,128)(2,1)S(1)} %get-tuple-element.30.hi.refs_1_, bf16[256,256]{1,0:T(8,128)(2,1)S(1)} %get-tuple-element.31.lo.refs_2_, bf16[1024,256]{1,0:T(8,128)(2,1)S(1)} %get-tuple-element.33.left, bf16[1024,15360]{1,0:T(8,128)(2,1)} %bitcast.40, ...), custom_call_target="tpu_custom_call" | custom-call | flops 268435456 | bytes 2621440 | tf_op jit(solution)/shard_map/send_part/pallas_call | solution.py:206
  262.3 4.7 %merge_part.20.rest_1_ = bf16[1024,7680]{1,0:T(8,128)(2,1)} custom-call(s32[1]{0:T(128)} %bitcast.place.refs_0_, bf16[256,256]{1,0:T(8,128)(2,1)S(1)} %get-tuple-element.30.hi.refs_1_, bf16[256,256]{1,0:T(8,128)(2,1)S(1)} %get-tuple-element.31.lo.refs_2_, bf16[1024,256]{1,0:T(8,128)(2,1)S(1)} %get-tuple-element.32.left.refs_3_, ...), custom_call_target="tpu_custom_call", output_to_operand_aliasing={{}: (8, {})} | custom-call | flops 1342177280 | bytes 4194304 | tf_op jit(solution)/shard_map/merge_part/pallas_call | solution.py:250
  267.0 12.0 %collective-permute-done.22.received = bf16[1024,512]{1,0:T(8,128)(2,1)} collective-permute-done((bf16[1024,512]{1,0:T(8,128)(2,1)}, bf16[1024,512]{1,0:T(8,128)(2,1)}, u32[]{:S(2)}, u32[]{:S(2)}) %collective-permute-start.22) | collective-permute-done | bytes 1048608 | tf_op jit(solution)/shard_map/ppermute | solution.py:22
  283.8 4.7 %merge_part.21.rest_1_ = bf16[1024,7680]{1,0:T(8,128)(2,1)} custom-call(s32[1]{0:T(128)} %bitcast.place.refs_0_, bf16[256,256]{1,0:T(8,128)(2,1)S(1)} %get-tuple-element.30.hi.refs_1_, bf16[256,256]{1,0:T(8,128)(2,1)S(1)} %get-tuple-element.31.lo.refs_2_, bf16[1024,256]{1,0:T(8,128)(2,1)S(1)} %get-tuple-element.32.left.refs_3_, ...), custom_call_target="tpu_custom_call", output_to_operand_aliasing={{}: (8, {})} | custom-call | flops 1342177280 | bytes 4194304 | tf_op jit(solution)/shard_map/merge_part/pallas_call | solution.py:250
  288.6 12.9 %collective-permute-done.27.received = bf16[1024,512]{1,0:T(8,128)(2,1)S(1)} collective-permute-done((bf16[1024,512]{1,0:T(8,128)(2,1)}, bf16[1024,512]{1,0:T(8,128)(2,1)S(1)}, u32[]{:S(2)}, u32[]{:S(2)}) %collective-permute-start.27) | collective-permute-done | bytes 1048608 | tf_op jit(solution)/shard_map/ppermute | solution.py:22
  307.3 4.7 %merge_part.22.rest_1_ = bf16[1024,7680]{1,0:T(8,128)(2,1)} custom-call(s32[1]{0:T(128)} %bitcast.place.refs_0_, bf16[256,256]{1,0:T(8,128)(2,1)S(1)} %get-tuple-element.30.hi.refs_1_, bf16[256,256]{1,0:T(8,128)(2,1)S(1)} %get-tuple-element.31.lo.refs_2_, bf16[1024,256]{1,0:T(8,128)(2,1)S(1)} %get-tuple-element.32.left.refs_3_, ...), custom_call_target="tpu_custom_call", output_to_operand_aliasing={{}: (8, {})} | custom-call | flops 1342177280 | bytes 4194304 | tf_op jit(solution)/shard_map/merge_part/pallas_call | solution.py:250
  312.0 11.9 %collective-permute-done.26.received = bf16[1024,512]{1,0:T(8,128)(2,1)S(1)} collective-permute-done((bf16[1024,512]{1,0:T(8,128)(2,1)}, bf16[1024,512]{1,0:T(8,128)(2,1)S(1)}, u32[]{:S(2)}, u32[]{:S(2)}) %collective-permute-start.26) | collective-permute-done | bytes 1048608 | tf_op jit(solution)/shard_map/ppermute | solution.py:22
  328.4 5.0 %merge_part.23.refs_10_ = bf16[1024,7680]{1,0:T(8,128)(2,1)} custom-call(s32[1]{0:T(128)} %bitcast.place.refs_0_, bf16[256,256]{1,0:T(8,128)(2,1)S(1)} %get-tuple-element.30.hi.refs_1_, bf16[256,256]{1,0:T(8,128)(2,1)S(1)} %get-tuple-element.31.lo.refs_2_, bf16[1024,256]{1,0:T(8,128)(2,1)S(1)} %get-tuple-element.32.left.refs_3_, ...), custom_call_target="tpu_custom_call", output_to_operand_aliasing={{}: (8, {})} | custom-call | flops 1342177280 | bytes 4194304 | tf_op jit(solution)/shard_map/merge_part/pallas_call | solution.py:250
  333.4 12.9 %collective-permute-done.25.received = bf16[1024,512]{1,0:T(8,128)(2,1)S(1)} collective-permute-done((bf16[1024,512]{1,0:T(8,128)(2,1)S(1)}, bf16[1024,512]{1,0:T(8,128)(2,1)S(1)}, u32[]{:S(2)}, u32[]{:S(2)}) %collective-permute-start.25) | collective-permute-done | bytes 1048608 | tf_op jit(solution)/shard_map/ppermute | solution.py:22
  350.9 5.3 %merge_part.24.refs_10_ = bf16[1024,7680]{1,0:T(8,128)(2,1)} custom-call(s32[1]{0:T(128)} %bitcast.place.refs_0_, bf16[256,256]{1,0:T(8,128)(2,1)S(1)} %get-tuple-element.30.hi.refs_1_, bf16[256,256]{1,0:T(8,128)(2,1)S(1)} %get-tuple-element.31.lo.refs_2_, bf16[1024,256]{1,0:T(8,128)(2,1)S(1)} %get-tuple-element.32.left.refs_3_, ...), custom_call_target="tpu_custom_call", output_to_operand_aliasing={{}: (10, {})} | custom-call | flops 1342177280 | bytes 4194304 | tf_op jit(solution)/shard_map/merge_part/pallas_call | solution.py:250
  356.2 5.3 %merge_part.25.rest_1_ = bf16[1024,7680]{1,0:T(8,128)(2,1)} custom-call(s32[1]{0:T(128)} %bitcast.place.refs_0_, bf16[256,256]{1,0:T(8,128)(2,1)S(1)} %get-tuple-element.30.hi.refs_1_, bf16[256,256]{1,0:T(8,128)(2,1)S(1)} %get-tuple-element.31.lo.refs_2_, bf16[1024,256]{1,0:T(8,128)(2,1)S(1)} %get-tuple-element.32.left.refs_3_, ...), custom_call_target="tpu_custom_call", output_to_operand_aliasing={{}: (10, {})} | custom-call | flops 1342177280 | bytes 4194304 | tf_op jit(solution)/shard_map/merge_part/pallas_call | solution.py:250
  361.5 4.7 %merge_part.26.rest_1_ = bf16[1024,7680]{1,0:T(8,128)(2,1)} custom-call(s32[1]{0:T(128)} %bitcast.place.refs_0_, bf16[256,256]{1,0:T(8,128)(2,1)S(1)} %get-tuple-element.30.hi.refs_1_, bf16[256,256]{1,0:T(8,128)(2,1)S(1)} %get-tuple-element.31.lo.refs_2_, bf16[1024,256]{1,0:T(8,128)(2,1)S(1)} %get-tuple-element.32.left.refs_3_, ...), custom_call_target="tpu_custom_call", output_to_operand_aliasing={{}: (8, {})} | custom-call | flops 1342177280 | bytes 4194304 | tf_op jit(solution)/shard_map/merge_part/pallas_call | solution.py:250
  366.2 4.7 %merge_part.27.rest_1_ = bf16[1024,7680]{1,0:T(8,128)(2,1)} custom-call(s32[1]{0:T(128)} %bitcast.place.refs_0_, bf16[256,256]{1,0:T(8,128)(2,1)S(1)} %get-tuple-element.30.hi.refs_1_, bf16[256,256]{1,0:T(8,128)(2,1)S(1)} %get-tuple-element.31.lo.refs_2_, bf16[1024,256]{1,0:T(8,128)(2,1)S(1)} %get-tuple-element.32.left.refs_3_, ...), custom_call_target="tpu_custom_call", output_to_operand_aliasing={{}: (8, {})} | custom-call | flops 1342177280 | bytes 4194304 | tf_op jit(solution)/shard_map/merge_part/pallas_call | solution.py:250
  370.9 4.7 %merge_part.28.rest_1_ = bf16[1024,7680]{1,0:T(8,128)(2,1)} custom-call(s32[1]{0:T(128)} %bitcast.place.refs_0_, bf16[256,256]{1,0:T(8,128)(2,1)S(1)} %get-tuple-element.30.hi.refs_1_, bf16[256,256]{1,0:T(8,128)(2,1)S(1)} %get-tuple-element.31.lo.refs_2_, bf16[1024,256]{1,0:T(8,128)(2,1)S(1)} %get-tuple-element.32.left.refs_3_, ...), custom_call_target="tpu_custom_call", output_to_operand_aliasing={{}: (8, {})} | custom-call | flops 1342177280 | bytes 4194304 | tf_op jit(solution)/shard_map/merge_part/pallas_call | solution.py:250
  375.7 5.1 %merge_part.29.rest_1_ = bf16[1024,7680]{1,0:T(8,128)(2,1)} custom-call(s32[1]{0:T(128)} %bitcast.place.refs_0_, bf16[256,256]{1,0:T(8,128)(2,1)S(1)} %get-tuple-element.30.hi.refs_1_, bf16[256,256]{1,0:T(8,128)(2,1)S(1)} %get-tuple-element.31.lo.refs_2_, bf16[1024,256]{1,0:T(8,128)(2,1)S(1)} %get-tuple-element.32.left.refs_3_, ...), custom_call_target="tpu_custom_call", output_to_operand_aliasing={{}: (8, {})} | custom-call | flops 1342177280 | bytes 4194304 | tf_op jit(solution)/shard_map/merge_part/pallas_call | solution.py:250
  380.7 4.1 %merge_part.30.rest_1_ = bf16[1024,7680]{1,0:T(8,128)(2,1)} custom-call(s32[1]{0:T(128)} %bitcast.place.refs_0_, bf16[256,256]{1,0:T(8,128)(2,1)S(1)} %get-tuple-element.30.hi.refs_1_, bf16[256,256]{1,0:T(8,128)(2,1)S(1)} %get-tuple-element.31.lo.refs_2_, bf16[1024,256]{1,0:T(8,128)(2,1)S(1)} %get-tuple-element.32.left.refs_3_, ...), custom_call_target="tpu_custom_call", output_to_operand_aliasing={{}: (8, {})} | custom-call | flops 671088640 | bytes 2097152 | tf_op jit(solution)/shard_map/merge_part/pallas_call | solution.py:250
  384.9 6.1 %collective-permute-done.28.received = bf16[1024,256]{1,0:T(8,128)(2,1)S(1)} collective-permute-done((bf16[1024,256]{1,0:T(8,128)(2,1)S(1)}, bf16[1024,256]{1,0:T(8,128)(2,1)S(1)}, u32[]{:S(2)}, u32[]{:S(2)}) %collective-permute-start.28) | collective-permute-done | bytes 524320 | tf_op jit(solution)/shard_map/ppermute | solution.py:22
  390.9 4.3 %merge_part.31 = bf16[1024,7680]{1,0:T(8,128)(2,1)} custom-call(s32[1]{0:T(128)} %bitcast.place.refs_0_, bf16[256,256]{1,0:T(8,128)(2,1)S(1)} %get-tuple-element.30.hi.refs_1_, bf16[256,256]{1,0:T(8,128)(2,1)S(1)} %get-tuple-element.31.lo.refs_2_, bf16[1024,256]{1,0:T(8,128)(2,1)S(1)} %get-tuple-element.32.left.refs_3_, ...), custom_call_target="tpu_custom_call", output_to_operand_aliasing={{}: (8, {})} | custom-call | flops 671088640 | bytes 2097152 | tf_op jit(solution)/shard_map/merge_part/pallas_call | solution.py:250
  (116 shorter events, 99.3 us)
Async XLA Ops:
  0.0 11.6 %copy-start.4 = (s32[1,1024]{1,0:T(1,128)S(1)}, s32[1,1024]{1,0:T(1,128)}, u32[]{:S(2)}) copy-start(s32[1,1024]{1,0:T(1,128)} %param.13) | copy-start | bytes 12292
  3.3 115.8 %collective-permute-start.8 = (bf16[1024,1024]{1,0:T(8,128)(2,1)}, bf16[1024,1024]{1,0:T(8,128)(2,1)}, u32[]{:S(2)}, u32[]{:S(2)}) collective-permute-start(bf16[1024,1024]{1,0:T(8,128)(2,1)} %dynamic-slice_bitcast_fusion), channel_id=1, source_target_pairs={{0,8},{8,0},{16,24},{24,16},{1,9},{9,1},{17,25},{25,17},{2,10},{10... | collective-permute-start | bytes 6291464 | tf_op jit(solution)/shard_map/ppermute | solution.py:22
  6.3 19.6 %collective-permute-start = (f32[32,256]{1,0:T(8,128)S(1)}, f32[32,256]{1,0:T(8,128)S(1)}, u32[]{:S(2)}, u32[]{:S(2)}) collective-permute-start(f32[32,256]{1,0:T(8,128)S(1)} %bitcast.58), channel_id=1, source_target_pairs={{0,4},{1,5},{2,6},{3,7},{4,0},{5,1},{6,2},{7,3},{8,12},{9,13},{10,... | collective-permute-start | bytes 98312 | tf_op jit(solution)/shard_map/ppermute | solution.py:22
  7.9 51.5 %collective-permute-start.3 = (bf16[1024,128]{1,0:T(8,128)(2,1)}, bf16[1024,128]{1,0:T(8,128)(2,1)}, u32[]{:S(2)}, u32[]{:S(2)}) collective-permute-start(bf16[1024,128]{1,0:T(8,128)(2,1)} %bitcast.4), channel_id=1, source_target_pairs={{0,1},{1,0},{2,3},{3,2},{4,5},{5,4},{6,7},{7,6},{8,9},{9,8},{10,11... | collective-permute-start | bytes 786440 | tf_op jit(solution)/shard_map/ppermute | solution.py:22
  9.4 49.8 %collective-permute-start.4 = (bf16[64,2048]{1,0:T(8,128)(2,1)S(1)}, bf16[64,2048]{1,0:T(8,128)(2,1)S(1)}, u32[]{:S(2)}, u32[]{:S(2)}) collective-permute-start(bf16[64,2048]{1,0:T(8,128)(2,1)S(1)} %dynamic-slice_bitcast_fusion.3), channel_id=1, source_target_pairs={{0,4},{2,6},{4,0},{6,2},{1,5},{3,7},{5,1},{7,3},{8,12},{10,14},{12... | collective-permute-start | bytes 786440 | tf_op jit(solution)/shard_map/ppermute | solution.py:22
  10.0 42.3 %collective-permute-start.19 = (f32[8,2]{0,1:T(2,128)S(1)}, f32[8,2]{0,1:T(2,128)S(1)}, u32[]{:S(2)}, u32[]{:S(2)}) collective-permute-start(f32[8,2]{0,1:T(2,128)S(1)} %convert_bitcast_fusion), channel_id=1, source_target_pairs={{0,8},{8,0},{16,24},{24,16},{1,9},{9,1},{17,25},{25,17},{2,10},{10... | collective-permute-start | bytes 200 | tf_op jit(solution)/shard_map/ppermute | solution.py:22
  26.0 66.5 %collective-permute-start.9 = (bf16[64,5632]{1,0:T(8,128)(2,1)S(1)}, bf16[64,5632]{1,0:T(8,128)(2,1)S(1)}, u32[]{:S(2)}, u32[]{:S(2)}) collective-permute-start(bf16[64,5632]{1,0:T(8,128)(2,1)S(1)} %dynamic-slice_bitcast_fusion.2), channel_id=1, source_target_pairs={{0,4},{2,6},{4,0},{6,2},{1,5},{3,7},{5,1},{7,3},{8,12},{10,14},{12... | collective-permute-start | bytes 2162696 | tf_op jit(solution)/shard_map/ppermute | solution.py:22
  52.3 1.3 collective-permute-start.1
  53.6 5.6 %collective-permute-start.2 = (f32[128,256]{1,0:T(8,128)S(1)}, f32[128,256]{1,0:T(8,128)S(1)}, u32[]{:S(2)}, u32[]{:S(2)}) collective-permute-start(f32[128,256]{1,0:T(8,128)S(1)} %pad_maximum_fusion.6), channel_id=1, source_target_pairs={{0,1},{1,0},{2,3},{3,2},{4,5},{5,4},{6,7},{7,6},{8,9},{9,8},{10,11... | collective-permute-start | bytes 393224 | tf_op jit(solution)/shard_map/ppermute | solution.py:22
  59.3 29.8 %collective-permute-start.5 = (bf16[128,2048]{1,0:T(8,128)(2,1)S(1)}, bf16[128,2048]{1,0:T(8,128)(2,1)S(1)}, u32[]{:S(2)}, u32[]{:S(2)}) collective-permute-start(bf16[128,2048]{1,0:T(8,128)(2,1)S(1)} %pad_maximum_fusion.3), channel_id=1, source_target_pairs={{0,2},{2,0},{4,6},{6,4},{1,3},{3,1},{5,7},{7,5},{8,10},{10,8},{12,... | collective-permute-start | bytes 1572872 | tf_op jit(solution)/shard_map/ppermute | solution.py:22
  87.2 39.7 %collective-permute-start.11 = (bf16[1024,128]{1,0:T(8,128)(2,1)S(1)}, bf16[1024,128]{1,0:T(8,128)(2,1)}, u32[]{:S(2)}, u32[]{:S(2)}) collective-permute-start(bf16[1024,128]{1,0:T(8,128)(2,1)S(1)} %constant_dynamic-slice_fusion), channel_id=1, source_target_pairs={{0,8},{8,0},{16,24},{24,16},{1,9},{9,1},{17,25},{25,17},{2,10},{10... | collective-permute-start | bytes 786440 | tf_op jit(solution)/shard_map/ppermute | solution.py:22
  92.1 26.8 %collective-permute-start.7 = (bf16[1024,512]{1,0:T(8,128)(2,1)S(1)}, bf16[1024,512]{1,0:T(8,128)(2,1)S(1)}, u32[]{:S(2)}, u32[]{:S(2)}) collective-permute-start(bf16[1024,512]{1,0:T(8,128)(2,1)S(1)} %send_part.15), channel_id=1, source_target_pairs={{0,8},{8,0},{16,24},{24,16},{1,9},{9,1},{17,25},{25,17},{2,10},{10... | collective-permute-start | bytes 3145736 | tf_op jit(solution)/shard_map/ppermute | solution.py:22
  92.6 29.6 %collective-permute-start.10 = (bf16[128,5632]{1,0:T(8,128)(2,1)S(1)}, bf16[128,5632]{1,0:T(8,128)(2,1)S(1)}, u32[]{:S(2)}, u32[]{:S(2)}) collective-permute-start(bf16[128,5632]{1,0:T(8,128)(2,1)S(1)} %pad_maximum_fusion), channel_id=1, source_target_pairs={{0,2},{2,0},{4,6},{6,4},{1,3},{3,1},{5,7},{7,5},{8,10},{10,8},{12,... | collective-permute-start | bytes 4325384 | tf_op jit(solution)/shard_map/ppermute | solution.py:22
  95.8 47.9 %collective-permute-start.6 = (bf16[1024,512]{1,0:T(8,128)(2,1)S(1)}, bf16[1024,512]{1,0:T(8,128)(2,1)S(1)}, u32[]{:S(2)}, u32[]{:S(2)}) collective-permute-start(bf16[1024,512]{1,0:T(8,128)(2,1)S(1)} %send_part.14), channel_id=1, source_target_pairs={{0,8},{8,0},{16,24},{24,16},{1,9},{9,1},{17,25},{25,17},{2,10},{10... | collective-permute-start | bytes 3145736 | tf_op jit(solution)/shard_map/ppermute | solution.py:22
  119.1 23.4 %collective-permute-start.12 = (bf16[64,7680]{1,0:T(8,128)(2,1)}, bf16[64,7680]{1,0:T(8,128)(2,1)}, u32[]{:S(2)}, u32[]{:S(2)}) collective-permute-start(bf16[64,7680]{1,0:T(8,128)(2,1)} %dynamic-slice_bitcast_fusion.1), channel_id=1, source_target_pairs={{0,4},{2,6},{4,0},{6,2},{1,5},{3,7},{5,1},{7,3},{8,12},{10,14},{12... | collective-permute-start | bytes 2949128 | tf_op jit(solution)/shard_map/ppermute | solution.py:22
  125.2 65.5 %collective-permute-start.15 = (bf16[1024,512]{1,0:T(8,128)(2,1)S(1)}, bf16[1024,512]{1,0:T(8,128)(2,1)S(1)}, u32[]{:S(2)}, u32[]{:S(2)}) collective-permute-start(bf16[1024,512]{1,0:T(8,128)(2,1)S(1)} %send_part.16), channel_id=1, source_target_pairs={{0,8},{8,0},{16,24},{24,16},{1,9},{9,1},{17,25},{25,17},{2,10},{10... | collective-permute-start | bytes 3145736 | tf_op jit(solution)/shard_map/ppermute | solution.py:22
  143.7 55.9 %collective-permute-start.17 = (bf16[128,7680]{1,0:T(8,128)(2,1)S(1)}, bf16[128,7680]{1,0:T(8,128)(2,1)}, u32[]{:S(2)}, u32[]{:S(2)}) collective-permute-start(bf16[128,7680]{1,0:T(8,128)(2,1)S(1)} %constant_dynamic-update-slice_fusion.2), channel_id=1, source_target_pairs={{0,2},{2,0},{4,6},{6,4},{1,3},{3,1},{5,7},{7,5},{8,10},{10,8},{12,... | collective-permute-start | bytes 5898248 | tf_op jit(solution)/shard_map/ppermute | solution.py:22
  146.8 42.3 %collective-permute-start.14 = (bf16[1024,512]{1,0:T(8,128)(2,1)S(1)}, bf16[1024,512]{1,0:T(8,128)(2,1)S(1)}, u32[]{:S(2)}, u32[]{:S(2)}) collective-permute-start(bf16[1024,512]{1,0:T(8,128)(2,1)S(1)} %send_part.17), channel_id=1, source_target_pairs={{0,8},{8,0},{16,24},{24,16},{1,9},{9,1},{17,25},{25,17},{2,10},{10... | collective-permute-start | bytes 3145736 | tf_op jit(solution)/shard_map/ppermute | solution.py:22
  148.8 40.3 %collective-permute-start.16 = (bf16[64,1024]{1,0:T(8,128)(2,1)S(1)}, bf16[64,1024]{1,0:T(8,128)(2,1)S(1)}, u32[]{:S(2)}, u32[]{:S(2)}) collective-permute-start(bf16[64,1024]{1,0:T(8,128)(2,1)S(1)} %fusion.2), channel_id=1, source_target_pairs={{0,8},{8,0},{16,24},{24,16},{1,9},{9,1},{17,25},{25,17},{2,10},{10... | collective-permute-start | bytes 393224 | tf_op jit(solution)/shard_map/ppermute | solution.py:22
  154.7 62.9 %collective-permute-start.13 = (bf16[1024,512]{1,0:T(8,128)(2,1)}, bf16[1024,512]{1,0:T(8,128)(2,1)S(1)}, u32[]{:S(2)}, u32[]{:S(2)}) collective-permute-start(bf16[1024,512]{1,0:T(8,128)(2,1)} %send_part.18), channel_id=1, source_target_pairs={{0,8},{8,0},{16,24},{24,16},{1,9},{9,1},{17,25},{25,17},{2,10},{10... | collective-permute-start | bytes 3145736 | tf_op jit(solution)/shard_map/ppermute | solution.py:22
  189.1 8.9 %collective-permute-start.20 = (bf16[64,1024]{1,0:T(8,128)(2,1)S(1)}, bf16[64,1024]{1,0:T(8,128)(2,1)S(1)}, u32[]{:S(2)}, u32[]{:S(2)}) collective-permute-start(bf16[64,1024]{1,0:T(8,128)(2,1)S(1)} %collective-permute-done.16), channel_id=1, source_target_pairs={{0,4},{2,6},{4,0},{6,2},{1,5},{3,7},{5,1},{7,3},{8,12},{10,14},{12... | collective-permute-start | bytes 393224 | tf_op jit(solution)/shard_map/ppermute | solution.py:22
  190.8 7.4 %collective-permute-start.18 = (bf16[1024,128]{1,0:T(8,128)(2,1)}, bf16[1024,128]{1,0:T(8,128)(2,1)S(1)}, u32[]{:S(2)}, u32[]{:S(2)}) collective-permute-start(bf16[1024,128]{1,0:T(8,128)(2,1)} %collective-permute-done.11), channel_id=1, source_target_pairs={{0,1},{1,0},{2,3},{3,2},{4,5},{5,4},{6,7},{7,6},{8,9},{9,8},{10,11... | collective-permute-start | bytes 786440 | tf_op jit(solution)/shard_map/ppermute | solution.py:22
  196.4 37.6 %collective-permute-start.24 = (bf16[1024,512]{1,0:T(8,128)(2,1)}, bf16[1024,512]{1,0:T(8,128)(2,1)S(1)}, u32[]{:S(2)}, u32[]{:S(2)}) collective-permute-start(bf16[1024,512]{1,0:T(8,128)(2,1)} %send_part.19), channel_id=1, source_target_pairs={{0,8},{8,0},{16,24},{24,16},{1,9},{9,1},{17,25},{25,17},{2,10},{10... | collective-permute-start | bytes 3145736 | tf_op jit(solution)/shard_map/ppermute | solution.py:22
  198.0 1.6 collective-permute-start.21
  211.4 45.1 %collective-permute-start.23 = (bf16[1024,512]{1,0:T(8,128)(2,1)}, bf16[1024,512]{1,0:T(8,128)(2,1)S(1)}, u32[]{:S(2)}, u32[]{:S(2)}) collective-permute-start(bf16[1024,512]{1,0:T(8,128)(2,1)} %send_part.20), channel_id=1, source_target_pairs={{0,8},{8,0},{16,24},{24,16},{1,9},{9,1},{17,25},{25,17},{2,10},{10... | collective-permute-start | bytes 3145736 | tf_op jit(solution)/shard_map/ppermute | solution.py:22
  221.7 57.4 %collective-permute-start.22 = (bf16[1024,512]{1,0:T(8,128)(2,1)}, bf16[1024,512]{1,0:T(8,128)(2,1)}, u32[]{:S(2)}, u32[]{:S(2)}) collective-permute-start(bf16[1024,512]{1,0:T(8,128)(2,1)} %send_part.21), channel_id=1, source_target_pairs={{0,8},{8,0},{16,24},{24,16},{1,9},{9,1},{17,25},{25,17},{2,10},{10... | collective-permute-start | bytes 3145736 | tf_op jit(solution)/shard_map/ppermute | solution.py:22
  238.1 63.3 %collective-permute-start.27 = (bf16[1024,512]{1,0:T(8,128)(2,1)}, bf16[1024,512]{1,0:T(8,128)(2,1)S(1)}, u32[]{:S(2)}, u32[]{:S(2)}) collective-permute-start(bf16[1024,512]{1,0:T(8,128)(2,1)} %send_part.22), channel_id=1, source_target_pairs={{0,8},{8,0},{16,24},{24,16},{1,9},{9,1},{17,25},{25,17},{2,10},{10... | collective-permute-start | bytes 3145736 | tf_op jit(solution)/shard_map/ppermute | solution.py:22
  260.6 63.3 %collective-permute-start.26 = (bf16[1024,512]{1,0:T(8,128)(2,1)}, bf16[1024,512]{1,0:T(8,128)(2,1)S(1)}, u32[]{:S(2)}, u32[]{:S(2)}) collective-permute-start(bf16[1024,512]{1,0:T(8,128)(2,1)} %send_part.23), channel_id=1, source_target_pairs={{0,8},{8,0},{16,24},{24,16},{1,9},{9,1},{17,25},{25,17},{2,10},{10... | collective-permute-start | bytes 3145736 | tf_op jit(solution)/shard_map/ppermute | solution.py:22
  282.0 64.3 %collective-permute-start.25 = (bf16[1024,512]{1,0:T(8,128)(2,1)S(1)}, bf16[1024,512]{1,0:T(8,128)(2,1)S(1)}, u32[]{:S(2)}, u32[]{:S(2)}) collective-permute-start(bf16[1024,512]{1,0:T(8,128)(2,1)S(1)} %send_part.24), channel_id=1, source_target_pairs={{0,8},{8,0},{16,24},{24,16},{1,9},{9,1},{17,25},{25,17},{2,10},{10... | collective-permute-start | bytes 3145736 | tf_op jit(solution)/shard_map/ppermute | solution.py:22
  305.5 70.1 %collective-permute-start.30 = (bf16[1024,512]{1,0:T(8,128)(2,1)}, bf16[1024,512]{1,0:T(8,128)(2,1)}, u32[]{:S(2)}, u32[]{:S(2)}) collective-permute-start(bf16[1024,512]{1,0:T(8,128)(2,1)} %send_part.25), channel_id=1, source_target_pairs={{0,8},{8,0},{16,24},{24,16},{1,9},{9,1},{17,25},{25,17},{2,10},{10... | collective-permute-start | bytes 3145736 | tf_op jit(solution)/shard_map/ppermute | solution.py:22
  326.6 54.1 %collective-permute-start.29 = (bf16[1024,256]{1,0:T(8,128)(2,1)S(1)}, bf16[1024,256]{1,0:T(8,128)(2,1)S(1)}, u32[]{:S(2)}, u32[]{:S(2)}) collective-permute-start(bf16[1024,256]{1,0:T(8,128)(2,1)S(1)} %send_part.26), channel_id=1, source_target_pairs={{0,8},{8,0},{16,24},{24,16},{1,9},{9,1},{17,25},{25,17},{2,10},{10... | collective-permute-start | bytes 1572872 | tf_op jit(solution)/shard_map/ppermute | solution.py:22
  349.1 41.9 %collective-permute-start.28 = (bf16[1024,256]{1,0:T(8,128)(2,1)S(1)}, bf16[1024,256]{1,0:T(8,128)(2,1)S(1)}, u32[]{:S(2)}, u32[]{:S(2)}) collective-permute-start(bf16[1024,256]{1,0:T(8,128)(2,1)S(1)} %send_part.27), channel_id=1, source_target_pairs={{0,8},{8,0},{16,24},{24,16},{1,9},{9,1},{17,25},{25,17},{2,10},{10... | collective-permute-start | bytes 1572872 | tf_op jit(solution)/shard_map/ppermute | solution.py:22
  (6 other events, 45.9 us)

commit v3 on v2

--- a/solution.py
+++ b/solution.py
@@ -264,6 +264,27 @@
     )(*operands)
 
 
+def join_kernel(own, received, _, out):
+    out[...] = (own[...].astype(jnp.float32) + received[...].astype(jnp.float32)).astype(jnp.bfloat16)
+
+
+def join_chunk(own, received, start, merged):
+    rows, width = own.shape
+    step_rows = rows // 2
+    part = pl.BlockSpec((step_rows, width), lambda i: (i, 0))
+    return pl.pallas_call(
+        join_kernel,
+        grid=(2,),
+        in_specs=[part, part, pl.BlockSpec(memory_space=pl.ANY)],
+        out_specs=pl.BlockSpec((step_rows, width), lambda i: (i, start // width)),
+        out_shape=jax.ShapeDtypeStruct(merged.shape, merged.dtype),
+        input_output_aliases={2: 0},
+        compiler_params=pltpu.CompilerParams(vmem_limit_bytes=VMEM_LIMIT),
+        cost_estimate=pl.CostEstimate(flops=rows * width, bytes_accessed=6 * rows * width, transcendentals=0),
+        name="join_part",
+    )(own, received, merged)
+
+
 def bits_of(axis):
     return [1 << bit for bit in reversed(range((lax.axis_size(axis) - 1).bit_length()))]
 
@@ -284,6 +305,14 @@
     for number, bits in enumerate(bits_of(axis)):
         place = place + jnp.where(apart & bits != 0, 1 << number, 0)
     return place * part + index % part
+
+
+def index_at(place, part, axis):
+    number = place // part
+    apart = jnp.zeros_like(place)
+    for bit, bits in enumerate(bits_of(axis)):
+        apart = apart + jnp.where(number & (1 << bit) != 0, bits, 0)
+    return (apart ^ lax.axis_index(axis)) * part + place % part
 
 
 def after(value, *others):
@@ -309,7 +338,6 @@
     panel = doubled(lower_in, "col", 1)
     order = pivot_order[0][:, None]
     every = jnp.arange(size, dtype=jnp.int32)
-    in_row_order = place_of(every, upper_in.shape[0], "row")
     in_col_order = place_of(every, lower_in.shape[1], "col")
     orders = (
         place_of(order, diag_block.shape[0], ("row", "col")),
@@ -318,13 +346,9 @@
     )
     block_rows = rows // block_mask.shape[1]
     flags = block_mask[0].astype(jnp.float32)
-    other_flags = partner(flags, "cube", 1)
-    other_flags = jnp.where(parity == 0, other_flags[:, :1], other_flags[:, 1:])
-    other_flags = jnp.repeat(other_flags, block_rows, axis=0)
+    own_flags = flags
     flags = jnp.repeat(flags, block_rows, axis=0)
     flags = jnp.where(parity == 0, flags[:, ::-1], flags)
-    chosen = (row_map[0][:, None] == jnp.arange(rows, dtype=jnp.int32)[None, :]).astype(jnp.bfloat16)
-
     def columns_of(place, first, last):
         return lax.dynamic_slice_in_dim(upper_in, place * half + first, last - first, 1)
 
@@ -340,10 +364,14 @@
     share = upper_in.shape[0]
     share_hi = lax.dynamic_slice_in_dim(hi, row * share, share, 0)
     share_lo = lax.dynamic_slice_in_dim(lo, row * share, share, 0)
-    same = (in_col_order[:, None, None] == jnp.arange(size)[None, :, None]) & (
-        in_row_order[:, None, None] == jnp.arange(size)[None, None, :]
-    )
-    same = jnp.any(same, axis=0).astype(jnp.bfloat16)
+    col_order = index_at(every, lower_in.shape[1], "col")
+    row_order = index_at(every, upper_in.shape[0], "row")
+    same = (after(col_order, hi)[:, None] == row_order[None, :]).astype(jnp.bfloat16)
+
+    def choice(order):
+        return (order[:, None] == jnp.arange(rows, dtype=jnp.int32)[None, :]).astype(jnp.bfloat16)
+
+    chosen = choice(after(row_map[0], hi))
 
     bounds = [width * chunk for chunk in range(RAW, CHUNKS + 1)]
     if width % 256 == 0:
@@ -367,40 +395,56 @@
             for step in range(1, len(bits_of("row"))):
                 late = next_doubled(after(late, sent[0]), "row", 0, step)
         if number == 2:
-            kept_upper = next_doubled(after(columns_of(parity, 0, half), raw_received), "row", 0, 0)
+            kept_upper = next_doubled(after(columns_of(parity, 0, half), raw_received, sent[1]), "row", 0, 0)
         if number == 3:
             before += [left_received]
-            raw_upper = after(early[:, :raw_end], received[0])
+            raw_upper = after(early[:, :raw_end], received[0], sent[2])
             right_share = (fast(share_hi, raw_upper) + fast(share_lo, raw_upper)).astype(jnp.bfloat16)
             right_received = partner(right_share, "cube", 1)
         if number == 4:
             before += [kept_upper]
             for step in range(1, len(bits_of("row"))):
-                kept_upper = next_doubled(after(kept_upper, received[1]), "row", 0, step)
+                kept_upper = next_doubled(after(kept_upper, received[1], sent[3]), "row", 0, step)
         if number == 5:
             before += [right_received]
-            other_left = doubled(after(left_received, received[2]), "col", 1)
-            other_left = (fast(other_left, same) * other_flags).astype(jnp.bfloat16)
+            other_left = doubled(after(left_received, received[2], sent[4]), "col", 1)
         if number == 6:
             before += [kept_upper]
-            other_right = doubled(after(right_received, received[3]), "row", 0)
+            other_right = doubled(after(right_received, received[3], sent[5]), "row", 0)
         if number == 7:
             before += [other_left, other_right]
+        if number == 9:
+            other_flags = jnp.where(parity == 0, other_flags[:, :1], other_flags[:, 1:])
+            other_left = fast(other_left, same) * jnp.repeat(other_flags, block_rows, axis=0)
+            other_left = other_left.astype(jnp.bfloat16)
+        if number == 10:
+            before += [other_chosen, other_left]
+        if number == 8:
+            other_flags = partner(after(own_flags, received[5], sent[7]), "cube", 1)
+            other_chosen = choice(partner(after(row_map[0], received[5], sent[7]), "cube", 1))
         if number >= BEHIND:
             merged = merge(number - BEHIND)
             before += [merged]
         place = after(sent_place, *before) if before else sent_place
         piece, first = (early, 0) if end <= cut else (late, cut)
         sent.append(send_chunk(place, hi, lo, sent_left, trailing, [piece], [first], start, end - start))
-        received.append(partner(sent[-1], "cube", 1))
+        outgoing = sent[-1]
+        if number == len(spans) - 1:
+            outgoing = fast(other_chosen, outgoing).astype(jnp.bfloat16)
+        received.append(partner(outgoing, "cube", 1))
 
     for start in range(0, raw_end, width):
         merged = merge_chunk(
             kept_place, hi, lo, kept_left, trailing, chosen, raw_received, [kept_upper], [0], start, width, merged,
             (0, other_left, other_right),
         )
-    for number in range(len(spans) - BEHIND, len(spans)):
+    for number in range(len(spans) - BEHIND, len(spans) - 1):
         merged = merge(number)
+    start, end = spans[-1]
+    own = send_chunk(
+        after(kept_place, merged), hi, lo, kept_left, trailing, [kept_upper], [0], start, end - start
+    )
+    merged = join_chunk(own, received[-1], start, merged)
     return merged[None]
 
 

time: 397 us -> 361 us (0.909)
  waiting for transfers between devices: 174 us -> 150 us
  other arithmetic: 14.8 us -> 6.23 us
  starting transfers between devices: 39.3 us -> 34.7 us
    ppermute x31 -> x32, waiting for transfers between devices: 174 us -> 150 us  [partner(): return lax.ppermute(block, axis, [(i, i ^ bits) for i in range(count)])]
    reduce_or x1 -> x0, other arithmetic: 11.1 us -> none  [local(): same = jnp.any(same, axis=0).astype(jnp.bfloat16)]
    ppermute x31 -> x32, starting transfers between devices: 39.3 us -> 34.7 us  [partner(): return lax.ppermute(block, axis, [(i, i ^ bits) for i in range(count)])]
    pallas_call x16 -> x15, Pallas kernels: 76.3 us -> 72.7 us  [merge_chunk(): pl.pallas_call(body, grid_spec=pltpu.PrefetchScalarGridSpec(num_scalar_pr...]
    pallas_call x14 -> x15, Pallas kernels: 48.9 us -> 50.4 us  [send_chunk(): pl.pallas_call(send_kernel, grid_spec=pltpu.PrefetchScalarGridSpec(num_sc...]
  transfers between devices with their start and end apart: 31 -> 32, of which waited for: 14 -> 13; matrix products, arithmetic and copies ran while one was open for 7% -> 4% of each run, Pallas kernels for 37% -> 42%
where the time goes in v3:
time: 361 us; the launch traced here: 359 us
  Pallas kernels  151 us (42%)
  waiting for transfers between devices  150 us (42%)
  starting transfers between devices  34.7 us (10%)
  local copies, waits for them, and re-layouts  14.8 us (4%)
  other arithmetic  6.23 us (2%)
    ppermute x32, waiting for transfers between devices, partner(): return lax.ppermute(block, axis, [(i, i ^ bits) for i in range(count)])  150 us
    pallas_call x15, Pallas kernels, merge_chunk(): pl.pallas_call(body, grid_spec=pltpu.PrefetchScalarGridSpec(num_scalar_pr...  72.7 us
    pallas_call x15, Pallas kernels, send_chunk(): pl.pallas_call(send_kernel, grid_spec=pltpu.PrefetchScalarGridSpec(num_sc...  50.4 us
    ppermute x32, starting transfers between devices, partner(): return lax.ppermute(block, axis, [(i, i ^ bits) for i in range(count)])  34.7 us
    pallas_call x1, Pallas kernels, factor(): pl.pallas_call(factor_kernel, out_shape=(jax.ShapeDtypeStruct((size, size...  26.7 us
  transfers between devices with their start and end apart: 32, of which 13 were waited for; matrix products, arithmetic and copies ran while one was open for 4% of the time, Pallas kernels for 42%

profile of v3, /device:TPU:0, one launch (start us, length us, event | category | flops | bytes accessed | tf_op | source)
XLA Modules:
  0.0 358.9 jit_solution(2590864733943737964)
XLA Ops:
  0.0 3.2 dynamic-slice_bitcast_fusion
  22.2 26.7 %factor.1 = (bf16[256,256]{1,0:T(8,128)(2,1)S(1)}, bf16[256,256]{1,0:T(8,128)(2,1)S(1)}, bf16[1024,256]{1,0:T(8,128)(2,1)S(1)}, bf16[1024,256]{1,0:T(8,128)(2,1)S(1)}, bf16[1024,256]{1,0:T(8,128)(2,1)S(1)}) custom-call(f32[256,256]{1,0:T(8,128)S(1)} %pad_maximum_fusion.4.block, s32[256,1]{1,0:T(8,128)S(1)} %get-tuple-element.64.order_of_diag, ...), custom_call_target="tpu_custom_call" | custom-call | flops 30000001024 | bytes 3000000 | tf_op jit(solution)/shard_map/factor/pallas_call | solution.py:118
  66.8 14.1 %collective-permute-done.6.received = bf16[1024,512]{1,0:T(8,128)(2,1)S(1)} collective-permute-done((bf16[1024,512]{1,0:T(8,128)(2,1)S(1)}, bf16[1024,512]{1,0:T(8,128)(2,1)S(1)}, u32[]{:S(2)}, u32[]{:S(2)}) %collective-permute-start.6) | collective-permute-done | bytes 1048608 | tf_op jit(solution)/shard_map/ppermute | solution.py:22
  87.8 15.6 %collective-permute-done.13.received = bf16[1024,512]{1,0:T(8,128)(2,1)S(1)} collective-permute-done((bf16[1024,512]{1,0:T(8,128)(2,1)S(1)}, bf16[1024,512]{1,0:T(8,128)(2,1)S(1)}, u32[]{:S(2)}, u32[]{:S(2)}) %collective-permute-start.13) | collective-permute-done | bytes 1048608 | tf_op jit(solution)/shard_map/ppermute | solution.py:22
  103.8 4.1 %send_part.19 = bf16[1024,512]{1,0:T(8,128)(2,1)} custom-call(s32[1]{0:T(128)} %bitcast.9.place, bf16[256,256]{1,0:T(8,128)(2,1)S(1)} %get-tuple-element.35.hi.refs_1_, bf16[256,256]{1,0:T(8,128)(2,1)S(1)} %get-tuple-element.36.lo.refs_2_, bf16[1024,256]{1,0:T(8,128)(2,1)S(1)} %get-tuple-element.39.left, bf16[1024,15360]{1,0:T(8,128)(2,1)} %bitcast.32, ...), custom_call_target="tpu_custom_call" | custom-call | flops 268435456 | bytes 2621440 | tf_op jit(solution)/shard_map/send_part/pallas_call | solution.py:206
  107.9 20.8 %collective-permute-done.15 = bf16[64,1024]{1,0:T(8,128)(2,1)S(1)} collective-permute-done((bf16[64,1024]{1,0:T(8,128)(2,1)S(1)}, bf16[64,1024]{1,0:T(8,128)(2,1)S(1)}, u32[]{:S(2)}, u32[]{:S(2)}) %collective-permute-start.15) | collective-permute-done | bytes 131104 | tf_op jit(solution)/shard_map/ppermute | solution.py:22
  131.6 18.8 %collective-permute-done.11.received = bf16[1024,512]{1,0:T(8,128)(2,1)S(1)} collective-permute-done((bf16[1024,512]{1,0:T(8,128)(2,1)S(1)}, bf16[1024,512]{1,0:T(8,128)(2,1)S(1)}, u32[]{:S(2)}, u32[]{:S(2)}) %collective-permute-start.11) | collective-permute-done | bytes 1048608 | tf_op jit(solution)/shard_map/ppermute | solution.py:22
  158.4 3.1 collective-permute-done.20
  165.4 4.7 %merge_part.15.rest_1_ = bf16[1024,7680]{1,0:T(8,128)(2,1)} custom-call(s32[1]{0:T(128)} %bitcast.place.refs_0_, bf16[256,256]{1,0:T(8,128)(2,1)S(1)} %get-tuple-element.35.hi.refs_1_, bf16[256,256]{1,0:T(8,128)(2,1)S(1)} %get-tuple-element.36.lo.refs_2_, bf16[1024,256]{1,0:T(8,128)(2,1)S(1)} %get-tuple-element.37.left.refs_3_, ...), custom_call_target="tpu_custom_call" | custom-call | flops 1342177280 | bytes 4194304 | tf_op jit(solution)/shard_map/merge_part/pallas_call | solution.py:250
  173.6 4.7 %merge_part.16.rest_1_ = bf16[1024,7680]{1,0:T(8,128)(2,1)} custom-call(s32[1]{0:T(128)} %bitcast.place.refs_0_, bf16[256,256]{1,0:T(8,128)(2,1)S(1)} %get-tuple-element.35.hi.refs_1_, bf16[256,256]{1,0:T(8,128)(2,1)S(1)} %get-tuple-element.36.lo.refs_2_, bf16[1024,256]{1,0:T(8,128)(2,1)S(1)} %get-tuple-element.37.left.refs_3_, ...), custom_call_target="tpu_custom_call", output_to_operand_aliasing={{}: (8, {})} | custom-call | flops 1342177280 | bytes 4194304 | tf_op jit(solution)/shard_map/merge_part/pallas_call | solution.py:250
  184.3 4.7 %merge_part.17.rest_1_ = bf16[1024,7680]{1,0:T(8,128)(2,1)} custom-call(s32[1]{0:T(128)} %bitcast.place.refs_0_, bf16[256,256]{1,0:T(8,128)(2,1)S(1)} %get-tuple-element.35.hi.refs_1_, bf16[256,256]{1,0:T(8,128)(2,1)S(1)} %get-tuple-element.36.lo.refs_2_, bf16[1024,256]{1,0:T(8,128)(2,1)S(1)} %get-tuple-element.37.left.refs_3_, ...), custom_call_target="tpu_custom_call", output_to_operand_aliasing={{}: (8, {})} | custom-call | flops 1342177280 | bytes 4194304 | tf_op jit(solution)/shard_map/merge_part/pallas_call | solution.py:250
  189.0 13.1 %collective-permute-done.18.received = bf16[1024,512]{1,0:T(8,128)(2,1)} collective-permute-done((bf16[1024,512]{1,0:T(8,128)(2,1)}, bf16[1024,512]{1,0:T(8,128)(2,1)}, u32[]{:S(2)}, u32[]{:S(2)}) %collective-permute-start.18) | collective-permute-done | bytes 1048608 | tf_op jit(solution)/shard_map/ppermute | solution.py:22
  203.8 4.1 %send_part.23 = bf16[1024,512]{1,0:T(8,128)(2,1)} custom-call(s32[1]{0:T(128)} %bitcast.9.place, bf16[256,256]{1,0:T(8,128)(2,1)S(1)} %get-tuple-element.35.hi.refs_1_, bf16[256,256]{1,0:T(8,128)(2,1)S(1)} %get-tuple-element.36.lo.refs_2_, bf16[1024,256]{1,0:T(8,128)(2,1)S(1)} %get-tuple-element.39.left, bf16[1024,15360]{1,0:T(8,128)(2,1)} %bitcast.39, ...), custom_call_target="tpu_custom_call" | custom-call | flops 268435456 | bytes 2621440 | tf_op jit(solution)/shard_map/send_part/pallas_call | solution.py:206
  208.3 4.7 %merge_part.18.rest_1_ = bf16[1024,7680]{1,0:T(8,128)(2,1)} custom-call(s32[1]{0:T(128)} %bitcast.place.refs_0_, bf16[256,256]{1,0:T(8,128)(2,1)S(1)} %get-tuple-element.35.hi.refs_1_, bf16[256,256]{1,0:T(8,128)(2,1)S(1)} %get-tuple-element.36.lo.refs_2_, bf16[1024,256]{1,0:T(8,128)(2,1)S(1)} %get-tuple-element.37.left.refs_3_, ...), custom_call_target="tpu_custom_call", output_to_operand_aliasing={{}: (8, {})} | custom-call | flops 1342177280 | bytes 4194304 | tf_op jit(solution)/shard_map/merge_part/pallas_call | solution.py:250
  213.0 34.1 %collective-permute-done.26 = f32[8,2]{0,1:T(2,128)S(1)} collective-permute-done((f32[8,2]{0,1:T(2,128)S(1)}, f32[8,2]{0,1:T(2,128)S(1)}, u32[]{:S(2)}, u32[]{:S(2)}) %collective-permute-start.26) | collective-permute-done | bytes 96 | tf_op jit(solution)/shard_map/ppermute | solution.py:22
  247.5 4.1 %send_part.24 = bf16[1024,512]{1,0:T(8,128)(2,1)} custom-call(s32[1]{0:T(128)} %bitcast.9.place, bf16[256,256]{1,0:T(8,128)(2,1)S(1)} %get-tuple-element.35.hi.refs_1_, bf16[256,256]{1,0:T(8,128)(2,1)S(1)} %get-tuple-element.36.lo.refs_2_, bf16[1024,256]{1,0:T(8,128)(2,1)S(1)} %get-tuple-element.39.left, bf16[1024,15360]{1,0:T(8,128)(2,1)} %bitcast.41, ...), custom_call_target="tpu_custom_call" | custom-call | flops 268435456 | bytes 2621440 | tf_op jit(solution)/shard_map/send_part/pallas_call | solution.py:206
  253.2 5.0 %merge_part.19.rest_1_ = bf16[1024,7680]{1,0:T(8,128)(2,1)} custom-call(s32[1]{0:T(128)} %bitcast.place.refs_0_, bf16[256,256]{1,0:T(8,128)(2,1)S(1)} %get-tuple-element.35.hi.refs_1_, bf16[256,256]{1,0:T(8,128)(2,1)S(1)} %get-tuple-element.36.lo.refs_2_, bf16[1024,256]{1,0:T(8,128)(2,1)S(1)} %get-tuple-element.37.left.refs_3_, ...), custom_call_target="tpu_custom_call", output_to_operand_aliasing={{}: (8, {})} | custom-call | flops 1342177280 | bytes 4194304 | tf_op jit(solution)/shard_map/merge_part/pallas_call | solution.py:250
  258.3 4.1 %send_part.25 = bf16[1024,512]{1,0:T(8,128)(2,1)} custom-call(s32[1]{0:T(128)} %bitcast.9.place, bf16[256,256]{1,0:T(8,128)(2,1)S(1)} %get-tuple-element.35.hi.refs_1_, bf16[256,256]{1,0:T(8,128)(2,1)S(1)} %get-tuple-element.36.lo.refs_2_, bf16[1024,256]{1,0:T(8,128)(2,1)S(1)} %get-tuple-element.39.left, bf16[1024,15360]{1,0:T(8,128)(2,1)} %bitcast.43, ...), custom_call_target="tpu_custom_call" | custom-call | flops 268435456 | bytes 2621440 | tf_op jit(solution)/shard_map/send_part/pallas_call | solution.py:206
  264.4 5.0 %merge_part.20.rest_1_ = bf16[1024,7680]{1,0:T(8,128)(2,1)} custom-call(s32[1]{0:T(128)} %bitcast.place.refs_0_, bf16[256,256]{1,0:T(8,128)(2,1)S(1)} %get-tuple-element.35.hi.refs_1_, bf16[256,256]{1,0:T(8,128)(2,1)S(1)} %get-tuple-element.36.lo.refs_2_, bf16[1024,256]{1,0:T(8,128)(2,1)S(1)} %get-tuple-element.37.left.refs_3_, ...), custom_call_target="tpu_custom_call", output_to_operand_aliasing={{}: (8, {})} | custom-call | flops 1342177280 | bytes 4194304 | tf_op jit(solution)/shard_map/merge_part/pallas_call | solution.py:250
  269.5 4.1 %send_part.26 = bf16[1024,512]{1,0:T(8,128)(2,1)} custom-call(s32[1]{0:T(128)} %bitcast.9.place, bf16[256,256]{1,0:T(8,128)(2,1)S(1)} %get-tuple-element.35.hi.refs_1_, bf16[256,256]{1,0:T(8,128)(2,1)S(1)} %get-tuple-element.36.lo.refs_2_, bf16[1024,256]{1,0:T(8,128)(2,1)S(1)} %get-tuple-element.39.left, bf16[1024,15360]{1,0:T(8,128)(2,1)} %bitcast.45, ...), custom_call_target="tpu_custom_call" | custom-call | flops 268435456 | bytes 2621440 | tf_op jit(solution)/shard_map/send_part/pallas_call | solution.py:206
  275.2 4.7 %merge_part.21.rest_1_ = bf16[1024,7680]{1,0:T(8,128)(2,1)} custom-call(s32[1]{0:T(128)} %bitcast.place.refs_0_, bf16[256,256]{1,0:T(8,128)(2,1)S(1)} %get-tuple-element.35.hi.refs_1_, bf16[256,256]{1,0:T(8,128)(2,1)S(1)} %get-tuple-element.36.lo.refs_2_, bf16[1024,256]{1,0:T(8,128)(2,1)S(1)} %get-tuple-element.37.left.refs_3_, ...), custom_call_target="tpu_custom_call", output_to_operand_aliasing={{}: (8, {})} | custom-call | flops 1342177280 | bytes 4194304 | tf_op jit(solution)/shard_map/merge_part/pallas_call | solution.py:250
  279.9 12.1 %collective-permute-done.23.received = bf16[1024,512]{1,0:T(8,128)(2,1)S(1)} collective-permute-done((bf16[1024,512]{1,0:T(8,128)(2,1)}, bf16[1024,512]{1,0:T(8,128)(2,1)S(1)}, u32[]{:S(2)}, u32[]{:S(2)}) %collective-permute-start.23) | collective-permute-done | bytes 1048608 | tf_op jit(solution)/shard_map/ppermute | solution.py:22
  292.0 3.7 %send_part.27 = bf16[1024,256]{1,0:T(8,128)(2,1)} custom-call(s32[1]{0:T(128)} %bitcast.9.place, bf16[256,256]{1,0:T(8,128)(2,1)S(1)} %get-tuple-element.35.hi.refs_1_, bf16[256,256]{1,0:T(8,128)(2,1)S(1)} %get-tuple-element.36.lo.refs_2_, bf16[1024,256]{1,0:T(8,128)(2,1)S(1)} %get-tuple-element.39.left, bf16[1024,15360]{1,0:T(8,128)(2,1)} %bitcast.47, ...), custom_call_target="tpu_custom_call" | custom-call | flops 134217728 | bytes 1310720 | tf_op jit(solution)/shard_map/send_part/pallas_call | solution.py:206
  297.3 4.7 %merge_part.22.refs_10_ = bf16[1024,7680]{1,0:T(8,128)(2,1)} custom-call(s32[1]{0:T(128)} %bitcast.place.refs_0_, bf16[256,256]{1,0:T(8,128)(2,1)S(1)} %get-tuple-element.35.hi.refs_1_, bf16[256,256]{1,0:T(8,128)(2,1)S(1)} %get-tuple-element.36.lo.refs_2_, bf16[1024,256]{1,0:T(8,128)(2,1)S(1)} %get-tuple-element.37.left.refs_3_, ...), custom_call_target="tpu_custom_call", output_to_operand_aliasing={{}: (8, {})} | custom-call | flops 1342177280 | bytes 4194304 | tf_op jit(solution)/shard_map/merge_part/pallas_call | solution.py:250
  302.0 12.4 %collective-permute-done.29.received = bf16[1024,512]{1,0:T(8,128)(2,1)S(1)} collective-permute-done((bf16[1024,512]{1,0:T(8,128)(2,1)}, bf16[1024,512]{1,0:T(8,128)(2,1)S(1)}, u32[]{:S(2)}, u32[]{:S(2)}) %collective-permute-start.29) | collective-permute-done | bytes 1048608 | tf_op jit(solution)/shard_map/ppermute | solution.py:22
  319.6 5.3 %merge_part.23.refs_10_ = bf16[1024,7680]{1,0:T(8,128)(2,1)} custom-call(s32[1]{0:T(128)} %bitcast.place.refs_0_, bf16[256,256]{1,0:T(8,128)(2,1)S(1)} %get-tuple-element.35.hi.refs_1_, bf16[256,256]{1,0:T(8,128)(2,1)S(1)} %get-tuple-element.36.lo.refs_2_, bf16[1024,256]{1,0:T(8,128)(2,1)S(1)} %get-tuple-element.37.left.refs_3_, ...), custom_call_target="tpu_custom_call", output_to_operand_aliasing={{}: (10, {})} | custom-call | flops 1342177280 | bytes 4194304 | tf_op jit(solution)/shard_map/merge_part/pallas_call | solution.py:250
  325.0 5.3 %merge_part.24.rest_1_ = bf16[1024,7680]{1,0:T(8,128)(2,1)} custom-call(s32[1]{0:T(128)} %bitcast.place.refs_0_, bf16[256,256]{1,0:T(8,128)(2,1)S(1)} %get-tuple-element.35.hi.refs_1_, bf16[256,256]{1,0:T(8,128)(2,1)S(1)} %get-tuple-element.36.lo.refs_2_, bf16[1024,256]{1,0:T(8,128)(2,1)S(1)} %get-tuple-element.37.left.refs_3_, ...), custom_call_target="tpu_custom_call", output_to_operand_aliasing={{}: (10, {})} | custom-call | flops 1342177280 | bytes 4194304 | tf_op jit(solution)/shard_map/merge_part/pallas_call | solution.py:250
  330.3 4.7 %merge_part.25.rest_1_ = bf16[1024,7680]{1,0:T(8,128)(2,1)} custom-call(s32[1]{0:T(128)} %bitcast.place.refs_0_, bf16[256,256]{1,0:T(8,128)(2,1)S(1)} %get-tuple-element.35.hi.refs_1_, bf16[256,256]{1,0:T(8,128)(2,1)S(1)} %get-tuple-element.36.lo.refs_2_, bf16[1024,256]{1,0:T(8,128)(2,1)S(1)} %get-tuple-element.37.left.refs_3_, ...), custom_call_target="tpu_custom_call", output_to_operand_aliasing={{}: (8, {})} | custom-call | flops 1342177280 | bytes 4194304 | tf_op jit(solution)/shard_map/merge_part/pallas_call | solution.py:250
  335.0 4.7 %merge_part.26.rest_1_ = bf16[1024,7680]{1,0:T(8,128)(2,1)} custom-call(s32[1]{0:T(128)} %bitcast.place.refs_0_, bf16[256,256]{1,0:T(8,128)(2,1)S(1)} %get-tuple-element.35.hi.refs_1_, bf16[256,256]{1,0:T(8,128)(2,1)S(1)} %get-tuple-element.36.lo.refs_2_, bf16[1024,256]{1,0:T(8,128)(2,1)S(1)} %get-tuple-element.37.left.refs_3_, ...), custom_call_target="tpu_custom_call", output_to_operand_aliasing={{}: (8, {})} | custom-call | flops 1342177280 | bytes 4194304 | tf_op jit(solution)/shard_map/merge_part/pallas_call | solution.py:250
  339.7 4.7 %merge_part.27.rest_1_ = bf16[1024,7680]{1,0:T(8,128)(2,1)} custom-call(s32[1]{0:T(128)} %bitcast.place.refs_0_, bf16[256,256]{1,0:T(8,128)(2,1)S(1)} %get-tuple-element.35.hi.refs_1_, bf16[256,256]{1,0:T(8,128)(2,1)S(1)} %get-tuple-element.36.lo.refs_2_, bf16[1024,256]{1,0:T(8,128)(2,1)S(1)} %get-tuple-element.37.left.refs_3_, ...), custom_call_target="tpu_custom_call", output_to_operand_aliasing={{}: (8, {})} | custom-call | flops 1342177280 | bytes 4194304 | tf_op jit(solution)/shard_map/merge_part/pallas_call | solution.py:250
  344.4 5.1 %merge_part.28.rest_1_ = bf16[1024,7680]{1,0:T(8,128)(2,1)} custom-call(s32[1]{0:T(128)} %bitcast.place.refs_0_, bf16[256,256]{1,0:T(8,128)(2,1)S(1)} %get-tuple-element.35.hi.refs_1_, bf16[256,256]{1,0:T(8,128)(2,1)S(1)} %get-tuple-element.36.lo.refs_2_, bf16[1024,256]{1,0:T(8,128)(2,1)S(1)} %get-tuple-element.37.left.refs_3_, ...), custom_call_target="tpu_custom_call", output_to_operand_aliasing={{}: (8, {})} | custom-call | flops 1342177280 | bytes 4194304 | tf_op jit(solution)/shard_map/merge_part/pallas_call | solution.py:250
  349.5 4.5 %merge_part.29._ = bf16[1024,7680]{1,0:T(8,128)(2,1)} custom-call(s32[1]{0:T(128)} %bitcast.place.refs_0_, bf16[256,256]{1,0:T(8,128)(2,1)S(1)} %get-tuple-element.35.hi.refs_1_, bf16[256,256]{1,0:T(8,128)(2,1)S(1)} %get-tuple-element.36.lo.refs_2_, bf16[1024,256]{1,0:T(8,128)(2,1)S(1)} %get-tuple-element.37.left.refs_3_, ...), custom_call_target="tpu_custom_call", output_to_operand_aliasing={{}: (8, {})} | custom-call | flops 671088640 | bytes 2097152 | tf_op jit(solution)/shard_map/merge_part/pallas_call | solution.py:250
  (152 shorter events, 87.4 us)
Async XLA Ops:
  3.2 56.8 %collective-permute-start.7 = (bf16[1024,1024]{1,0:T(8,128)(2,1)}, bf16[1024,1024]{1,0:T(8,128)(2,1)}, u32[]{:S(2)}, u32[]{:S(2)}) collective-permute-start(bf16[1024,1024]{1,0:T(8,128)(2,1)} %dynamic-slice_bitcast_fusion), channel_id=1, source_target_pairs={{0,8},{8,0},{16,24},{24,16},{1,9},{9,1},{17,25},{25,17},{2,10},{10... | collective-permute-start | bytes 6291464 | tf_op jit(solution)/shard_map/ppermute | solution.py:22
  6.3 6.7 %collective-permute-start = (f32[32,256]{1,0:T(8,128)S(1)}, f32[32,256]{1,0:T(8,128)S(1)}, u32[]{:S(2)}, u32[]{:S(2)}) collective-permute-start(f32[32,256]{1,0:T(8,128)S(1)} %bitcast.59), channel_id=1, source_target_pairs={{0,4},{1,5},{2,6},{3,7},{4,0},{5,1},{6,2},{7,3},{8,12},{9,13},{10,... | collective-permute-start | bytes 98312 | tf_op jit(solution)/shard_map/ppermute | solution.py:22
  7.8 13.3 %collective-permute-start.3 = (bf16[1024,128]{1,0:T(8,128)(2,1)}, bf16[1024,128]{1,0:T(8,128)(2,1)}, u32[]{:S(2)}, u32[]{:S(2)}) collective-permute-start(bf16[1024,128]{1,0:T(8,128)(2,1)} %bitcast.4), channel_id=1, source_target_pairs={{0,1},{1,0},{2,3},{3,2},{4,5},{5,4},{6,7},{7,6},{8,9},{9,8},{10,11... | collective-permute-start | bytes 786440 | tf_op jit(solution)/shard_map/ppermute | solution.py:22
  9.3 10.7 %collective-permute-start.4 = (bf16[64,2048]{1,0:T(8,128)(2,1)S(1)}, bf16[64,2048]{1,0:T(8,128)(2,1)}, u32[]{:S(2)}, u32[]{:S(2)}) collective-permute-start(bf16[64,2048]{1,0:T(8,128)(2,1)S(1)} %dynamic-slice_bitcast_fusion.3), channel_id=1, source_target_pairs={{0,4},{2,6},{4,0},{6,2},{1,5},{3,7},{5,1},{7,3},{8,12},{10,14},{12... | collective-permute-start | bytes 786440 | tf_op jit(solution)/shard_map/ppermute | solution.py:22
  9.9 39.6 %collective-permute-start.8 = (bf16[64,5632]{1,0:T(8,128)(2,1)S(1)}, bf16[64,5632]{1,0:T(8,128)(2,1)}, u32[]{:S(2)}, u32[]{:S(2)}) collective-permute-start(bf16[64,5632]{1,0:T(8,128)(2,1)S(1)} %dynamic-slice_bitcast_fusion.2), channel_id=1, source_target_pairs={{0,4},{2,6},{4,0},{6,2},{1,5},{3,7},{5,1},{7,3},{8,12},{10,14},{12... | collective-permute-start | bytes 2162696 | tf_op jit(solution)/shard_map/ppermute | solution.py:22
  13.0 1.3 collective-permute-start.1
  14.4 5.6 %collective-permute-start.2 = (f32[128,256]{1,0:T(8,128)S(1)}, f32[128,256]{1,0:T(8,128)S(1)}, u32[]{:S(2)}, u32[]{:S(2)}) collective-permute-start(f32[128,256]{1,0:T(8,128)S(1)} %pad_maximum_fusion.6), channel_id=1, source_target_pairs={{0,1},{1,0},{2,3},{3,2},{4,5},{5,4},{6,7},{7,6},{8,9},{9,8},{10,11... | collective-permute-start | bytes 393224 | tf_op jit(solution)/shard_map/ppermute | solution.py:22
  21.0 29.7 %collective-permute-start.5 = (bf16[128,2048]{1,0:T(8,128)(2,1)S(1)}, bf16[128,2048]{1,0:T(8,128)(2,1)S(1)}, u32[]{:S(2)}, u32[]{:S(2)}) collective-permute-start(bf16[128,2048]{1,0:T(8,128)(2,1)S(1)} %pad_maximum_fusion.3), channel_id=1, source_target_pairs={{0,2},{2,0},{4,6},{6,4},{1,3},{3,1},{5,7},{7,5},{8,10},{10,8},{12,... | collective-permute-start | bytes 1572872 | tf_op jit(solution)/shard_map/ppermute | solution.py:22
  49.0 32.4 %collective-permute-start.10 = (bf16[1024,128]{1,0:T(8,128)(2,1)S(1)}, bf16[1024,128]{1,0:T(8,128)(2,1)S(1)}, u32[]{:S(2)}, u32[]{:S(2)}) collective-permute-start(bf16[1024,128]{1,0:T(8,128)(2,1)S(1)} %constant_dynamic-slice_fusion), channel_id=1, source_target_pairs={{0,8},{8,0},{16,24},{24,16},{1,9},{9,1},{17,25},{25,17},{2,10},{10... | collective-permute-start | bytes 786440 | tf_op jit(solution)/shard_map/ppermute | solution.py:22
  54.8 26.1 %collective-permute-start.6 = (bf16[1024,512]{1,0:T(8,128)(2,1)S(1)}, bf16[1024,512]{1,0:T(8,128)(2,1)S(1)}, u32[]{:S(2)}, u32[]{:S(2)}) collective-permute-start(bf16[1024,512]{1,0:T(8,128)(2,1)S(1)} %send_part.15), channel_id=1, source_target_pairs={{0,8},{8,0},{16,24},{24,16},{1,9},{9,1},{17,25},{25,17},{2,10},{10... | collective-permute-start | bytes 3145736 | tf_op jit(solution)/shard_map/ppermute | solution.py:22
  56.4 4.8 %collective-permute-start.9 = (bf16[128,5632]{1,0:T(8,128)(2,1)S(1)}, bf16[128,5632]{1,0:T(8,128)(2,1)}, u32[]{:S(2)}, u32[]{:S(2)}) collective-permute-start(bf16[128,5632]{1,0:T(8,128)(2,1)S(1)} %pad_maximum_fusion), channel_id=1, source_target_pairs={{0,2},{2,0},{4,6},{6,4},{1,3},{3,1},{5,7},{7,5},{8,10},{10,8},{12,... | collective-permute-start | bytes 4325384 | tf_op jit(solution)/shard_map/ppermute | solution.py:22
  59.4 43.9 %collective-permute-start.13 = (bf16[1024,512]{1,0:T(8,128)(2,1)S(1)}, bf16[1024,512]{1,0:T(8,128)(2,1)S(1)}, u32[]{:S(2)}, u32[]{:S(2)}) collective-permute-start(bf16[1024,512]{1,0:T(8,128)(2,1)S(1)} %send_part.16), channel_id=1, source_target_pairs={{0,8},{8,0},{16,24},{24,16},{1,9},{9,1},{17,25},{25,17},{2,10},{10... | collective-permute-start | bytes 3145736 | tf_op jit(solution)/shard_map/ppermute | solution.py:22
  60.7 25.8 %collective-permute-start.14 = (bf16[64,7680]{1,0:T(8,128)(2,1)S(1)}, bf16[64,7680]{1,0:T(8,128)(2,1)}, u32[]{:S(2)}, u32[]{:S(2)}) collective-permute-start(bf16[64,7680]{1,0:T(8,128)(2,1)S(1)} %copy-done.11), channel_id=1, source_target_pairs={{0,4},{2,6},{4,0},{6,2},{1,5},{3,7},{5,1},{7,3},{8,12},{10,14},{12... | collective-permute-start | bytes 2949128 | tf_op jit(solution)/shard_map/ppermute | solution.py:22
  65.7 62.9 %collective-permute-start.12 = (bf16[1024,512]{1,0:T(8,128)(2,1)S(1)}, bf16[1024,512]{1,0:T(8,128)(2,1)S(1)}, u32[]{:S(2)}, u32[]{:S(2)}) collective-permute-start(bf16[1024,512]{1,0:T(8,128)(2,1)S(1)} %send_part.17), channel_id=1, source_target_pairs={{0,8},{8,0},{16,24},{24,16},{1,9},{9,1},{17,25},{25,17},{2,10},{10... | collective-permute-start | bytes 3145736 | tf_op jit(solution)/shard_map/ppermute | solution.py:22
  81.3 47.3 %collective-permute-start.15 = (bf16[64,1024]{1,0:T(8,128)(2,1)S(1)}, bf16[64,1024]{1,0:T(8,128)(2,1)S(1)}, u32[]{:S(2)}, u32[]{:S(2)}) collective-permute-start(bf16[64,1024]{1,0:T(8,128)(2,1)S(1)} %fusion.5), channel_id=1, source_target_pairs={{0,8},{8,0},{16,24},{24,16},{1,9},{9,1},{17,25},{25,17},{2,10},{10... | collective-permute-start | bytes 393224 | tf_op jit(solution)/shard_map/ppermute | solution.py:22
  86.0 64.5 %collective-permute-start.11 = (bf16[1024,512]{1,0:T(8,128)(2,1)S(1)}, bf16[1024,512]{1,0:T(8,128)(2,1)S(1)}, u32[]{:S(2)}, u32[]{:S(2)}) collective-permute-start(bf16[1024,512]{1,0:T(8,128)(2,1)S(1)} %send_part.18), channel_id=1, source_target_pairs={{0,8},{8,0},{16,24},{24,16},{1,9},{9,1},{17,25},{25,17},{2,10},{10... | collective-permute-start | bytes 3145736 | tf_op jit(solution)/shard_map/ppermute | solution.py:22
  103.3 58.3 %collective-permute-start.16 = (bf16[128,7680]{1,0:T(8,128)(2,1)S(1)}, bf16[128,7680]{1,0:T(8,128)(2,1)}, u32[]{:S(2)}, u32[]{:S(2)}) collective-permute-start(bf16[128,7680]{1,0:T(8,128)(2,1)S(1)} %constant_dynamic-update-slice_fusion.2), channel_id=1, source_target_pairs={{0,2},{2,0},{4,6},{6,4},{1,3},{3,1},{5,7},{7,5},{8,10},{10,8},{12,... | collective-permute-start | bytes 5898248 | tf_op jit(solution)/shard_map/ppermute | solution.py:22
  151.4 5.0 %collective-permute-start.21 = (bf16[64,1024]{1,0:T(8,128)(2,1)S(1)}, bf16[64,1024]{1,0:T(8,128)(2,1)S(1)}, u32[]{:S(2)}, u32[]{:S(2)}) collective-permute-start(bf16[64,1024]{1,0:T(8,128)(2,1)S(1)} %collective-permute-done.15), channel_id=1, source_target_pairs={{0,4},{2,6},{4,0},{6,2},{1,5},{3,7},{5,1},{7,3},{8,12},{10,14},{12... | collective-permute-start | bytes 393224 | tf_op jit(solution)/shard_map/ppermute | solution.py:22
  153.2 26.5 %collective-permute-start.19 = (bf16[1024,512]{1,0:T(8,128)(2,1)}, bf16[1024,512]{1,0:T(8,128)(2,1)}, u32[]{:S(2)}, u32[]{:S(2)}) collective-permute-start(bf16[1024,512]{1,0:T(8,128)(2,1)} %send_part.19), channel_id=1, source_target_pairs={{0,8},{8,0},{16,24},{24,16},{1,9},{9,1},{17,25},{25,17},{2,10},{10... | collective-permute-start | bytes 3145736 | tf_op jit(solution)/shard_map/ppermute | solution.py:22
  154.9 6.6 %collective-permute-start.20 = (bf16[1024,128]{1,0:T(8,128)(2,1)S(1)}, bf16[1024,128]{1,0:T(8,128)(2,1)S(1)}, u32[]{:S(2)}, u32[]{:S(2)}) collective-permute-start(bf16[1024,128]{1,0:T(8,128)(2,1)S(1)} %copy-done.14), channel_id=1, source_target_pairs={{0,1},{1,0},{2,3},{3,2},{4,5},{5,4},{6,7},{7,6},{8,9},{9,8},{10,11... | collective-permute-start | bytes 786440 | tf_op jit(solution)/shard_map/ppermute | solution.py:22
  156.5 5.1 %collective-permute-start.22 = (bf16[128,1024]{1,0:T(8,128)(2,1)S(1)}, bf16[128,1024]{1,0:T(8,128)(2,1)S(1)}, u32[]{:S(2)}, u32[]{:S(2)}) collective-permute-start(bf16[128,1024]{1,0:T(8,128)(2,1)S(1)} %pad_maximum_fusion.5), channel_id=1, source_target_pairs={{0,2},{2,0},{4,6},{6,4},{1,3},{3,1},{5,7},{7,5},{8,10},{10,8},{12,... | collective-permute-start | bytes 786440 | tf_op jit(solution)/shard_map/ppermute | solution.py:22
  156.6 45.6 %collective-permute-start.18 = (bf16[1024,512]{1,0:T(8,128)(2,1)}, bf16[1024,512]{1,0:T(8,128)(2,1)}, u32[]{:S(2)}, u32[]{:S(2)}) collective-permute-start(bf16[1024,512]{1,0:T(8,128)(2,1)} %copy-done.10), channel_id=1, source_target_pairs={{0,8},{8,0},{16,24},{24,16},{1,9},{9,1},{17,25},{25,17},{2,10},{10... | collective-permute-start | bytes 3145736 | tf_op jit(solution)/shard_map/ppermute | solution.py:22
  173.0 74.5 %collective-permute-start.17 = (bf16[1024,512]{1,0:T(8,128)(2,1)S(1)}, bf16[1024,512]{1,0:T(8,128)(2,1)S(1)}, u32[]{:S(2)}, u32[]{:S(2)}) collective-permute-start(bf16[1024,512]{1,0:T(8,128)(2,1)S(1)} %send_part.21), channel_id=1, source_target_pairs={{0,8},{8,0},{16,24},{24,16},{1,9},{9,1},{17,25},{25,17},{2,10},{10... | collective-permute-start | bytes 3145736 | tf_op jit(solution)/shard_map/ppermute | solution.py:22
  182.7 75.6 %collective-permute-start.25 = (bf16[1024,512]{1,0:T(8,128)(2,1)S(1)}, bf16[1024,512]{1,0:T(8,128)(2,1)S(1)}, u32[]{:S(2)}, u32[]{:S(2)}) collective-permute-start(bf16[1024,512]{1,0:T(8,128)(2,1)S(1)} %send_part.22), channel_id=1, source_target_pairs={{0,8},{8,0},{16,24},{24,16},{1,9},{9,1},{17,25},{25,17},{2,10},{10... | collective-permute-start | bytes 3145736 | tf_op jit(solution)/shard_map/ppermute | solution.py:22
  202.2 44.9 %collective-permute-start.26 = (f32[8,2]{0,1:T(2,128)S(1)}, f32[8,2]{0,1:T(2,128)S(1)}, u32[]{:S(2)}, u32[]{:S(2)}) collective-permute-start(f32[8,2]{0,1:T(2,128)S(1)} %copy-done.18), channel_id=1, source_target_pairs={{0,8},{8,0},{16,24},{24,16},{1,9},{9,1},{17,25},{25,17},{2,10},{10... | collective-permute-start | bytes 200 | tf_op jit(solution)/shard_map/ppermute | solution.py:22
  207.8 61.7 %collective-permute-start.24 = (bf16[1024,512]{1,0:T(8,128)(2,1)}, bf16[1024,512]{1,0:T(8,128)(2,1)S(1)}, u32[]{:S(2)}, u32[]{:S(2)}) collective-permute-start(bf16[1024,512]{1,0:T(8,128)(2,1)} %send_part.23), channel_id=1, source_target_pairs={{0,8},{8,0},{16,24},{24,16},{1,9},{9,1},{17,25},{25,17},{2,10},{10... | collective-permute-start | bytes 3145736 | tf_op jit(solution)/shard_map/ppermute | solution.py:22
  251.7 40.3 %collective-permute-start.23 = (bf16[1024,512]{1,0:T(8,128)(2,1)}, bf16[1024,512]{1,0:T(8,128)(2,1)S(1)}, u32[]{:S(2)}, u32[]{:S(2)}) collective-permute-start(bf16[1024,512]{1,0:T(8,128)(2,1)} %send_part.24), channel_id=1, source_target_pairs={{0,8},{8,0},{16,24},{24,16},{1,9},{9,1},{17,25},{25,17},{2,10},{10... | collective-permute-start | bytes 3145736 | tf_op jit(solution)/shard_map/ppermute | solution.py:22
  262.4 52.0 %collective-permute-start.29 = (bf16[1024,512]{1,0:T(8,128)(2,1)}, bf16[1024,512]{1,0:T(8,128)(2,1)S(1)}, u32[]{:S(2)}, u32[]{:S(2)}) collective-permute-start(bf16[1024,512]{1,0:T(8,128)(2,1)} %send_part.25), channel_id=1, source_target_pairs={{0,8},{8,0},{16,24},{24,16},{1,9},{9,1},{17,25},{25,17},{2,10},{10... | collective-permute-start | bytes 3145736 | tf_op jit(solution)/shard_map/ppermute | solution.py:22
  262.9 54.3 %collective-permute-start.30 = (s32[1024]{0:T(1024)S(1)}, s32[1024]{0:T(1024)S(1)}, u32[]{:S(2)}, u32[]{:S(2)}) collective-permute-start(s32[1024]{0:T(1024)S(1)} %bitcast.64), channel_id=1, source_target_pairs={{0,8},{8,0},{16,24},{24,16},{1,9},{9,1},{17,25},{25,17},{2,10},{10... | collective-permute-start | bytes 12296 | tf_op jit(solution)/shard_map/ppermute | solution.py:22
  273.6 70.9 %collective-permute-start.28 = (bf16[1024,512]{1,0:T(8,128)(2,1)}, bf16[1024,512]{1,0:T(8,128)(2,1)}, u32[]{:S(2)}, u32[]{:S(2)}) collective-permute-start(bf16[1024,512]{1,0:T(8,128)(2,1)} %send_part.26), channel_id=1, source_target_pairs={{0,8},{8,0},{16,24},{24,16},{1,9},{9,1},{17,25},{25,17},{2,10},{10... | collective-permute-start | bytes 3145736 | tf_op jit(solution)/shard_map/ppermute | solution.py:22
  295.7 53.8 %collective-permute-start.27 = (bf16[1024,256]{1,0:T(8,128)(2,1)}, bf16[1024,256]{1,0:T(8,128)(2,1)}, u32[]{:S(2)}, u32[]{:S(2)}) collective-permute-start(bf16[1024,256]{1,0:T(8,128)(2,1)} %send_part.27), channel_id=1, source_target_pairs={{0,8},{8,0},{16,24},{24,16},{1,9},{9,1},{17,25},{25,17},{2,10},{10... | collective-permute-start | bytes 1572872 | tf_op jit(solution)/shard_map/ppermute | solution.py:22
  318.0 39.1 %collective-permute-start.31 = (bf16[1024,256]{1,0:T(8,128)(2,1)S(1)}, bf16[1024,256]{1,0:T(8,128)(2,1)S(1)}, u32[]{:S(2)}, u32[]{:S(2)}) collective-permute-start(bf16[1024,256]{1,0:T(8,128)(2,1)S(1)} %fusion.4), channel_id=1, source_target_pairs={{0,8},{8,0},{16,24},{24,16},{1,9},{9,1},{17,25},{25,17},{2,10},{10... | collective-permute-start | bytes 1572872 | tf_op jit(solution)/shard_map/ppermute | solution.py:22
  (23 other events, 301.7 us)

commit v4 on v3

--- a/solution.py
+++ b/solution.py
@@ -9,9 +9,11 @@
 
 CHUNKS = 15
 RAW = 2
-EARLY = 2
+EARLY = 3
+PARTS = (2, 3, 5, 7, 9, 11, 13, 14, 15)
+EVEN_PARTS = (2, 3, 5, 7, 9, 11, 12, 13, 14, 15)
 AHEAD = 3
-BEHIND = 6
+MERGES = {6: (0,), 7: (1, 2), 8: (3, 4)}
 ROW_STEPS = 4
 HIGH = lax.Precision.HIGHEST
 VMEM_LIMIT = 48 * 1024 * 1024
@@ -138,7 +140,7 @@
 def send_kernel(place, hi, lo, left, trailing, *rest):
     *pieces, out, right = rest
 
-    @pl.when(pl.program_id(0) == 0)
+    @pl.when(pl.program_id(1) == 0)
     def _():
         right[...] = panel_tile(hi, lo, pieces)
 
@@ -148,7 +150,7 @@
 def merge_kernel(place, hi, lo, left, trailing, chosen, received, *rest):
     *pieces, out, right = rest
 
-    @pl.when(pl.program_id(0) == 0)
+    @pl.when(pl.program_id(1) == 0)
     def _():
         right[...] = panel_tile(hi, lo, pieces)
 
@@ -164,7 +166,7 @@
 def merge_raw_kernel(place, hi, lo, left, trailing, chosen, received, other_left, other_right, *rest):
     *pieces, out, right, updated = rest
 
-    @pl.when(pl.program_id(0) == 0)
+    @pl.when(pl.program_id(1) == 0)
     def _():
         size = out.shape[0]
         for first in range(0, received.shape[0], size):
@@ -183,58 +185,59 @@
     size = hi.shape[0]
     rows = left.shape[0] // ROW_STEPS
     half_blocks, chunk = columns // 2 // width, start // width
-    whole = pl.BlockSpec((size, size), lambda i, place: (0, 0))
+    whole = pl.BlockSpec((size, size), lambda j, i, place: (0, 0))
     specs = [
         whole,
         whole,
-        pl.BlockSpec((rows, size), lambda i, place: (i, 0)),
-        pl.BlockSpec((rows, width), lambda i, place: (i, place[0] * half_blocks + chunk)),
+        pl.BlockSpec((rows, size), lambda j, i, place: (i, 0)),
+        pl.BlockSpec((rows, width), lambda j, i, place: (i, place[0] * half_blocks + chunk + j)),
     ]
-    piece_specs = []
-    for piece, first in zip(pieces, starts):
-        block = (piece.shape[0], width)
-        if first is None:
-            piece_specs.append(pl.BlockSpec(block, lambda i, place: (0, place[0] * half_blocks + chunk)))
-        else:
-            piece_specs.append(pl.BlockSpec(block, lambda i, place, at=(start - first) // width: (0, at)))
+    piece_specs = [
+        pl.BlockSpec((piece.shape[0], width), lambda j, i, place, at=(start - first) // width: (0, at + j))
+        for piece, first in zip(pieces, starts)
+    ]
     return specs, piece_specs
 
 
-def send_chunk(place, hi, lo, left, trailing, pieces, starts, start, width):
+def cost(rows, width, flops, passes):
+    return pl.CostEstimate(flops=flops * rows * width, bytes_accessed=passes * rows * width, transcendentals=0)
+
+
+def send_chunk(place, hi, lo, left, trailing, pieces, starts, start, end, width):
     rows, columns = trailing.shape
     specs, piece_specs = specs_for(hi, left, columns, width, start, pieces, starts)
     return pl.pallas_call(
         send_kernel,
         grid_spec=pltpu.PrefetchScalarGridSpec(
             num_scalar_prefetch=1,
-            grid=(ROW_STEPS,),
+            grid=((end - start) // width, ROW_STEPS),
             in_specs=specs + piece_specs,
-            out_specs=pl.BlockSpec((rows // ROW_STEPS, width), lambda i, place: (i, 0)),
+            out_specs=pl.BlockSpec((rows // ROW_STEPS, width), lambda j, i, place: (i, j)),
             scratch_shapes=[pltpu.VMEM((hi.shape[0], width), jnp.bfloat16)],
         ),
-        out_shape=jax.ShapeDtypeStruct((rows, width), jnp.bfloat16),
+        out_shape=jax.ShapeDtypeStruct((rows, end - start), jnp.bfloat16),
         compiler_params=pltpu.CompilerParams(vmem_limit_bytes=VMEM_LIMIT),
-        cost_estimate=pl.CostEstimate(flops=2 * rows * 256 * width, bytes_accessed=5 * rows * width, transcendentals=0),
+        cost_estimate=cost(rows, end - start, 512, 5),
         name="send_part",
     )(place, hi, lo, left, trailing, *pieces)
 
 
-def merge_chunk(place, hi, lo, left, trailing, chosen, received, pieces, starts, start, width, merged, raw=None):
+def merge_chunk(
+    place, hi, lo, left, trailing, chosen, received, pieces, starts, start, end, width, merged, raw=None
+):
     rows, columns = trailing.shape
     step_rows = rows // ROW_STEPS
     specs, piece_specs = specs_for(hi, left, columns, width, start, pieces, starts)
-    specs.append(pl.BlockSpec((step_rows, rows), lambda i, place: (i, 0)))
+    specs.append(pl.BlockSpec((step_rows, rows), lambda j, i, place: (i, 0)))
+    specs.append(pl.BlockSpec((rows, width), lambda j, i, place: (0, j)))
     operands = [place, hi, lo, left, trailing, chosen, received]
     scratch = [pltpu.VMEM((hi.shape[0], width), jnp.bfloat16)]
     body, body_into = merge_kernel, merge_kernel_into
-    if raw is None:
-        specs.append(pl.BlockSpec((rows, width), lambda i, place: (0, 0)))
-    else:
-        first, other_left, other_right = raw
-        at = (start - first) // width
-        specs.append(pl.BlockSpec((rows, width), lambda i, place: (0, at)))
-        specs.append(pl.BlockSpec(other_left.shape, lambda i, place: (0, 0)))
-        specs.append(pl.BlockSpec((other_right.shape[0], width), lambda i, place: (0, at)))
+    chunk = start // width
+    if raw is not None:
+        other_left, other_right = raw
+        specs.append(pl.BlockSpec(other_left.shape, lambda j, i, place: (0, 0)))
+        specs.append(pl.BlockSpec((other_right.shape[0], width), lambda j, i, place: (0, chunk + j)))
         operands += [other_left, other_right]
         scratch.append(pltpu.VMEM((rows, width), jnp.bfloat16))
         body, body_into = merge_raw_kernel, merge_raw_kernel_into
@@ -246,20 +249,19 @@
         operands.append(merged)
         specs.append(pl.BlockSpec(memory_space=pl.ANY))
         body = body_into
-    chunk = start // width
     return pl.pallas_call(
         body,
         grid_spec=pltpu.PrefetchScalarGridSpec(
             num_scalar_prefetch=1,
-            grid=(ROW_STEPS,),
+            grid=((end - start) // width, ROW_STEPS),
             in_specs=specs,
-            out_specs=pl.BlockSpec((step_rows, width), lambda i, place: (i, chunk)),
+            out_specs=pl.BlockSpec((step_rows, width), lambda j, i, place: (i, chunk + j)),
             scratch_shapes=scratch,
         ),
         out_shape=jax.ShapeDtypeStruct((rows, columns // 2), jnp.bfloat16),
         input_output_aliases=aliases,
         compiler_params=pltpu.CompilerParams(vmem_limit_bytes=VMEM_LIMIT),
-        cost_estimate=pl.CostEstimate(flops=2 * rows * (rows + 256) * width, bytes_accessed=8 * rows * width, transcendentals=0),
+        cost_estimate=cost(rows, end - start, 2560, 8),
         name="merge_part",
     )(*operands)
 
@@ -280,7 +282,7 @@
         out_shape=jax.ShapeDtypeStruct(merged.shape, merged.dtype),
         input_output_aliases={2: 0},
         compiler_params=pltpu.CompilerParams(vmem_limit_bytes=VMEM_LIMIT),
-        cost_estimate=pl.CostEstimate(flops=rows * width, bytes_accessed=6 * rows * width, transcendentals=0),
+        cost_estimate=cost(rows, width, 1, 6),
         name="join_part",
     )(own, received, merged)
 
@@ -331,11 +333,20 @@
     kept_place = parity.astype(jnp.int32).reshape(1)
     raw_end = RAW * width
 
-    raw = lax.dynamic_slice_in_dim(trailing, (1 - parity) * half, raw_end, 1)
-    raw_received = partner(raw, "cube", 1)
-
-    whole_block = doubled(after(diag_block, raw), ("row", "col"), 0)
-    panel = doubled(lower_in, "col", 1)
+    raw_width = width // 2 if width % 256 == 0 else width
+    raw_bounds = (0, raw_width, raw_end)
+    small = jnp.concatenate([row_map[0], block_mask[0].reshape(-1)])
+    other_small = partner(small, "cube", 1)
+    raw = [
+        lax.dynamic_slice_in_dim(
+            trailing if first == 0 else after(trailing, other_small), (1 - parity) * half + first, last - first, 1
+        )
+        for first, last in zip(raw_bounds, raw_bounds[1:])
+    ]
+    raw_received = [partner(piece, "cube", 1) for piece in raw]
+
+    whole_block = doubled(after(diag_block, raw[0]), ("row", "col"), 0)
+    panel = after(doubled(lower_in, "col", 1), raw_received[0])
     order = pivot_order[0][:, None]
     every = jnp.arange(size, dtype=jnp.int32)
     in_col_order = place_of(every, lower_in.shape[1], "col")
@@ -346,7 +357,6 @@
     )
     block_rows = rows // block_mask.shape[1]
     flags = block_mask[0].astype(jnp.float32)
-    own_flags = flags
     flags = jnp.repeat(flags, block_rows, axis=0)
     flags = jnp.where(parity == 0, flags[:, ::-1], flags)
     def columns_of(place, first, last):
@@ -354,7 +364,7 @@
 
     cut = raw_end + EARLY * width
     early = doubled(columns_of(1 - parity, 0, cut), "row", 0)
-    late = columns_of(1 - parity, cut, half)
+    late = after(columns_of(1 - parity, cut, half), panel)
     late = next_doubled(late, "row", 0, 0)
 
     hi, lo, plain_left, sent_left, kept_left = factor(whole_block, orders, panel, flags)
@@ -373,76 +383,78 @@
 
     chosen = choice(after(row_map[0], hi))
 
-    bounds = [width * chunk for chunk in range(RAW, CHUNKS + 1)]
-    if width % 256 == 0:
-        bounds.insert(-1, half - width // 2)
+    bounds = [width * unit for unit in PARTS]
+    bounds.insert(-1, half - raw_width)
+    if raw_width == width:
+        bounds = [width * unit for unit in EVEN_PARTS]
     spans = list(zip(bounds, bounds[1:]))
-    sent, received, merged_after = [], [], []
+    sent, received = [], []
     merged = None
 
     def merge(number):
         start, end = spans[number]
         return merge_chunk(
-            kept_place, hi, lo, kept_left, trailing, chosen, received[number], [kept_upper], [0], start, end - start,
-            merged,
+            kept_place, hi, lo, kept_left, trailing, chosen, received[number], [kept_upper], [0], start, end,
+            min(width, end - start), merged,
         )
 
     for number, (start, end) in enumerate(spans):
         before = []
         if number >= AHEAD - 1:
-            before += [([raw_received] + received)[number - AHEAD + 1], sent[-1]]
+            before += [(raw_received[1:] + received)[number - AHEAD + 1], sent[-1]]
         if number == 1:
             for step in range(1, len(bits_of("row"))):
                 late = next_doubled(after(late, sent[0]), "row", 0, step)
-        if number == 2:
-            kept_upper = next_doubled(after(columns_of(parity, 0, half), raw_received, sent[1]), "row", 0, 0)
         if number == 3:
             before += [left_received]
-            raw_upper = after(early[:, :raw_end], received[0], sent[2])
+        if number == 4:
+            kept_upper = next_doubled(after(columns_of(parity, 0, half), received[0], sent[3]), "row", 0, 0)
+            before += [kept_upper]
+        if number == 5:
+            for step in range(1, len(bits_of("row"))):
+                kept_upper = next_doubled(after(kept_upper, received[1], sent[4]), "row", 0, step)
+            raw_upper = after(early[:, :raw_end], received[1], sent[4])
             right_share = (fast(share_hi, raw_upper) + fast(share_lo, raw_upper)).astype(jnp.bfloat16)
             right_received = partner(right_share, "cube", 1)
-        if number == 4:
             before += [kept_upper]
-            for step in range(1, len(bits_of("row"))):
-                kept_upper = next_doubled(after(kept_upper, received[1], sent[3]), "row", 0, step)
-        if number == 5:
+        if number == 6:
+            other_left = doubled(after(left_received, received[2], sent[5]), "col", 1)
+            before += [other_left]
+        if number == 7:
             before += [right_received]
-            other_left = doubled(after(left_received, received[2], sent[4]), "col", 1)
-        if number == 6:
-            before += [kept_upper]
-            other_right = doubled(after(right_received, received[3], sent[5]), "row", 0)
-        if number == 7:
-            before += [other_left, other_right]
-        if number == 9:
+        if number == 8:
+            other_right = doubled(after(right_received, received[4], sent[7]), "row", 0)
+            other_flags = after(other_small[rows:], received[4]).reshape(block_mask.shape[1:]).astype(jnp.float32)
             other_flags = jnp.where(parity == 0, other_flags[:, :1], other_flags[:, 1:])
             other_left = fast(other_left, same) * jnp.repeat(other_flags, block_rows, axis=0)
             other_left = other_left.astype(jnp.bfloat16)
-        if number == 10:
-            before += [other_chosen, other_left]
-        if number == 8:
-            other_flags = partner(after(own_flags, received[5], sent[7]), "cube", 1)
-            other_chosen = choice(partner(after(row_map[0], received[5], sent[7]), "cube", 1))
-        if number >= BEHIND:
-            merged = merge(number - BEHIND)
+            other_chosen = choice(after(other_small[:rows], received[4]))
+            before += [other_left, other_right, other_chosen]
+        for ready in MERGES.get(number, ()):
+            merged = merge(ready)
             before += [merged]
         place = after(sent_place, *before) if before else sent_place
         piece, first = (early, 0) if end <= cut else (late, cut)
-        sent.append(send_chunk(place, hi, lo, sent_left, trailing, [piece], [first], start, end - start))
+        sent.append(
+            send_chunk(
+                place, hi, lo, sent_left, trailing, [piece], [first], start, end, min(width, end - start)
+            )
+        )
         outgoing = sent[-1]
         if number == len(spans) - 1:
             outgoing = fast(other_chosen, outgoing).astype(jnp.bfloat16)
         received.append(partner(outgoing, "cube", 1))
 
-    for start in range(0, raw_end, width):
+    for (first, last), arrived in zip(zip(raw_bounds, raw_bounds[1:]), raw_received):
         merged = merge_chunk(
-            kept_place, hi, lo, kept_left, trailing, chosen, raw_received, [kept_upper], [0], start, width, merged,
-            (0, other_left, other_right),
+            kept_place, hi, lo, kept_left, trailing, chosen, arrived, [kept_upper], [0], first, last, raw_width,
+            merged, (other_left, other_right),
         )
-    for number in range(len(spans) - BEHIND, len(spans) - 1):
+    for number in range(1 + max(map(max, MERGES.values())), len(spans) - 1):
         merged = merge(number)
     start, end = spans[-1]
     own = send_chunk(
-        after(kept_place, merged), hi, lo, kept_left, trailing, [kept_upper], [0], start, end - start
+        after(kept_place, merged), hi, lo, kept_left, trailing, [kept_upper], [0], start, end, end - start
     )
     merged = join_chunk(own, received[-1], start, merged)
     return merged[None]

time: 361 us -> 413 us (1.14)
  local copies, waits for them, and re-layouts: 14.8 us -> 61.3 us
  waiting for transfers between devices: 150 us -> 164 us
  starting transfers between devices: 34.7 us -> 25.9 us
    unnamed x52 -> x77, local copies, waits for them, and re-layouts: 4.74 us -> 39.3 us
    ppermute x32 -> x27, waiting for transfers between devices: 150 us -> 164 us  [partner(): return lax.ppermute(block, axis, [(i, i ^ bits) for i in range(count)])]
    ppermute x32 -> x27, starting transfers between devices: 34.7 us -> 25.9 us  [partner(): return lax.ppermute(block, axis, [(i, i ^ bits) for i in range(count)])]
    pallas_call x15 -> x10, Pallas kernels: 50.4 us -> 48.6 us  [send_chunk(): pl.pallas_call(send_kernel, grid_spec=pltpu.PrefetchScalarGridSpec(num_sc...]
    pallas_call x15 -> x10, Pallas kernels: 72.7 us -> 71.8 us  [merge_chunk(): pl.pallas_call(body, grid_spec=pltpu.PrefetchScalarGridSpec(num_scalar_pr...]
  transfers between devices with their start and end apart: 32 -> 27, of which waited for: 13 -> 7; matrix products, arithmetic and copies ran while one was open for 4% -> 15% of each run, Pallas kernels for 42% -> 34%
where the time goes in v4:
time: 413 us; the launch traced here: 410 us
  waiting for transfers between devices  164 us (40%)
  Pallas kernels  148 us (36%)
  local copies, waits for them, and re-layouts  61.3 us (15%)
  starting transfers between devices  25.9 us (6%)
  other arithmetic  8.66 us (2%)
    ppermute x27, waiting for transfers between devices, partner(): return lax.ppermute(block, axis, [(i, i ^ bits) for i in range(count)])  164 us
    pallas_call x10, Pallas kernels, merge_chunk(): pl.pallas_call(body, grid_spec=pltpu.PrefetchScalarGridSpec(num_scalar_pr...  71.8 us
    pallas_call x10, Pallas kernels, send_chunk(): pl.pallas_call(send_kernel, grid_spec=pltpu.PrefetchScalarGridSpec(num_sc...  48.6 us
    unnamed x77, local copies, waits for them, and re-layouts  39.3 us
    pallas_call x1, Pallas kernels, factor(): pl.pallas_call(factor_kernel, out_shape=(jax.ShapeDtypeStruct((size, size...  26.7 us
    ppermute x27, starting transfers between devices, partner(): return lax.ppermute(block, axis, [(i, i ^ bits) for i in range(count)])  25.9 us
  transfers between devices with their start and end apart: 27, of which 7 were waited for; matrix products, arithmetic and copies ran while one was open for 15% of the time, Pallas kernels for 34%

profile of v4, /device:TPU:0, one launch (start us, length us, event | category | flops | bytes accessed | tf_op | source)
XLA Modules:
  0.0 410.3 jit_solution(453102926448182358)
XLA Ops:
  2.0 3.0 collective-permute-start.4
  14.9 3.8 rev.3
  20.6 2.7 constant_dynamic-slice_fusion.1
  23.3 2.0 collective-permute-start.10
  31.7 26.7 %factor.1 = (bf16[256,256]{1,0:T(8,128)(2,1)S(1)}, bf16[256,256]{1,0:T(8,128)(2,1)S(1)}, bf16[1024,256]{1,0:T(8,128)(2,1)S(1)}, bf16[1024,256]{1,0:T(8,128)(2,1)S(1)}, bf16[1024,256]{1,0:T(8,128)(2,1)S(1)}) custom-call(f32[256,256]{1,0:T(8,128)S(1)} %pad_maximum_fusion.4.block, s32[256,1]{1,0:T(8,128)S(1)} %copy-done.23, ...), custom_call_target="tpu_custom_call" | custom-call | flops 30000001024 | bytes 3000000 | tf_op jit(solution)/shard_map/factor/pallas_call | solution.py:120
  59.6 4.3 %send_part.11 = bf16[1024,512]{1,0:T(8,128)(2,1)} custom-call(s32[1]{0:T(128)} %bitcast.9.place, bf16[256,256]{1,0:T(8,128)(2,1)S(1)} %get-tuple-element.34.hi.refs_1_, bf16[256,256]{1,0:T(8,128)(2,1)S(1)} %get-tuple-element.35.lo.refs_2_, bf16[1024,256]{1,0:T(8,128)(2,1)S(1)} %get-tuple-element.38.left, bf16[1024,15360]{1,0:T(8,128)(2,1)} %bitcast.27, ...), custom_call_target="tpu_custom_call" | custom-call | flops 268435456 | bytes 2621440 | tf_op jit(solution)/shard_map/send_part/pallas_call | solution.py:209
  67.4 5.8 %send_part.10 = bf16[1024,1024]{1,0:T(8,128)(2,1)S(1)} custom-call(s32[1]{0:T(128)} %bitcast.9.place, bf16[256,256]{1,0:T(8,128)(2,1)S(1)} %get-tuple-element.34.hi.refs_1_, bf16[256,256]{1,0:T(8,128)(2,1)S(1)} %get-tuple-element.35.lo.refs_2_, bf16[1024,256]{1,0:T(8,128)(2,1)S(1)} %get-tuple-element.38.left, bf16[1024,15360]{1,0:T(8,128)(2,1)} %bitcast.28, ...), custom_call_target="tpu_custom_call" | custom-call | flops 536870912 | bytes 5242880 | tf_op jit(solution)/shard_map/send_part/pallas_call | solution.py:209
  76.9 6.0 %send_part.12 = bf16[1024,1024]{1,0:T(8,128)(2,1)S(1)} custom-call(s32[1]{0:T(128)} %bitcast.9.place, bf16[256,256]{1,0:T(8,128)(2,1)S(1)} %get-tuple-element.34.hi.refs_1_, bf16[256,256]{1,0:T(8,128)(2,1)S(1)} %get-tuple-element.35.lo.refs_2_, bf16[1024,256]{1,0:T(8,128)(2,1)S(1)} %get-tuple-element.38.left, bf16[1024,15360]{1,0:T(8,128)(2,1)} %bitcast.29, ...), custom_call_target="tpu_custom_call" | custom-call | flops 536870912 | bytes 5242880 | tf_op jit(solution)/shard_map/send_part/pallas_call | solution.py:209
  84.2 12.7 %collective-permute-done.8.received = bf16[1024,512]{1,0:T(8,128)(2,1)S(1)} collective-permute-done((bf16[1024,512]{1,0:T(8,128)(2,1)}, bf16[1024,512]{1,0:T(8,128)(2,1)S(1)}, u32[]{:S(2)}, u32[]{:S(2)}) %collective-permute-start.8) | collective-permute-done | bytes 1048608 | tf_op jit(solution)/shard_map/ppermute | solution.py:24
  97.0 5.9 %send_part.13 = bf16[1024,1024]{1,0:T(8,128)(2,1)S(1)} custom-call(s32[1]{0:T(128)} %bitcast.9.place, bf16[256,256]{1,0:T(8,128)(2,1)S(1)} %get-tuple-element.34.hi.refs_1_, bf16[256,256]{1,0:T(8,128)(2,1)S(1)} %get-tuple-element.35.lo.refs_2_, bf16[1024,256]{1,0:T(8,128)(2,1)S(1)} %get-tuple-element.38.left, bf16[1024,15360]{1,0:T(8,128)(2,1)} %bitcast.30, ...), custom_call_target="tpu_custom_call" | custom-call | flops 536870912 | bytes 5242880 | tf_op jit(solution)/shard_map/send_part/pallas_call | solution.py:209
  104.6 21.0 %collective-permute-done.14 = bf16[64,7680]{1,0:T(8,128)(2,1)S(1)} collective-permute-done((bf16[64,7680]{1,0:T(8,128)(2,1)S(1)}, bf16[64,7680]{1,0:T(8,128)(2,1)S(1)}, u32[]{:S(2)}, u32[]{:S(2)}) %collective-permute-start.14) | collective-permute-done | bytes 983072 | tf_op jit(solution)/shard_map/ppermute | solution.py:24
  126.6 14.7 %collective-permute-done.7.received = bf16[1024,1024]{1,0:T(8,128)(2,1)S(1)} collective-permute-done((bf16[1024,1024]{1,0:T(8,128)(2,1)S(1)}, bf16[1024,1024]{1,0:T(8,128)(2,1)S(1)}, u32[]{:S(2)}, u32[]{:S(2)}) %collective-permute-start.7) | collective-permute-done | bytes 2097184 | tf_op jit(solution)/shard_map/ppermute | solution.py:24
  141.3 7.2 %send_part.14 = bf16[1024,1024]{1,0:T(8,128)(2,1)} custom-call(s32[1]{0:T(128)} %bitcast.9.place, bf16[256,256]{1,0:T(8,128)(2,1)S(1)} %get-tuple-element.34.hi.refs_1_, bf16[256,256]{1,0:T(8,128)(2,1)S(1)} %get-tuple-element.35.lo.refs_2_, bf16[1024,256]{1,0:T(8,128)(2,1)S(1)} %get-tuple-element.38.left, bf16[1024,15360]{1,0:T(8,128)(2,1)} %bitcast.31, ...), custom_call_target="tpu_custom_call" | custom-call | flops 536870912 | bytes 5242880 | tf_op jit(solution)/shard_map/send_part/pallas_call | solution.py:209
  160.8 84.8 %collective-permute-done.17.received = bf16[1024,1024]{1,0:T(8,128)(2,1)S(1)} collective-permute-done((bf16[1024,1024]{1,0:T(8,128)(2,1)}, bf16[1024,1024]{1,0:T(8,128)(2,1)S(1)}, u32[]{:S(2)}, u32[]{:S(2)}) %collective-permute-start.17) | collective-permute-done | bytes 2097184 | tf_op jit(solution)/shard_map/ppermute | solution.py:24
  246.9 7.0 %send_part.15 = bf16[1024,1024]{1,0:T(8,128)(2,1)} custom-call(s32[1]{0:T(128)} %bitcast.9.place, bf16[256,256]{1,0:T(8,128)(2,1)S(1)} %get-tuple-element.34.hi.refs_1_, bf16[256,256]{1,0:T(8,128)(2,1)S(1)} %get-tuple-element.35.lo.refs_2_, bf16[1024,256]{1,0:T(8,128)(2,1)S(1)} %get-tuple-element.38.left, bf16[1024,15360]{1,0:T(8,128)(2,1)} %bitcast.32, ...), custom_call_target="tpu_custom_call" | custom-call | flops 536870912 | bytes 5242880 | tf_op jit(solution)/shard_map/send_part/pallas_call | solution.py:209
  257.8 4.7 %merge_part.10.rest_1_ = bf16[1024,7680]{1,0:T(8,128)(2,1)} custom-call(s32[1]{0:T(128)} %bitcast.place.refs_0_, bf16[256,256]{1,0:T(8,128)(2,1)S(1)} %get-tuple-element.34.hi.refs_1_, bf16[256,256]{1,0:T(8,128)(2,1)S(1)} %get-tuple-element.35.lo.refs_2_, bf16[1024,256]{1,0:T(8,128)(2,1)S(1)} %get-tuple-element.36.left.refs_3_, ...), custom_call_target="tpu_custom_call" | custom-call | flops 1342177280 | bytes 4194304 | tf_op jit(solution)/shard_map/merge_part/pallas_call | solution.py:252
  262.5 28.0 %collective-permute-done.15.received = bf16[1024,1024]{1,0:T(8,128)(2,1)S(1)} collective-permute-done((bf16[1024,1024]{1,0:T(8,128)(2,1)}, bf16[1024,1024]{1,0:T(8,128)(2,1)S(1)}, u32[]{:S(2)}, u32[]{:S(2)}) %collective-permute-start.15) | collective-permute-done | bytes 2097184 | tf_op jit(solution)/shard_map/ppermute | solution.py:24
  295.5 8.3 %merge_part.11 = bf16[1024,7680]{1,0:T(8,128)(2,1)} custom-call(s32[1]{0:T(128)} %bitcast.place.refs_0_, bf16[256,256]{1,0:T(8,128)(2,1)S(1)} %get-tuple-element.34.hi.refs_1_, bf16[256,256]{1,0:T(8,128)(2,1)S(1)} %get-tuple-element.35.lo.refs_2_, bf16[1024,256]{1,0:T(8,128)(2,1)S(1)} %get-tuple-element.36.left.refs_3_, ...), custom_call_target="tpu_custom_call", output_to_operand_aliasing={{}: (8, {})} | custom-call | flops 2684354560 | bytes 8388608 | tf_op jit(solution)/shard_map/merge_part/pallas_call | solution.py:252
  303.8 13.4 %copy.31.rest_1_ = bf16[1024,7680]{1,0:T(8,128)(2,1)} copy(bf16[1024,7680]{1,0:T(8,128)(2,1)} %merge_part.11) | data formatting | bytes 31457280
  317.2 4.3 %send_part.16 = bf16[1024,512]{1,0:T(8,128)(2,1)} custom-call(s32[1]{0:T(128)} %bitcast.9.place, bf16[256,256]{1,0:T(8,128)(2,1)S(1)} %get-tuple-element.34.hi.refs_1_, bf16[256,256]{1,0:T(8,128)(2,1)S(1)} %get-tuple-element.35.lo.refs_2_, bf16[1024,256]{1,0:T(8,128)(2,1)S(1)} %get-tuple-element.38.left, bf16[1024,15360]{1,0:T(8,128)(2,1)} %bitcast.35, ...), custom_call_target="tpu_custom_call" | custom-call | flops 268435456 | bytes 2621440 | tf_op jit(solution)/shard_map/send_part/pallas_call | solution.py:209
  323.0 8.3 %merge_part.12.rest_1_ = bf16[1024,7680]{1,0:T(8,128)(2,1)} custom-call(s32[1]{0:T(128)} %bitcast.place.refs_0_, bf16[256,256]{1,0:T(8,128)(2,1)S(1)} %get-tuple-element.34.hi.refs_1_, bf16[256,256]{1,0:T(8,128)(2,1)S(1)} %get-tuple-element.35.lo.refs_2_, bf16[1024,256]{1,0:T(8,128)(2,1)S(1)} %get-tuple-element.36.left.refs_3_, ...), custom_call_target="tpu_custom_call", output_to_operand_aliasing={{}: (8, {})} | custom-call | flops 2684354560 | bytes 8388608 | tf_op jit(solution)/shard_map/merge_part/pallas_call | solution.py:252
  331.4 2.7 send_part.17
  335.1 8.9 %merge_part.13 = bf16[1024,7680]{1,0:T(8,128)(2,1)} custom-call(s32[1]{0:T(128)} %bitcast.place.refs_0_, bf16[256,256]{1,0:T(8,128)(2,1)S(1)} %get-tuple-element.34.hi.refs_1_, bf16[256,256]{1,0:T(8,128)(2,1)S(1)} %get-tuple-element.35.lo.refs_2_, bf16[1024,256]{1,0:T(8,128)(2,1)S(1)} %get-tuple-element.36.left.refs_3_, ...), custom_call_target="tpu_custom_call", output_to_operand_aliasing={{}: (8, {})} | custom-call | flops 2684354560 | bytes 8388608 | tf_op jit(solution)/shard_map/merge_part/pallas_call | solution.py:252
  344.0 13.3 %copy.35.rest_1_ = bf16[1024,7680]{1,0:T(8,128)(2,1)} copy(bf16[1024,7680]{1,0:T(8,128)(2,1)} %merge_part.13) | data formatting | bytes 31457280
  357.4 8.5 %merge_part.14.refs_10_ = bf16[1024,7680]{1,0:T(8,128)(2,1)} custom-call(s32[1]{0:T(128)} %bitcast.place.refs_0_, bf16[256,256]{1,0:T(8,128)(2,1)S(1)} %get-tuple-element.34.hi.refs_1_, bf16[256,256]{1,0:T(8,128)(2,1)S(1)} %get-tuple-element.35.lo.refs_2_, bf16[1024,256]{1,0:T(8,128)(2,1)S(1)} %get-tuple-element.36.left.refs_3_, ...), custom_call_target="tpu_custom_call", output_to_operand_aliasing={{}: (8, {})} | custom-call | flops 2684354560 | bytes 8388608 | tf_op jit(solution)/shard_map/merge_part/pallas_call | solution.py:252
  367.5 2.7 send_part.19
  372.7 4.3 %merge_part.15.refs_10_ = bf16[1024,7680]{1,0:T(8,128)(2,1)} custom-call(s32[1]{0:T(128)} %bitcast.place.refs_0_, bf16[256,256]{1,0:T(8,128)(2,1)S(1)} %get-tuple-element.34.hi.refs_1_, bf16[256,256]{1,0:T(8,128)(2,1)S(1)} %get-tuple-element.35.lo.refs_2_, bf16[1024,256]{1,0:T(8,128)(2,1)S(1)} %get-tuple-element.36.left.refs_3_, ...), custom_call_target="tpu_custom_call", output_to_operand_aliasing={{}: (10, {})} | custom-call | flops 671088640 | bytes 2097152 | tf_op jit(solution)/shard_map/merge_part/pallas_call | solution.py:252
  377.0 10.5 %merge_part.16.rest_1_ = bf16[1024,7680]{1,0:T(8,128)(2,1)} custom-call(s32[1]{0:T(128)} %bitcast.place.refs_0_, bf16[256,256]{1,0:T(8,128)(2,1)S(1)} %get-tuple-element.34.hi.refs_1_, bf16[256,256]{1,0:T(8,128)(2,1)S(1)} %get-tuple-element.35.lo.refs_2_, bf16[1024,256]{1,0:T(8,128)(2,1)S(1)} %get-tuple-element.36.left.refs_3_, ...), custom_call_target="tpu_custom_call", output_to_operand_aliasing={{}: (10, {})} | custom-call | flops 2013265920 | bytes 6291456 | tf_op jit(solution)/shard_map/merge_part/pallas_call | solution.py:252
  387.5 8.9 %merge_part.17.rest_1_ = bf16[1024,7680]{1,0:T(8,128)(2,1)} custom-call(s32[1]{0:T(128)} %bitcast.place.refs_0_, bf16[256,256]{1,0:T(8,128)(2,1)S(1)} %get-tuple-element.34.hi.refs_1_, bf16[256,256]{1,0:T(8,128)(2,1)S(1)} %get-tuple-element.35.lo.refs_2_, bf16[1024,256]{1,0:T(8,128)(2,1)S(1)} %get-tuple-element.36.left.refs_3_, ...), custom_call_target="tpu_custom_call", output_to_operand_aliasing={{}: (8, {})} | custom-call | flops 2684354560 | bytes 8388608 | tf_op jit(solution)/shard_map/merge_part/pallas_call | solution.py:252
  396.4 5.1 %merge_part.18.rest_1_ = bf16[1024,7680]{1,0:T(8,128)(2,1)} custom-call(s32[1]{0:T(128)} %bitcast.place.refs_0_, bf16[256,256]{1,0:T(8,128)(2,1)S(1)} %get-tuple-element.34.hi.refs_1_, bf16[256,256]{1,0:T(8,128)(2,1)S(1)} %get-tuple-element.35.lo.refs_2_, bf16[1024,256]{1,0:T(8,128)(2,1)S(1)} %get-tuple-element.36.left.refs_3_, ...), custom_call_target="tpu_custom_call", output_to_operand_aliasing={{}: (8, {})} | custom-call | flops 1342177280 | bytes 4194304 | tf_op jit(solution)/shard_map/merge_part/pallas_call | solution.py:252
  401.5 4.3 %merge_part.19._ = bf16[1024,7680]{1,0:T(8,128)(2,1)} custom-call(s32[1]{0:T(128)} %bitcast.place.refs_0_, bf16[256,256]{1,0:T(8,128)(2,1)S(1)} %get-tuple-element.34.hi.refs_1_, bf16[256,256]{1,0:T(8,128)(2,1)S(1)} %get-tuple-element.35.lo.refs_2_, bf16[1024,256]{1,0:T(8,128)(2,1)S(1)} %get-tuple-element.36.left.refs_3_, ...), custom_call_target="tpu_custom_call", output_to_operand_aliasing={{}: (8, {})} | custom-call | flops 671088640 | bytes 2097152 | tf_op jit(solution)/shard_map/merge_part/pallas_call | solution.py:252
  405.8 2.7 send_part.18.own
  (164 shorter events, 63.1 us)
Async XLA Ops:
  2.0 27.4 %collective-permute-start.4 = (bf16[1024,256]{1,0:T(8,128)(2,1)}, bf16[1024,256]{1,0:T(8,128)(2,1)S(1)}, u32[]{:S(2)}, u32[]{:S(2)}) collective-permute-start(bf16[1024,256]{1,0:T(8,128)(2,1)} %dynamic-slice_bitcast_fusion.2), channel_id=1, source_target_pairs={{0,8},{8,0},{16,24},{24,16},{1,9},{9,1},{17,25},{25,17},{2,10},{10... | collective-permute-start | bytes 1572872 | tf_op jit(solution)/shard_map/ppermute | solution.py:24
  5.1 8.3 %collective-permute-start = (f32[32,256]{1,0:T(8,128)}, f32[32,256]{1,0:T(8,128)S(1)}, u32[]{:S(2)}, u32[]{:S(2)}) collective-permute-start(f32[32,256]{1,0:T(8,128)} %bitcast.48), channel_id=1, source_target_pairs={{0,4},{1,5},{2,6},{3,7},{4,0},{5,1},{6,2},{7,3},{8,12},{9,13},{10,... | collective-permute-start | bytes 98312 | tf_op jit(solution)/shard_map/ppermute | solution.py:24
  6.6 20.7 %collective-permute-start.3 = (bf16[1024,128]{1,0:T(8,128)(2,1)}, bf16[1024,128]{1,0:T(8,128)(2,1)}, u32[]{:S(2)}, u32[]{:S(2)}) collective-permute-start(bf16[1024,128]{1,0:T(8,128)(2,1)} %bitcast.52), channel_id=1, source_target_pairs={{0,1},{1,0},{2,3},{3,2},{4,5},{5,4},{6,7},{7,6},{8,9},{9,8},{10,11... | collective-permute-start | bytes 786440 | tf_op jit(solution)/shard_map/ppermute | solution.py:24
  8.1 20.2 %collective-permute-start.5 = (bf16[64,2560]{1,0:T(8,128)(2,1)S(1)}, bf16[64,2560]{1,0:T(8,128)(2,1)}, u32[]{:S(2)}, u32[]{:S(2)}) collective-permute-start(bf16[64,2560]{1,0:T(8,128)(2,1)S(1)} %dynamic-slice_bitcast_fusion.3), channel_id=1, source_target_pairs={{0,4},{2,6},{4,0},{6,2},{1,5},{3,7},{5,1},{7,3},{8,12},{10,14},{12... | collective-permute-start | bytes 983048 | tf_op jit(solution)/shard_map/ppermute | solution.py:24
  10.2 9.3 %collective-permute-start.9 = (s32[1040]{0:T(1024)S(1)}, s32[1040]{0:T(1024)}, u32[]{:S(2)}, u32[]{:S(2)}) collective-permute-start(s32[1040]{0:T(1024)S(1)} %pad_add_fusion), channel_id=1, source_target_pairs={{0,8},{8,0},{16,24},{24,16},{1,9},{9,1},{17,25},{25,17},{2,10},{10... | collective-permute-start | bytes 12488 | tf_op jit(solution)/shard_map/ppermute | solution.py:24
  14.0 5.6 %collective-permute-start.1 = (f32[64,256]{1,0:T(8,128)}, f32[64,256]{1,0:T(8,128)}, u32[]{:S(2)}, u32[]{:S(2)}) collective-permute-start(f32[64,256]{1,0:T(8,128)} %pad_maximum_fusion.7), channel_id=1, source_target_pairs={{0,2},{1,3},{2,0},{3,1},{4,6},{5,7},{6,4},{7,5},{8,10},{9,11},{10,... | collective-permute-start | bytes 196616 | tf_op jit(solution)/shard_map/ppermute | solution.py:24
  20.4 6.0 %collective-permute-start.2 = (f32[128,256]{1,0:T(8,128)S(1)}, f32[128,256]{1,0:T(8,128)S(1)}, u32[]{:S(2)}, u32[]{:S(2)}) collective-permute-start(f32[128,256]{1,0:T(8,128)S(1)} %pad_maximum_fusion.6), channel_id=1, source_target_pairs={{0,1},{1,0},{2,3},{3,2},{4,5},{5,4},{6,7},{7,6},{8,9},{9,8},{10,11... | collective-permute-start | bytes 393224 | tf_op jit(solution)/shard_map/ppermute | solution.py:24
  23.3 51.7 %collective-permute-start.10 = (bf16[1024,768]{1,0:T(8,128)(2,1)}, bf16[1024,768]{1,0:T(8,128)(2,1)S(1)}, u32[]{:S(2)}, u32[]{:S(2)}) collective-permute-start(bf16[1024,768]{1,0:T(8,128)(2,1)} %constant_dynamic-slice_fusion.1), channel_id=1, source_target_pairs={{0,8},{8,0},{16,24},{24,16},{1,9},{9,1},{17,25},{25,17},{2,10},{10... | collective-permute-start | bytes 4718600 | tf_op jit(solution)/shard_map/ppermute | solution.py:24
  29.3 29.1 %collective-permute-start.6 = (bf16[128,2560]{1,0:T(8,128)(2,1)S(1)}, bf16[128,2560]{1,0:T(8,128)(2,1)S(1)}, u32[]{:S(2)}, u32[]{:S(2)}) collective-permute-start(bf16[128,2560]{1,0:T(8,128)(2,1)S(1)} %pad_maximum_fusion.2), channel_id=1, source_target_pairs={{0,2},{2,0},{4,6},{6,4},{1,3},{3,1},{5,7},{7,5},{8,10},{10,8},{12,... | collective-permute-start | bytes 1966088 | tf_op jit(solution)/shard_map/ppermute | solution.py:24
  30.2 33.7 %collective-permute-start.11 = (bf16[64,5120]{1,0:T(8,128)(2,1)S(1)}, bf16[64,5120]{1,0:T(8,128)(2,1)S(1)}, u32[]{:S(2)}, u32[]{:S(2)}) collective-permute-start(bf16[64,5120]{1,0:T(8,128)(2,1)S(1)} %copy-done.27), channel_id=1, source_target_pairs={{0,4},{2,6},{4,0},{6,2},{1,5},{3,7},{5,1},{7,3},{8,12},{10,14},{12... | collective-permute-start | bytes 1966088 | tf_op jit(solution)/shard_map/ppermute | solution.py:24
  31.7 26.7 %copy-start.26 = (bf16[64,2560]{1,0:T(8,128)(2,1)S(1)}, bf16[64,2560]{1,0:T(8,128)(2,1)}, u32[]{:S(2)}) copy-start(bf16[64,2560]{1,0:T(8,128)(2,1)} %copy-done.25) | copy-start | bytes 983044
  64.0 10.9 %collective-permute-start.12 = (bf16[128,5120]{1,0:T(8,128)(2,1)S(1)}, bf16[128,5120]{1,0:T(8,128)(2,1)}, u32[]{:S(2)}, u32[]{:S(2)}) collective-permute-start(bf16[128,5120]{1,0:T(8,128)(2,1)S(1)} %pad_maximum_fusion.1), channel_id=1, source_target_pairs={{0,2},{2,0},{4,6},{6,4},{1,3},{3,1},{5,7},{7,5},{8,10},{10,8},{12,... | collective-permute-start | bytes 3932168 | tf_op jit(solution)/shard_map/ppermute | solution.py:24
  65.3 17.7 %collective-permute-start.13 = (bf16[1024,128]{1,0:T(8,128)(2,1)S(1)}, bf16[1024,128]{1,0:T(8,128)(2,1)}, u32[]{:S(2)}, u32[]{:S(2)}) collective-permute-start(bf16[1024,128]{1,0:T(8,128)(2,1)S(1)} %constant_dynamic-slice_fusion), channel_id=1, source_target_pairs={{0,8},{8,0},{16,24},{24,16},{1,9},{9,1},{17,25},{25,17},{2,10},{10... | collective-permute-start | bytes 786440 | tf_op jit(solution)/shard_map/ppermute | solution.py:24
  66.9 30.0 %collective-permute-start.8 = (bf16[1024,512]{1,0:T(8,128)(2,1)}, bf16[1024,512]{1,0:T(8,128)(2,1)S(1)}, u32[]{:S(2)}, u32[]{:S(2)}) collective-permute-start(bf16[1024,512]{1,0:T(8,128)(2,1)} %send_part.11), channel_id=1, source_target_pairs={{0,8},{8,0},{16,24},{24,16},{1,9},{9,1},{17,25},{25,17},{2,10},{10... | collective-permute-start | bytes 3145736 | tf_op jit(solution)/shard_map/ppermute | solution.py:24
  73.2 68.1 %collective-permute-start.7 = (bf16[1024,1024]{1,0:T(8,128)(2,1)S(1)}, bf16[1024,1024]{1,0:T(8,128)(2,1)S(1)}, u32[]{:S(2)}, u32[]{:S(2)}) collective-permute-start(bf16[1024,1024]{1,0:T(8,128)(2,1)S(1)} %send_part.10), channel_id=1, source_target_pairs={{0,8},{8,0},{16,24},{24,16},{1,9},{9,1},{17,25},{25,17},{2,10},{10... | collective-permute-start | bytes 6291464 | tf_op jit(solution)/shard_map/ppermute | solution.py:24
  76.9 64.4 %copy-start.4 = (bf16[256,5120]{1,0:T(8,128)(2,1)}, bf16[256,5120]{1,0:T(8,128)(2,1)S(1)}, u32[]{:S(2)}) copy-start(bf16[256,5120]{1,0:T(8,128)(2,1)S(1)} %constant_dynamic-update-slice_fusion.rest_0_) | copy-start | bytes 7864324
  102.9 22.6 %collective-permute-start.14 = (bf16[64,7680]{1,0:T(8,128)(2,1)S(1)}, bf16[64,7680]{1,0:T(8,128)(2,1)S(1)}, u32[]{:S(2)}, u32[]{:S(2)}) collective-permute-start(bf16[64,7680]{1,0:T(8,128)(2,1)S(1)} %copy-done.24), channel_id=1, source_target_pairs={{0,4},{2,6},{4,0},{6,2},{1,5},{3,7},{5,1},{7,3},{8,12},{10,14},{12... | collective-permute-start | bytes 2949128 | tf_op jit(solution)/shard_map/ppermute | solution.py:24
  148.5 10.3 %collective-permute-start.18 = (bf16[128,7680]{1,0:T(8,128)(2,1)}, bf16[128,7680]{1,0:T(8,128)(2,1)}, u32[]{:S(2)}, u32[]{:S(2)}) collective-permute-start(bf16[128,7680]{1,0:T(8,128)(2,1)} %constant_dynamic-update-slice_fusion.2), channel_id=1, source_target_pairs={{0,2},{2,0},{4,6},{6,4},{1,3},{3,1},{5,7},{7,5},{8,10},{10,8},{12,... | collective-permute-start | bytes 5898248 | tf_op jit(solution)/shard_map/ppermute | solution.py:24
  152.0 142.0 %collective-permute-start.16 = (bf16[1024,1024]{1,0:T(8,128)(2,1)}, bf16[1024,1024]{1,0:T(8,128)(2,1)}, u32[]{:S(2)}, u32[]{:S(2)}) collective-permute-start(bf16[1024,1024]{1,0:T(8,128)(2,1)} %copy-done.10), channel_id=1, source_target_pairs={{0,8},{8,0},{16,24},{24,16},{1,9},{9,1},{17,25},{25,17},{2,10},{10... | collective-permute-start | bytes 6291464 | tf_op jit(solution)/shard_map/ppermute | solution.py:24
  153.6 92.0 %collective-permute-start.17 = (bf16[1024,1024]{1,0:T(8,128)(2,1)}, bf16[1024,1024]{1,0:T(8,128)(2,1)S(1)}, u32[]{:S(2)}, u32[]{:S(2)}) collective-permute-start(bf16[1024,1024]{1,0:T(8,128)(2,1)} %copy-done.13), channel_id=1, source_target_pairs={{0,8},{8,0},{16,24},{24,16},{1,9},{9,1},{17,25},{25,17},{2,10},{10... | collective-permute-start | bytes 6291464 | tf_op jit(solution)/shard_map/ppermute | solution.py:24
  154.1 136.5 %collective-permute-start.15 = (bf16[1024,1024]{1,0:T(8,128)(2,1)}, bf16[1024,1024]{1,0:T(8,128)(2,1)S(1)}, u32[]{:S(2)}, u32[]{:S(2)}) collective-permute-start(bf16[1024,1024]{1,0:T(8,128)(2,1)} %send_part.14), channel_id=1, source_target_pairs={{0,8},{8,0},{16,24},{24,16},{1,9},{9,1},{17,25},{25,17},{2,10},{10... | collective-permute-start | bytes 6291464 | tf_op jit(solution)/shard_map/ppermute | solution.py:24
  158.4 88.5 %copy-start.5 = (bf16[256,5120]{1,0:T(8,128)(2,1)S(1)}, bf16[256,5120]{1,0:T(8,128)(2,1)}, u32[]{:S(2)}) copy-start(bf16[256,5120]{1,0:T(8,128)(2,1)} %copy-done.4) | copy-start | bytes 7864324
  158.4 173.0 %collective-permute-start.20 = (bf16[64,1024]{1,0:T(8,128)(2,1)}, bf16[64,1024]{1,0:T(8,128)(2,1)S(1)}, u32[]{:S(2)}, u32[]{:S(2)}) collective-permute-start(bf16[64,1024]{1,0:T(8,128)(2,1)} %fusion.5), channel_id=1, source_target_pairs={{0,8},{8,0},{16,24},{24,16},{1,9},{9,1},{17,25},{25,17},{2,10},{10... | collective-permute-start | bytes 393224 | tf_op jit(solution)/shard_map/ppermute | solution.py:24
  160.8 93.2 %copy-start.2 = (bf16[256,7680]{1,0:T(8,128)(2,1)}, bf16[256,7680]{1,0:T(8,128)(2,1)S(1)}, u32[]{:S(2)}) copy-start(bf16[256,7680]{1,0:T(8,128)(2,1)S(1)} %constant_dynamic-update-slice_fusion.4.rest_0_.refs_9_) | copy-start | bytes 11796484
  160.8 97.0 %copy-start.19 = (bf16[1024,512]{1,0:T(8,128)(2,1)S(1)}, bf16[1024,512]{1,0:T(8,128)(2,1)}, u32[]{:S(2)}) copy-start(bf16[1024,512]{1,0:T(8,128)(2,1)} %copy-done.18) | copy-start | bytes 3145732
  253.9 113.6 %collective-permute-start.23 = (bf16[1024,1024]{1,0:T(8,128)(2,1)}, bf16[1024,1024]{1,0:T(8,128)(2,1)}, u32[]{:S(2)}, u32[]{:S(2)}) collective-permute-start(bf16[1024,1024]{1,0:T(8,128)(2,1)} %send_part.15), channel_id=1, source_target_pairs={{0,8},{8,0},{16,24},{24,16},{1,9},{9,1},{17,25},{25,17},{2,10},{10... | collective-permute-start | bytes 6291464 | tf_op jit(solution)/shard_map/ppermute | solution.py:24
  255.5 36.7 %collective-permute-start.19 = (bf16[1024,128]{1,0:T(8,128)(2,1)}, bf16[1024,128]{1,0:T(8,128)(2,1)}, u32[]{:S(2)}, u32[]{:S(2)}) collective-permute-start(bf16[1024,128]{1,0:T(8,128)(2,1)} %collective-permute-done.13), channel_id=1, source_target_pairs={{0,1},{1,0},{2,3},{3,2},{4,5},{5,4},{6,7},{7,6},{8,9},{9,8},{10,11... | collective-permute-start | bytes 786440 | tf_op jit(solution)/shard_map/ppermute | solution.py:24
  321.5 74.9 %collective-permute-start.22 = (bf16[1024,512]{1,0:T(8,128)(2,1)}, bf16[1024,512]{1,0:T(8,128)(2,1)}, u32[]{:S(2)}, u32[]{:S(2)}) collective-permute-start(bf16[1024,512]{1,0:T(8,128)(2,1)} %send_part.16), channel_id=1, source_target_pairs={{0,8},{8,0},{16,24},{24,16},{1,9},{9,1},{17,25},{25,17},{2,10},{10... | collective-permute-start | bytes 3145736 | tf_op jit(solution)/shard_map/ppermute | solution.py:24
  334.1 67.5 %collective-permute-start.21 = (bf16[1024,256]{1,0:T(8,128)(2,1)S(1)}, bf16[1024,256]{1,0:T(8,128)(2,1)S(1)}, u32[]{:S(2)}, u32[]{:S(2)}) collective-permute-start(bf16[1024,256]{1,0:T(8,128)(2,1)S(1)} %send_part.17), channel_id=1, source_target_pairs={{0,8},{8,0},{16,24},{24,16},{1,9},{9,1},{17,25},{25,17},{2,10},{10... | collective-permute-start | bytes 1572872 | tf_op jit(solution)/shard_map/ppermute | solution.py:24
  334.6 31.2 %collective-permute-start.24 = (bf16[64,1024]{1,0:T(8,128)(2,1)S(1)}, bf16[64,1024]{1,0:T(8,128)(2,1)S(1)}, u32[]{:S(2)}, u32[]{:S(2)}) collective-permute-start(bf16[64,1024]{1,0:T(8,128)(2,1)S(1)} %collective-permute-done.20), channel_id=1, source_target_pairs={{0,4},{2,6},{4,0},{6,2},{1,5},{3,7},{5,1},{7,3},{8,12},{10,14},{12... | collective-permute-start | bytes 393224 | tf_op jit(solution)/shard_map/ppermute | solution.py:24
  365.8 1.6 collective-permute-start.25
  371.1 37.4 %collective-permute-start.26 = (bf16[1024,256]{1,0:T(8,128)(2,1)S(1)}, bf16[1024,256]{1,0:T(8,128)(2,1)S(1)}, u32[]{:S(2)}, u32[]{:S(2)}) collective-permute-start(bf16[1024,256]{1,0:T(8,128)(2,1)S(1)} %fusion.4), channel_id=1, source_target_pairs={{0,8},{8,0},{16,24},{24,16},{1,9},{9,1},{17,25},{25,17},{2,10},{10... | collective-permute-start | bytes 1572872 | tf_op jit(solution)/shard_map/ppermute | solution.py:24
  (29 other events, 246.8 us)

commit v5 on v3

--- a/solution.py
+++ b/solution.py
@@ -11,7 +11,7 @@
 RAW = 2
 EARLY = 2
 AHEAD = 3
-BEHIND = 6
+MERGES = {6: (0,), 7: (1,), 8: (2, 3), 9: (4,), 10: ("raw",), 11: (5, 6), 12: (7, 8)}
 ROW_STEPS = 4
 HIGH = lax.Precision.HIGHEST
 VMEM_LIMIT = 48 * 1024 * 1024
@@ -74,7 +74,9 @@
     return lower, upper
 
 
-def factor_kernel(block, order_of_diag, order_of_upper, order_of_lower, panel, mask, hi, lo, plain, sent, kept):
+def factor_kernel(
+    block, order_of_diag, order_of_upper, order, order_of_lower, panel, mask, hi, lo, kept_hi, kept_lo, plain, sent, kept
+):
     size = block.shape[0]
     half = size // 2
     lane = lax.broadcasted_iota(jnp.int32, (size, size), 1)
@@ -98,6 +100,7 @@
         [jnp.concatenate([upper_one, corner_upper], 1), jnp.concatenate([zero, upper_two], 1)], 0
     )
     hi[...], lo[...] = split(exact(lower_inv, chosen(order_of_upper)))
+    kept_hi[...], kept_lo[...] = split(exact(lower_inv, chosen(order)))
     row = lax.broadcasted_iota(jnp.int32, (size, size), 0)
     in_order = jnp.where(order_of_lower[...] == row, 1.0, 0.0)
     upper_hi, upper_lo = split(exact(in_order, upper_inv))
@@ -120,6 +123,8 @@
         out_shape=(
             jax.ShapeDtypeStruct((size, size), half_type),
             jax.ShapeDtypeStruct((size, size), half_type),
+            jax.ShapeDtypeStruct((size, size), half_type),
+            jax.ShapeDtypeStruct((size, size), half_type),
             jax.ShapeDtypeStruct((rows, size), half_type),
             jax.ShapeDtypeStruct((rows, size), half_type),
             jax.ShapeDtypeStruct((rows, size), half_type),
@@ -133,6 +138,31 @@
 def panel_tile(hi, lo, pieces):
     columns = jnp.concatenate([piece[...] for piece in pieces], axis=0)
     return (fast(hi[...], columns) + fast(lo[...], columns)).astype(jnp.bfloat16)
+
+
+def copy_kernel(place, source, out):
+    out[...] = source[...]
+
+
+def take_raw(place, trailing, end):
+    rows, columns = trailing.shape
+    step_rows = rows // 8
+    half_blocks = columns // 2 // end
+    if columns // 2 % end:
+        return lax.dynamic_slice_in_dim(trailing, place[0] * (columns // 2), end, 1)
+    return pl.pallas_call(
+        copy_kernel,
+        grid_spec=pltpu.PrefetchScalarGridSpec(
+            num_scalar_prefetch=1,
+            grid=(8,),
+            in_specs=[pl.BlockSpec((step_rows, end), lambda i, place: (i, place[0] * half_blocks))],
+            out_specs=pl.BlockSpec((step_rows, end), lambda i, place: (i, 0)),
+        ),
+        out_shape=jax.ShapeDtypeStruct((rows, end), trailing.dtype),
+        compiler_params=pltpu.CompilerParams(vmem_limit_bytes=VMEM_LIMIT),
+        cost_estimate=pl.CostEstimate(flops=0, bytes_accessed=4 * rows * end, transcendentals=0),
+        name="raw_part",
+    )(place, trailing)
 
 
 def send_kernel(place, hi, lo, left, trailing, *rest):
@@ -286,7 +316,11 @@
 
 
 def bits_of(axis):
-    return [1 << bit for bit in reversed(range((lax.axis_size(axis) - 1).bit_length()))]
+    bits = [1 << bit for bit in reversed(range((lax.axis_size(axis) - 1).bit_length()))]
+    if not isinstance(axis, str):
+        last = lax.axis_size(axis[1:])
+        bits = [bit for bit in bits if bit != last] + [last]
+    return bits
 
 
 def doubled(block, axis, dimension):
@@ -305,14 +339,6 @@
     for number, bits in enumerate(bits_of(axis)):
         place = place + jnp.where(apart & bits != 0, 1 << number, 0)
     return place * part + index % part
-
-
-def index_at(place, part, axis):
-    number = place // part
-    apart = jnp.zeros_like(place)
-    for bit, bits in enumerate(bits_of(axis)):
-        apart = apart + jnp.where(number & (1 << bit) != 0, bits, 0)
-    return (apart ^ lax.axis_index(axis)) * part + place % part
 
 
 def after(value, *others):
@@ -331,7 +357,7 @@
     kept_place = parity.astype(jnp.int32).reshape(1)
     raw_end = RAW * width
 
-    raw = lax.dynamic_slice_in_dim(trailing, (1 - parity) * half, raw_end, 1)
+    raw = take_raw(sent_place, trailing, raw_end)
     raw_received = partner(raw, "cube", 1)
 
     whole_block = doubled(after(diag_block, raw), ("row", "col"), 0)
@@ -342,13 +368,12 @@
     orders = (
         place_of(order, diag_block.shape[0], ("row", "col")),
         place_of(order, upper_in.shape[0], "row"),
+        order,
         in_col_order[None, :],
     )
     block_rows = rows // block_mask.shape[1]
     flags = block_mask[0].astype(jnp.float32)
-    own_flags = flags
-    flags = jnp.repeat(flags, block_rows, axis=0)
-    flags = jnp.where(parity == 0, flags[:, ::-1], flags)
+    flags = jnp.repeat(jnp.where(parity == 0, flags[:, ::-1], flags), block_rows, axis=0)
     def columns_of(place, first, last):
         return lax.dynamic_slice_in_dim(upper_in, place * half + first, last - first, 1)
 
@@ -357,17 +382,20 @@
     late = columns_of(1 - parity, cut, half)
     late = next_doubled(late, "row", 0, 0)
 
-    hi, lo, plain_left, sent_left, kept_left = factor(whole_block, orders, panel, flags)
+    hi, lo, kept_hi, kept_lo, plain_left, sent_left, kept_left = factor(whole_block, orders, panel, flags)
 
     left_share = lax.dynamic_slice_in_dim(plain_left, col * lower_in.shape[1], lower_in.shape[1], 1)
-    left_received = partner(left_share, "cube", 1)
     share = upper_in.shape[0]
     share_hi = lax.dynamic_slice_in_dim(hi, row * share, share, 0)
     share_lo = lax.dynamic_slice_in_dim(lo, row * share, share, 0)
-    col_order = index_at(every, lower_in.shape[1], "col")
-    row_order = index_at(every, upper_in.shape[0], "row")
-    same = (after(col_order, hi)[:, None] == row_order[None, :]).astype(jnp.bfloat16)
-
+    raw_upper = early[:, :raw_end]
+    right_share = (fast(share_hi, raw_upper) + fast(share_lo, raw_upper)).astype(jnp.bfloat16)
+    wide = left_share.shape[1]
+    stacked = [right_share[:, at : at + wide] for at in range(0, raw_end, wide)]
+    mask = block_mask[0].reshape(-1)
+    digits = jnp.concatenate([row_map[0] // 32, row_map[0] % 32, mask, jnp.zeros(16 * wide - mask.shape[0], mask.dtype)])
+    bundle = jnp.concatenate([left_share, *stacked, digits.astype(jnp.bfloat16).reshape(-1, wide)], axis=0)
+    bundle = partner(bundle, "cube", 1)
     def choice(order):
         return (order[:, None] == jnp.arange(rows, dtype=jnp.int32)[None, :]).astype(jnp.bfloat16)
 
@@ -383,9 +411,18 @@
     def merge(number):
         start, end = spans[number]
         return merge_chunk(
-            kept_place, hi, lo, kept_left, trailing, chosen, received[number], [kept_upper], [0], start, end - start,
+            kept_place, kept_hi, kept_lo, kept_left, trailing, chosen, received[number], [kept_upper], [0], start, end - start,
             merged,
         )
+
+    def merge_raw():
+        result = merged
+        for start in range(0, raw_end, width):
+            result = merge_chunk(
+                kept_place, kept_hi, kept_lo, kept_left, trailing, chosen, raw_received, [kept_upper], [0], start,
+                width, result, (0, other_left, other_right),
+            )
+        return result
 
     for number, (start, end) in enumerate(spans):
         before = []
@@ -395,35 +432,33 @@
             for step in range(1, len(bits_of("row"))):
                 late = next_doubled(after(late, sent[0]), "row", 0, step)
         if number == 2:
-            kept_upper = next_doubled(after(columns_of(parity, 0, half), raw_received, sent[1]), "row", 0, 0)
+            before += [bundle]
         if number == 3:
-            before += [left_received]
-            raw_upper = after(early[:, :raw_end], received[0], sent[2])
-            right_share = (fast(share_hi, raw_upper) + fast(share_lo, raw_upper)).astype(jnp.bfloat16)
-            right_received = partner(right_share, "cube", 1)
-        if number == 4:
-            before += [kept_upper]
-            for step in range(1, len(bits_of("row"))):
-                kept_upper = next_doubled(after(kept_upper, received[1], sent[3]), "row", 0, step)
+            kept_upper = after(columns_of(parity, 0, half), received[0], sent[2])
+            kept_upper = lax.all_gather(kept_upper, "row", axis=0, tiled=True)
         if number == 5:
-            before += [right_received]
-            other_left = doubled(after(left_received, received[2], sent[4]), "col", 1)
+            arrived = after(bundle, received[2], sent[4])
+            left_received = arrived[:rows]
+            stacked = arrived[rows : rows + share * (raw_end // wide)].reshape(raw_end // wide, share, wide)
+            right_received = jnp.concatenate(list(stacked), axis=1)
+            digits = arrived[rows + share * (raw_end // wide) :].reshape(-1).astype(jnp.float32)
+            other_order = (32 * digits[:rows] + digits[rows : 2 * rows]).astype(jnp.int32)
+            other_flags = digits[2 * rows : 2 * rows + mask.shape[0]].reshape(block_mask.shape[1:])
+            other_flags = jnp.where(parity == 0, other_flags[:, :1], other_flags[:, 1:])
+            other_chosen = choice(other_order)
+            other_left = lax.all_gather(left_received, "col", axis=1, tiled=True)
+            other_left = other_left.astype(jnp.float32) * jnp.repeat(other_flags, block_rows, axis=0)
+            other_left = other_left.astype(jnp.bfloat16)
         if number == 6:
             before += [kept_upper]
-            other_right = doubled(after(right_received, received[3], sent[5]), "row", 0)
         if number == 7:
-            before += [other_left, other_right]
+            other_right = lax.all_gather(after(right_received, received[4], sent[6]), "row", axis=0, tiled=True)
         if number == 9:
-            other_flags = jnp.where(parity == 0, other_flags[:, :1], other_flags[:, 1:])
-            other_left = fast(other_left, same) * jnp.repeat(other_flags, block_rows, axis=0)
-            other_left = other_left.astype(jnp.bfloat16)
-        if number == 10:
-            before += [other_chosen, other_left]
-        if number == 8:
-            other_flags = partner(after(own_flags, received[5], sent[7]), "cube", 1)
-            other_chosen = choice(partner(after(row_map[0], received[5], sent[7]), "cube", 1))
-        if number >= BEHIND:
-            merged = merge(number - BEHIND)
+            before += [other_left, other_right, other_chosen]
+        ready = MERGES.get(number, ())
+        for item in ready:
+            merged = merge_raw() if item == "raw" else merge(item)
+        if ready:
             before += [merged]
         place = after(sent_place, *before) if before else sent_place
         piece, first = (early, 0) if end <= cut else (late, cut)
@@ -433,16 +468,11 @@
             outgoing = fast(other_chosen, outgoing).astype(jnp.bfloat16)
         received.append(partner(outgoing, "cube", 1))
 
-    for start in range(0, raw_end, width):
-        merged = merge_chunk(
-            kept_place, hi, lo, kept_left, trailing, chosen, raw_received, [kept_upper], [0], start, width, merged,
-            (0, other_left, other_right),
-        )
-    for number in range(len(spans) - BEHIND, len(spans) - 1):
+    for number in range(1 + MERGES[max(MERGES)][-1], len(spans) - 1):
         merged = merge(number)
     start, end = spans[-1]
     own = send_chunk(
-        after(kept_place, merged), hi, lo, kept_left, trailing, [kept_upper], [0], start, end - start
+        after(kept_place, merged), kept_hi, kept_lo, kept_left, trailing, [kept_upper], [0], start, end - start
     )
     merged = join_chunk(own, received[-1], start, merged)
     return merged[None]

time: 361 us -> 381 us (1.055)
  starting transfers between devices: 34.7 us -> 19.8 us
  blocking collectives: 0 us -> 14.2 us
  between operations: 0.55 us -> 13.9 us
  local copies, waits for them, and re-layouts: 14.8 us -> 26.5 us
  waiting for transfers between devices: 150 us -> 145 us
    ppermute x32 -> x24, starting transfers between devices: 34.7 us -> 19.8 us  [partner(): return lax.ppermute(block, axis, [(i, i ^ bits) for i in range(count)])]
    all_gather x0 -> x2, blocking collectives: none -> 14.2 us  [the longest x1 7.45 us: local(): other_left = lax.all_gather(left_received, 'col', axis=1, tiled=True)]
    unnamed x52 -> x71, local copies, waits for them, and re-layouts: 4.74 us -> 15.7 us
    ppermute x32 -> x24, waiting for transfers between devices: 150 us -> 145 us  [partner(): return lax.ppermute(block, axis, [(i, i ^ bits) for i in range(count)])]
    concatenate x5 -> x1, local copies, waits for them, and re-layouts: 4.67 us -> 0.09 us  [next_doubled(): jnp.concatenate([block, partner(block, axis, bits_of(axis)[step])], axis=...]
  transfers between devices with their start and end apart: 32 -> 25, of which waited for: 13 -> 15; matrix products, arithmetic and copies ran while one was open for 4% -> 6% of each run, Pallas kernels for 42% -> 40%
where the time goes in v5:
time: 381 us; the launch traced here: 379 us
  Pallas kernels  153 us (40%)
  waiting for transfers between devices  145 us (38%)
  local copies, waits for them, and re-layouts  26.5 us (7%)
  starting transfers between devices  19.8 us (5%)
  blocking collectives  14.2 us (4%)
  between operations  13.9 us (4%)
  other arithmetic  5.09 us (1%)
    ppermute x24, waiting for transfers between devices, partner(): return lax.ppermute(block, axis, [(i, i ^ bits) for i in range(count)])  145 us
    pallas_call x15, Pallas kernels, merge_chunk(): pl.pallas_call(body, grid_spec=pltpu.PrefetchScalarGridSpec(num_scalar_pr...  72.6 us
    pallas_call x15, Pallas kernels, send_chunk(): pl.pallas_call(send_kernel, grid_spec=pltpu.PrefetchScalarGridSpec(num_sc...  52.2 us
    pallas_call x1, Pallas kernels, factor(): pl.pallas_call(factor_kernel, out_shape=(jax.ShapeDtypeStruct((size, size...  27.1 us
    ppermute x24, starting transfers between devices, partner(): return lax.ppermute(block, axis, [(i, i ^ bits) for i in range(count)])  19.8 us
    unnamed x71, local copies, waits for them, and re-layouts  15.7 us
  transfers between devices with their start and end apart: 25, of which 15 were waited for; matrix products, arithmetic and copies ran while one was open for 6% of the time, Pallas kernels for 40%

profile of v5, /device:TPU:0, one launch (start us, length us, event | category | flops | bytes accessed | tf_op | source)
XLA Modules:
  0.0 378.6 jit_solution(3926466467059385761)
XLA Ops:
  26.9 27.1 %factor.1 = (bf16[256,256]{1,0:T(8,128)(2,1)S(1)}, bf16[256,256]{1,0:T(8,128)(2,1)S(1)}, bf16[256,256]{1,0:T(8,128)(2,1)S(1)}, bf16[256,256]{1,0:T(8,128)(2,1)S(...) custom-call(f32[256,256]{1,0:T(8,128)S(1)} %pad_maximum_fusion.4.block, ...), custom_call_target="tpu_custom_call" | custom-call | flops 30000001024 | bytes 3000000 | tf_op jit(solution)/shard_map/factor/pallas_call | solution.py:121
  65.7 27.0 %collective-permute-done.8 = bf16[1568,128]{1,0:T(8,128)(2,1)} collective-permute-done((bf16[1568,128]{1,0:T(8,128)(2,1)S(1)}, bf16[1568,128]{1,0:T(8,128)(2,1)}, u32[]{:S(2)}, u32[]{:S(2)}) %collective-permute-start.8) | collective-permute-done | bytes 401440 | tf_op jit(solution)/shard_map/ppermute | solution.py:22
  92.8 4.3 %send_part.17 = bf16[1024,512]{1,0:T(8,128)(2,1)} custom-call(s32[1]{0:T(128)} %bitcast.9.place, bf16[256,256]{1,0:T(8,128)(2,1)S(1)} %get-tuple-element.35.hi, bf16[256,256]{1,0:T(8,128)(2,1)S(1)} %get-tuple-element.37.lo, bf16[1024,256]{1,0:T(8,128)(2,1)S(1)} %get-tuple-element.38.left, bf16[1024,15360]{1,0:T(8,128)(2,1)} %bitcast.31, ...), custom_call_target="tpu_custom_call" | custom-call | flops 268435456 | bytes 2621440 | tf_op jit(solution)/shard_map/send_part/pallas_call | solution.py:236
  107.9 16.6 %collective-permute-done.13.received = bf16[1024,512]{1,0:T(8,128)(2,1)S(1)} collective-permute-done((bf16[1024,512]{1,0:T(8,128)(2,1)}, bf16[1024,512]{1,0:T(8,128)(2,1)S(1)}, u32[]{:S(2)}, u32[]{:S(2)}) %collective-permute-start.13) | collective-permute-done | bytes 1048608 | tf_op jit(solution)/shard_map/ppermute | solution.py:22
  124.5 4.2 %send_part.19 = bf16[1024,512]{1,0:T(8,128)(2,1)} custom-call(s32[1]{0:T(128)} %bitcast.9.place, bf16[256,256]{1,0:T(8,128)(2,1)S(1)} %get-tuple-element.35.hi, bf16[256,256]{1,0:T(8,128)(2,1)S(1)} %copy-done.7, bf16[1024,256]{1,0:T(8,128)(2,1)S(1)} %get-tuple-element.38.left, bf16[1024,15360]{1,0:T(8,128)(2,1)} %bitcast.33, bf16[256,5632]{1,0:T(8,128)(2,1)S(1)} %copy-done.4), custom_call_target="tpu_custom_call" | custom-call | flops 268435456 | bytes 2621440 | tf_op jit(solution)/shard_map/send_part/pallas_call | solution.py:236
  129.2 17.8 %collective-permute-done.12.received = bf16[1024,512]{1,0:T(8,128)(2,1)S(1)} collective-permute-done((bf16[1024,512]{1,0:T(8,128)(2,1)}, bf16[1024,512]{1,0:T(8,128)(2,1)S(1)}, u32[]{:S(2)}, u32[]{:S(2)}) %collective-permute-start.12) | collective-permute-done | bytes 1048608 | tf_op jit(solution)/shard_map/ppermute | solution.py:22
  147.0 4.3 %send_part.20 = bf16[1024,512]{1,0:T(8,128)(2,1)} custom-call(s32[1]{0:T(128)} %bitcast.9.place, bf16[256,256]{1,0:T(8,128)(2,1)S(1)} %get-tuple-element.35.hi, bf16[256,256]{1,0:T(8,128)(2,1)S(1)} %copy-done.7, bf16[1024,256]{1,0:T(8,128)(2,1)S(1)} %get-tuple-element.38.left, bf16[1024,15360]{1,0:T(8,128)(2,1)} %bitcast.34, bf16[256,5632]{1,0:T(8,128)(2,1)S(1)} %copy-done.4), custom_call_target="tpu_custom_call" | custom-call | flops 268435456 | bytes 2621440 | tf_op jit(solution)/shard_map/send_part/pallas_call | solution.py:236
  163.7 7.4 %all_gather.10 = bf16[1024,256]{1,0:T(8,128)(2,1)S(1)} all-gather(bf16[1024,128]{1,0:T(8,128)(2,1)} %slice.77), channel_id=1, replica_groups=mesh['cube'=4,'row'=4,'col'=2] {'col'}, dimensions={1}, use_global_device_ids=true | all-gather | bytes 786432 | tf_op jit(solution)/shard_map/all_gather | solution.py:449
  174.7 4.9 %merge_part.15.rest_1_ = bf16[1024,7680]{1,0:T(8,128)(2,1)} custom-call(s32[1]{0:T(128)} %bitcast.place.refs_0_, bf16[256,256]{1,0:T(8,128)(2,1)S(1)} %get-tuple-element.32.hi.refs_1_, bf16[256,256]{1,0:T(8,128)(2,1)S(1)} %get-tuple-element.33.lo.refs_2_, bf16[1024,256]{1,0:T(8,128)(2,1)S(1)} %get-tuple-element.34.left.refs_3_, ...), custom_call_target="tpu_custom_call" | custom-call | flops 1342177280 | bytes 4194304 | tf_op jit(solution)/shard_map/merge_part/pallas_call | solution.py:280
  185.6 4.7 %merge_part.16.rest_1_ = bf16[1024,7680]{1,0:T(8,128)(2,1)} custom-call(s32[1]{0:T(128)} %bitcast.place.refs_0_, bf16[256,256]{1,0:T(8,128)(2,1)S(1)} %get-tuple-element.32.hi.refs_1_, bf16[256,256]{1,0:T(8,128)(2,1)S(1)} %get-tuple-element.33.lo.refs_2_, bf16[1024,256]{1,0:T(8,128)(2,1)S(1)} %get-tuple-element.34.left.refs_3_, ...), custom_call_target="tpu_custom_call", output_to_operand_aliasing={{}: (8, {})} | custom-call | flops 1342177280 | bytes 4194304 | tf_op jit(solution)/shard_map/merge_part/pallas_call | solution.py:280
  196.8 4.7 %merge_part.17.rest_1_ = bf16[1024,7680]{1,0:T(8,128)(2,1)} custom-call(s32[1]{0:T(128)} %bitcast.place.refs_0_, bf16[256,256]{1,0:T(8,128)(2,1)S(1)} %get-tuple-element.32.hi.refs_1_, bf16[256,256]{1,0:T(8,128)(2,1)S(1)} %get-tuple-element.33.lo.refs_2_, bf16[1024,256]{1,0:T(8,128)(2,1)S(1)} %get-tuple-element.34.left.refs_3_, ...), custom_call_target="tpu_custom_call", output_to_operand_aliasing={{}: (8, {})} | custom-call | flops 1342177280 | bytes 4194304 | tf_op jit(solution)/shard_map/merge_part/pallas_call | solution.py:280
  201.6 5.0 %merge_part.18.rest_1_ = bf16[1024,7680]{1,0:T(8,128)(2,1)} custom-call(s32[1]{0:T(128)} %bitcast.place.refs_0_, bf16[256,256]{1,0:T(8,128)(2,1)S(1)} %get-tuple-element.32.hi.refs_1_, bf16[256,256]{1,0:T(8,128)(2,1)S(1)} %get-tuple-element.33.lo.refs_2_, bf16[1024,256]{1,0:T(8,128)(2,1)S(1)} %get-tuple-element.34.left.refs_3_, ...), custom_call_target="tpu_custom_call", output_to_operand_aliasing={{}: (8, {})} | custom-call | flops 1342177280 | bytes 4194304 | tf_op jit(solution)/shard_map/merge_part/pallas_call | solution.py:280
  206.6 7.9 %collective-permute-done.15.received = bf16[1024,512]{1,0:T(8,128)(2,1)} collective-permute-done((bf16[1024,512]{1,0:T(8,128)(2,1)}, bf16[1024,512]{1,0:T(8,128)(2,1)}, u32[]{:S(2)}, u32[]{:S(2)}) %collective-permute-start.15) | collective-permute-done | bytes 1048608 | tf_op jit(solution)/shard_map/ppermute | solution.py:22
  219.1 5.0 %merge_part.19.refs_10_ = bf16[1024,7680]{1,0:T(8,128)(2,1)} custom-call(s32[1]{0:T(128)} %bitcast.place.refs_0_, bf16[256,256]{1,0:T(8,128)(2,1)S(1)} %get-tuple-element.32.hi.refs_1_, bf16[256,256]{1,0:T(8,128)(2,1)S(1)} %get-tuple-element.33.lo.refs_2_, bf16[1024,256]{1,0:T(8,128)(2,1)S(1)} %get-tuple-element.34.left.refs_3_, ...), custom_call_target="tpu_custom_call", output_to_operand_aliasing={{}: (8, {})} | custom-call | flops 1342177280 | bytes 4194304 | tf_op jit(solution)/shard_map/merge_part/pallas_call | solution.py:280
  224.1 6.7 %all_gather.11.refs_8_ = bf16[256,1024]{1,0:T(8,128)(2,1)S(1)} all-gather(bf16[64,1024]{1,0:T(8,128)(2,1)} %constant_dynamic-update-slice_fusion.11), channel_id=1, replica_groups=mesh['cube'=4,'row'=4,'col'=2] {'row'}, dimensions={0}, use_global_device_ids=true | all-gather | bytes 655360 | tf_op jit(solution)/shard_map/all_gather | solution.py:455
  230.8 6.1 %collective-permute-done.14.received = bf16[1024,512]{1,0:T(8,128)(2,1)S(1)} collective-permute-done((bf16[1024,512]{1,0:T(8,128)(2,1)S(1)}, bf16[1024,512]{1,0:T(8,128)(2,1)S(1)}, u32[]{:S(2)}, u32[]{:S(2)}) %collective-permute-start.14) | collective-permute-done | bytes 1048608 | tf_op jit(solution)/shard_map/ppermute | solution.py:22
  240.4 5.3 %merge_part.20.refs_10_ = bf16[1024,7680]{1,0:T(8,128)(2,1)} custom-call(s32[1]{0:T(128)} %bitcast.place.refs_0_, bf16[256,256]{1,0:T(8,128)(2,1)S(1)} %get-tuple-element.32.hi.refs_1_, bf16[256,256]{1,0:T(8,128)(2,1)S(1)} %get-tuple-element.33.lo.refs_2_, bf16[1024,256]{1,0:T(8,128)(2,1)S(1)} %get-tuple-element.34.left.refs_3_, ...), custom_call_target="tpu_custom_call", output_to_operand_aliasing={{}: (10, {})} | custom-call | flops 1342177280 | bytes 4194304 | tf_op jit(solution)/shard_map/merge_part/pallas_call | solution.py:280
  245.7 5.3 %merge_part.21.rest_1_ = bf16[1024,7680]{1,0:T(8,128)(2,1)} custom-call(s32[1]{0:T(128)} %bitcast.place.refs_0_, bf16[256,256]{1,0:T(8,128)(2,1)S(1)} %get-tuple-element.32.hi.refs_1_, bf16[256,256]{1,0:T(8,128)(2,1)S(1)} %get-tuple-element.33.lo.refs_2_, bf16[1024,256]{1,0:T(8,128)(2,1)S(1)} %get-tuple-element.34.left.refs_3_, ...), custom_call_target="tpu_custom_call", output_to_operand_aliasing={{}: (10, {})} | custom-call | flops 1342177280 | bytes 4194304 | tf_op jit(solution)/shard_map/merge_part/pallas_call | solution.py:280
  251.0 8.3 %collective-permute-done.19.received = bf16[1024,512]{1,0:T(8,128)(2,1)S(1)} collective-permute-done((bf16[1024,512]{1,0:T(8,128)(2,1)S(1)}, bf16[1024,512]{1,0:T(8,128)(2,1)S(1)}, u32[]{:S(2)}, u32[]{:S(2)}) %collective-permute-start.19) | collective-permute-done | bytes 1048608 | tf_op jit(solution)/shard_map/ppermute | solution.py:22
  263.9 5.0 %merge_part.22.rest_1_ = bf16[1024,7680]{1,0:T(8,128)(2,1)} custom-call(s32[1]{0:T(128)} %bitcast.place.refs_0_, bf16[256,256]{1,0:T(8,128)(2,1)S(1)} %get-tuple-element.32.hi.refs_1_, bf16[256,256]{1,0:T(8,128)(2,1)S(1)} %get-tuple-element.33.lo.refs_2_, bf16[1024,256]{1,0:T(8,128)(2,1)S(1)} %get-tuple-element.34.left.refs_3_, ...), custom_call_target="tpu_custom_call", output_to_operand_aliasing={{}: (8, {})} | custom-call | flops 1342177280 | bytes 4194304 | tf_op jit(solution)/shard_map/merge_part/pallas_call | solution.py:280
  268.9 4.7 %merge_part.23.rest_1_ = bf16[1024,7680]{1,0:T(8,128)(2,1)} custom-call(s32[1]{0:T(128)} %bitcast.place.refs_0_, bf16[256,256]{1,0:T(8,128)(2,1)S(1)} %get-tuple-element.32.hi.refs_1_, bf16[256,256]{1,0:T(8,128)(2,1)S(1)} %get-tuple-element.33.lo.refs_2_, bf16[1024,256]{1,0:T(8,128)(2,1)S(1)} %get-tuple-element.34.left.refs_3_, ...), custom_call_target="tpu_custom_call", output_to_operand_aliasing={{}: (8, {})} | custom-call | flops 1342177280 | bytes 4194304 | tf_op jit(solution)/shard_map/merge_part/pallas_call | solution.py:280
  273.7 8.1 %collective-permute-done.18.received = bf16[1024,512]{1,0:T(8,128)(2,1)S(1)} collective-permute-done((bf16[1024,512]{1,0:T(8,128)(2,1)}, bf16[1024,512]{1,0:T(8,128)(2,1)S(1)}, u32[]{:S(2)}, u32[]{:S(2)}) %collective-permute-start.18) | collective-permute-done | bytes 1048608 | tf_op jit(solution)/shard_map/ppermute | solution.py:22
  285.3 4.7 %merge_part.24.rest_1_ = bf16[1024,7680]{1,0:T(8,128)(2,1)} custom-call(s32[1]{0:T(128)} %bitcast.place.refs_0_, bf16[256,256]{1,0:T(8,128)(2,1)S(1)} %get-tuple-element.32.hi.refs_1_, bf16[256,256]{1,0:T(8,128)(2,1)S(1)} %get-tuple-element.33.lo.refs_2_, bf16[1024,256]{1,0:T(8,128)(2,1)S(1)} %get-tuple-element.34.left.refs_3_, ...), custom_call_target="tpu_custom_call", output_to_operand_aliasing={{}: (8, {})} | custom-call | flops 1342177280 | bytes 4194304 | tf_op jit(solution)/shard_map/merge_part/pallas_call | solution.py:280
  290.1 4.7 %merge_part.25.rest_1_ = bf16[1024,7680]{1,0:T(8,128)(2,1)} custom-call(s32[1]{0:T(128)} %bitcast.place.refs_0_, bf16[256,256]{1,0:T(8,128)(2,1)S(1)} %get-tuple-element.32.hi.refs_1_, bf16[256,256]{1,0:T(8,128)(2,1)S(1)} %get-tuple-element.33.lo.refs_2_, bf16[1024,256]{1,0:T(8,128)(2,1)S(1)} %get-tuple-element.34.left.refs_3_, ...), custom_call_target="tpu_custom_call", output_to_operand_aliasing={{}: (8, {})} | custom-call | flops 1342177280 | bytes 4194304 | tf_op jit(solution)/shard_map/merge_part/pallas_call | solution.py:280
  294.8 9.5 %collective-permute-done.17.received = bf16[1024,512]{1,0:T(8,128)(2,1)S(1)} collective-permute-done((bf16[1024,512]{1,0:T(8,128)(2,1)S(1)}, bf16[1024,512]{1,0:T(8,128)(2,1)S(1)}, u32[]{:S(2)}, u32[]{:S(2)}) %collective-permute-start.17) | collective-permute-done | bytes 1048608 | tf_op jit(solution)/shard_map/ppermute | solution.py:22
  307.5 19.3 %collective-permute-done.22.received = bf16[1024,512]{1,0:T(8,128)(2,1)S(1)} collective-permute-done((bf16[1024,512]{1,0:T(8,128)(2,1)}, bf16[1024,512]{1,0:T(8,128)(2,1)S(1)}, u32[]{:S(2)}, u32[]{:S(2)}) %collective-permute-start.22) | collective-permute-done | bytes 1048608 | tf_op jit(solution)/shard_map/ppermute | solution.py:22
  330.8 4.7 %merge_part.26.rest_1_ = bf16[1024,7680]{1,0:T(8,128)(2,1)} custom-call(s32[1]{0:T(128)} %bitcast.place.refs_0_, bf16[256,256]{1,0:T(8,128)(2,1)S(1)} %get-tuple-element.32.hi.refs_1_, bf16[256,256]{1,0:T(8,128)(2,1)S(1)} %get-tuple-element.33.lo.refs_2_, bf16[1024,256]{1,0:T(8,128)(2,1)S(1)} %get-tuple-element.34.left.refs_3_, ...), custom_call_target="tpu_custom_call", output_to_operand_aliasing={{}: (8, {})} | custom-call | flops 1342177280 | bytes 4194304 | tf_op jit(solution)/shard_map/merge_part/pallas_call | solution.py:280
  335.5 4.7 %merge_part.27.rest_1_ = bf16[1024,7680]{1,0:T(8,128)(2,1)} custom-call(s32[1]{0:T(128)} %bitcast.place.refs_0_, bf16[256,256]{1,0:T(8,128)(2,1)S(1)} %get-tuple-element.32.hi.refs_1_, bf16[256,256]{1,0:T(8,128)(2,1)S(1)} %get-tuple-element.33.lo.refs_2_, bf16[1024,256]{1,0:T(8,128)(2,1)S(1)} %get-tuple-element.34.left.refs_3_, ...), custom_call_target="tpu_custom_call", output_to_operand_aliasing={{}: (8, {})} | custom-call | flops 1342177280 | bytes 4194304 | tf_op jit(solution)/shard_map/merge_part/pallas_call | solution.py:280
  340.3 9.0 %collective-permute-done.21.received = bf16[1024,512]{1,0:T(8,128)(2,1)S(1)} collective-permute-done((bf16[1024,512]{1,0:T(8,128)(2,1)S(1)}, bf16[1024,512]{1,0:T(8,128)(2,1)S(1)}, u32[]{:S(2)}, u32[]{:S(2)}) %collective-permute-start.21) | collective-permute-done | bytes 1048608 | tf_op jit(solution)/shard_map/ppermute | solution.py:22
  349.2 4.7 %merge_part.28.rest_1_ = bf16[1024,7680]{1,0:T(8,128)(2,1)} custom-call(s32[1]{0:T(128)} %bitcast.place.refs_0_, bf16[256,256]{1,0:T(8,128)(2,1)S(1)} %get-tuple-element.32.hi.refs_1_, bf16[256,256]{1,0:T(8,128)(2,1)S(1)} %get-tuple-element.33.lo.refs_2_, bf16[1024,256]{1,0:T(8,128)(2,1)S(1)} %get-tuple-element.34.left.refs_3_, ...), custom_call_target="tpu_custom_call", output_to_operand_aliasing={{}: (8, {})} | custom-call | flops 1342177280 | bytes 4194304 | tf_op jit(solution)/shard_map/merge_part/pallas_call | solution.py:280
  354.0 6.5 %collective-permute-done.20.received = bf16[1024,256]{1,0:T(8,128)(2,1)S(1)} collective-permute-done((bf16[1024,256]{1,0:T(8,128)(2,1)S(1)}, bf16[1024,256]{1,0:T(8,128)(2,1)S(1)}, u32[]{:S(2)}, u32[]{:S(2)}) %collective-permute-start.20) | collective-permute-done | bytes 524320 | tf_op jit(solution)/shard_map/ppermute | solution.py:22
  360.5 4.1 %merge_part.29._ = bf16[1024,7680]{1,0:T(8,128)(2,1)} custom-call(s32[1]{0:T(128)} %bitcast.place.refs_0_, bf16[256,256]{1,0:T(8,128)(2,1)S(1)} %get-tuple-element.32.hi.refs_1_, bf16[256,256]{1,0:T(8,128)(2,1)S(1)} %get-tuple-element.33.lo.refs_2_, bf16[1024,256]{1,0:T(8,128)(2,1)S(1)} %get-tuple-element.34.left.refs_3_, ...), custom_call_target="tpu_custom_call", output_to_operand_aliasing={{}: (8, {})} | custom-call | flops 671088640 | bytes 2097152 | tf_op jit(solution)/shard_map/merge_part/pallas_call | solution.py:280
  (162 shorter events, 102.0 us)
Async XLA Ops:
  6.5 166.9 %all-gather.2.cloned.1.call-start = ((), (), s32[]{:S(2)}) async-start(), calls=%async_computation | async-start | bytes 4915200 | tf_op jit(solution)/shard_map/all_gather | solution.py:438
  6.6 12.3 %copy-start.26 = (s32[1,256]{1,0:T(1,128)S(1)}, s32[1,256]{1,0:T(1,128)}, u32[]{:S(2)}) copy-start(s32[1,256]{1,0:T(1,128)} %param.8) | copy-start | bytes 3076
  9.8 10.6 %copy-start.24 = (s32[1,1024]{1,0:T(1,128)S(1)}, s32[1,1024]{1,0:T(1,128)}, u32[]{:S(2)}) copy-start(s32[1,1024]{1,0:T(1,128)} %param.13) | copy-start | bytes 12292
  9.8 11.2 %copy-start.25 = (s32[1,8,2]{1,2,0:T(2,128)S(1)}, s32[1,8,2]{1,2,0:T(2,128)}, u32[]{:S(2)}) copy-start(s32[1,8,2]{1,2,0:T(2,128)} %param.12) | copy-start | bytes 196
  9.8 82.9 %collective-permute-start.7 = (bf16[1024,1024]{1,0:T(8,128)(2,1)}, bf16[1024,1024]{1,0:T(8,128)(2,1)}, u32[]{:S(2)}, u32[]{:S(2)}) collective-permute-start(bf16[1024,1024]{1,0:T(8,128)(2,1)} %dynamic-slice_bitcast_fusion), channel_id=1, source_target_pairs={{0,8},{8,0},{16,24},{24,16},{1,9},{9,1},{17,25},{25,17},{2,10},{10... | collective-permute-start | bytes 6291464 | tf_op jit(solution)/shard_map/ppermute | solution.py:22
  12.8 7.6 %collective-permute-start = (f32[32,256]{1,0:T(8,128)S(1)}, f32[32,256]{1,0:T(8,128)S(1)}, u32[]{:S(2)}, u32[]{:S(2)}) collective-permute-start(f32[32,256]{1,0:T(8,128)S(1)} %bitcast.59), channel_id=1, source_target_pairs={{0,4},{1,5},{2,6},{3,7},{4,0},{5,1},{6,2},{7,3},{8,12},{9,13},{10,... | collective-permute-start | bytes 98312 | tf_op jit(solution)/shard_map/ppermute | solution.py:22
  14.4 12.1 %collective-permute-start.3 = (bf16[1024,128]{1,0:T(8,128)(2,1)S(1)}, bf16[1024,128]{1,0:T(8,128)(2,1)S(1)}, u32[]{:S(2)}, u32[]{:S(2)}) collective-permute-start(bf16[1024,128]{1,0:T(8,128)(2,1)S(1)} %bitcast.63), channel_id=1, source_target_pairs={{0,1},{1,0},{2,3},{3,2},{4,5},{5,4},{6,7},{7,6},{8,9},{9,8},{10,11... | collective-permute-start | bytes 786440 | tf_op jit(solution)/shard_map/ppermute | solution.py:22
  15.9 10.3 %collective-permute-start.4 = (bf16[64,2048]{1,0:T(8,128)(2,1)S(1)}, bf16[64,2048]{1,0:T(8,128)(2,1)S(1)}, u32[]{:S(2)}, u32[]{:S(2)}) collective-permute-start(bf16[64,2048]{1,0:T(8,128)(2,1)S(1)} %dynamic-slice_bitcast_fusion.3), channel_id=1, source_target_pairs={{0,4},{2,6},{4,0},{6,2},{1,5},{3,7},{5,1},{7,3},{8,12},{10,14},{12... | collective-permute-start | bytes 786440 | tf_op jit(solution)/shard_map/ppermute | solution.py:22
  17.4 36.7 %collective-permute-start.9 = (bf16[64,5632]{1,0:T(8,128)(2,1)}, bf16[64,5632]{1,0:T(8,128)(2,1)}, u32[]{:S(2)}, u32[]{:S(2)}) collective-permute-start(bf16[64,5632]{1,0:T(8,128)(2,1)} %dynamic-slice_bitcast_fusion.2), channel_id=1, source_target_pairs={{0,4},{2,6},{4,0},{6,2},{1,5},{3,7},{5,1},{7,3},{8,12},{10,14},{12... | collective-permute-start | bytes 2162696 | tf_op jit(solution)/shard_map/ppermute | solution.py:22
  20.4 4.3 %collective-permute-start.1 = (f32[64,256]{1,0:T(8,128)S(1)}, f32[64,256]{1,0:T(8,128)S(1)}, u32[]{:S(2)}, u32[]{:S(2)}) collective-permute-start(f32[64,256]{1,0:T(8,128)S(1)} %pad_maximum_fusion.6), channel_id=1, source_target_pairs={{0,1},{1,0},{2,3},{3,2},{4,5},{5,4},{6,7},{7,6},{8,9},{9,8},{10,11... | collective-permute-start | bytes 196616 | tf_op jit(solution)/shard_map/ppermute | solution.py:22
  24.8 1.4 collective-permute-start.2
  26.3 29.3 %collective-permute-start.5 = (bf16[128,2048]{1,0:T(8,128)(2,1)S(1)}, bf16[128,2048]{1,0:T(8,128)(2,1)S(1)}, u32[]{:S(2)}, u32[]{:S(2)}) collective-permute-start(bf16[128,2048]{1,0:T(8,128)(2,1)S(1)} %pad_maximum_fusion.3), channel_id=1, source_target_pairs={{0,2},{2,0},{4,6},{6,4},{1,3},{3,1},{5,7},{7,5},{8,10},{10,8},{12,... | collective-permute-start | bytes 1572872 | tf_op jit(solution)/shard_map/ppermute | solution.py:22
  54.0 38.8 %copy-start.6 = (bf16[256,256]{1,0:T(8,128)(2,1)}, bf16[256,256]{1,0:T(8,128)(2,1)S(1)}, u32[]{:S(2)}) copy-start(bf16[256,256]{1,0:T(8,128)(2,1)S(1)} %get-tuple-element.37.lo) | copy-start | bytes 393220
  58.7 38.4 %collective-permute-start.6 = (bf16[1024,512]{1,0:T(8,128)(2,1)S(1)}, bf16[1024,512]{1,0:T(8,128)(2,1)S(1)}, u32[]{:S(2)}, u32[]{:S(2)}) collective-permute-start(bf16[1024,512]{1,0:T(8,128)(2,1)S(1)} %send_part.15), channel_id=1, source_target_pairs={{0,8},{8,0},{16,24},{24,16},{1,9},{9,1},{17,25},{25,17},{2,10},{10... | collective-permute-start | bytes 3145736 | tf_op jit(solution)/shard_map/ppermute | solution.py:22
  59.2 33.5 %collective-permute-start.10 = (bf16[128,5632]{1,0:T(8,128)(2,1)S(1)}, bf16[128,5632]{1,0:T(8,128)(2,1)S(1)}, u32[]{:S(2)}, u32[]{:S(2)}) collective-permute-start(bf16[128,5632]{1,0:T(8,128)(2,1)S(1)} %pad_maximum_fusion), channel_id=1, source_target_pairs={{0,2},{2,0},{4,6},{6,4},{1,3},{3,1},{5,7},{7,5},{8,10},{10,8},{12,... | collective-permute-start | bytes 4325384 | tf_op jit(solution)/shard_map/ppermute | solution.py:22
  59.8 32.9 %collective-permute-start.8 = (bf16[1568,128]{1,0:T(8,128)(2,1)S(1)}, bf16[1568,128]{1,0:T(8,128)(2,1)}, u32[]{:S(2)}, u32[]{:S(2)}) collective-permute-start(bf16[1568,128]{1,0:T(8,128)(2,1)S(1)} %constant_dynamic-update-slice_fusion), channel_id=1, source_target_pairs={{0,8},{8,0},{16,24},{24,16},{1,9},{9,1},{17,25},{25,17},{2,10},{10... | collective-permute-start | bytes 1204232 | tf_op jit(solution)/shard_map/ppermute | solution.py:22
  98.1 26.4 %collective-permute-start.13 = (bf16[1024,512]{1,0:T(8,128)(2,1)}, bf16[1024,512]{1,0:T(8,128)(2,1)S(1)}, u32[]{:S(2)}, u32[]{:S(2)}) collective-permute-start(bf16[1024,512]{1,0:T(8,128)(2,1)} %send_part.16), channel_id=1, source_target_pairs={{0,8},{8,0},{16,24},{24,16},{1,9},{9,1},{17,25},{25,17},{2,10},{10... | collective-permute-start | bytes 3145736 | tf_op jit(solution)/shard_map/ppermute | solution.py:22
  98.7 48.3 %collective-permute-start.12 = (bf16[1024,512]{1,0:T(8,128)(2,1)}, bf16[1024,512]{1,0:T(8,128)(2,1)S(1)}, u32[]{:S(2)}, u32[]{:S(2)}) collective-permute-start(bf16[1024,512]{1,0:T(8,128)(2,1)} %send_part.17), channel_id=1, source_target_pairs={{0,8},{8,0},{16,24},{24,16},{1,9},{9,1},{17,25},{25,17},{2,10},{10... | collective-permute-start | bytes 3145736 | tf_op jit(solution)/shard_map/ppermute | solution.py:22
  107.5 72.0 %collective-permute-start.11 = (bf16[1024,512]{1,0:T(8,128)(2,1)}, bf16[1024,512]{1,0:T(8,128)(2,1)}, u32[]{:S(2)}, u32[]{:S(2)}) collective-permute-start(bf16[1024,512]{1,0:T(8,128)(2,1)} %send_part.18), channel_id=1, source_target_pairs={{0,8},{8,0},{16,24},{24,16},{1,9},{9,1},{17,25},{25,17},{2,10},{10... | collective-permute-start | bytes 3145736 | tf_op jit(solution)/shard_map/ppermute | solution.py:22
  128.8 63.3 %collective-permute-start.16 = (bf16[1024,512]{1,0:T(8,128)(2,1)}, bf16[1024,512]{1,0:T(8,128)(2,1)}, u32[]{:S(2)}, u32[]{:S(2)}) collective-permute-start(bf16[1024,512]{1,0:T(8,128)(2,1)} %send_part.19), channel_id=1, source_target_pairs={{0,8},{8,0},{16,24},{24,16},{1,9},{9,1},{17,25},{25,17},{2,10},{10... | collective-permute-start | bytes 3145736 | tf_op jit(solution)/shard_map/ppermute | solution.py:22
  151.3 63.2 %collective-permute-start.15 = (bf16[1024,512]{1,0:T(8,128)(2,1)}, bf16[1024,512]{1,0:T(8,128)(2,1)}, u32[]{:S(2)}, u32[]{:S(2)}) collective-permute-start(bf16[1024,512]{1,0:T(8,128)(2,1)} %send_part.20), channel_id=1, source_target_pairs={{0,8},{8,0},{16,24},{24,16},{1,9},{9,1},{17,25},{25,17},{2,10},{10... | collective-permute-start | bytes 3145736 | tf_op jit(solution)/shard_map/ppermute | solution.py:22
  154.1 25.5 %copy-start.22 = (f32[32,128]{1,0:T(8,128)}, f32[32,128]{1,0:T(8,128)S(1)}, u32[]{:S(2)}) copy-start(f32[32,128]{1,0:T(8,128)S(1)} %slice_convert_fusion) | copy-start | bytes 49156
  182.6 54.2 %collective-permute-start.14 = (bf16[1024,512]{1,0:T(8,128)(2,1)S(1)}, bf16[1024,512]{1,0:T(8,128)(2,1)S(1)}, u32[]{:S(2)}, u32[]{:S(2)}) collective-permute-start(bf16[1024,512]{1,0:T(8,128)(2,1)S(1)} %send_part.21), channel_id=1, source_target_pairs={{0,8},{8,0},{16,24},{24,16},{1,9},{9,1},{17,25},{25,17},{2,10},{10... | collective-permute-start | bytes 3145736 | tf_op jit(solution)/shard_map/ppermute | solution.py:22
  195.0 64.3 %collective-permute-start.19 = (bf16[1024,512]{1,0:T(8,128)(2,1)S(1)}, bf16[1024,512]{1,0:T(8,128)(2,1)S(1)}, u32[]{:S(2)}, u32[]{:S(2)}) collective-permute-start(bf16[1024,512]{1,0:T(8,128)(2,1)S(1)} %send_part.22), channel_id=1, source_target_pairs={{0,8},{8,0},{16,24},{24,16},{1,9},{9,1},{17,25},{25,17},{2,10},{10... | collective-permute-start | bytes 3145736 | tf_op jit(solution)/shard_map/ppermute | solution.py:22
  218.6 63.2 %collective-permute-start.18 = (bf16[1024,512]{1,0:T(8,128)(2,1)}, bf16[1024,512]{1,0:T(8,128)(2,1)S(1)}, u32[]{:S(2)}, u32[]{:S(2)}) collective-permute-start(bf16[1024,512]{1,0:T(8,128)(2,1)} %send_part.23), channel_id=1, source_target_pairs={{0,8},{8,0},{16,24},{24,16},{1,9},{9,1},{17,25},{25,17},{2,10},{10... | collective-permute-start | bytes 3145736 | tf_op jit(solution)/shard_map/ppermute | solution.py:22
  239.8 64.5 %collective-permute-start.17 = (bf16[1024,512]{1,0:T(8,128)(2,1)S(1)}, bf16[1024,512]{1,0:T(8,128)(2,1)S(1)}, u32[]{:S(2)}, u32[]{:S(2)}) collective-permute-start(bf16[1024,512]{1,0:T(8,128)(2,1)S(1)} %send_part.24), channel_id=1, source_target_pairs={{0,8},{8,0},{16,24},{24,16},{1,9},{9,1},{17,25},{25,17},{2,10},{10... | collective-permute-start | bytes 3145736 | tf_op jit(solution)/shard_map/ppermute | solution.py:22
  263.4 63.3 %collective-permute-start.22 = (bf16[1024,512]{1,0:T(8,128)(2,1)}, bf16[1024,512]{1,0:T(8,128)(2,1)S(1)}, u32[]{:S(2)}, u32[]{:S(2)}) collective-permute-start(bf16[1024,512]{1,0:T(8,128)(2,1)} %send_part.25), channel_id=1, source_target_pairs={{0,8},{8,0},{16,24},{24,16},{1,9},{9,1},{17,25},{25,17},{2,10},{10... | collective-permute-start | bytes 3145736 | tf_op jit(solution)/shard_map/ppermute | solution.py:22
  273.7 11.6 %copy-start.23 = (f32[32,128]{1,0:T(8,128)S(1)}, f32[32,128]{1,0:T(8,128)}, u32[]{:S(2)}) copy-start(f32[32,128]{1,0:T(8,128)} %copy-done.22) | copy-start | bytes 49156
  284.8 64.4 %collective-permute-start.21 = (bf16[1024,512]{1,0:T(8,128)(2,1)S(1)}, bf16[1024,512]{1,0:T(8,128)(2,1)S(1)}, u32[]{:S(2)}, u32[]{:S(2)}) collective-permute-start(bf16[1024,512]{1,0:T(8,128)(2,1)S(1)} %send_part.26), channel_id=1, source_target_pairs={{0,8},{8,0},{16,24},{24,16},{1,9},{9,1},{17,25},{25,17},{2,10},{10... | collective-permute-start | bytes 3145736 | tf_op jit(solution)/shard_map/ppermute | solution.py:22
  307.0 53.5 %collective-permute-start.20 = (bf16[1024,256]{1,0:T(8,128)(2,1)S(1)}, bf16[1024,256]{1,0:T(8,128)(2,1)S(1)}, u32[]{:S(2)}, u32[]{:S(2)}) collective-permute-start(bf16[1024,256]{1,0:T(8,128)(2,1)S(1)} %send_part.27), channel_id=1, source_target_pairs={{0,8},{8,0},{16,24},{24,16},{1,9},{9,1},{17,25},{25,17},{2,10},{10... | collective-permute-start | bytes 1572872 | tf_op jit(solution)/shard_map/ppermute | solution.py:22
  330.3 39.7 %collective-permute-start.23 = (bf16[1024,256]{1,0:T(8,128)(2,1)S(1)}, bf16[1024,256]{1,0:T(8,128)(2,1)S(1)}, u32[]{:S(2)}, u32[]{:S(2)}) collective-permute-start(bf16[1024,256]{1,0:T(8,128)(2,1)S(1)} %fusion.3), channel_id=1, source_target_pairs={{0,8},{8,0},{16,24},{24,16},{1,9},{9,1},{17,25},{25,17},{2,10},{10... | collective-permute-start | bytes 1572872 | tf_op jit(solution)/shard_map/ppermute | solution.py:22
  354.0 10.6 %copy-start.2 = (bf16[256,7680]{1,0:T(8,128)(2,1)S(1)}, bf16[256,7680]{1,0:T(8,128)(2,1)}, u32[]{:S(2)}) copy-start(bf16[256,7680]{1,0:T(8,128)(2,1)} %all-gather.2.cloned.1.call-done.rest_0_.refs_9_) | copy-start | bytes 11796484
  (20 other events, 89.2 us)
Sparse Core Ops, SparseCore 0:
  98.3 31.6 all-gather.1

commit v6 on v5

--- a/solution.py
+++ b/solution.py
@@ -75,7 +75,7 @@
 
 
 def factor_kernel(
-    block, order_of_diag, order_of_upper, order, order_of_lower, panel, mask, hi, lo, kept_hi, kept_lo, plain, sent, kept
+    block, order_of_diag, order_of_upper, order_of_lower, panel, mask, hi, lo, plain, sent, kept
 ):
     size = block.shape[0]
     half = size // 2
@@ -100,7 +100,6 @@
         [jnp.concatenate([upper_one, corner_upper], 1), jnp.concatenate([zero, upper_two], 1)], 0
     )
     hi[...], lo[...] = split(exact(lower_inv, chosen(order_of_upper)))
-    kept_hi[...], kept_lo[...] = split(exact(lower_inv, chosen(order)))
     row = lax.broadcasted_iota(jnp.int32, (size, size), 0)
     in_order = jnp.where(order_of_lower[...] == row, 1.0, 0.0)
     upper_hi, upper_lo = split(exact(in_order, upper_inv))
@@ -121,8 +120,6 @@
     return pl.pallas_call(
         factor_kernel,
         out_shape=(
-            jax.ShapeDtypeStruct((size, size), half_type),
-            jax.ShapeDtypeStruct((size, size), half_type),
             jax.ShapeDtypeStruct((size, size), half_type),
             jax.ShapeDtypeStruct((size, size), half_type),
             jax.ShapeDtypeStruct((rows, size), half_type),
@@ -368,7 +365,6 @@
     orders = (
         place_of(order, diag_block.shape[0], ("row", "col")),
         place_of(order, upper_in.shape[0], "row"),
-        order,
         in_col_order[None, :],
     )
     block_rows = rows // block_mask.shape[1]
@@ -379,23 +375,24 @@
 
     cut = raw_end + EARLY * width
     early = doubled(columns_of(1 - parity, 0, cut), "row", 0)
-    late = columns_of(1 - parity, cut, half)
-    late = next_doubled(late, "row", 0, 0)
-
-    hi, lo, kept_hi, kept_lo, plain_left, sent_left, kept_left = factor(whole_block, orders, panel, flags)
+    late, kept_upper = columns_of(1 - parity, cut, half), columns_of(parity, 0, half)
+    rest = partner(jnp.concatenate([late, kept_upper], axis=1), "row", bits_of("row")[0])
+    late = jnp.concatenate([late, rest[:, : half - cut]], axis=0)
+    kept_upper = jnp.concatenate([kept_upper, rest[:, half - cut :]], axis=0)
+
+    hi, lo, plain_left, sent_left, kept_left = factor(whole_block, orders, panel, flags)
 
     left_share = lax.dynamic_slice_in_dim(plain_left, col * lower_in.shape[1], lower_in.shape[1], 1)
     share = upper_in.shape[0]
     share_hi = lax.dynamic_slice_in_dim(hi, row * share, share, 0)
     share_lo = lax.dynamic_slice_in_dim(lo, row * share, share, 0)
-    raw_upper = early[:, :raw_end]
-    right_share = (fast(share_hi, raw_upper) + fast(share_lo, raw_upper)).astype(jnp.bfloat16)
-    wide = left_share.shape[1]
-    stacked = [right_share[:, at : at + wide] for at in range(0, raw_end, wide)]
+    left_received = partner(left_share, "cube", 1)
     mask = block_mask[0].reshape(-1)
-    digits = jnp.concatenate([row_map[0] // 32, row_map[0] % 32, mask, jnp.zeros(16 * wide - mask.shape[0], mask.dtype)])
-    bundle = jnp.concatenate([left_share, *stacked, digits.astype(jnp.bfloat16).reshape(-1, wide)], axis=0)
-    bundle = partner(bundle, "cube", 1)
+    mask_rows = -(-(2 * rows + mask.shape[0]) // (16 * raw_end)) * 16
+    fill = jnp.zeros(mask_rows * raw_end - 2 * rows - mask.shape[0], mask.dtype)
+    digits = jnp.concatenate([row_map[0] // 32, row_map[0] % 32, mask, fill])
+    digits = digits.astype(jnp.bfloat16).reshape(mask_rows, raw_end)
+
     def choice(order):
         return (order[:, None] == jnp.arange(rows, dtype=jnp.int32)[None, :]).astype(jnp.bfloat16)
 
@@ -411,7 +408,7 @@
     def merge(number):
         start, end = spans[number]
         return merge_chunk(
-            kept_place, kept_hi, kept_lo, kept_left, trailing, chosen, received[number], [kept_upper], [0], start, end - start,
+            kept_place, hi, lo, kept_left, trailing, chosen, received[number], [kept_upper], [0], start, end - start,
             merged,
         )
 
@@ -419,7 +416,7 @@
         result = merged
         for start in range(0, raw_end, width):
             result = merge_chunk(
-                kept_place, kept_hi, kept_lo, kept_left, trailing, chosen, raw_received, [kept_upper], [0], start,
+                kept_place, hi, lo, kept_left, trailing, chosen, raw_received, [kept_upper], [0], start,
                 width, result, (0, other_left, other_right),
             )
         return result
@@ -431,28 +428,29 @@
         if number == 1:
             for step in range(1, len(bits_of("row"))):
                 late = next_doubled(after(late, sent[0]), "row", 0, step)
-        if number == 2:
-            before += [bundle]
         if number == 3:
-            kept_upper = after(columns_of(parity, 0, half), received[0], sent[2])
-            kept_upper = lax.all_gather(kept_upper, "row", axis=0, tiled=True)
+            before += [left_received]
+            for step in range(1, len(bits_of("row"))):
+                kept_upper = next_doubled(after(kept_upper, raw_received, sent[2]), "row", 0, step)
+            raw_upper = after(early[:, :raw_end], received[0], sent[2])
+            right_share = (fast(share_hi, raw_upper) + fast(share_lo, raw_upper)).astype(jnp.bfloat16)
+            bundle = partner(jnp.concatenate([right_share, digits], axis=0), "cube", 1)
         if number == 5:
-            arrived = after(bundle, received[2], sent[4])
-            left_received = arrived[:rows]
-            stacked = arrived[rows : rows + share * (raw_end // wide)].reshape(raw_end // wide, share, wide)
-            right_received = jnp.concatenate(list(stacked), axis=1)
-            digits = arrived[rows + share * (raw_end // wide) :].reshape(-1).astype(jnp.float32)
+            before += [bundle, kept_upper]
+        if number == 6:
+            arrived = after(bundle, received[3], sent[5])
+            right_received = arrived[:share]
+            digits = arrived[share:].reshape(-1).astype(jnp.float32)
             other_order = (32 * digits[:rows] + digits[rows : 2 * rows]).astype(jnp.int32)
             other_flags = digits[2 * rows : 2 * rows + mask.shape[0]].reshape(block_mask.shape[1:])
             other_flags = jnp.where(parity == 0, other_flags[:, :1], other_flags[:, 1:])
             other_chosen = choice(other_order)
+            left_received = after(left_received, received[3], sent[5])
             other_left = lax.all_gather(left_received, "col", axis=1, tiled=True)
             other_left = other_left.astype(jnp.float32) * jnp.repeat(other_flags, block_rows, axis=0)
             other_left = other_left.astype(jnp.bfloat16)
-        if number == 6:
-            before += [kept_upper]
-        if number == 7:
-            other_right = lax.all_gather(after(right_received, received[4], sent[6]), "row", axis=0, tiled=True)
+        if number == 8:
+            other_right = lax.all_gather(after(right_received, received[5], sent[7]), "row", axis=0, tiled=True)
         if number == 9:
             before += [other_left, other_right, other_chosen]
         ready = MERGES.get(number, ())
@@ -472,7 +470,7 @@
         merged = merge(number)
     start, end = spans[-1]
     own = send_chunk(
-        after(kept_place, merged), kept_hi, kept_lo, kept_left, trailing, [kept_upper], [0], start, end - start
+        after(kept_place, merged), hi, lo, kept_left, trailing, [kept_upper], [0], start, end - start
     )
     merged = join_chunk(own, received[-1], start, merged)
     return merged[None]

time: 381 us -> 365 us (0.958)
  between operations: 13.9 us -> 0.6 us
  other arithmetic: 5.09 us -> 12 us
  waiting for transfers between devices: 145 us -> 139 us
    unnamed x71 -> x62, local copies, waits for them, and re-layouts: 15.7 us -> 7.81 us
    ppermute x24 -> x26, waiting for transfers between devices: 145 us -> 139 us  [partner(): return lax.ppermute(block, axis, [(i, i ^ bits) for i in range(count)])]
    convert_element_type x1 -> x2, local copies, waits for them, and re-layouts: 1.98 us -> 6.17 us  [the longest x1 5.54 us: local(): digits = arrived[share:].reshape(-1).astype(jnp.float32)]
    ppermute x24 -> x26, starting transfers between devices: 19.8 us -> 16.5 us  [partner(): return lax.ppermute(block, axis, [(i, i ^ bits) for i in range(count)])]
  transfers between devices with their start and end apart: 25 -> 26, of which waited for: 15 -> 14; matrix products, arithmetic and copies ran while one was open for 6% -> 8% of each run, Pallas kernels for 40% -> 42%
where the time goes in v6:
time: 365 us; the launch traced here: 362 us
  Pallas kernels  153 us (42%)
  waiting for transfers between devices  139 us (38%)
  local copies, waits for them, and re-layouts  25.8 us (7%)
  starting transfers between devices  16.5 us (5%)
  blocking collectives  14.2 us (4%)
  other arithmetic  12 us (3%)
    ppermute x26, waiting for transfers between devices, partner(): return lax.ppermute(block, axis, [(i, i ^ bits) for i in range(count)])  139 us
    pallas_call x15, Pallas kernels, merge_chunk(): pl.pallas_call(body, grid_spec=pltpu.PrefetchScalarGridSpec(num_scalar_pr...  72.7 us
    pallas_call x15, Pallas kernels, send_chunk(): pl.pallas_call(send_kernel, grid_spec=pltpu.PrefetchScalarGridSpec(num_sc...  52.3 us
    pallas_call x1, Pallas kernels, factor(): pl.pallas_call(factor_kernel, out_shape=(jax.ShapeDtypeStruct((size, size...  26.9 us
    ppermute x26, starting transfers between devices, partner(): return lax.ppermute(block, axis, [(i, i ^ bits) for i in range(count)])  16.5 us
    unnamed x62, local copies, waits for them, and re-layouts  7.81 us
    all_gather x1, blocking collectives, local(): other_left = lax.all_gather(left_received, 'col', axis=1, tiled=True)  7.48 us
  transfers between devices with their start and end apart: 26, of which 14 were waited for; matrix products, arithmetic and copies ran while one was open for 8% of the time, Pallas kernels for 42%

profile of v6, /device:TPU:0, one launch (start us, length us, event | category | flops | bytes accessed | tf_op | source)
XLA Modules:
  0.0 362.2 jit_solution(14867394137960656052)
XLA Ops:
  26.5 26.9 %factor.1 = (bf16[256,256]{1,0:T(8,128)(2,1)S(1)}, bf16[256,256]{1,0:T(8,128)(2,1)S(1)}, bf16[1024,256]{1,0:T(8,128)(2,1)S(1)}, bf16[1024,256]{1,0:T(8,128)(2,1)S(1)}, bf16[1024,256]{1,0:T(8,128)(2,1)S(1)}) custom-call(f32[256,256]{1,0:T(8,128)S(1)} %pad_maximum_fusion.6.block, s32[256,1]{1,0:T(8,128)S(1)} %get-tuple-element.58.order_of_diag, ...), custom_call_target="tpu_custom_call" | custom-call | flops 30000001024 | bytes 3000000 | tf_op jit(solution)/shard_map/factor/pallas_call | solution.py:120
  56.6 4.2 %send_part.16 = bf16[1024,512]{1,0:T(8,128)(2,1)} custom-call(s32[1]{0:T(128)} %bitcast.9.place, bf16[256,256]{1,0:T(8,128)(2,1)S(1)} %get-tuple-element.32.hi.refs_1_, bf16[256,256]{1,0:T(8,128)(2,1)S(1)} %get-tuple-element.33.lo.refs_2_, bf16[1024,256]{1,0:T(8,128)(2,1)S(1)} %get-tuple-element.36.left, bf16[1024,15360]{1,0:T(8,128)(2,1)} %bitcast.29, ...), custom_call_target="tpu_custom_call" | custom-call | flops 268435456 | bytes 2621440 | tf_op jit(solution)/shard_map/send_part/pallas_call | solution.py:233
  67.3 4.3 %send_part.17 = bf16[1024,512]{1,0:T(8,128)(2,1)} custom-call(s32[1]{0:T(128)} %bitcast.9.place, bf16[256,256]{1,0:T(8,128)(2,1)S(1)} %get-tuple-element.32.hi.refs_1_, bf16[256,256]{1,0:T(8,128)(2,1)S(1)} %get-tuple-element.33.lo.refs_2_, bf16[1024,256]{1,0:T(8,128)(2,1)S(1)} %get-tuple-element.36.left, bf16[1024,15360]{1,0:T(8,128)(2,1)} %bitcast.30, ...), custom_call_target="tpu_custom_call" | custom-call | flops 268435456 | bytes 2621440 | tf_op jit(solution)/shard_map/send_part/pallas_call | solution.py:233
  76.6 6.0 %collective-permute-done.6.received = bf16[1024,512]{1,0:T(8,128)(2,1)S(1)} collective-permute-done((bf16[1024,512]{1,0:T(8,128)(2,1)S(1)}, bf16[1024,512]{1,0:T(8,128)(2,1)S(1)}, u32[]{:S(2)}, u32[]{:S(2)}) %collective-permute-start.6) | collective-permute-done | bytes 1048608 | tf_op jit(solution)/shard_map/ppermute | solution.py:22
  92.4 18.3 %collective-permute-done.13.received = bf16[1024,512]{1,0:T(8,128)(2,1)S(1)} collective-permute-done((bf16[1024,512]{1,0:T(8,128)(2,1)}, bf16[1024,512]{1,0:T(8,128)(2,1)S(1)}, u32[]{:S(2)}, u32[]{:S(2)}) %collective-permute-start.13) | collective-permute-done | bytes 1048608 | tf_op jit(solution)/shard_map/ppermute | solution.py:22
  116.5 20.2 %collective-permute-done.14 = bf16[80,1024]{1,0:T(8,128)(2,1)S(1)} collective-permute-done((bf16[80,1024]{1,0:T(8,128)(2,1)S(1)}, bf16[80,1024]{1,0:T(8,128)(2,1)S(1)}, u32[]{:S(2)}, u32[]{:S(2)}) %collective-permute-start.14) | collective-permute-done | bytes 163872 | tf_op jit(solution)/shard_map/ppermute | solution.py:22
  136.7 4.3 %send_part.20 = bf16[1024,512]{1,0:T(8,128)(2,1)} custom-call(s32[1]{0:T(128)} %bitcast.9.place, bf16[256,256]{1,0:T(8,128)(2,1)S(1)} %get-tuple-element.32.hi.refs_1_, bf16[256,256]{1,0:T(8,128)(2,1)S(1)} %get-tuple-element.33.lo.refs_2_, bf16[1024,256]{1,0:T(8,128)(2,1)S(1)} %get-tuple-element.36.left, bf16[1024,15360]{1,0:T(8,128)(2,1)} %bitcast.33, ...), custom_call_target="tpu_custom_call" | custom-call | flops 268435456 | bytes 2621440 | tf_op jit(solution)/shard_map/send_part/pallas_call | solution.py:233
  142.2 4.7 %merge_part.15.rest_1_ = bf16[1024,7680]{1,0:T(8,128)(2,1)} custom-call(s32[1]{0:T(128)} %bitcast.place.refs_0_, bf16[256,256]{1,0:T(8,128)(2,1)S(1)} %get-tuple-element.32.hi.refs_1_, bf16[256,256]{1,0:T(8,128)(2,1)S(1)} %get-tuple-element.33.lo.refs_2_, bf16[1024,256]{1,0:T(8,128)(2,1)S(1)} %get-tuple-element.34.left.refs_3_, ...), custom_call_target="tpu_custom_call" | custom-call | flops 1342177280 | bytes 4194304 | tf_op jit(solution)/shard_map/merge_part/pallas_call | solution.py:277
  147.0 12.3 %collective-permute-done.11.received = bf16[1024,512]{1,0:T(8,128)(2,1)} collective-permute-done((bf16[1024,512]{1,0:T(8,128)(2,1)}, bf16[1024,512]{1,0:T(8,128)(2,1)}, u32[]{:S(2)}, u32[]{:S(2)}) %collective-permute-start.11) | collective-permute-done | bytes 1048608 | tf_op jit(solution)/shard_map/ppermute | solution.py:22
  163.4 4.8 %merge_part.16.rest_1_ = bf16[1024,7680]{1,0:T(8,128)(2,1)} custom-call(s32[1]{0:T(128)} %bitcast.place.refs_0_, bf16[256,256]{1,0:T(8,128)(2,1)S(1)} %get-tuple-element.32.hi.refs_1_, bf16[256,256]{1,0:T(8,128)(2,1)S(1)} %get-tuple-element.33.lo.refs_2_, bf16[1024,256]{1,0:T(8,128)(2,1)S(1)} %get-tuple-element.34.left.refs_3_, ...), custom_call_target="tpu_custom_call", output_to_operand_aliasing={{}: (8, {})} | custom-call | flops 1342177280 | bytes 4194304 | tf_op jit(solution)/shard_map/merge_part/pallas_call | solution.py:277
  168.1 13.5 %collective-permute-done.18.received = bf16[1024,512]{1,0:T(8,128)(2,1)S(1)} collective-permute-done((bf16[1024,512]{1,0:T(8,128)(2,1)}, bf16[1024,512]{1,0:T(8,128)(2,1)S(1)}, u32[]{:S(2)}, u32[]{:S(2)}) %collective-permute-start.18) | collective-permute-done | bytes 1048608 | tf_op jit(solution)/shard_map/ppermute | solution.py:22
  182.6 5.5 %reshape.442 = f32[8192,2]{1,0:T(8,128)} reshape(f32[16,1024]{1,0:T(8,128)S(1)} %slice_convert_fusion) | data formatting | bytes 131072 | tf_op jit(solution)/shard_map/convert_element_type | solution.py:443
  194.1 4.8 %merge_part.17.rest_1_ = bf16[1024,7680]{1,0:T(8,128)(2,1)} custom-call(s32[1]{0:T(128)} %bitcast.place.refs_0_, bf16[256,256]{1,0:T(8,128)(2,1)S(1)} %get-tuple-element.32.hi.refs_1_, bf16[256,256]{1,0:T(8,128)(2,1)S(1)} %get-tuple-element.33.lo.refs_2_, bf16[1024,256]{1,0:T(8,128)(2,1)S(1)} %get-tuple-element.34.left.refs_3_, ...), custom_call_target="tpu_custom_call", output_to_operand_aliasing={{}: (8, {})} | custom-call | flops 1342177280 | bytes 4194304 | tf_op jit(solution)/shard_map/merge_part/pallas_call | solution.py:277
  198.9 5.2 %merge_part.18.rest_1_ = bf16[1024,7680]{1,0:T(8,128)(2,1)} custom-call(s32[1]{0:T(128)} %bitcast.place.refs_0_, bf16[256,256]{1,0:T(8,128)(2,1)S(1)} %get-tuple-element.32.hi.refs_1_, bf16[256,256]{1,0:T(8,128)(2,1)S(1)} %get-tuple-element.33.lo.refs_2_, bf16[1024,256]{1,0:T(8,128)(2,1)S(1)} %get-tuple-element.34.left.refs_3_, ...), custom_call_target="tpu_custom_call", output_to_operand_aliasing={{}: (8, {})} | custom-call | flops 1342177280 | bytes 4194304 | tf_op jit(solution)/shard_map/merge_part/pallas_call | solution.py:277
  204.1 7.5 %all_gather.6 = bf16[1024,256]{1,0:T(8,128)(2,1)S(1)} all-gather(bf16[1024,128]{1,0:T(8,128)(2,1)S(1)} %copy-done.25), channel_id=1, replica_groups=mesh['cube'=4,'row'=4,'col'=2] {'col'}, dimensions={1}, use_global_device_ids=true | all-gather | bytes 786432 | tf_op jit(solution)/shard_map/all_gather | solution.py:449
  216.6 4.7 %merge_part.19.refs_10_ = bf16[1024,7680]{1,0:T(8,128)(2,1)} custom-call(s32[1]{0:T(128)} %bitcast.place.refs_0_, bf16[256,256]{1,0:T(8,128)(2,1)S(1)} %get-tuple-element.32.hi.refs_1_, bf16[256,256]{1,0:T(8,128)(2,1)S(1)} %get-tuple-element.33.lo.refs_2_, bf16[1024,256]{1,0:T(8,128)(2,1)S(1)} %get-tuple-element.34.left.refs_3_, ...), custom_call_target="tpu_custom_call", output_to_operand_aliasing={{}: (8, {})} | custom-call | flops 1342177280 | bytes 4194304 | tf_op jit(solution)/shard_map/merge_part/pallas_call | solution.py:277
  221.3 6.7 %all_gather.7.refs_8_ = bf16[256,1024]{1,0:T(8,128)(2,1)S(1)} all-gather(bf16[64,1024]{1,0:T(8,128)(2,1)S(1)} %slice-done), channel_id=1, replica_groups=mesh['cube'=4,'row'=4,'col'=2] {'row'}, dimensions={0}, use_global_device_ids=true | all-gather | bytes 655360 | tf_op jit(solution)/shard_map/all_gather | solution.py:453
  231.5 5.3 %merge_part.20.refs_10_ = bf16[1024,7680]{1,0:T(8,128)(2,1)} custom-call(s32[1]{0:T(128)} %bitcast.place.refs_0_, bf16[256,256]{1,0:T(8,128)(2,1)S(1)} %get-tuple-element.32.hi.refs_1_, bf16[256,256]{1,0:T(8,128)(2,1)S(1)} %get-tuple-element.33.lo.refs_2_, bf16[1024,256]{1,0:T(8,128)(2,1)S(1)} %get-tuple-element.34.left.refs_3_, ...), custom_call_target="tpu_custom_call", output_to_operand_aliasing={{}: (10, {})} | custom-call | flops 1342177280 | bytes 4194304 | tf_op jit(solution)/shard_map/merge_part/pallas_call | solution.py:277
  236.8 5.3 %merge_part.21.rest_1_ = bf16[1024,7680]{1,0:T(8,128)(2,1)} custom-call(s32[1]{0:T(128)} %bitcast.place.refs_0_, bf16[256,256]{1,0:T(8,128)(2,1)S(1)} %get-tuple-element.32.hi.refs_1_, bf16[256,256]{1,0:T(8,128)(2,1)S(1)} %get-tuple-element.33.lo.refs_2_, bf16[1024,256]{1,0:T(8,128)(2,1)S(1)} %get-tuple-element.34.left.refs_3_, ...), custom_call_target="tpu_custom_call", output_to_operand_aliasing={{}: (10, {})} | custom-call | flops 1342177280 | bytes 4194304 | tf_op jit(solution)/shard_map/merge_part/pallas_call | solution.py:277
  242.1 6.9 %collective-permute-done.21.received = bf16[1024,512]{1,0:T(8,128)(2,1)S(1)} collective-permute-done((bf16[1024,512]{1,0:T(8,128)(2,1)S(1)}, bf16[1024,512]{1,0:T(8,128)(2,1)S(1)}, u32[]{:S(2)}, u32[]{:S(2)}) %collective-permute-start.21) | collective-permute-done | bytes 1048608 | tf_op jit(solution)/shard_map/ppermute | solution.py:22
  253.1 5.1 %merge_part.22.rest_1_ = bf16[1024,7680]{1,0:T(8,128)(2,1)} custom-call(s32[1]{0:T(128)} %bitcast.place.refs_0_, bf16[256,256]{1,0:T(8,128)(2,1)S(1)} %get-tuple-element.32.hi.refs_1_, bf16[256,256]{1,0:T(8,128)(2,1)S(1)} %get-tuple-element.33.lo.refs_2_, bf16[1024,256]{1,0:T(8,128)(2,1)S(1)} %get-tuple-element.34.left.refs_3_, ...), custom_call_target="tpu_custom_call", output_to_operand_aliasing={{}: (8, {})} | custom-call | flops 1342177280 | bytes 4194304 | tf_op jit(solution)/shard_map/merge_part/pallas_call | solution.py:277
  258.2 5.0 %merge_part.23.rest_1_ = bf16[1024,7680]{1,0:T(8,128)(2,1)} custom-call(s32[1]{0:T(128)} %bitcast.place.refs_0_, bf16[256,256]{1,0:T(8,128)(2,1)S(1)} %get-tuple-element.32.hi.refs_1_, bf16[256,256]{1,0:T(8,128)(2,1)S(1)} %get-tuple-element.33.lo.refs_2_, bf16[1024,256]{1,0:T(8,128)(2,1)S(1)} %get-tuple-element.34.left.refs_3_, ...), custom_call_target="tpu_custom_call", output_to_operand_aliasing={{}: (8, {})} | custom-call | flops 1342177280 | bytes 4194304 | tf_op jit(solution)/shard_map/merge_part/pallas_call | solution.py:277
  263.2 8.3 %collective-permute-done.20.received = bf16[1024,512]{1,0:T(8,128)(2,1)S(1)} collective-permute-done((bf16[1024,512]{1,0:T(8,128)(2,1)S(1)}, bf16[1024,512]{1,0:T(8,128)(2,1)S(1)}, u32[]{:S(2)}, u32[]{:S(2)}) %collective-permute-start.20) | collective-permute-done | bytes 1048608 | tf_op jit(solution)/shard_map/ppermute | solution.py:22
  275.4 4.8 %merge_part.24.rest_1_ = bf16[1024,7680]{1,0:T(8,128)(2,1)} custom-call(s32[1]{0:T(128)} %bitcast.place.refs_0_, bf16[256,256]{1,0:T(8,128)(2,1)S(1)} %get-tuple-element.32.hi.refs_1_, bf16[256,256]{1,0:T(8,128)(2,1)S(1)} %get-tuple-element.33.lo.refs_2_, bf16[1024,256]{1,0:T(8,128)(2,1)S(1)} %get-tuple-element.34.left.refs_3_, ...), custom_call_target="tpu_custom_call", output_to_operand_aliasing={{}: (8, {})} | custom-call | flops 1342177280 | bytes 4194304 | tf_op jit(solution)/shard_map/merge_part/pallas_call | solution.py:277
  280.2 4.7 %merge_part.25.rest_1_ = bf16[1024,7680]{1,0:T(8,128)(2,1)} custom-call(s32[1]{0:T(128)} %bitcast.place.refs_0_, bf16[256,256]{1,0:T(8,128)(2,1)S(1)} %get-tuple-element.32.hi.refs_1_, bf16[256,256]{1,0:T(8,128)(2,1)S(1)} %get-tuple-element.33.lo.refs_2_, bf16[1024,256]{1,0:T(8,128)(2,1)S(1)} %get-tuple-element.34.left.refs_3_, ...), custom_call_target="tpu_custom_call", output_to_operand_aliasing={{}: (8, {})} | custom-call | flops 1342177280 | bytes 4194304 | tf_op jit(solution)/shard_map/merge_part/pallas_call | solution.py:277
  284.9 9.1 %collective-permute-done.19.received = bf16[1024,512]{1,0:T(8,128)(2,1)S(1)} collective-permute-done((bf16[1024,512]{1,0:T(8,128)(2,1)S(1)}, bf16[1024,512]{1,0:T(8,128)(2,1)S(1)}, u32[]{:S(2)}, u32[]{:S(2)}) %collective-permute-start.19) | collective-permute-done | bytes 1048608 | tf_op jit(solution)/shard_map/ppermute | solution.py:22
  296.8 19.7 %collective-permute-done.24.received = bf16[1024,512]{1,0:T(8,128)(2,1)S(1)} collective-permute-done((bf16[1024,512]{1,0:T(8,128)(2,1)}, bf16[1024,512]{1,0:T(8,128)(2,1)S(1)}, u32[]{:S(2)}, u32[]{:S(2)}) %collective-permute-start.24) | collective-permute-done | bytes 1048608 | tf_op jit(solution)/shard_map/ppermute | solution.py:22
  320.1 4.8 %merge_part.26.rest_1_ = bf16[1024,7680]{1,0:T(8,128)(2,1)} custom-call(s32[1]{0:T(128)} %bitcast.place.refs_0_, bf16[256,256]{1,0:T(8,128)(2,1)S(1)} %get-tuple-element.32.hi.refs_1_, bf16[256,256]{1,0:T(8,128)(2,1)S(1)} %get-tuple-element.33.lo.refs_2_, bf16[1024,256]{1,0:T(8,128)(2,1)S(1)} %get-tuple-element.34.left.refs_3_, ...), custom_call_target="tpu_custom_call", output_to_operand_aliasing={{}: (8, {})} | custom-call | flops 1342177280 | bytes 4194304 | tf_op jit(solution)/shard_map/merge_part/pallas_call | solution.py:277
  324.8 4.7 %merge_part.27.rest_1_ = bf16[1024,7680]{1,0:T(8,128)(2,1)} custom-call(s32[1]{0:T(128)} %bitcast.place.refs_0_, bf16[256,256]{1,0:T(8,128)(2,1)S(1)} %get-tuple-element.32.hi.refs_1_, bf16[256,256]{1,0:T(8,128)(2,1)S(1)} %get-tuple-element.33.lo.refs_2_, bf16[1024,256]{1,0:T(8,128)(2,1)S(1)} %get-tuple-element.34.left.refs_3_, ...), custom_call_target="tpu_custom_call", output_to_operand_aliasing={{}: (8, {})} | custom-call | flops 1342177280 | bytes 4194304 | tf_op jit(solution)/shard_map/merge_part/pallas_call | solution.py:277
  329.6 9.4 %collective-permute-done.23.received = bf16[1024,512]{1,0:T(8,128)(2,1)S(1)} collective-permute-done((bf16[1024,512]{1,0:T(8,128)(2,1)S(1)}, bf16[1024,512]{1,0:T(8,128)(2,1)S(1)}, u32[]{:S(2)}, u32[]{:S(2)}) %collective-permute-start.23) | collective-permute-done | bytes 1048608 | tf_op jit(solution)/shard_map/ppermute | solution.py:22
  338.9 4.7 %merge_part.28.rest_1_ = bf16[1024,7680]{1,0:T(8,128)(2,1)} custom-call(s32[1]{0:T(128)} %bitcast.place.refs_0_, bf16[256,256]{1,0:T(8,128)(2,1)S(1)} %get-tuple-element.32.hi.refs_1_, bf16[256,256]{1,0:T(8,128)(2,1)S(1)} %get-tuple-element.33.lo.refs_2_, bf16[1024,256]{1,0:T(8,128)(2,1)S(1)} %get-tuple-element.34.left.refs_3_, ...), custom_call_target="tpu_custom_call", output_to_operand_aliasing={{}: (8, {})} | custom-call | flops 1342177280 | bytes 4194304 | tf_op jit(solution)/shard_map/merge_part/pallas_call | solution.py:277
  343.7 6.5 %collective-permute-done.22.received = bf16[1024,256]{1,0:T(8,128)(2,1)S(1)} collective-permute-done((bf16[1024,256]{1,0:T(8,128)(2,1)S(1)}, bf16[1024,256]{1,0:T(8,128)(2,1)S(1)}, u32[]{:S(2)}, u32[]{:S(2)}) %collective-permute-start.22) | collective-permute-done | bytes 524320 | tf_op jit(solution)/shard_map/ppermute | solution.py:22
  (162 shorter events, 103.4 us)
Async XLA Ops:
  3.2 64.0 %collective-permute-start.7 = (bf16[1024,1024]{1,0:T(8,128)(2,1)}, bf16[1024,1024]{1,0:T(8,128)(2,1)}, u32[]{:S(2)}, u32[]{:S(2)}) collective-permute-start(bf16[1024,1024]{1,0:T(8,128)(2,1)} %dynamic-slice_bitcast_fusion), channel_id=1, source_target_pairs={{0,8},{8,0},{16,24},{24,16},{1,9},{9,1},{17,25},{25,17},{2,10},{10... | collective-permute-start | bytes 6291464 | tf_op jit(solution)/shard_map/ppermute | solution.py:22
  6.3 8.4 %collective-permute-start = (f32[32,256]{1,0:T(8,128)S(1)}, f32[32,256]{1,0:T(8,128)S(1)}, u32[]{:S(2)}, u32[]{:S(2)}) collective-permute-start(f32[32,256]{1,0:T(8,128)S(1)} %bitcast.58), channel_id=1, source_target_pairs={{0,4},{1,5},{2,6},{3,7},{4,0},{5,1},{6,2},{7,3},{8,12},{9,13},{10,... | collective-permute-start | bytes 98312 | tf_op jit(solution)/shard_map/ppermute | solution.py:22
  7.8 17.5 %collective-permute-start.3 = (bf16[1024,128]{1,0:T(8,128)(2,1)}, bf16[1024,128]{1,0:T(8,128)(2,1)}, u32[]{:S(2)}, u32[]{:S(2)}) collective-permute-start(bf16[1024,128]{1,0:T(8,128)(2,1)} %bitcast.4), channel_id=1, source_target_pairs={{0,1},{1,0},{2,3},{3,2},{4,5},{5,4},{6,7},{7,6},{8,9},{9,8},{10,11... | collective-permute-start | bytes 786440 | tf_op jit(solution)/shard_map/ppermute | solution.py:22
  9.3 15.4 %collective-permute-start.4 = (bf16[64,2048]{1,0:T(8,128)(2,1)S(1)}, bf16[64,2048]{1,0:T(8,128)(2,1)S(1)}, u32[]{:S(2)}, u32[]{:S(2)}) collective-permute-start(bf16[64,2048]{1,0:T(8,128)(2,1)S(1)} %dynamic-slice_bitcast_fusion.3), channel_id=1, source_target_pairs={{0,4},{2,6},{4,0},{6,2},{1,5},{3,7},{5,1},{7,3},{8,12},{10,14},{12... | collective-permute-start | bytes 786440 | tf_op jit(solution)/shard_map/ppermute | solution.py:22
  11.0 49.8 %collective-permute-start.8 = (bf16[64,13312]{1,0:T(8,128)(2,1)S(1)}, bf16[64,13312]{1,0:T(8,128)(2,1)}, u32[]{:S(2)}, u32[]{:S(2)}) collective-permute-start(bf16[64,13312]{1,0:T(8,128)(2,1)S(1)} %pad_maximum_fusion.1), channel_id=1, source_target_pairs={{0,4},{2,6},{4,0},{6,2},{1,5},{3,7},{5,1},{7,3},{8,12},{10,14},{12... | collective-permute-start | bytes 5111816 | tf_op jit(solution)/shard_map/ppermute | solution.py:22
  15.3 4.6 %collective-permute-start.1 = (f32[64,256]{1,0:T(8,128)}, f32[64,256]{1,0:T(8,128)}, u32[]{:S(2)}, u32[]{:S(2)}) collective-permute-start(f32[64,256]{1,0:T(8,128)} %pad_maximum_fusion.9), channel_id=1, source_target_pairs={{0,1},{1,0},{2,3},{3,2},{4,5},{5,4},{6,7},{7,6},{8,9},{9,8},{10,11... | collective-permute-start | bytes 196616 | tf_op jit(solution)/shard_map/ppermute | solution.py:22
  21.4 2.4 collective-permute-start.2
  24.7 28.7 %collective-permute-start.5 = (bf16[128,2048]{1,0:T(8,128)(2,1)S(1)}, bf16[128,2048]{1,0:T(8,128)(2,1)S(1)}, u32[]{:S(2)}, u32[]{:S(2)}) collective-permute-start(bf16[128,2048]{1,0:T(8,128)(2,1)S(1)} %pad_maximum_fusion.5), channel_id=1, source_target_pairs={{0,2},{2,0},{4,6},{6,4},{1,3},{3,1},{5,7},{7,5},{8,10},{10,8},{12,... | collective-permute-start | bytes 1572872 | tf_op jit(solution)/shard_map/ppermute | solution.py:22
  26.5 26.9 %copy-start.18 = (bf16[64,2048]{1,0:T(8,128)(2,1)S(1)}, bf16[64,2048]{1,0:T(8,128)(2,1)}, u32[]{:S(2)}) copy-start(bf16[64,2048]{1,0:T(8,128)(2,1)} %copy-done.17) | copy-start | bytes 786436
  26.5 26.9 %copy-start.20 = (bf16[64,2048]{1,0:T(8,128)(2,1)S(1)}, bf16[64,2048]{1,0:T(8,128)(2,1)}, u32[]{:S(2)}) copy-start(bf16[64,2048]{1,0:T(8,128)(2,1)} %copy-done.19) | copy-start | bytes 786436
  56.5 26.1 %collective-permute-start.6 = (bf16[1024,512]{1,0:T(8,128)(2,1)S(1)}, bf16[1024,512]{1,0:T(8,128)(2,1)S(1)}, u32[]{:S(2)}, u32[]{:S(2)}) collective-permute-start(bf16[1024,512]{1,0:T(8,128)(2,1)S(1)} %send_part.15), channel_id=1, source_target_pairs={{0,8},{8,0},{16,24},{24,16},{1,9},{9,1},{17,25},{25,17},{2,10},{10... | collective-permute-start | bytes 3145736 | tf_op jit(solution)/shard_map/ppermute | solution.py:22
  62.1 5.1 %collective-permute-start.9 = (bf16[128,5632]{1,0:T(8,128)(2,1)S(1)}, bf16[128,5632]{1,0:T(8,128)(2,1)S(1)}, u32[]{:S(2)}, u32[]{:S(2)}) collective-permute-start(bf16[128,5632]{1,0:T(8,128)(2,1)S(1)} %pad_maximum_fusion.2), channel_id=1, source_target_pairs={{0,2},{2,0},{4,6},{6,4},{1,3},{3,1},{5,7},{7,5},{8,10},{10,8},{12,... | collective-permute-start | bytes 4325384 | tf_op jit(solution)/shard_map/ppermute | solution.py:22
  67.3 92.0 %copy-start.4 = (bf16[256,5632]{1,0:T(8,128)(2,1)}, bf16[256,5632]{1,0:T(8,128)(2,1)S(1)}, u32[]{:S(2)}) copy-start(bf16[256,5632]{1,0:T(8,128)(2,1)S(1)} %constant_dynamic-update-slice_fusion.rest_0_) | copy-start | bytes 8650756
  71.6 43.2 %collective-permute-start.15 = (bf16[128,7680]{1,0:T(8,128)(2,1)}, bf16[128,7680]{1,0:T(8,128)(2,1)}, u32[]{:S(2)}, u32[]{:S(2)}) collective-permute-start(bf16[128,7680]{1,0:T(8,128)(2,1)} %pad_maximum_fusion), channel_id=1, source_target_pairs={{0,2},{2,0},{4,6},{6,4},{1,3},{3,1},{5,7},{7,5},{8,10},{10,8},{12,... | collective-permute-start | bytes 5898248 | tf_op jit(solution)/shard_map/ppermute | solution.py:22
  72.1 16.2 %collective-permute-start.10 = (bf16[1024,128]{1,0:T(8,128)(2,1)S(1)}, bf16[1024,128]{1,0:T(8,128)(2,1)S(1)}, u32[]{:S(2)}, u32[]{:S(2)}) collective-permute-start(bf16[1024,128]{1,0:T(8,128)(2,1)S(1)} %constant_dynamic-slice_fusion), channel_id=1, source_target_pairs={{0,8},{8,0},{16,24},{24,16},{1,9},{9,1},{17,25},{25,17},{2,10},{10... | collective-permute-start | bytes 786440 | tf_op jit(solution)/shard_map/ppermute | solution.py:22
  74.5 36.2 %collective-permute-start.13 = (bf16[1024,512]{1,0:T(8,128)(2,1)}, bf16[1024,512]{1,0:T(8,128)(2,1)S(1)}, u32[]{:S(2)}, u32[]{:S(2)}) collective-permute-start(bf16[1024,512]{1,0:T(8,128)(2,1)} %send_part.16), channel_id=1, source_target_pairs={{0,8},{8,0},{16,24},{24,16},{1,9},{9,1},{17,25},{25,17},{2,10},{10... | collective-permute-start | bytes 3145736 | tf_op jit(solution)/shard_map/ppermute | solution.py:22
  74.7 62.0 %collective-permute-start.12 = (bf16[1024,512]{1,0:T(8,128)(2,1)}, bf16[1024,512]{1,0:T(8,128)(2,1)S(1)}, u32[]{:S(2)}, u32[]{:S(2)}) collective-permute-start(bf16[1024,512]{1,0:T(8,128)(2,1)} %send_part.17), channel_id=1, source_target_pairs={{0,8},{8,0},{16,24},{24,16},{1,9},{9,1},{17,25},{25,17},{2,10},{10... | collective-permute-start | bytes 3145736 | tf_op jit(solution)/shard_map/ppermute | solution.py:22
  84.9 51.7 %collective-permute-start.14 = (bf16[80,1024]{1,0:T(8,128)(2,1)S(1)}, bf16[80,1024]{1,0:T(8,128)(2,1)S(1)}, u32[]{:S(2)}, u32[]{:S(2)}) collective-permute-start(bf16[80,1024]{1,0:T(8,128)(2,1)S(1)} %pad_maximum_fusion.7), channel_id=1, source_target_pairs={{0,8},{8,0},{16,24},{24,16},{1,9},{9,1},{17,25},{25,17},{2,10},{10... | collective-permute-start | bytes 491528 | tf_op jit(solution)/shard_map/ppermute | solution.py:22
  92.4 66.8 %collective-permute-start.11 = (bf16[1024,512]{1,0:T(8,128)(2,1)}, bf16[1024,512]{1,0:T(8,128)(2,1)}, u32[]{:S(2)}, u32[]{:S(2)}) collective-permute-start(bf16[1024,512]{1,0:T(8,128)(2,1)} %send_part.18), channel_id=1, source_target_pairs={{0,8},{8,0},{16,24},{24,16},{1,9},{9,1},{17,25},{25,17},{2,10},{10... | collective-permute-start | bytes 3145736 | tf_op jit(solution)/shard_map/ppermute | solution.py:22
  114.8 66.9 %collective-permute-start.18 = (bf16[1024,512]{1,0:T(8,128)(2,1)}, bf16[1024,512]{1,0:T(8,128)(2,1)S(1)}, u32[]{:S(2)}, u32[]{:S(2)}) collective-permute-start(bf16[1024,512]{1,0:T(8,128)(2,1)} %send_part.19), channel_id=1, source_target_pairs={{0,8},{8,0},{16,24},{24,16},{1,9},{9,1},{17,25},{25,17},{2,10},{10... | collective-permute-start | bytes 3145736 | tf_op jit(solution)/shard_map/ppermute | solution.py:22
  116.5 24.5 %copy-start.2 = (bf16[256,7680]{1,0:T(8,128)(2,1)}, bf16[256,7680]{1,0:T(8,128)(2,1)S(1)}, u32[]{:S(2)}) copy-start(bf16[256,7680]{1,0:T(8,128)(2,1)S(1)} %constant_dynamic-update-slice_fusion.2.rest_0_.refs_9_) | copy-start | bytes 11796484
  136.7 26.7 %copy-start.21 = (bf16[80,1024]{1,0:T(8,128)(2,1)}, bf16[80,1024]{1,0:T(8,128)(2,1)S(1)}, u32[]{:S(2)}) copy-start(bf16[80,1024]{1,0:T(8,128)(2,1)S(1)} %collective-permute-done.14) | copy-start | bytes 491524
  141.0 70.8 %collective-permute-start.17 = (bf16[1024,512]{1,0:T(8,128)(2,1)}, bf16[1024,512]{1,0:T(8,128)(2,1)}, u32[]{:S(2)}, u32[]{:S(2)}) collective-permute-start(bf16[1024,512]{1,0:T(8,128)(2,1)} %send_part.20), channel_id=1, source_target_pairs={{0,8},{8,0},{16,24},{24,16},{1,9},{9,1},{17,25},{25,17},{2,10},{10... | collective-permute-start | bytes 3145736 | tf_op jit(solution)/shard_map/ppermute | solution.py:22
  163.4 64.7 %collective-permute-start.16 = (bf16[1024,512]{1,0:T(8,128)(2,1)}, bf16[1024,512]{1,0:T(8,128)(2,1)}, u32[]{:S(2)}, u32[]{:S(2)}) collective-permute-start(bf16[1024,512]{1,0:T(8,128)(2,1)} %send_part.21), channel_id=1, source_target_pairs={{0,8},{8,0},{16,24},{24,16},{1,9},{9,1},{17,25},{25,17},{2,10},{10... | collective-permute-start | bytes 3145736 | tf_op jit(solution)/shard_map/ppermute | solution.py:22
  163.4 18.3 %copy-start.22 = (f32[16,1024]{1,0:T(8,128)}, f32[16,1024]{1,0:T(8,128)S(1)}, u32[]{:S(2)}) copy-start(f32[16,1024]{1,0:T(8,128)S(1)} %slice_convert_fusion) | copy-start | bytes 196612
  193.1 56.0 %collective-permute-start.21 = (bf16[1024,512]{1,0:T(8,128)(2,1)S(1)}, bf16[1024,512]{1,0:T(8,128)(2,1)S(1)}, u32[]{:S(2)}, u32[]{:S(2)}) collective-permute-start(bf16[1024,512]{1,0:T(8,128)(2,1)S(1)} %send_part.22), channel_id=1, source_target_pairs={{0,8},{8,0},{16,24},{24,16},{1,9},{9,1},{17,25},{25,17},{2,10},{10... | collective-permute-start | bytes 3145736 | tf_op jit(solution)/shard_map/ppermute | solution.py:22
  214.9 56.6 %collective-permute-start.20 = (bf16[1024,512]{1,0:T(8,128)(2,1)S(1)}, bf16[1024,512]{1,0:T(8,128)(2,1)S(1)}, u32[]{:S(2)}, u32[]{:S(2)}) collective-permute-start(bf16[1024,512]{1,0:T(8,128)(2,1)S(1)} %send_part.23), channel_id=1, source_target_pairs={{0,8},{8,0},{16,24},{24,16},{1,9},{9,1},{17,25},{25,17},{2,10},{10... | collective-permute-start | bytes 3145736 | tf_op jit(solution)/shard_map/ppermute | solution.py:22
  231.0 63.0 %collective-permute-start.19 = (bf16[1024,512]{1,0:T(8,128)(2,1)S(1)}, bf16[1024,512]{1,0:T(8,128)(2,1)S(1)}, u32[]{:S(2)}, u32[]{:S(2)}) collective-permute-start(bf16[1024,512]{1,0:T(8,128)(2,1)S(1)} %send_part.24), channel_id=1, source_target_pairs={{0,8},{8,0},{16,24},{24,16},{1,9},{9,1},{17,25},{25,17},{2,10},{10... | collective-permute-start | bytes 3145736 | tf_op jit(solution)/shard_map/ppermute | solution.py:22
  253.1 63.3 %collective-permute-start.24 = (bf16[1024,512]{1,0:T(8,128)(2,1)}, bf16[1024,512]{1,0:T(8,128)(2,1)S(1)}, u32[]{:S(2)}, u32[]{:S(2)}) collective-permute-start(bf16[1024,512]{1,0:T(8,128)(2,1)} %send_part.25), channel_id=1, source_target_pairs={{0,8},{8,0},{16,24},{24,16},{1,9},{9,1},{17,25},{25,17},{2,10},{10... | collective-permute-start | bytes 3145736 | tf_op jit(solution)/shard_map/ppermute | solution.py:22
  274.5 64.4 %collective-permute-start.23 = (bf16[1024,512]{1,0:T(8,128)(2,1)S(1)}, bf16[1024,512]{1,0:T(8,128)(2,1)S(1)}, u32[]{:S(2)}, u32[]{:S(2)}) collective-permute-start(bf16[1024,512]{1,0:T(8,128)(2,1)S(1)} %send_part.26), channel_id=1, source_target_pairs={{0,8},{8,0},{16,24},{24,16},{1,9},{9,1},{17,25},{25,17},{2,10},{10... | collective-permute-start | bytes 3145736 | tf_op jit(solution)/shard_map/ppermute | solution.py:22
  296.7 53.5 %collective-permute-start.22 = (bf16[1024,256]{1,0:T(8,128)(2,1)S(1)}, bf16[1024,256]{1,0:T(8,128)(2,1)S(1)}, u32[]{:S(2)}, u32[]{:S(2)}) collective-permute-start(bf16[1024,256]{1,0:T(8,128)(2,1)S(1)} %send_part.27), channel_id=1, source_target_pairs={{0,8},{8,0},{16,24},{24,16},{1,9},{9,1},{17,25},{25,17},{2,10},{10... | collective-permute-start | bytes 1572872 | tf_op jit(solution)/shard_map/ppermute | solution.py:22
  320.0 40.5 %collective-permute-start.25 = (bf16[1024,256]{1,0:T(8,128)(2,1)S(1)}, bf16[1024,256]{1,0:T(8,128)(2,1)S(1)}, u32[]{:S(2)}, u32[]{:S(2)}) collective-permute-start(bf16[1024,256]{1,0:T(8,128)(2,1)S(1)} %fusion.3), channel_id=1, source_target_pairs={{0,8},{8,0},{16,24},{24,16},{1,9},{9,1},{17,25},{25,17},{2,10},{10... | collective-permute-start | bytes 1572872 | tf_op jit(solution)/shard_map/ppermute | solution.py:22
  (25 other events, 137.0 us)

commit v7 on v6

--- a/solution.py
+++ b/solution.py
@@ -75,16 +75,17 @@
 
 
 def factor_kernel(
-    block, order_of_diag, order_of_upper, order_of_lower, panel, mask, hi, lo, plain, sent, kept
+    place, mask, first, second, orders, left_panel, right_panel, hi, lo, plain, sent, kept
 ):
-    size = block.shape[0]
+    size = first.shape[1]
     half = size // 2
-    lane = lax.broadcasted_iota(jnp.int32, (size, size), 1)
-
-    def chosen(order):
-        return jnp.where(order[...] == lane, 1.0, 0.0)
-
-    pivoted = exact(chosen(order_of_diag), block[...])
+    block = jnp.concatenate([first[...], second[...]], axis=0)
+    row = lax.broadcasted_iota(jnp.int32, (size, size), 0)
+
+    def chosen(number):
+        return jnp.where(orders[number : number + 1, :] == row, 1.0, 0.0)
+
+    pivoted = exact(chosen(0).T, block)
     lower_one, upper_one = inverses(pivoted[:half, :half])
     lower_side = exact(pivoted[half:, :half], upper_one)
     upper_side = exact(lower_one, pivoted[:half, half:])
@@ -99,26 +100,33 @@
     upper_inv = jnp.concatenate(
         [jnp.concatenate([upper_one, corner_upper], 1), jnp.concatenate([zero, upper_two], 1)], 0
     )
-    hi[...], lo[...] = split(exact(lower_inv, chosen(order_of_upper)))
-    row = lax.broadcasted_iota(jnp.int32, (size, size), 0)
-    in_order = jnp.where(order_of_lower[...] == row, 1.0, 0.0)
-    upper_hi, upper_lo = split(exact(in_order, upper_inv))
-    for start in range(0, panel.shape[0], size):
-        rows = slice(start, start + size)
-        part = panel[rows, :]
-        result = fast(part, upper_hi) + fast(part, upper_lo)
-        plain[rows, :] = result.astype(jnp.bfloat16)
-        result = result.astype(jnp.bfloat16).astype(jnp.float32)
-        sent[rows, :] = (result * mask[rows, 0:1]).astype(jnp.bfloat16)
-        kept[rows, :] = (result * mask[rows, 1:2]).astype(jnp.bfloat16)
-
-
-def factor(block, orders, panel, mask):
-    size = block.shape[0]
-    rows = panel.shape[0]
+    hi[...], lo[...] = split(exact(lower_inv, chosen(1).T))
+    upper_hi, upper_lo = split(exact(chosen(2), upper_inv))
+    rows = left_panel.shape[0]
+    block_rows = rows // mask.shape[0]
+    for start in range(0, rows, size):
+        part = jnp.concatenate(
+            [left_panel[start : start + size, :], right_panel[start : start + size, :]], axis=1
+        )
+        result = (fast(part, upper_hi) + fast(part, upper_lo)).astype(jnp.bfloat16)
+        plain[start : start + size, :] = result
+        result = result.astype(jnp.float32)
+        for at in range(start, start + size, block_rows):
+            piece = result[at - start : at - start + block_rows]
+            number = at // block_rows
+            sent[at : at + block_rows, :] = (piece * mask[number, place[0]].astype(jnp.float32)).astype(jnp.bfloat16)
+            kept[at : at + block_rows, :] = (piece * mask[number, 1 - place[0]].astype(jnp.float32)).astype(jnp.bfloat16)
+
+
+def factor(place, mask, first, second, orders, left_panel, right_panel):
+    size = first.shape[1]
+    rows = left_panel.shape[0]
     half_type = jnp.bfloat16
+    scalars = pl.BlockSpec(memory_space=pltpu.SMEM)
+    arrays = pl.BlockSpec(memory_space=pltpu.VMEM)
     return pl.pallas_call(
         factor_kernel,
+        in_specs=[scalars] * 2 + [arrays] * 5,
         out_shape=(
             jax.ShapeDtypeStruct((size, size), half_type),
             jax.ShapeDtypeStruct((size, size), half_type),
@@ -129,7 +137,7 @@
         compiler_params=pltpu.CompilerParams(vmem_limit_bytes=VMEM_LIMIT),
         cost_estimate=pl.CostEstimate(flops=30_000_000_000, bytes_accessed=3_000_000, transcendentals=0),
         name="factor",
-    )(block, *orders, panel, mask)
+    )(place, mask, first, second, orders, left_panel, right_panel)
 
 
 def panel_tile(hi, lo, pieces):
@@ -141,19 +149,17 @@
     out[...] = source[...]
 
 
-def take_raw(place, trailing, end):
+def take_raw(place, trailing, end, width):
     rows, columns = trailing.shape
-    step_rows = rows // 8
-    half_blocks = columns // 2 // end
-    if columns // 2 % end:
-        return lax.dynamic_slice_in_dim(trailing, place[0] * (columns // 2), end, 1)
+    step_rows = rows // 4
+    half_blocks = columns // 2 // width
     return pl.pallas_call(
         copy_kernel,
         grid_spec=pltpu.PrefetchScalarGridSpec(
             num_scalar_prefetch=1,
-            grid=(8,),
-            in_specs=[pl.BlockSpec((step_rows, end), lambda i, place: (i, place[0] * half_blocks))],
-            out_specs=pl.BlockSpec((step_rows, end), lambda i, place: (i, 0)),
+            grid=(4, end // width),
+            in_specs=[pl.BlockSpec((step_rows, width), lambda i, j, place: (i, place[0] * half_blocks + j))],
+            out_specs=pl.BlockSpec((step_rows, width), lambda i, j, place: (i, j)),
         ),
         out_shape=jax.ShapeDtypeStruct((rows, end), trailing.dtype),
         compiler_params=pltpu.CompilerParams(vmem_limit_bytes=VMEM_LIMIT),
@@ -326,6 +332,13 @@
     return block
 
 
+def halves(block, axis, dimension):
+    steps = len(bits_of(axis))
+    for step in range(steps - 1):
+        block = next_doubled(block, axis, dimension, step)
+    return block, partner(block, axis, bits_of(axis)[steps - 1])
+
+
 def next_doubled(block, axis, dimension, step):
     return jnp.concatenate([block, partner(block, axis, bits_of(axis)[step])], axis=dimension)
 
@@ -354,22 +367,20 @@
     kept_place = parity.astype(jnp.int32).reshape(1)
     raw_end = RAW * width
 
-    raw = take_raw(sent_place, trailing, raw_end)
+    raw = take_raw(sent_place, trailing, raw_end, width)
     raw_received = partner(raw, "cube", 1)
 
-    whole_block = doubled(after(diag_block, raw), ("row", "col"), 0)
-    panel = doubled(lower_in, "col", 1)
-    order = pivot_order[0][:, None]
+    diag_halves = halves(after(diag_block, raw), ("row", "col"), 0)
+    panel_halves = halves(lower_in, "col", 1)
+    order = pivot_order[0]
     every = jnp.arange(size, dtype=jnp.int32)
-    in_col_order = place_of(every, lower_in.shape[1], "col")
-    orders = (
+    orders = jnp.stack([
         place_of(order, diag_block.shape[0], ("row", "col")),
         place_of(order, upper_in.shape[0], "row"),
-        in_col_order[None, :],
-    )
+        place_of(every, lower_in.shape[1], "col"),
+    ])
     block_rows = rows // block_mask.shape[1]
-    flags = block_mask[0].astype(jnp.float32)
-    flags = jnp.repeat(jnp.where(parity == 0, flags[:, ::-1], flags), block_rows, axis=0)
+
     def columns_of(place, first, last):
         return lax.dynamic_slice_in_dim(upper_in, place * half + first, last - first, 1)
 
@@ -380,17 +391,17 @@
     late = jnp.concatenate([late, rest[:, : half - cut]], axis=0)
     kept_upper = jnp.concatenate([kept_upper, rest[:, half - cut :]], axis=0)
 
-    hi, lo, plain_left, sent_left, kept_left = factor(whole_block, orders, panel, flags)
+    hi, lo, plain_left, sent_left, kept_left = factor(sent_place, block_mask[0], *diag_halves, orders, *panel_halves)
 
     left_share = lax.dynamic_slice_in_dim(plain_left, col * lower_in.shape[1], lower_in.shape[1], 1)
     share = upper_in.shape[0]
     share_hi = lax.dynamic_slice_in_dim(hi, row * share, share, 0)
     share_lo = lax.dynamic_slice_in_dim(lo, row * share, share, 0)
     left_received = partner(left_share, "cube", 1)
-    mask = block_mask[0].reshape(-1)
+    small, mask = after((row_map[0], block_mask[0].reshape(-1)), hi)
     mask_rows = -(-(2 * rows + mask.shape[0]) // (16 * raw_end)) * 16
     fill = jnp.zeros(mask_rows * raw_end - 2 * rows - mask.shape[0], mask.dtype)
-    digits = jnp.concatenate([row_map[0] // 32, row_map[0] % 32, mask, fill])
+    digits = jnp.concatenate([small // 32, small % 32, mask, fill])
     digits = digits.astype(jnp.bfloat16).reshape(mask_rows, raw_end)
 
     def choice(order):

time: 365 us -> 365 us (level)
  Pallas kernels: 153 us -> 159 us
  local copies, waits for them, and re-layouts: 25.8 us -> 19.9 us
  other arithmetic: 12 us -> 7.67 us
  starting transfers between devices: 16.5 us -> 20.6 us
    pallas_call x1 -> x2, Pallas kernels: 26.9 us -> 33.1 us  [the longest x1 27.3 us: factor(): pl.pallas_call(factor_kernel, in_specs=[scalars] * 2 + [arrays] * 5, out_...]
    ppermute x26, starting transfers between devices: 16.5 us -> 20.6 us  [partner(): return lax.ppermute(block, axis, [(i, i ^ bits) for i in range(count)])]
    unnamed x62 -> x63, local copies, waits for them, and re-layouts: 7.81 us -> 8.83 us
  transfers between devices with their start and end apart: 26 -> 26, of which waited for: 14 -> 16; matrix products, arithmetic and copies ran while one was open for 8% -> 6% of each run, Pallas kernels for 42% -> 42%
where the time goes in v7:
time: 365 us; the launch traced here: 363 us
  Pallas kernels  159 us (44%)
  waiting for transfers between devices  140 us (38%)
  starting transfers between devices  20.6 us (6%)
  local copies, waits for them, and re-layouts  19.9 us (5%)
  blocking collectives  14.4 us (4%)
  other arithmetic  7.67 us (2%)
    ppermute x26, waiting for transfers between devices, partner(): return lax.ppermute(block, axis, [(i, i ^ bits) for i in range(count)])  140 us
    pallas_call x15, Pallas kernels, merge_chunk(): pl.pallas_call(body, grid_spec=pltpu.PrefetchScalarGridSpec(num_scalar_pr...  72.9 us
    pallas_call x15, Pallas kernels, send_chunk(): pl.pallas_call(send_kernel, grid_spec=pltpu.PrefetchScalarGridSpec(num_sc...  52.2 us
    pallas_call x1, Pallas kernels, factor(): pl.pallas_call(factor_kernel, in_specs=[scalars] * 2 + [arrays] * 5, out_...  27.3 us
    ppermute x26, starting transfers between devices, partner(): return lax.ppermute(block, axis, [(i, i ^ bits) for i in range(count)])  20.6 us
    unnamed x63, local copies, waits for them, and re-layouts  8.83 us
    all_gather x1, blocking collectives, local(): other_left = lax.all_gather(left_received, 'col', axis=1, tiled=True)  7.89 us
  transfers between devices with their start and end apart: 26, of which 16 were waited for; matrix products, arithmetic and copies ran while one was open for 6% of the time, Pallas kernels for 42%

profile of v7, /device:TPU:0, one launch (start us, length us, event | category | flops | bytes accessed | tf_op | source)
XLA Modules:
  0.0 362.9 jit_solution(8861723876857209051)
XLA Ops:
  0.0 5.8 %raw_part.1 = bf16[1024,1024]{1,0:T(8,128)(2,1)} custom-call(s32[1]{0:T(128)} %bitcast.1.place, bf16[1024,15360]{1,0:T(8,128)(2,1)} %bitcast.22), custom_call_target="tpu_custom_call" | custom-call | bytes 4194304 | tf_op jit(solution)/shard_map/raw_part/pallas_call | solution.py:156
  25.0 27.3 %factor.1 = (bf16[256,256]{1,0:T(8,128)(2,1)S(1)}, bf16[256,256]{1,0:T(8,128)(2,1)S(1)}, bf16[1024,256]{1,0:T(8,128)(2,1)S(1)}, bf16[1024,256]{1,0:T(8,128)(2,1)S(1)}, bf16[1024,256]{1,0:T(8,128)(2,1)S(1)}) custom-call(s32[1]{0:T(128)} %bitcast.1.place, s32[8,2]{1,0:T(8,128)S(1)} %copy.29.mask, f32[128,256]{1,0:T(8,128)S(1)} %constant_dynamic-update-slice_fusion.first, ...), custom_call_target="tpu_custom_call" | custom-call | flops 30000001024 | bytes 3000000 | tf_op jit(solution)/shard_map/factor/pallas_call | solution.py:127
  66.1 4.3 %send_part.17 = bf16[1024,512]{1,0:T(8,128)(2,1)} custom-call(s32[1]{0:T(128)} %bitcast.1.place, bf16[256,256]{1,0:T(8,128)(2,1)S(1)} %get-tuple-element.34.hi.refs_1_, bf16[256,256]{1,0:T(8,128)(2,1)S(1)} %get-tuple-element.35.lo.refs_2_, bf16[1024,256]{1,0:T(8,128)(2,1)S(1)} %get-tuple-element.38.left, bf16[1024,15360]{1,0:T(8,128)(2,1)} %bitcast.25, ...), custom_call_target="tpu_custom_call" | custom-call | flops 268435456 | bytes 2621440 | tf_op jit(solution)/shard_map/send_part/pallas_call | solution.py:239
  74.8 8.0 %collective-permute-done.6.received = bf16[1024,512]{1,0:T(8,128)(2,1)S(1)} collective-permute-done((bf16[1024,512]{1,0:T(8,128)(2,1)S(1)}, bf16[1024,512]{1,0:T(8,128)(2,1)S(1)}, u32[]{:S(2)}, u32[]{:S(2)}) %collective-permute-start.6) | collective-permute-done | bytes 1048608 | tf_op jit(solution)/shard_map/ppermute | solution.py:22
  93.1 17.8 %collective-permute-done.13.received = bf16[1024,512]{1,0:T(8,128)(2,1)S(1)} collective-permute-done((bf16[1024,512]{1,0:T(8,128)(2,1)}, bf16[1024,512]{1,0:T(8,128)(2,1)S(1)}, u32[]{:S(2)}, u32[]{:S(2)}) %collective-permute-start.13) | collective-permute-done | bytes 1048608 | tf_op jit(solution)/shard_map/ppermute | solution.py:22
  117.1 19.8 %collective-permute-done.14 = bf16[80,1024]{1,0:T(8,128)(2,1)S(1)} collective-permute-done((bf16[80,1024]{1,0:T(8,128)(2,1)S(1)}, bf16[80,1024]{1,0:T(8,128)(2,1)S(1)}, u32[]{:S(2)}, u32[]{:S(2)}) %collective-permute-start.14) | collective-permute-done | bytes 163872 | tf_op jit(solution)/shard_map/ppermute | solution.py:22
  136.9 4.3 %send_part.20 = bf16[1024,512]{1,0:T(8,128)(2,1)} custom-call(s32[1]{0:T(128)} %bitcast.1.place, bf16[256,256]{1,0:T(8,128)(2,1)S(1)} %get-tuple-element.34.hi.refs_1_, bf16[256,256]{1,0:T(8,128)(2,1)S(1)} %get-tuple-element.35.lo.refs_2_, bf16[1024,256]{1,0:T(8,128)(2,1)S(1)} %get-tuple-element.38.left, bf16[1024,15360]{1,0:T(8,128)(2,1)} %bitcast.28, ...), custom_call_target="tpu_custom_call" | custom-call | flops 268435456 | bytes 2621440 | tf_op jit(solution)/shard_map/send_part/pallas_call | solution.py:239
  142.9 4.7 %merge_part.15.rest_1_ = bf16[1024,7680]{1,0:T(8,128)(2,1)} custom-call(s32[1]{0:T(128)} %bitcast.place.refs_0_, bf16[256,256]{1,0:T(8,128)(2,1)S(1)} %get-tuple-element.34.hi.refs_1_, bf16[256,256]{1,0:T(8,128)(2,1)S(1)} %get-tuple-element.35.lo.refs_2_, bf16[1024,256]{1,0:T(8,128)(2,1)S(1)} %get-tuple-element.36.left.refs_3_, ...), custom_call_target="tpu_custom_call" | custom-call | flops 1342177280 | bytes 4194304 | tf_op jit(solution)/shard_map/merge_part/pallas_call | solution.py:283
  147.6 11.8 %collective-permute-done.11.received = bf16[1024,512]{1,0:T(8,128)(2,1)} collective-permute-done((bf16[1024,512]{1,0:T(8,128)(2,1)}, bf16[1024,512]{1,0:T(8,128)(2,1)}, u32[]{:S(2)}, u32[]{:S(2)}) %collective-permute-start.11) | collective-permute-done | bytes 1048608 | tf_op jit(solution)/shard_map/ppermute | solution.py:22
  164.0 4.8 %merge_part.16.rest_1_ = bf16[1024,7680]{1,0:T(8,128)(2,1)} custom-call(s32[1]{0:T(128)} %bitcast.place.refs_0_, bf16[256,256]{1,0:T(8,128)(2,1)S(1)} %get-tuple-element.34.hi.refs_1_, bf16[256,256]{1,0:T(8,128)(2,1)S(1)} %get-tuple-element.35.lo.refs_2_, bf16[1024,256]{1,0:T(8,128)(2,1)S(1)} %get-tuple-element.36.left.refs_3_, ...), custom_call_target="tpu_custom_call", output_to_operand_aliasing={{}: (8, {})} | custom-call | flops 1342177280 | bytes 4194304 | tf_op jit(solution)/shard_map/merge_part/pallas_call | solution.py:283
  168.8 13.0 %collective-permute-done.18.received = bf16[1024,512]{1,0:T(8,128)(2,1)S(1)} collective-permute-done((bf16[1024,512]{1,0:T(8,128)(2,1)}, bf16[1024,512]{1,0:T(8,128)(2,1)S(1)}, u32[]{:S(2)}, u32[]{:S(2)}) %collective-permute-start.18) | collective-permute-done | bytes 1048608 | tf_op jit(solution)/shard_map/ppermute | solution.py:22
  182.8 5.6 %reshape.101 = f32[8192,2]{1,0:T(8,128)} reshape(f32[16,1024]{1,0:T(8,128)S(1)} %slice_convert_fusion) | data formatting | bytes 131072 | tf_op jit(solution)/shard_map/convert_element_type | solution.py:454
  194.7 4.8 %merge_part.17.rest_1_ = bf16[1024,7680]{1,0:T(8,128)(2,1)} custom-call(s32[1]{0:T(128)} %bitcast.place.refs_0_, bf16[256,256]{1,0:T(8,128)(2,1)S(1)} %get-tuple-element.34.hi.refs_1_, bf16[256,256]{1,0:T(8,128)(2,1)S(1)} %get-tuple-element.35.lo.refs_2_, bf16[1024,256]{1,0:T(8,128)(2,1)S(1)} %get-tuple-element.36.left.refs_3_, ...), custom_call_target="tpu_custom_call", output_to_operand_aliasing={{}: (8, {})} | custom-call | flops 1342177280 | bytes 4194304 | tf_op jit(solution)/shard_map/merge_part/pallas_call | solution.py:283
  199.6 5.4 %merge_part.18.rest_1_ = bf16[1024,7680]{1,0:T(8,128)(2,1)} custom-call(s32[1]{0:T(128)} %bitcast.place.refs_0_, bf16[256,256]{1,0:T(8,128)(2,1)S(1)} %get-tuple-element.34.hi.refs_1_, bf16[256,256]{1,0:T(8,128)(2,1)S(1)} %get-tuple-element.35.lo.refs_2_, bf16[1024,256]{1,0:T(8,128)(2,1)S(1)} %get-tuple-element.36.left.refs_3_, ...), custom_call_target="tpu_custom_call", output_to_operand_aliasing={{}: (8, {})} | custom-call | flops 1342177280 | bytes 4194304 | tf_op jit(solution)/shard_map/merge_part/pallas_call | solution.py:283
  204.9 7.9 %all_gather.6 = bf16[1024,256]{1,0:T(8,128)(2,1)S(1)} all-gather(bf16[1024,128]{1,0:T(8,128)(2,1)S(1)} %copy-done.24), channel_id=1, replica_groups=mesh['cube'=4,'row'=4,'col'=2] {'col'}, dimensions={1}, use_global_device_ids=true | all-gather | bytes 786432 | tf_op jit(solution)/shard_map/all_gather | solution.py:460
  217.8 4.7 %merge_part.19.refs_10_ = bf16[1024,7680]{1,0:T(8,128)(2,1)} custom-call(s32[1]{0:T(128)} %bitcast.place.refs_0_, bf16[256,256]{1,0:T(8,128)(2,1)S(1)} %get-tuple-element.34.hi.refs_1_, bf16[256,256]{1,0:T(8,128)(2,1)S(1)} %get-tuple-element.35.lo.refs_2_, bf16[1024,256]{1,0:T(8,128)(2,1)S(1)} %get-tuple-element.36.left.refs_3_, ...), custom_call_target="tpu_custom_call", output_to_operand_aliasing={{}: (8, {})} | custom-call | flops 1342177280 | bytes 4194304 | tf_op jit(solution)/shard_map/merge_part/pallas_call | solution.py:283
  222.5 6.5 %all_gather.7.refs_8_ = bf16[256,1024]{1,0:T(8,128)(2,1)S(1)} all-gather(bf16[64,1024]{1,0:T(8,128)(2,1)S(1)} %slice-done), channel_id=1, replica_groups=mesh['cube'=4,'row'=4,'col'=2] {'row'}, dimensions={0}, use_global_device_ids=true | all-gather | bytes 655360 | tf_op jit(solution)/shard_map/all_gather | solution.py:464
  232.5 5.4 %merge_part.20.refs_10_ = bf16[1024,7680]{1,0:T(8,128)(2,1)} custom-call(s32[1]{0:T(128)} %bitcast.place.refs_0_, bf16[256,256]{1,0:T(8,128)(2,1)S(1)} %get-tuple-element.34.hi.refs_1_, bf16[256,256]{1,0:T(8,128)(2,1)S(1)} %get-tuple-element.35.lo.refs_2_, bf16[1024,256]{1,0:T(8,128)(2,1)S(1)} %get-tuple-element.36.left.refs_3_, ...), custom_call_target="tpu_custom_call", output_to_operand_aliasing={{}: (10, {})} | custom-call | flops 1342177280 | bytes 4194304 | tf_op jit(solution)/shard_map/merge_part/pallas_call | solution.py:283
  237.8 5.3 %merge_part.21.rest_1_ = bf16[1024,7680]{1,0:T(8,128)(2,1)} custom-call(s32[1]{0:T(128)} %bitcast.place.refs_0_, bf16[256,256]{1,0:T(8,128)(2,1)S(1)} %get-tuple-element.34.hi.refs_1_, bf16[256,256]{1,0:T(8,128)(2,1)S(1)} %get-tuple-element.35.lo.refs_2_, bf16[1024,256]{1,0:T(8,128)(2,1)S(1)} %get-tuple-element.36.left.refs_3_, ...), custom_call_target="tpu_custom_call", output_to_operand_aliasing={{}: (10, {})} | custom-call | flops 1342177280 | bytes 4194304 | tf_op jit(solution)/shard_map/merge_part/pallas_call | solution.py:283
  243.2 6.1 %collective-permute-done.21.received = bf16[1024,512]{1,0:T(8,128)(2,1)S(1)} collective-permute-done((bf16[1024,512]{1,0:T(8,128)(2,1)S(1)}, bf16[1024,512]{1,0:T(8,128)(2,1)S(1)}, u32[]{:S(2)}, u32[]{:S(2)}) %collective-permute-start.21) | collective-permute-done | bytes 1048608 | tf_op jit(solution)/shard_map/ppermute | solution.py:22
  253.8 5.0 %merge_part.22.rest_1_ = bf16[1024,7680]{1,0:T(8,128)(2,1)} custom-call(s32[1]{0:T(128)} %bitcast.place.refs_0_, bf16[256,256]{1,0:T(8,128)(2,1)S(1)} %get-tuple-element.34.hi.refs_1_, bf16[256,256]{1,0:T(8,128)(2,1)S(1)} %get-tuple-element.35.lo.refs_2_, bf16[1024,256]{1,0:T(8,128)(2,1)S(1)} %get-tuple-element.36.left.refs_3_, ...), custom_call_target="tpu_custom_call", output_to_operand_aliasing={{}: (8, {})} | custom-call | flops 1342177280 | bytes 4194304 | tf_op jit(solution)/shard_map/merge_part/pallas_call | solution.py:283
  258.8 5.0 %merge_part.23.rest_1_ = bf16[1024,7680]{1,0:T(8,128)(2,1)} custom-call(s32[1]{0:T(128)} %bitcast.place.refs_0_, bf16[256,256]{1,0:T(8,128)(2,1)S(1)} %get-tuple-element.34.hi.refs_1_, bf16[256,256]{1,0:T(8,128)(2,1)S(1)} %get-tuple-element.35.lo.refs_2_, bf16[1024,256]{1,0:T(8,128)(2,1)S(1)} %get-tuple-element.36.left.refs_3_, ...), custom_call_target="tpu_custom_call", output_to_operand_aliasing={{}: (8, {})} | custom-call | flops 1342177280 | bytes 4194304 | tf_op jit(solution)/shard_map/merge_part/pallas_call | solution.py:283
  263.9 7.8 %collective-permute-done.20.received = bf16[1024,512]{1,0:T(8,128)(2,1)S(1)} collective-permute-done((bf16[1024,512]{1,0:T(8,128)(2,1)S(1)}, bf16[1024,512]{1,0:T(8,128)(2,1)S(1)}, u32[]{:S(2)}, u32[]{:S(2)}) %collective-permute-start.20) | collective-permute-done | bytes 1048608 | tf_op jit(solution)/shard_map/ppermute | solution.py:22
  276.0 4.8 %merge_part.24.rest_1_ = bf16[1024,7680]{1,0:T(8,128)(2,1)} custom-call(s32[1]{0:T(128)} %bitcast.place.refs_0_, bf16[256,256]{1,0:T(8,128)(2,1)S(1)} %get-tuple-element.34.hi.refs_1_, bf16[256,256]{1,0:T(8,128)(2,1)S(1)} %get-tuple-element.35.lo.refs_2_, bf16[1024,256]{1,0:T(8,128)(2,1)S(1)} %get-tuple-element.36.left.refs_3_, ...), custom_call_target="tpu_custom_call", output_to_operand_aliasing={{}: (8, {})} | custom-call | flops 1342177280 | bytes 4194304 | tf_op jit(solution)/shard_map/merge_part/pallas_call | solution.py:283
  280.8 4.7 %merge_part.25.rest_1_ = bf16[1024,7680]{1,0:T(8,128)(2,1)} custom-call(s32[1]{0:T(128)} %bitcast.place.refs_0_, bf16[256,256]{1,0:T(8,128)(2,1)S(1)} %get-tuple-element.34.hi.refs_1_, bf16[256,256]{1,0:T(8,128)(2,1)S(1)} %get-tuple-element.35.lo.refs_2_, bf16[1024,256]{1,0:T(8,128)(2,1)S(1)} %get-tuple-element.36.left.refs_3_, ...), custom_call_target="tpu_custom_call", output_to_operand_aliasing={{}: (8, {})} | custom-call | flops 1342177280 | bytes 4194304 | tf_op jit(solution)/shard_map/merge_part/pallas_call | solution.py:283
  285.5 8.6 %collective-permute-done.19.received = bf16[1024,512]{1,0:T(8,128)(2,1)S(1)} collective-permute-done((bf16[1024,512]{1,0:T(8,128)(2,1)S(1)}, bf16[1024,512]{1,0:T(8,128)(2,1)S(1)}, u32[]{:S(2)}, u32[]{:S(2)}) %collective-permute-start.19) | collective-permute-done | bytes 1048608 | tf_op jit(solution)/shard_map/ppermute | solution.py:22
  297.4 19.3 %collective-permute-done.24.received = bf16[1024,512]{1,0:T(8,128)(2,1)S(1)} collective-permute-done((bf16[1024,512]{1,0:T(8,128)(2,1)}, bf16[1024,512]{1,0:T(8,128)(2,1)S(1)}, u32[]{:S(2)}, u32[]{:S(2)}) %collective-permute-start.24) | collective-permute-done | bytes 1048608 | tf_op jit(solution)/shard_map/ppermute | solution.py:22
  320.7 4.7 %merge_part.26.rest_1_ = bf16[1024,7680]{1,0:T(8,128)(2,1)} custom-call(s32[1]{0:T(128)} %bitcast.place.refs_0_, bf16[256,256]{1,0:T(8,128)(2,1)S(1)} %get-tuple-element.34.hi.refs_1_, bf16[256,256]{1,0:T(8,128)(2,1)S(1)} %get-tuple-element.35.lo.refs_2_, bf16[1024,256]{1,0:T(8,128)(2,1)S(1)} %get-tuple-element.36.left.refs_3_, ...), custom_call_target="tpu_custom_call", output_to_operand_aliasing={{}: (8, {})} | custom-call | flops 1342177280 | bytes 4194304 | tf_op jit(solution)/shard_map/merge_part/pallas_call | solution.py:283
  325.4 4.7 %merge_part.27.rest_1_ = bf16[1024,7680]{1,0:T(8,128)(2,1)} custom-call(s32[1]{0:T(128)} %bitcast.place.refs_0_, bf16[256,256]{1,0:T(8,128)(2,1)S(1)} %get-tuple-element.34.hi.refs_1_, bf16[256,256]{1,0:T(8,128)(2,1)S(1)} %get-tuple-element.35.lo.refs_2_, bf16[1024,256]{1,0:T(8,128)(2,1)S(1)} %get-tuple-element.36.left.refs_3_, ...), custom_call_target="tpu_custom_call", output_to_operand_aliasing={{}: (8, {})} | custom-call | flops 1342177280 | bytes 4194304 | tf_op jit(solution)/shard_map/merge_part/pallas_call | solution.py:283
  330.2 9.0 %collective-permute-done.23.received = bf16[1024,512]{1,0:T(8,128)(2,1)S(1)} collective-permute-done((bf16[1024,512]{1,0:T(8,128)(2,1)S(1)}, bf16[1024,512]{1,0:T(8,128)(2,1)S(1)}, u32[]{:S(2)}, u32[]{:S(2)}) %collective-permute-start.23) | collective-permute-done | bytes 1048608 | tf_op jit(solution)/shard_map/ppermute | solution.py:22
  339.1 4.7 %merge_part.28.rest_1_ = bf16[1024,7680]{1,0:T(8,128)(2,1)} custom-call(s32[1]{0:T(128)} %bitcast.place.refs_0_, bf16[256,256]{1,0:T(8,128)(2,1)S(1)} %get-tuple-element.34.hi.refs_1_, bf16[256,256]{1,0:T(8,128)(2,1)S(1)} %get-tuple-element.35.lo.refs_2_, bf16[1024,256]{1,0:T(8,128)(2,1)S(1)} %get-tuple-element.36.left.refs_3_, ...), custom_call_target="tpu_custom_call", output_to_operand_aliasing={{}: (8, {})} | custom-call | flops 1342177280 | bytes 4194304 | tf_op jit(solution)/shard_map/merge_part/pallas_call | solution.py:283
  343.8 6.5 %collective-permute-done.22.received = bf16[1024,256]{1,0:T(8,128)(2,1)S(1)} collective-permute-done((bf16[1024,256]{1,0:T(8,128)(2,1)S(1)}, bf16[1024,256]{1,0:T(8,128)(2,1)S(1)}, u32[]{:S(2)}, u32[]{:S(2)}) %collective-permute-start.22) | collective-permute-done | bytes 524320 | tf_op jit(solution)/shard_map/ppermute | solution.py:22
  (157 shorter events, 104.3 us)
Async XLA Ops:
  5.8 60.0 %collective-permute-start.7 = (bf16[1024,1024]{1,0:T(8,128)(2,1)}, bf16[1024,1024]{1,0:T(8,128)(2,1)}, u32[]{:S(2)}, u32[]{:S(2)}) collective-permute-start(bf16[1024,1024]{1,0:T(8,128)(2,1)} %raw_part.1), channel_id=1, source_target_pairs={{0,8},{8,0},{16,24},{24,16},{1,9},{9,1},{17,25},{25,17},{2,10},{10... | collective-permute-start | bytes 6291464 | tf_op jit(solution)/shard_map/ppermute | solution.py:22
  8.9 7.7 %collective-permute-start = (f32[32,256]{1,0:T(8,128)S(1)}, f32[32,256]{1,0:T(8,128)S(1)}, u32[]{:S(2)}, u32[]{:S(2)}) collective-permute-start(f32[32,256]{1,0:T(8,128)S(1)} %bitcast.53), channel_id=1, source_target_pairs={{0,4},{1,5},{2,6},{3,7},{4,0},{5,1},{6,2},{7,3},{8,12},{9,13},{10,... | collective-permute-start | bytes 98312 | tf_op jit(solution)/shard_map/ppermute | solution.py:22
  10.4 13.0 %collective-permute-start.3 = (bf16[1024,128]{1,0:T(8,128)(2,1)S(1)}, bf16[1024,128]{1,0:T(8,128)(2,1)S(1)}, u32[]{:S(2)}, u32[]{:S(2)}) collective-permute-start(bf16[1024,128]{1,0:T(8,128)(2,1)S(1)} %bitcast.20), channel_id=1, source_target_pairs={{0,1},{1,0},{2,3},{3,2},{4,5},{5,4},{6,7},{7,6},{8,9},{9,8},{10,11... | collective-permute-start | bytes 786440 | tf_op jit(solution)/shard_map/ppermute | solution.py:22
  12.6 9.6 %collective-permute-start.4 = (bf16[64,2048]{1,0:T(8,128)(2,1)}, bf16[64,2048]{1,0:T(8,128)(2,1)}, u32[]{:S(2)}, u32[]{:S(2)}) collective-permute-start(bf16[64,2048]{1,0:T(8,128)(2,1)} %dynamic-slice_bitcast_fusion.2), channel_id=1, source_target_pairs={{0,4},{2,6},{4,0},{6,2},{1,5},{3,7},{5,1},{7,3},{8,12},{10,14},{12... | collective-permute-start | bytes 786440 | tf_op jit(solution)/shard_map/ppermute | solution.py:22
  14.7 46.7 %collective-permute-start.8 = (bf16[64,13312]{1,0:T(8,128)(2,1)}, bf16[64,13312]{1,0:T(8,128)(2,1)}, u32[]{:S(2)}, u32[]{:S(2)}) collective-permute-start(bf16[64,13312]{1,0:T(8,128)(2,1)} %pad_maximum_fusion.1), channel_id=1, source_target_pairs={{0,4},{2,6},{4,0},{6,2},{1,5},{3,7},{5,1},{7,3},{8,12},{10,14},{12... | collective-permute-start | bytes 5111816 | tf_op jit(solution)/shard_map/ppermute | solution.py:22
  16.6 4.3 %collective-permute-start.1 = (f32[64,256]{1,0:T(8,128)S(1)}, f32[64,256]{1,0:T(8,128)S(1)}, u32[]{:S(2)}, u32[]{:S(2)}) collective-permute-start(f32[64,256]{1,0:T(8,128)S(1)} %pad_maximum_fusion.6), channel_id=1, source_target_pairs={{0,1},{1,0},{2,3},{3,2},{4,5},{5,4},{6,7},{7,6},{8,9},{9,8},{10,11... | collective-permute-start | bytes 196616 | tf_op jit(solution)/shard_map/ppermute | solution.py:22
  20.9 2.4 collective-permute-start.2
  22.2 30.2 %copy-start.26 = (s32[1,1024]{1,0:T(1,128)S(1)}, s32[1,1024]{1,0:T(1,128)}, u32[]{:S(2)}) copy-start(s32[1,1024]{1,0:T(1,128)} %param.13) | copy-start | bytes 12292
  23.3 29.2 %collective-permute-start.5 = (bf16[128,2048]{1,0:T(8,128)(2,1)S(1)}, bf16[128,2048]{1,0:T(8,128)(2,1)}, u32[]{:S(2)}, u32[]{:S(2)}) collective-permute-start(bf16[128,2048]{1,0:T(8,128)(2,1)S(1)} %pad_maximum_fusion.4), channel_id=1, source_target_pairs={{0,2},{2,0},{4,6},{6,4},{1,3},{3,1},{5,7},{7,5},{8,10},{10,8},{12,... | collective-permute-start | bytes 1572872 | tf_op jit(solution)/shard_map/ppermute | solution.py:22
  56.8 26.0 %collective-permute-start.6 = (bf16[1024,512]{1,0:T(8,128)(2,1)S(1)}, bf16[1024,512]{1,0:T(8,128)(2,1)S(1)}, u32[]{:S(2)}, u32[]{:S(2)}) collective-permute-start(bf16[1024,512]{1,0:T(8,128)(2,1)S(1)} %send_part.15), channel_id=1, source_target_pairs={{0,8},{8,0},{16,24},{24,16},{1,9},{9,1},{17,25},{25,17},{2,10},{10... | collective-permute-start | bytes 3145736 | tf_op jit(solution)/shard_map/ppermute | solution.py:22
  62.7 3.3 collective-permute-start.9
  66.1 93.4 %copy-start.4 = (bf16[256,5632]{1,0:T(8,128)(2,1)}, bf16[256,5632]{1,0:T(8,128)(2,1)S(1)}, u32[]{:S(2)}) copy-start(bf16[256,5632]{1,0:T(8,128)(2,1)S(1)} %constant_dynamic-update-slice_fusion.3.rest_0_) | copy-start | bytes 8650756
  70.4 45.0 %collective-permute-start.15 = (bf16[128,7680]{1,0:T(8,128)(2,1)}, bf16[128,7680]{1,0:T(8,128)(2,1)}, u32[]{:S(2)}, u32[]{:S(2)}) collective-permute-start(bf16[128,7680]{1,0:T(8,128)(2,1)} %pad_maximum_fusion), channel_id=1, source_target_pairs={{0,2},{2,0},{4,6},{6,4},{1,3},{3,1},{5,7},{7,5},{8,10},{10,8},{12,... | collective-permute-start | bytes 5898248 | tf_op jit(solution)/shard_map/ppermute | solution.py:22
  70.6 17.8 %collective-permute-start.10 = (bf16[1024,128]{1,0:T(8,128)(2,1)S(1)}, bf16[1024,128]{1,0:T(8,128)(2,1)S(1)}, u32[]{:S(2)}, u32[]{:S(2)}) collective-permute-start(bf16[1024,128]{1,0:T(8,128)(2,1)S(1)} %constant_dynamic-slice_fusion), channel_id=1, source_target_pairs={{0,8},{8,0},{16,24},{24,16},{1,9},{9,1},{17,25},{25,17},{2,10},{10... | collective-permute-start | bytes 786440 | tf_op jit(solution)/shard_map/ppermute | solution.py:22
  72.7 38.2 %collective-permute-start.13 = (bf16[1024,512]{1,0:T(8,128)(2,1)}, bf16[1024,512]{1,0:T(8,128)(2,1)S(1)}, u32[]{:S(2)}, u32[]{:S(2)}) collective-permute-start(bf16[1024,512]{1,0:T(8,128)(2,1)} %send_part.16), channel_id=1, source_target_pairs={{0,8},{8,0},{16,24},{24,16},{1,9},{9,1},{17,25},{25,17},{2,10},{10... | collective-permute-start | bytes 3145736 | tf_op jit(solution)/shard_map/ppermute | solution.py:22
  73.2 63.6 %collective-permute-start.12 = (bf16[1024,512]{1,0:T(8,128)(2,1)}, bf16[1024,512]{1,0:T(8,128)(2,1)S(1)}, u32[]{:S(2)}, u32[]{:S(2)}) collective-permute-start(bf16[1024,512]{1,0:T(8,128)(2,1)} %send_part.17), channel_id=1, source_target_pairs={{0,8},{8,0},{16,24},{24,16},{1,9},{9,1},{17,25},{25,17},{2,10},{10... | collective-permute-start | bytes 3145736 | tf_op jit(solution)/shard_map/ppermute | solution.py:22
  85.1 51.8 %collective-permute-start.14 = (bf16[80,1024]{1,0:T(8,128)(2,1)S(1)}, bf16[80,1024]{1,0:T(8,128)(2,1)S(1)}, u32[]{:S(2)}, u32[]{:S(2)}) collective-permute-start(bf16[80,1024]{1,0:T(8,128)(2,1)S(1)} %pad_maximum_fusion.5), channel_id=1, source_target_pairs={{0,8},{8,0},{16,24},{24,16},{1,9},{9,1},{17,25},{25,17},{2,10},{10... | collective-permute-start | bytes 491528 | tf_op jit(solution)/shard_map/ppermute | solution.py:22
  92.6 66.8 %collective-permute-start.11 = (bf16[1024,512]{1,0:T(8,128)(2,1)}, bf16[1024,512]{1,0:T(8,128)(2,1)}, u32[]{:S(2)}, u32[]{:S(2)}) collective-permute-start(bf16[1024,512]{1,0:T(8,128)(2,1)} %send_part.18), channel_id=1, source_target_pairs={{0,8},{8,0},{16,24},{24,16},{1,9},{9,1},{17,25},{25,17},{2,10},{10... | collective-permute-start | bytes 3145736 | tf_op jit(solution)/shard_map/ppermute | solution.py:22
  115.0 66.9 %collective-permute-start.18 = (bf16[1024,512]{1,0:T(8,128)(2,1)}, bf16[1024,512]{1,0:T(8,128)(2,1)S(1)}, u32[]{:S(2)}, u32[]{:S(2)}) collective-permute-start(bf16[1024,512]{1,0:T(8,128)(2,1)} %send_part.19), channel_id=1, source_target_pairs={{0,8},{8,0},{16,24},{24,16},{1,9},{9,1},{17,25},{25,17},{2,10},{10... | collective-permute-start | bytes 3145736 | tf_op jit(solution)/shard_map/ppermute | solution.py:22
  117.1 24.1 %copy-start.2 = (bf16[256,7680]{1,0:T(8,128)(2,1)}, bf16[256,7680]{1,0:T(8,128)(2,1)S(1)}, u32[]{:S(2)}) copy-start(bf16[256,7680]{1,0:T(8,128)(2,1)S(1)} %constant_dynamic-update-slice_fusion.5.rest_0_.refs_9_) | copy-start | bytes 11796484
  136.9 27.1 %copy-start.21 = (bf16[80,1024]{1,0:T(8,128)(2,1)}, bf16[80,1024]{1,0:T(8,128)(2,1)S(1)}, u32[]{:S(2)}) copy-start(bf16[80,1024]{1,0:T(8,128)(2,1)S(1)} %collective-permute-done.14) | copy-start | bytes 491524
  141.2 71.8 %collective-permute-start.17 = (bf16[1024,512]{1,0:T(8,128)(2,1)}, bf16[1024,512]{1,0:T(8,128)(2,1)}, u32[]{:S(2)}, u32[]{:S(2)}) collective-permute-start(bf16[1024,512]{1,0:T(8,128)(2,1)} %send_part.20), channel_id=1, source_target_pairs={{0,8},{8,0},{16,24},{24,16},{1,9},{9,1},{17,25},{25,17},{2,10},{10... | collective-permute-start | bytes 3145736 | tf_op jit(solution)/shard_map/ppermute | solution.py:22
  163.6 65.5 %collective-permute-start.16 = (bf16[1024,512]{1,0:T(8,128)(2,1)}, bf16[1024,512]{1,0:T(8,128)(2,1)}, u32[]{:S(2)}, u32[]{:S(2)}) collective-permute-start(bf16[1024,512]{1,0:T(8,128)(2,1)} %send_part.21), channel_id=1, source_target_pairs={{0,8},{8,0},{16,24},{24,16},{1,9},{9,1},{17,25},{25,17},{2,10},{10... | collective-permute-start | bytes 3145736 | tf_op jit(solution)/shard_map/ppermute | solution.py:22
  164.0 17.8 %copy-start.22 = (f32[16,1024]{1,0:T(8,128)}, f32[16,1024]{1,0:T(8,128)S(1)}, u32[]{:S(2)}) copy-start(f32[16,1024]{1,0:T(8,128)S(1)} %slice_convert_fusion) | copy-start | bytes 196612
  193.3 56.0 %collective-permute-start.21 = (bf16[1024,512]{1,0:T(8,128)(2,1)S(1)}, bf16[1024,512]{1,0:T(8,128)(2,1)S(1)}, u32[]{:S(2)}, u32[]{:S(2)}) collective-permute-start(bf16[1024,512]{1,0:T(8,128)(2,1)S(1)} %send_part.22), channel_id=1, source_target_pairs={{0,8},{8,0},{16,24},{24,16},{1,9},{9,1},{17,25},{25,17},{2,10},{10... | collective-permute-start | bytes 3145736 | tf_op jit(solution)/shard_map/ppermute | solution.py:22
  199.5 13.5 %copy-start.6 = (bf16[256,5632]{1,0:T(8,128)(2,1)S(1)}, bf16[256,5632]{1,0:T(8,128)(2,1)}, u32[]{:S(2)}) copy-start(bf16[256,5632]{1,0:T(8,128)(2,1)} %copy-done.4) | copy-start | bytes 8650756
  216.1 55.6 %collective-permute-start.20 = (bf16[1024,512]{1,0:T(8,128)(2,1)S(1)}, bf16[1024,512]{1,0:T(8,128)(2,1)S(1)}, u32[]{:S(2)}, u32[]{:S(2)}) collective-permute-start(bf16[1024,512]{1,0:T(8,128)(2,1)S(1)} %send_part.23), channel_id=1, source_target_pairs={{0,8},{8,0},{16,24},{24,16},{1,9},{9,1},{17,25},{25,17},{2,10},{10... | collective-permute-start | bytes 3145736 | tf_op jit(solution)/shard_map/ppermute | solution.py:22
  232.0 62.2 %collective-permute-start.19 = (bf16[1024,512]{1,0:T(8,128)(2,1)S(1)}, bf16[1024,512]{1,0:T(8,128)(2,1)S(1)}, u32[]{:S(2)}, u32[]{:S(2)}) collective-permute-start(bf16[1024,512]{1,0:T(8,128)(2,1)S(1)} %send_part.24), channel_id=1, source_target_pairs={{0,8},{8,0},{16,24},{24,16},{1,9},{9,1},{17,25},{25,17},{2,10},{10... | collective-permute-start | bytes 3145736 | tf_op jit(solution)/shard_map/ppermute | solution.py:22
  253.3 63.3 %collective-permute-start.24 = (bf16[1024,512]{1,0:T(8,128)(2,1)}, bf16[1024,512]{1,0:T(8,128)(2,1)S(1)}, u32[]{:S(2)}, u32[]{:S(2)}) collective-permute-start(bf16[1024,512]{1,0:T(8,128)(2,1)} %send_part.25), channel_id=1, source_target_pairs={{0,8},{8,0},{16,24},{24,16},{1,9},{9,1},{17,25},{25,17},{2,10},{10... | collective-permute-start | bytes 3145736 | tf_op jit(solution)/shard_map/ppermute | solution.py:22
  274.7 64.5 %collective-permute-start.23 = (bf16[1024,512]{1,0:T(8,128)(2,1)S(1)}, bf16[1024,512]{1,0:T(8,128)(2,1)S(1)}, u32[]{:S(2)}, u32[]{:S(2)}) collective-permute-start(bf16[1024,512]{1,0:T(8,128)(2,1)S(1)} %send_part.26), channel_id=1, source_target_pairs={{0,8},{8,0},{16,24},{24,16},{1,9},{9,1},{17,25},{25,17},{2,10},{10... | collective-permute-start | bytes 3145736 | tf_op jit(solution)/shard_map/ppermute | solution.py:22
  296.9 53.5 %collective-permute-start.22 = (bf16[1024,256]{1,0:T(8,128)(2,1)S(1)}, bf16[1024,256]{1,0:T(8,128)(2,1)S(1)}, u32[]{:S(2)}, u32[]{:S(2)}) collective-permute-start(bf16[1024,256]{1,0:T(8,128)(2,1)S(1)} %send_part.27), channel_id=1, source_target_pairs={{0,8},{8,0},{16,24},{24,16},{1,9},{9,1},{17,25},{25,17},{2,10},{10... | collective-permute-start | bytes 1572872 | tf_op jit(solution)/shard_map/ppermute | solution.py:22
  320.2 41.0 %collective-permute-start.25 = (bf16[1024,256]{1,0:T(8,128)(2,1)S(1)}, bf16[1024,256]{1,0:T(8,128)(2,1)S(1)}, u32[]{:S(2)}, u32[]{:S(2)}) collective-permute-start(bf16[1024,256]{1,0:T(8,128)(2,1)S(1)} %fusion.3), channel_id=1, source_target_pairs={{0,8},{8,0},{16,24},{24,16},{1,9},{9,1},{17,25},{25,17},{2,10},{10... | collective-permute-start | bytes 1572872 | tf_op jit(solution)/shard_map/ppermute | solution.py:22
  (24 other events, 117.1 us)

commit v8 on v7

--- a/solution.py
+++ b/solution.py
@@ -143,29 +143,6 @@
 def panel_tile(hi, lo, pieces):
     columns = jnp.concatenate([piece[...] for piece in pieces], axis=0)
     return (fast(hi[...], columns) + fast(lo[...], columns)).astype(jnp.bfloat16)
-
-
-def copy_kernel(place, source, out):
-    out[...] = source[...]
-
-
-def take_raw(place, trailing, end, width):
-    rows, columns = trailing.shape
-    step_rows = rows // 4
-    half_blocks = columns // 2 // width
-    return pl.pallas_call(
-        copy_kernel,
-        grid_spec=pltpu.PrefetchScalarGridSpec(
-            num_scalar_prefetch=1,
-            grid=(4, end // width),
-            in_specs=[pl.BlockSpec((step_rows, width), lambda i, j, place: (i, place[0] * half_blocks + j))],
-            out_specs=pl.BlockSpec((step_rows, width), lambda i, j, place: (i, j)),
-        ),
-        out_shape=jax.ShapeDtypeStruct((rows, end), trailing.dtype),
-        compiler_params=pltpu.CompilerParams(vmem_limit_bytes=VMEM_LIMIT),
-        cost_estimate=pl.CostEstimate(flops=0, bytes_accessed=4 * rows * end, transcendentals=0),
-        name="raw_part",
-    )(place, trailing)
 
 
 def send_kernel(place, hi, lo, left, trailing, *rest):
@@ -365,9 +342,10 @@
     parity = lax.axis_index("cube") % 2
     sent_place = (1 - parity).astype(jnp.int32).reshape(1)
     kept_place = parity.astype(jnp.int32).reshape(1)
-    raw_end = RAW * width
-
-    raw = take_raw(sent_place, trailing, raw_end, width)
+    raw_rest = width // 4 if width % 512 == 0 else 0
+    raw_end = RAW * width + raw_rest
+
+    raw = lax.dynamic_slice_in_dim(trailing, (1 - parity) * half, raw_end, 1)
     raw_received = partner(raw, "cube", 1)
 
     diag_halves = halves(after(diag_block, raw), ("row", "col"), 0)
@@ -384,7 +362,7 @@
     def columns_of(place, first, last):
         return lax.dynamic_slice_in_dim(upper_in, place * half + first, last - first, 1)
 
-    cut = raw_end + EARLY * width
+    cut = (RAW + EARLY) * width
     early = doubled(columns_of(1 - parity, 0, cut), "row", 0)
     late, kept_upper = columns_of(1 - parity, cut, half), columns_of(parity, 0, half)
     rest = partner(jnp.concatenate([late, kept_upper], axis=1), "row", bits_of("row")[0])
@@ -412,6 +390,7 @@
     bounds = [width * chunk for chunk in range(RAW, CHUNKS + 1)]
     if width % 256 == 0:
         bounds.insert(-1, half - width // 2)
+    bounds[0] = raw_end
     spans = list(zip(bounds, bounds[1:]))
     sent, received, merged_after = [], [], []
     merged = None
@@ -425,10 +404,13 @@
 
     def merge_raw():
         result = merged
-        for start in range(0, raw_end, width):
+        tiles = [(start, width) for start in range(0, raw_end - raw_rest, width)]
+        if raw_rest:
+            tiles.append((raw_end - raw_rest, raw_rest))
+        for start, tile in tiles:
             result = merge_chunk(
-                kept_place, hi, lo, kept_left, trailing, chosen, raw_received, [kept_upper], [0], start,
-                width, result, (0, other_left, other_right),
+                kept_place, hi, lo, kept_left, trailing, chosen, raw_received, [kept_upper], [0], start, tile, result,
+                (0, other_left, other_right),
             )
         return result
 

time: 365 us -> 366 us (level)
  waiting for transfers between devices: 140 us -> 128 us
  starting transfers between devices: 20.6 us -> 29.4 us
    ppermute x26, waiting for transfers between devices: 140 us -> 128 us  [partner(): return lax.ppermute(block, axis, [(i, i ^ bits) for i in range(count)])]
    ppermute x26, starting transfers between devices: 20.6 us -> 29.4 us  [partner(): return lax.ppermute(block, axis, [(i, i ^ bits) for i in range(count)])]
    pallas_call x1 -> x0, Pallas kernels: 5.81 us -> none  [take_raw(): pl.pallas_call(copy_kernel, grid_spec=pltpu.PrefetchScalarGridSpec(num_sc...]
    pallas_call x15 -> x16, Pallas kernels: 72.9 us -> 77.9 us  [merge_chunk(): pl.pallas_call(body, grid_spec=pltpu.PrefetchScalarGridSpec(num_scalar_pr...]
  transfers between devices with their start and end apart: 26 -> 26, of which waited for: 16 -> 14; matrix products, arithmetic and copies ran while one was open for 6% -> 6% of each run, Pallas kernels for 42% -> 44%
where the time goes in v8:
time: 366 us; the launch traced here: 363 us
  Pallas kernels  160 us (44%)
  waiting for transfers between devices  128 us (35%)
  starting transfers between devices  29.4 us (8%)
  local copies, waits for them, and re-layouts  23.3 us (6%)
  blocking collectives  14.4 us (4%)
  other arithmetic  6.82 us (2%)
    ppermute x26, waiting for transfers between devices, partner(): return lax.ppermute(block, axis, [(i, i ^ bits) for i in range(count)])  128 us
    pallas_call x16, Pallas kernels, merge_chunk(): pl.pallas_call(body, grid_spec=pltpu.PrefetchScalarGridSpec(num_scalar_pr...  77.9 us
    pallas_call x15, Pallas kernels, send_chunk(): pl.pallas_call(send_kernel, grid_spec=pltpu.PrefetchScalarGridSpec(num_sc...  53.5 us
    ppermute x26, starting transfers between devices, partner(): return lax.ppermute(block, axis, [(i, i ^ bits) for i in range(count)])  29.4 us
    pallas_call x1, Pallas kernels, factor(): pl.pallas_call(factor_kernel, in_specs=[scalars] * 2 + [arrays] * 5, out_...  27.3 us
    all_gather x1, blocking collectives, local(): other_left = lax.all_gather(left_received, 'col', axis=1, tiled=True)  7.74 us
    unnamed x63, local copies, waits for them, and re-layouts  7.42 us
  transfers between devices with their start and end apart: 26, of which 14 were waited for; matrix products, arithmetic and copies ran while one was open for 6% of the time, Pallas kernels for 44%

profile of v8, /device:TPU:0, one launch (start us, length us, event | category | flops | bytes accessed | tf_op | source)
XLA Modules:
  0.0 363.4 jit_solution(14775615297982884260)
XLA Ops:
  22.6 27.3 %factor.1 = (bf16[256,256]{1,0:T(8,128)(2,1)S(1)}, bf16[256,256]{1,0:T(8,128)(2,1)S(1)}, bf16[1024,256]{1,0:T(8,128)(2,1)S(1)}, bf16[1024,256]{1,0:T(8,128)(2,1)S(1)}, bf16[1024,256]{1,0:T(8,128)(2,1)S(1)}) custom-call(s32[1]{0:T(128)} %bitcast.1.place, s32[8,2]{1,0:T(8,128)S(1)} %copy.30.mask, f32[128,256]{1,0:T(8,128)S(1)} %constant_dynamic-update-slice_fusion.first, ...), custom_call_target="tpu_custom_call" | custom-call | flops 30000001024 | bytes 3000000 | tf_op jit(solution)/shard_map/factor/pallas_call | solution.py:127
  63.3 4.3 %send_part.17 = bf16[1024,512]{1,0:T(8,128)(2,1)} custom-call(s32[1]{0:T(128)} %bitcast.1.place, bf16[256,256]{1,0:T(8,128)(2,1)S(1)} %get-tuple-element.34.hi.refs_1_, bf16[256,256]{1,0:T(8,128)(2,1)S(1)} %get-tuple-element.35.lo.refs_2_, bf16[1024,256]{1,0:T(8,128)(2,1)S(1)} %get-tuple-element.38.left, bf16[1024,15360]{1,0:T(8,128)(2,1)} %bitcast.25, ...), custom_call_target="tpu_custom_call" | custom-call | flops 268435456 | bytes 2621440 | tf_op jit(solution)/shard_map/send_part/pallas_call | solution.py:216
  73.8 14.9 %collective-permute-done.6.received = bf16[1024,384]{1,0:T(8,128)(2,1)S(1)} collective-permute-done((bf16[1024,384]{1,0:T(8,128)(2,1)S(1)}, bf16[1024,384]{1,0:T(8,128)(2,1)S(1)}, u32[]{:S(2)}, u32[]{:S(2)}) %collective-permute-start.6) | collective-permute-done | bytes 786464 | tf_op jit(solution)/shard_map/ppermute | solution.py:22
  95.3 15.8 %collective-permute-done.13.received = bf16[1024,512]{1,0:T(8,128)(2,1)S(1)} collective-permute-done((bf16[1024,512]{1,0:T(8,128)(2,1)S(1)}, bf16[1024,512]{1,0:T(8,128)(2,1)S(1)}, u32[]{:S(2)}, u32[]{:S(2)}) %collective-permute-start.13) | collective-permute-done | bytes 1048608 | tf_op jit(solution)/shard_map/ppermute | solution.py:22
  118.5 19.1 %collective-permute-done.14 = bf16[80,1152]{1,0:T(8,128)(2,1)S(1)} collective-permute-done((bf16[80,1152]{1,0:T(8,128)(2,1)S(1)}, bf16[80,1152]{1,0:T(8,128)(2,1)S(1)}, u32[]{:S(2)}, u32[]{:S(2)}) %collective-permute-start.14) | collective-permute-done | bytes 184352 | tf_op jit(solution)/shard_map/ppermute | solution.py:22
  137.6 4.3 %send_part.20 = bf16[1024,512]{1,0:T(8,128)(2,1)} custom-call(s32[1]{0:T(128)} %bitcast.1.place, bf16[256,256]{1,0:T(8,128)(2,1)S(1)} %get-tuple-element.34.hi.refs_1_, bf16[256,256]{1,0:T(8,128)(2,1)S(1)} %get-tuple-element.35.lo.refs_2_, bf16[1024,256]{1,0:T(8,128)(2,1)S(1)} %get-tuple-element.38.left, bf16[1024,15360]{1,0:T(8,128)(2,1)} %bitcast.28, ...), custom_call_target="tpu_custom_call" | custom-call | flops 268435456 | bytes 2621440 | tf_op jit(solution)/shard_map/send_part/pallas_call | solution.py:216
  143.5 4.6 %merge_part.16.rest_1_ = bf16[1024,7680]{1,0:T(8,128)(2,1)} custom-call(s32[1]{0:T(128)} %bitcast.place.refs_0_, bf16[256,256]{1,0:T(8,128)(2,1)S(1)} %get-tuple-element.34.hi.refs_1_, bf16[256,256]{1,0:T(8,128)(2,1)S(1)} %get-tuple-element.35.lo.refs_2_, bf16[1024,256]{1,0:T(8,128)(2,1)S(1)} %get-tuple-element.36.left.refs_3_, ...), custom_call_target="tpu_custom_call" | custom-call | flops 1006632960 | bytes 3145728 | tf_op jit(solution)/shard_map/merge_part/pallas_call | solution.py:260
  148.1 12.0 %collective-permute-done.11.received = bf16[1024,512]{1,0:T(8,128)(2,1)} collective-permute-done((bf16[1024,512]{1,0:T(8,128)(2,1)}, bf16[1024,512]{1,0:T(8,128)(2,1)}, u32[]{:S(2)}, u32[]{:S(2)}) %collective-permute-start.11) | collective-permute-done | bytes 1048608 | tf_op jit(solution)/shard_map/ppermute | solution.py:22
  165.8 4.8 %merge_part.17.rest_1_ = bf16[1024,7680]{1,0:T(8,128)(2,1)} custom-call(s32[1]{0:T(128)} %bitcast.place.refs_0_, bf16[256,256]{1,0:T(8,128)(2,1)S(1)} %get-tuple-element.34.hi.refs_1_, bf16[256,256]{1,0:T(8,128)(2,1)S(1)} %get-tuple-element.35.lo.refs_2_, bf16[1024,256]{1,0:T(8,128)(2,1)S(1)} %get-tuple-element.36.left.refs_3_, ...), custom_call_target="tpu_custom_call", output_to_operand_aliasing={{}: (8, {})} | custom-call | flops 1342177280 | bytes 4194304 | tf_op jit(solution)/shard_map/merge_part/pallas_call | solution.py:260
  170.6 11.9 %collective-permute-done.18.received = bf16[1024,512]{1,0:T(8,128)(2,1)S(1)} collective-permute-done((bf16[1024,512]{1,0:T(8,128)(2,1)}, bf16[1024,512]{1,0:T(8,128)(2,1)S(1)}, u32[]{:S(2)}, u32[]{:S(2)}) %collective-permute-start.18) | collective-permute-done | bytes 1048608 | tf_op jit(solution)/shard_map/ppermute | solution.py:22
  183.5 6.2 %reshape.97 = f32[9216,2]{1,0:T(8,128)} reshape(f32[16,1152]{1,0:T(8,128)S(1)} %slice_convert_fusion) | data formatting | bytes 147456 | tf_op jit(solution)/shard_map/convert_element_type | solution.py:436
  196.2 4.7 %merge_part.18.rest_1_ = bf16[1024,7680]{1,0:T(8,128)(2,1)} custom-call(s32[1]{0:T(128)} %bitcast.place.refs_0_, bf16[256,256]{1,0:T(8,128)(2,1)S(1)} %get-tuple-element.34.hi.refs_1_, bf16[256,256]{1,0:T(8,128)(2,1)S(1)} %get-tuple-element.35.lo.refs_2_, bf16[1024,256]{1,0:T(8,128)(2,1)S(1)} %get-tuple-element.36.left.refs_3_, ...), custom_call_target="tpu_custom_call", output_to_operand_aliasing={{}: (8, {})} | custom-call | flops 1342177280 | bytes 4194304 | tf_op jit(solution)/shard_map/merge_part/pallas_call | solution.py:260
  200.9 7.7 %all_gather.6 = bf16[1024,256]{1,0:T(8,128)(2,1)S(1)} all-gather(bf16[1024,128]{1,0:T(8,128)(2,1)} %collective-permute-done.10), channel_id=1, replica_groups=mesh['cube'=4,'row'=4,'col'=2] {'col'}, dimensions={1}, use_global_device_ids=true | all-gather | bytes 786432 | tf_op jit(solution)/shard_map/all_gather | solution.py:442
  209.7 5.3 %merge_part.19.rest_1_ = bf16[1024,7680]{1,0:T(8,128)(2,1)} custom-call(s32[1]{0:T(128)} %bitcast.place.refs_0_, bf16[256,256]{1,0:T(8,128)(2,1)S(1)} %get-tuple-element.34.hi.refs_1_, bf16[256,256]{1,0:T(8,128)(2,1)S(1)} %get-tuple-element.35.lo.refs_2_, bf16[1024,256]{1,0:T(8,128)(2,1)S(1)} %get-tuple-element.36.left.refs_3_, ...), custom_call_target="tpu_custom_call", output_to_operand_aliasing={{}: (8, {})} | custom-call | flops 1342177280 | bytes 4194304 | tf_op jit(solution)/shard_map/merge_part/pallas_call | solution.py:260
  215.3 4.2 %send_part.23 = bf16[1024,512]{1,0:T(8,128)(2,1)} custom-call(s32[1]{0:T(128)} %bitcast.1.place, bf16[256,256]{1,0:T(8,128)(2,1)S(1)} %get-tuple-element.34.hi.refs_1_, bf16[256,256]{1,0:T(8,128)(2,1)S(1)} %get-tuple-element.35.lo.refs_2_, bf16[1024,256]{1,0:T(8,128)(2,1)S(1)} %get-tuple-element.38.left, bf16[1024,15360]{1,0:T(8,128)(2,1)} %bitcast.35, ...), custom_call_target="tpu_custom_call" | custom-call | flops 268435456 | bytes 2621440 | tf_op jit(solution)/shard_map/send_part/pallas_call | solution.py:216
  220.0 4.7 %merge_part.20.refs_10_ = bf16[1024,7680]{1,0:T(8,128)(2,1)} custom-call(s32[1]{0:T(128)} %bitcast.place.refs_0_, bf16[256,256]{1,0:T(8,128)(2,1)S(1)} %get-tuple-element.34.hi.refs_1_, bf16[256,256]{1,0:T(8,128)(2,1)S(1)} %get-tuple-element.35.lo.refs_2_, bf16[1024,256]{1,0:T(8,128)(2,1)S(1)} %get-tuple-element.36.left.refs_3_, ...), custom_call_target="tpu_custom_call", output_to_operand_aliasing={{}: (8, {})} | custom-call | flops 1342177280 | bytes 4194304 | tf_op jit(solution)/shard_map/merge_part/pallas_call | solution.py:260
  224.7 6.7 %all_gather.7.refs_8_ = bf16[256,1152]{1,0:T(8,128)(2,1)S(1)} all-gather(bf16[64,1152]{1,0:T(8,128)(2,1)S(1)} %slice-done), channel_id=1, replica_groups=mesh['cube'=4,'row'=4,'col'=2] {'row'}, dimensions={0}, use_global_device_ids=true | all-gather | bytes 737280 | tf_op jit(solution)/shard_map/all_gather | solution.py:446
  237.0 5.3 %merge_part.21.refs_10_ = bf16[1024,7680]{1,0:T(8,128)(2,1)} custom-call(s32[1]{0:T(128)} %bitcast.place.refs_0_, bf16[256,256]{1,0:T(8,128)(2,1)S(1)} %get-tuple-element.34.hi.refs_1_, bf16[256,256]{1,0:T(8,128)(2,1)S(1)} %get-tuple-element.35.lo.refs_2_, bf16[1024,256]{1,0:T(8,128)(2,1)S(1)} %get-tuple-element.36.left.refs_3_, ...), custom_call_target="tpu_custom_call", output_to_operand_aliasing={{}: (10, {})} | custom-call | flops 1342177280 | bytes 4194304 | tf_op jit(solution)/shard_map/merge_part/pallas_call | solution.py:260
  242.3 5.3 %merge_part.22.refs_10_ = bf16[1024,7680]{1,0:T(8,128)(2,1)} custom-call(s32[1]{0:T(128)} %bitcast.place.refs_0_, bf16[256,256]{1,0:T(8,128)(2,1)S(1)} %get-tuple-element.34.hi.refs_1_, bf16[256,256]{1,0:T(8,128)(2,1)S(1)} %get-tuple-element.35.lo.refs_2_, bf16[1024,256]{1,0:T(8,128)(2,1)S(1)} %get-tuple-element.36.left.refs_3_, ...), custom_call_target="tpu_custom_call", output_to_operand_aliasing={{}: (10, {})} | custom-call | flops 1342177280 | bytes 4194304 | tf_op jit(solution)/shard_map/merge_part/pallas_call | solution.py:260
  251.8 4.4 %send_part.25 = bf16[1024,512]{1,0:T(8,128)(2,1)} custom-call(s32[1]{0:T(128)} %bitcast.1.place, bf16[256,256]{1,0:T(8,128)(2,1)S(1)} %get-tuple-element.34.hi.refs_1_, bf16[256,256]{1,0:T(8,128)(2,1)S(1)} %get-tuple-element.35.lo.refs_2_, bf16[1024,256]{1,0:T(8,128)(2,1)S(1)} %get-tuple-element.38.left, bf16[1024,15360]{1,0:T(8,128)(2,1)} %bitcast.41, ...), custom_call_target="tpu_custom_call" | custom-call | flops 268435456 | bytes 2621440 | tf_op jit(solution)/shard_map/send_part/pallas_call | solution.py:216
  256.6 5.1 %merge_part.24.rest_1_ = bf16[1024,7680]{1,0:T(8,128)(2,1)} custom-call(s32[1]{0:T(128)} %bitcast.place.refs_0_, bf16[256,256]{1,0:T(8,128)(2,1)S(1)} %get-tuple-element.34.hi.refs_1_, bf16[256,256]{1,0:T(8,128)(2,1)S(1)} %get-tuple-element.35.lo.refs_2_, bf16[1024,256]{1,0:T(8,128)(2,1)S(1)} %get-tuple-element.36.left.refs_3_, ...), custom_call_target="tpu_custom_call", output_to_operand_aliasing={{}: (8, {})} | custom-call | flops 1342177280 | bytes 4194304 | tf_op jit(solution)/shard_map/merge_part/pallas_call | solution.py:260
  261.7 5.2 %merge_part.25.rest_1_ = bf16[1024,7680]{1,0:T(8,128)(2,1)} custom-call(s32[1]{0:T(128)} %bitcast.place.refs_0_, bf16[256,256]{1,0:T(8,128)(2,1)S(1)} %get-tuple-element.34.hi.refs_1_, bf16[256,256]{1,0:T(8,128)(2,1)S(1)} %get-tuple-element.35.lo.refs_2_, bf16[1024,256]{1,0:T(8,128)(2,1)S(1)} %get-tuple-element.36.left.refs_3_, ...), custom_call_target="tpu_custom_call", output_to_operand_aliasing={{}: (8, {})} | custom-call | flops 1342177280 | bytes 4194304 | tf_op jit(solution)/shard_map/merge_part/pallas_call | solution.py:260
  266.9 5.5 %collective-permute-done.20.received = bf16[1024,512]{1,0:T(8,128)(2,1)} collective-permute-done((bf16[1024,512]{1,0:T(8,128)(2,1)}, bf16[1024,512]{1,0:T(8,128)(2,1)}, u32[]{:S(2)}, u32[]{:S(2)}) %collective-permute-start.20) | collective-permute-done | bytes 1048608 | tf_op jit(solution)/shard_map/ppermute | solution.py:22
  277.1 4.7 %merge_part.26.rest_1_ = bf16[1024,7680]{1,0:T(8,128)(2,1)} custom-call(s32[1]{0:T(128)} %bitcast.place.refs_0_, bf16[256,256]{1,0:T(8,128)(2,1)S(1)} %get-tuple-element.34.hi.refs_1_, bf16[256,256]{1,0:T(8,128)(2,1)S(1)} %get-tuple-element.35.lo.refs_2_, bf16[1024,256]{1,0:T(8,128)(2,1)S(1)} %get-tuple-element.36.left.refs_3_, ...), custom_call_target="tpu_custom_call", output_to_operand_aliasing={{}: (8, {})} | custom-call | flops 1342177280 | bytes 4194304 | tf_op jit(solution)/shard_map/merge_part/pallas_call | solution.py:260
  281.8 5.0 %merge_part.27.rest_1_ = bf16[1024,7680]{1,0:T(8,128)(2,1)} custom-call(s32[1]{0:T(128)} %bitcast.place.refs_0_, bf16[256,256]{1,0:T(8,128)(2,1)S(1)} %get-tuple-element.34.hi.refs_1_, bf16[256,256]{1,0:T(8,128)(2,1)S(1)} %get-tuple-element.35.lo.refs_2_, bf16[1024,256]{1,0:T(8,128)(2,1)S(1)} %get-tuple-element.36.left.refs_3_, ...), custom_call_target="tpu_custom_call", output_to_operand_aliasing={{}: (8, {})} | custom-call | flops 1342177280 | bytes 4194304 | tf_op jit(solution)/shard_map/merge_part/pallas_call | solution.py:260
  286.9 8.1 %collective-permute-done.19.received = bf16[1024,512]{1,0:T(8,128)(2,1)} collective-permute-done((bf16[1024,512]{1,0:T(8,128)(2,1)}, bf16[1024,512]{1,0:T(8,128)(2,1)}, u32[]{:S(2)}, u32[]{:S(2)}) %collective-permute-start.19) | collective-permute-done | bytes 1048608 | tf_op jit(solution)/shard_map/ppermute | solution.py:22
  299.3 18.1 %collective-permute-done.24.received = bf16[1024,512]{1,0:T(8,128)(2,1)} collective-permute-done((bf16[1024,512]{1,0:T(8,128)(2,1)}, bf16[1024,512]{1,0:T(8,128)(2,1)}, u32[]{:S(2)}, u32[]{:S(2)}) %collective-permute-start.24) | collective-permute-done | bytes 1048608 | tf_op jit(solution)/shard_map/ppermute | solution.py:22
  322.6 5.0 %merge_part.28.rest_1_ = bf16[1024,7680]{1,0:T(8,128)(2,1)} custom-call(s32[1]{0:T(128)} %bitcast.place.refs_0_, bf16[256,256]{1,0:T(8,128)(2,1)S(1)} %get-tuple-element.34.hi.refs_1_, bf16[256,256]{1,0:T(8,128)(2,1)S(1)} %get-tuple-element.35.lo.refs_2_, bf16[1024,256]{1,0:T(8,128)(2,1)S(1)} %get-tuple-element.36.left.refs_3_, ...), custom_call_target="tpu_custom_call", output_to_operand_aliasing={{}: (8, {})} | custom-call | flops 1342177280 | bytes 4194304 | tf_op jit(solution)/shard_map/merge_part/pallas_call | solution.py:260
  327.6 5.0 %merge_part.29.rest_1_ = bf16[1024,7680]{1,0:T(8,128)(2,1)} custom-call(s32[1]{0:T(128)} %bitcast.place.refs_0_, bf16[256,256]{1,0:T(8,128)(2,1)S(1)} %get-tuple-element.34.hi.refs_1_, bf16[256,256]{1,0:T(8,128)(2,1)S(1)} %get-tuple-element.35.lo.refs_2_, bf16[1024,256]{1,0:T(8,128)(2,1)S(1)} %get-tuple-element.36.left.refs_3_, ...), custom_call_target="tpu_custom_call", output_to_operand_aliasing={{}: (8, {})} | custom-call | flops 1342177280 | bytes 4194304 | tf_op jit(solution)/shard_map/merge_part/pallas_call | solution.py:260
  332.7 7.1 %collective-permute-done.23.received = bf16[1024,512]{1,0:T(8,128)(2,1)S(1)} collective-permute-done((bf16[1024,512]{1,0:T(8,128)(2,1)S(1)}, bf16[1024,512]{1,0:T(8,128)(2,1)S(1)}, u32[]{:S(2)}, u32[]{:S(2)}) %collective-permute-start.23) | collective-permute-done | bytes 1048608 | tf_op jit(solution)/shard_map/ppermute | solution.py:22
  339.8 4.7 %merge_part.30.rest_1_ = bf16[1024,7680]{1,0:T(8,128)(2,1)} custom-call(s32[1]{0:T(128)} %bitcast.place.refs_0_, bf16[256,256]{1,0:T(8,128)(2,1)S(1)} %get-tuple-element.34.hi.refs_1_, bf16[256,256]{1,0:T(8,128)(2,1)S(1)} %get-tuple-element.35.lo.refs_2_, bf16[1024,256]{1,0:T(8,128)(2,1)S(1)} %get-tuple-element.36.left.refs_3_, ...), custom_call_target="tpu_custom_call", output_to_operand_aliasing={{}: (8, {})} | custom-call | flops 1342177280 | bytes 4194304 | tf_op jit(solution)/shard_map/merge_part/pallas_call | solution.py:260
  344.5 6.5 %collective-permute-done.22.received = bf16[1024,256]{1,0:T(8,128)(2,1)S(1)} collective-permute-done((bf16[1024,256]{1,0:T(8,128)(2,1)S(1)}, bf16[1024,256]{1,0:T(8,128)(2,1)S(1)}, u32[]{:S(2)}, u32[]{:S(2)}) %collective-permute-start.22) | collective-permute-done | bytes 524320 | tf_op jit(solution)/shard_map/ppermute | solution.py:22
  (159 shorter events, 109.1 us)
Async XLA Ops:
  3.4 59.6 %collective-permute-start.7 = (bf16[1024,1152]{1,0:T(8,128)(2,1)}, bf16[1024,1152]{1,0:T(8,128)(2,1)}, u32[]{:S(2)}, u32[]{:S(2)}) collective-permute-start(bf16[1024,1152]{1,0:T(8,128)(2,1)} %dynamic-slice_bitcast_fusion), channel_id=1, source_target_pairs={{0,8},{8,0},{16,24},{24,16},{1,9},{9,1},{17,25},{25,17},{2,10},{10... | collective-permute-start | bytes 7077896 | tf_op jit(solution)/shard_map/ppermute | solution.py:22
  6.5 7.8 %collective-permute-start = (f32[32,256]{1,0:T(8,128)S(1)}, f32[32,256]{1,0:T(8,128)S(1)}, u32[]{:S(2)}, u32[]{:S(2)}) collective-permute-start(f32[32,256]{1,0:T(8,128)S(1)} %bitcast.54), channel_id=1, source_target_pairs={{0,4},{1,5},{2,6},{3,7},{4,0},{5,1},{6,2},{7,3},{8,12},{9,13},{10,... | collective-permute-start | bytes 98312 | tf_op jit(solution)/shard_map/ppermute | solution.py:22
  8.0 13.0 %collective-permute-start.3 = (bf16[1024,128]{1,0:T(8,128)(2,1)S(1)}, bf16[1024,128]{1,0:T(8,128)(2,1)S(1)}, u32[]{:S(2)}, u32[]{:S(2)}) collective-permute-start(bf16[1024,128]{1,0:T(8,128)(2,1)S(1)} %bitcast.21), channel_id=1, source_target_pairs={{0,1},{1,0},{2,3},{3,2},{4,5},{5,4},{6,7},{7,6},{8,9},{9,8},{10,11... | collective-permute-start | bytes 786440 | tf_op jit(solution)/shard_map/ppermute | solution.py:22
  10.2 9.6 %collective-permute-start.4 = (bf16[64,2048]{1,0:T(8,128)(2,1)}, bf16[64,2048]{1,0:T(8,128)(2,1)}, u32[]{:S(2)}, u32[]{:S(2)}) collective-permute-start(bf16[64,2048]{1,0:T(8,128)(2,1)} %dynamic-slice_bitcast_fusion.3), channel_id=1, source_target_pairs={{0,4},{2,6},{4,0},{6,2},{1,5},{3,7},{5,1},{7,3},{8,12},{10,14},{12... | collective-permute-start | bytes 786440 | tf_op jit(solution)/shard_map/ppermute | solution.py:22
  10.9 10.8 %copy-start.15 = (bf16[1,1024,128]{2,1,0:T(8,128)(2,1)S(1)}, bf16[1,1024,128]{2,1,0:T(8,128)(2,1)}, u32[]{:S(2)}) copy-start(bf16[1,1024,128]{2,1,0:T(8,128)(2,1)} %param.9) | copy-start | bytes 786436
  12.4 46.3 %collective-permute-start.8 = (bf16[64,13312]{1,0:T(8,128)(2,1)}, bf16[64,13312]{1,0:T(8,128)(2,1)}, u32[]{:S(2)}, u32[]{:S(2)}) collective-permute-start(bf16[64,13312]{1,0:T(8,128)(2,1)} %pad_maximum_fusion.1), channel_id=1, source_target_pairs={{0,4},{2,6},{4,0},{6,2},{1,5},{3,7},{5,1},{7,3},{8,12},{10,14},{12... | collective-permute-start | bytes 5111816 | tf_op jit(solution)/shard_map/ppermute | solution.py:22
  14.2 4.3 %collective-permute-start.1 = (f32[64,256]{1,0:T(8,128)S(1)}, f32[64,256]{1,0:T(8,128)S(1)}, u32[]{:S(2)}, u32[]{:S(2)}) collective-permute-start(f32[64,256]{1,0:T(8,128)S(1)} %pad_maximum_fusion.6), channel_id=1, source_target_pairs={{0,1},{1,0},{2,3},{3,2},{4,5},{5,4},{6,7},{7,6},{8,9},{9,8},{10,11... | collective-permute-start | bytes 196616 | tf_op jit(solution)/shard_map/ppermute | solution.py:22
  18.6 2.4 collective-permute-start.2
  20.9 30.5 %collective-permute-start.5 = (bf16[128,2048]{1,0:T(8,128)(2,1)S(1)}, bf16[128,2048]{1,0:T(8,128)(2,1)}, u32[]{:S(2)}, u32[]{:S(2)}) collective-permute-start(bf16[128,2048]{1,0:T(8,128)(2,1)S(1)} %pad_maximum_fusion.4), channel_id=1, source_target_pairs={{0,2},{2,0},{4,6},{6,4},{1,3},{3,1},{5,7},{7,5},{8,10},{10,8},{12,... | collective-permute-start | bytes 1572872 | tf_op jit(solution)/shard_map/ppermute | solution.py:22
  22.6 27.3 %copy-start.26 = (s32[1,1024]{1,0:T(1,128)S(1)}, s32[1,1024]{1,0:T(1,128)}, u32[]{:S(2)}) copy-start(s32[1,1024]{1,0:T(1,128)} %param.13) | copy-start | bytes 12292
  50.9 39.9 %collective-permute-start.10 = (bf16[1024,128]{1,0:T(8,128)(2,1)}, bf16[1024,128]{1,0:T(8,128)(2,1)}, u32[]{:S(2)}, u32[]{:S(2)}) collective-permute-start(bf16[1024,128]{1,0:T(8,128)(2,1)} %constant_dynamic-slice_fusion), channel_id=1, source_target_pairs={{0,8},{8,0},{16,24},{24,16},{1,9},{9,1},{17,25},{25,17},{2,10},{10... | collective-permute-start | bytes 786440 | tf_op jit(solution)/shard_map/ppermute | solution.py:22
  59.9 3.3 collective-permute-start.9
  63.3 96.8 %copy-start.4 = (bf16[256,5632]{1,0:T(8,128)(2,1)}, bf16[256,5632]{1,0:T(8,128)(2,1)S(1)}, u32[]{:S(2)}) copy-start(bf16[256,5632]{1,0:T(8,128)(2,1)S(1)} %constant_dynamic-update-slice_fusion.3.rest_0_) | copy-start | bytes 8650756
  67.6 49.1 %collective-permute-start.15 = (bf16[128,7680]{1,0:T(8,128)(2,1)}, bf16[128,7680]{1,0:T(8,128)(2,1)}, u32[]{:S(2)}, u32[]{:S(2)}) collective-permute-start(bf16[128,7680]{1,0:T(8,128)(2,1)} %pad_maximum_fusion), channel_id=1, source_target_pairs={{0,2},{2,0},{4,6},{6,4},{1,3},{3,1},{5,7},{7,5},{8,10},{10,8},{12,... | collective-permute-start | bytes 5898248 | tf_op jit(solution)/shard_map/ppermute | solution.py:22
  68.2 20.4 %collective-permute-start.6 = (bf16[1024,384]{1,0:T(8,128)(2,1)S(1)}, bf16[1024,384]{1,0:T(8,128)(2,1)S(1)}, u32[]{:S(2)}, u32[]{:S(2)}) collective-permute-start(bf16[1024,384]{1,0:T(8,128)(2,1)S(1)} %send_part.15), channel_id=1, source_target_pairs={{0,8},{8,0},{16,24},{24,16},{1,9},{9,1},{17,25},{25,17},{2,10},{10... | collective-permute-start | bytes 2359304 | tf_op jit(solution)/shard_map/ppermute | solution.py:22
  69.9 41.2 %collective-permute-start.13 = (bf16[1024,512]{1,0:T(8,128)(2,1)S(1)}, bf16[1024,512]{1,0:T(8,128)(2,1)S(1)}, u32[]{:S(2)}, u32[]{:S(2)}) collective-permute-start(bf16[1024,512]{1,0:T(8,128)(2,1)S(1)} %send_part.16), channel_id=1, source_target_pairs={{0,8},{8,0},{16,24},{24,16},{1,9},{9,1},{17,25},{25,17},{2,10},{10... | collective-permute-start | bytes 3145736 | tf_op jit(solution)/shard_map/ppermute | solution.py:22
  72.1 65.4 %collective-permute-start.12 = (bf16[1024,512]{1,0:T(8,128)(2,1)}, bf16[1024,512]{1,0:T(8,128)(2,1)S(1)}, u32[]{:S(2)}, u32[]{:S(2)}) collective-permute-start(bf16[1024,512]{1,0:T(8,128)(2,1)} %send_part.17), channel_id=1, source_target_pairs={{0,8},{8,0},{16,24},{24,16},{1,9},{9,1},{17,25},{25,17},{2,10},{10... | collective-permute-start | bytes 3145736 | tf_op jit(solution)/shard_map/ppermute | solution.py:22
  89.1 48.4 %collective-permute-start.14 = (bf16[80,1152]{1,0:T(8,128)(2,1)S(1)}, bf16[80,1152]{1,0:T(8,128)(2,1)S(1)}, u32[]{:S(2)}, u32[]{:S(2)}) collective-permute-start(bf16[80,1152]{1,0:T(8,128)(2,1)S(1)} %pad_maximum_fusion.5), channel_id=1, source_target_pairs={{0,8},{8,0},{16,24},{24,16},{1,9},{9,1},{17,25},{25,17},{2,10},{10... | collective-permute-start | bytes 552968 | tf_op jit(solution)/shard_map/ppermute | solution.py:22
  94.9 65.2 %collective-permute-start.11 = (bf16[1024,512]{1,0:T(8,128)(2,1)}, bf16[1024,512]{1,0:T(8,128)(2,1)}, u32[]{:S(2)}, u32[]{:S(2)}) collective-permute-start(bf16[1024,512]{1,0:T(8,128)(2,1)} %send_part.18), channel_id=1, source_target_pairs={{0,8},{8,0},{16,24},{24,16},{1,9},{9,1},{17,25},{25,17},{2,10},{10... | collective-permute-start | bytes 3145736 | tf_op jit(solution)/shard_map/ppermute | solution.py:22
  115.2 67.3 %collective-permute-start.18 = (bf16[1024,512]{1,0:T(8,128)(2,1)}, bf16[1024,512]{1,0:T(8,128)(2,1)S(1)}, u32[]{:S(2)}, u32[]{:S(2)}) collective-permute-start(bf16[1024,512]{1,0:T(8,128)(2,1)} %send_part.19), channel_id=1, source_target_pairs={{0,8},{8,0},{16,24},{24,16},{1,9},{9,1},{17,25},{25,17},{2,10},{10... | collective-permute-start | bytes 3145736 | tf_op jit(solution)/shard_map/ppermute | solution.py:22
  118.5 23.4 %copy-start.2 = (bf16[256,7680]{1,0:T(8,128)(2,1)}, bf16[256,7680]{1,0:T(8,128)(2,1)S(1)}, u32[]{:S(2)}) copy-start(bf16[256,7680]{1,0:T(8,128)(2,1)S(1)} %constant_dynamic-update-slice_fusion.5.rest_0_.refs_9_) | copy-start | bytes 11796484
  137.5 28.2 %copy-start.24 = (bf16[80,1152]{1,0:T(8,128)(2,1)}, bf16[80,1152]{1,0:T(8,128)(2,1)S(1)}, u32[]{:S(2)}) copy-start(bf16[80,1152]{1,0:T(8,128)(2,1)S(1)} %collective-permute-done.14) | copy-start | bytes 552964
  141.9 73.4 %collective-permute-start.17 = (bf16[1024,512]{1,0:T(8,128)(2,1)}, bf16[1024,512]{1,0:T(8,128)(2,1)}, u32[]{:S(2)}, u32[]{:S(2)}) collective-permute-start(bf16[1024,512]{1,0:T(8,128)(2,1)} %send_part.20), channel_id=1, source_target_pairs={{0,8},{8,0},{16,24},{24,16},{1,9},{9,1},{17,25},{25,17},{2,10},{10... | collective-permute-start | bytes 3145736 | tf_op jit(solution)/shard_map/ppermute | solution.py:22
  164.2 67.2 %collective-permute-start.16 = (bf16[1024,512]{1,0:T(8,128)(2,1)}, bf16[1024,512]{1,0:T(8,128)(2,1)}, u32[]{:S(2)}, u32[]{:S(2)}) collective-permute-start(bf16[1024,512]{1,0:T(8,128)(2,1)} %send_part.21), channel_id=1, source_target_pairs={{0,8},{8,0},{16,24},{24,16},{1,9},{9,1},{17,25},{25,17},{2,10},{10... | collective-permute-start | bytes 3145736 | tf_op jit(solution)/shard_map/ppermute | solution.py:22
  165.8 16.7 %copy-start.22 = (f32[16,1152]{1,0:T(8,128)}, f32[16,1152]{1,0:T(8,128)S(1)}, u32[]{:S(2)}) copy-start(f32[16,1152]{1,0:T(8,128)S(1)} %slice_convert_fusion) | copy-start | bytes 221188
  194.6 57.2 %collective-permute-start.21 = (bf16[1024,512]{1,0:T(8,128)(2,1)S(1)}, bf16[1024,512]{1,0:T(8,128)(2,1)S(1)}, u32[]{:S(2)}, u32[]{:S(2)}) collective-permute-start(bf16[1024,512]{1,0:T(8,128)(2,1)S(1)} %send_part.22), channel_id=1, source_target_pairs={{0,8},{8,0},{16,24},{24,16},{1,9},{9,1},{17,25},{25,17},{2,10},{10... | collective-permute-start | bytes 3145736 | tf_op jit(solution)/shard_map/ppermute | solution.py:22
  219.5 53.0 %collective-permute-start.20 = (bf16[1024,512]{1,0:T(8,128)(2,1)}, bf16[1024,512]{1,0:T(8,128)(2,1)}, u32[]{:S(2)}, u32[]{:S(2)}) collective-permute-start(bf16[1024,512]{1,0:T(8,128)(2,1)} %send_part.23), channel_id=1, source_target_pairs={{0,8},{8,0},{16,24},{24,16},{1,9},{9,1},{17,25},{25,17},{2,10},{10... | collective-permute-start | bytes 3145736 | tf_op jit(solution)/shard_map/ppermute | solution.py:22
  235.5 59.5 %collective-permute-start.19 = (bf16[1024,512]{1,0:T(8,128)(2,1)}, bf16[1024,512]{1,0:T(8,128)(2,1)}, u32[]{:S(2)}, u32[]{:S(2)}) collective-permute-start(bf16[1024,512]{1,0:T(8,128)(2,1)} %send_part.24), channel_id=1, source_target_pairs={{0,8},{8,0},{16,24},{24,16},{1,9},{9,1},{17,25},{25,17},{2,10},{10... | collective-permute-start | bytes 3145736 | tf_op jit(solution)/shard_map/ppermute | solution.py:22
  256.1 61.3 %collective-permute-start.24 = (bf16[1024,512]{1,0:T(8,128)(2,1)}, bf16[1024,512]{1,0:T(8,128)(2,1)}, u32[]{:S(2)}, u32[]{:S(2)}) collective-permute-start(bf16[1024,512]{1,0:T(8,128)(2,1)} %send_part.25), channel_id=1, source_target_pairs={{0,8},{8,0},{16,24},{24,16},{1,9},{9,1},{17,25},{25,17},{2,10},{10... | collective-permute-start | bytes 3145736 | tf_op jit(solution)/shard_map/ppermute | solution.py:22
  275.5 64.3 %collective-permute-start.23 = (bf16[1024,512]{1,0:T(8,128)(2,1)S(1)}, bf16[1024,512]{1,0:T(8,128)(2,1)S(1)}, u32[]{:S(2)}, u32[]{:S(2)}) collective-permute-start(bf16[1024,512]{1,0:T(8,128)(2,1)S(1)} %send_part.26), channel_id=1, source_target_pairs={{0,8},{8,0},{16,24},{24,16},{1,9},{9,1},{17,25},{25,17},{2,10},{10... | collective-permute-start | bytes 3145736 | tf_op jit(solution)/shard_map/ppermute | solution.py:22
  297.6 53.4 %collective-permute-start.22 = (bf16[1024,256]{1,0:T(8,128)(2,1)S(1)}, bf16[1024,256]{1,0:T(8,128)(2,1)S(1)}, u32[]{:S(2)}, u32[]{:S(2)}) collective-permute-start(bf16[1024,256]{1,0:T(8,128)(2,1)S(1)} %send_part.27), channel_id=1, source_target_pairs={{0,8},{8,0},{16,24},{24,16},{1,9},{9,1},{17,25},{25,17},{2,10},{10... | collective-permute-start | bytes 1572872 | tf_op jit(solution)/shard_map/ppermute | solution.py:22
  320.9 40.7 %collective-permute-start.25 = (bf16[1024,256]{1,0:T(8,128)(2,1)S(1)}, bf16[1024,256]{1,0:T(8,128)(2,1)S(1)}, u32[]{:S(2)}, u32[]{:S(2)}) collective-permute-start(bf16[1024,256]{1,0:T(8,128)(2,1)S(1)} %fusion.4), channel_id=1, source_target_pairs={{0,8},{8,0},{16,24},{24,16},{1,9},{9,1},{17,25},{25,17},{2,10},{10... | collective-permute-start | bytes 1572872 | tf_op jit(solution)/shard_map/ppermute | solution.py:22
  (24 other events, 119.2 us)

commit v9 on v8

--- a/solution.py
+++ b/solution.py
@@ -10,6 +10,8 @@
 CHUNKS = 15
 RAW = 2
 EARLY = 2
+LATE_CUT = 6
+KEPT_CUTS = (0, 4, 8, 12, 15)
 AHEAD = 3
 MERGES = {6: (0,), 7: (1,), 8: (2, 3), 9: (4,), 10: ("raw",), 11: (5, 6), 12: (7, 8)}
 ROW_STEPS = 4
@@ -392,13 +394,24 @@
         bounds.insert(-1, half - width // 2)
     bounds[0] = raw_end
     spans = list(zip(bounds, bounds[1:]))
-    sent, received, merged_after = [], [], []
+    sent, received, kept_parts = [], [], []
+
+    def finished(block, first, last, *before):
+        block = after(block[:, first:last], *before)
+        for step in range(1, len(bits_of("row"))):
+            block = next_doubled(block, "row", 0, step)
+        return block
+
+    def kept_at(start):
+        number = max(n for n in range(4) if KEPT_CUTS[n] * width <= start)
+        return [kept_parts[number]], [KEPT_CUTS[number] * width]
+
     merged = None
 
     def merge(number):
         start, end = spans[number]
         return merge_chunk(
-            kept_place, hi, lo, kept_left, trailing, chosen, received[number], [kept_upper], [0], start, end - start,
+            kept_place, hi, lo, kept_left, trailing, chosen, received[number], *kept_at(start), start, end - start,
             merged,
         )
 
@@ -409,7 +422,7 @@
             tiles.append((raw_end - raw_rest, raw_rest))
         for start, tile in tiles:
             result = merge_chunk(
-                kept_place, hi, lo, kept_left, trailing, chosen, raw_received, [kept_upper], [0], start, tile, result,
+                kept_place, hi, lo, kept_left, trailing, chosen, raw_received, *kept_at(start), start, tile, result,
                 (0, other_left, other_right),
             )
         return result
@@ -419,26 +432,30 @@
         if number >= AHEAD - 1:
             before += [([raw_received] + received)[number - AHEAD + 1], sent[-1]]
         if number == 1:
-            for step in range(1, len(bits_of("row"))):
-                late = next_doubled(after(late, sent[0]), "row", 0, step)
+            late = [finished(late, 0, LATE_CUT * width - cut, sent[0]), late]
+        if number == 3:
+            late[1] = finished(late[1], LATE_CUT * width - cut, half - cut, raw_received, sent[2])
+        if 4 <= number < 8:
+            first, last = KEPT_CUTS[number - 4] * width, KEPT_CUTS[number - 3] * width
+            kept_parts.append(finished(kept_upper, first, last, received[number - 4], sent[-1]))
+        if 6 <= number < 10:
+            before += [kept_parts[number - 6]]
         if number == 3:
             before += [left_received]
-            for step in range(1, len(bits_of("row"))):
-                kept_upper = next_doubled(after(kept_upper, raw_received, sent[2]), "row", 0, step)
             raw_upper = after(early[:, :raw_end], received[0], sent[2])
             right_share = (fast(share_hi, raw_upper) + fast(share_lo, raw_upper)).astype(jnp.bfloat16)
             bundle = partner(jnp.concatenate([right_share, digits], axis=0), "cube", 1)
         if number == 5:
-            before += [bundle, kept_upper]
-        if number == 6:
-            arrived = after(bundle, received[3], sent[5])
+            before += [bundle]
+        if number == 7:
+            arrived = after(bundle, received[4], sent[6])
             right_received = arrived[:share]
             digits = arrived[share:].reshape(-1).astype(jnp.float32)
             other_order = (32 * digits[:rows] + digits[rows : 2 * rows]).astype(jnp.int32)
             other_flags = digits[2 * rows : 2 * rows + mask.shape[0]].reshape(block_mask.shape[1:])
             other_flags = jnp.where(parity == 0, other_flags[:, :1], other_flags[:, 1:])
             other_chosen = choice(other_order)
-            left_received = after(left_received, received[3], sent[5])
+            left_received = after(left_received, received[4], sent[6])
             other_left = lax.all_gather(left_received, "col", axis=1, tiled=True)
             other_left = other_left.astype(jnp.float32) * jnp.repeat(other_flags, block_rows, axis=0)
             other_left = other_left.astype(jnp.bfloat16)
@@ -452,7 +469,12 @@
         if ready:
             before += [merged]
         place = after(sent_place, *before) if before else sent_place
-        piece, first = (early, 0) if end <= cut else (late, cut)
+        if end <= cut:
+            piece, first = early, 0
+        elif end <= LATE_CUT * width:
+            piece, first = late[0], cut
+        else:
+            piece, first = late[1], LATE_CUT * width
         sent.append(send_chunk(place, hi, lo, sent_left, trailing, [piece], [first], start, end - start))
         outgoing = sent[-1]
         if number == len(spans) - 1:
@@ -463,7 +485,7 @@
         merged = merge(number)
     start, end = spans[-1]
     own = send_chunk(
-        after(kept_place, merged), hi, lo, kept_left, trailing, [kept_upper], [0], start, end - start
+        after(kept_place, merged), hi, lo, kept_left, trailing, *kept_at(start), start, end - start
     )
     merged = join_chunk(own, received[-1], start, merged)
     return merged[None]

time: 366 us -> 358 us (0.978)
  waiting for transfers between devices: 128 us -> 111 us
  local copies, waits for them, and re-layouts: 23.3 us -> 31.7 us
    ppermute x26 -> x30, waiting for transfers between devices: 128 us -> 111 us  [partner(): return lax.ppermute(block, axis, [(i, i ^ bits) for i in range(count)])]
    unnamed x63 -> x81, local copies, waits for them, and re-layouts: 7.42 us -> 11.4 us
    ppermute x26 -> x30, starting transfers between devices: 29.4 us -> 30 us  [partner(): return lax.ppermute(block, axis, [(i, i ^ bits) for i in range(count)])]
  transfers between devices with their start and end apart: 26 -> 30, of which waited for: 14 -> 12; matrix products, arithmetic and copies ran while one was open for 6% -> 8% of each run, Pallas kernels for 44% -> 44%
where the time goes in v9:
time: 358 us; the launch traced here: 356 us
  Pallas kernels  157 us (44%)
  waiting for transfers between devices  111 us (31%)
  local copies, waits for them, and re-layouts  31.7 us (9%)
  starting transfers between devices  30 us (8%)
  blocking collectives  15 us (4%)
  other arithmetic  9.13 us (3%)
    ppermute x30, waiting for transfers between devices, partner(): return lax.ppermute(block, axis, [(i, i ^ bits) for i in range(count)])  111 us
    pallas_call x16, Pallas kernels, merge_chunk(): pl.pallas_call(body, grid_spec=pltpu.PrefetchScalarGridSpec(num_scalar_pr...  76.7 us
    pallas_call x15, Pallas kernels, send_chunk(): pl.pallas_call(send_kernel, grid_spec=pltpu.PrefetchScalarGridSpec(num_sc...  52.6 us
    ppermute x30, starting transfers between devices, partner(): return lax.ppermute(block, axis, [(i, i ^ bits) for i in range(count)])  30 us
    pallas_call x1, Pallas kernels, factor(): pl.pallas_call(factor_kernel, in_specs=[scalars] * 2 + [arrays] * 5, out_...  27.3 us
    unnamed x81, local copies, waits for them, and re-layouts  11.4 us
    all_gather x1, blocking collectives, local(): lax.all_gather(after(right_received, received[5], sent[7]), 'row', axis=0...  7.55 us
    all_gather x1, blocking collectives, local(): other_left = lax.all_gather(left_received, 'col', axis=1, tiled=True)  7.4 us
  transfers between devices with their start and end apart: 30, of which 12 were waited for; matrix products, arithmetic and copies ran while one was open for 8% of the time, Pallas kernels for 44%

profile of v9, /device:TPU:0, one launch (start us, length us, event | category | flops | bytes accessed | tf_op | source)
XLA Modules:
  0.0 355.7 jit_solution(7713535501857973074)
XLA Ops:
  23.3 27.3 %factor.1 = (bf16[256,256]{1,0:T(8,128)(2,1)S(1)}, bf16[256,256]{1,0:T(8,128)(2,1)S(1)}, bf16[1024,256]{1,0:T(8,128)(2,1)S(1)}, bf16[1024,256]{1,0:T(8,128)(2,1)S(1)}, bf16[1024,256]{1,0:T(8,128)(2,1)S(1)}) custom-call(s32[1]{0:T(128)} %bitcast.1.place, s32[8,2]{1,0:T(8,128)S(1)} %copy.30.mask, f32[128,256]{1,0:T(8,128)S(1)} %constant_dynamic-update-slice_fusion.first, ...), custom_call_target="tpu_custom_call" | custom-call | flops 30000001024 | bytes 3000000 | tf_op jit(solution)/shard_map/factor/pallas_call | solution.py:129
  73.3 7.9 %collective-permute-done.6.received = bf16[1024,384]{1,0:T(8,128)(2,1)S(1)} collective-permute-done((bf16[1024,384]{1,0:T(8,128)(2,1)S(1)}, bf16[1024,384]{1,0:T(8,128)(2,1)S(1)}, u32[]{:S(2)}, u32[]{:S(2)}) %collective-permute-start.6) | collective-permute-done | bytes 786464 | tf_op jit(solution)/shard_map/ppermute | solution.py:24
  88.0 15.7 %collective-permute-done.13.received = bf16[1024,512]{1,0:T(8,128)(2,1)S(1)} collective-permute-done((bf16[1024,512]{1,0:T(8,128)(2,1)S(1)}, bf16[1024,512]{1,0:T(8,128)(2,1)S(1)}, u32[]{:S(2)}, u32[]{:S(2)}) %collective-permute-start.13) | collective-permute-done | bytes 1048608 | tf_op jit(solution)/shard_map/ppermute | solution.py:24
  105.8 4.8 %merge_part.16.rest_1_ = bf16[1024,7680]{1,0:T(8,128)(2,1)} custom-call(s32[1]{0:T(128)} %bitcast.place.refs_0_, bf16[256,256]{1,0:T(8,128)(2,1)S(1)} %get-tuple-element.38.hi.refs_1_, bf16[256,256]{1,0:T(8,128)(2,1)S(1)} %get-tuple-element.39.lo.refs_2_, bf16[1024,256]{1,0:T(8,128)(2,1)S(1)} %get-tuple-element.40.left.refs_3_, ...), custom_call_target="tpu_custom_call" | custom-call | flops 1006632960 | bytes 3145728 | tf_op jit(solution)/shard_map/merge_part/pallas_call | solution.py:262
  112.0 4.5 %send_part.19 = bf16[1024,512]{1,0:T(8,128)(2,1)} custom-call(s32[1]{0:T(128)} %bitcast.1.place, bf16[256,256]{1,0:T(8,128)(2,1)S(1)} %get-tuple-element.38.hi.refs_1_, bf16[256,256]{1,0:T(8,128)(2,1)S(1)} %get-tuple-element.39.lo.refs_2_, bf16[1024,256]{1,0:T(8,128)(2,1)S(1)} %get-tuple-element.42.left, bf16[1024,15360]{1,0:T(8,128)(2,1)} %bitcast.28, ...), custom_call_target="tpu_custom_call" | custom-call | flops 268435456 | bytes 2621440 | tf_op jit(solution)/shard_map/send_part/pallas_call | solution.py:218
  116.5 36.1 %collective-permute-done.15 = bf16[80,1152]{1,0:T(8,128)(2,1)S(1)} collective-permute-done((bf16[80,1152]{1,0:T(8,128)(2,1)S(1)}, bf16[80,1152]{1,0:T(8,128)(2,1)S(1)}, u32[]{:S(2)}, u32[]{:S(2)}) %collective-permute-start.15) | collective-permute-done | bytes 184352 | tf_op jit(solution)/shard_map/ppermute | solution.py:24
  155.7 4.5 %send_part.21 = bf16[1024,512]{1,0:T(8,128)(2,1)} custom-call(s32[1]{0:T(128)} %bitcast.1.place, bf16[256,256]{1,0:T(8,128)(2,1)S(1)} %get-tuple-element.38.hi.refs_1_, bf16[256,256]{1,0:T(8,128)(2,1)S(1)} %get-tuple-element.39.lo.refs_2_, bf16[1024,256]{1,0:T(8,128)(2,1)S(1)} %get-tuple-element.42.left, bf16[1024,15360]{1,0:T(8,128)(2,1)} %bitcast.30, ...), custom_call_target="tpu_custom_call" | custom-call | flops 268435456 | bytes 2621440 | tf_op jit(solution)/shard_map/send_part/pallas_call | solution.py:218
  164.0 4.7 %merge_part.17.rest_1_ = bf16[1024,7680]{1,0:T(8,128)(2,1)} custom-call(s32[1]{0:T(128)} %bitcast.place.refs_0_, bf16[256,256]{1,0:T(8,128)(2,1)S(1)} %get-tuple-element.38.hi.refs_1_, bf16[256,256]{1,0:T(8,128)(2,1)S(1)} %get-tuple-element.39.lo.refs_2_, bf16[1024,256]{1,0:T(8,128)(2,1)S(1)} %get-tuple-element.40.left.refs_3_, ...), custom_call_target="tpu_custom_call", output_to_operand_aliasing={{}: (8, {})} | custom-call | flops 1342177280 | bytes 4194304 | tf_op jit(solution)/shard_map/merge_part/pallas_call | solution.py:262
  175.0 4.2 %send_part.22 = bf16[1024,512]{1,0:T(8,128)(2,1)} custom-call(s32[1]{0:T(128)} %bitcast.1.place, bf16[256,256]{1,0:T(8,128)(2,1)S(1)} %get-tuple-element.38.hi.refs_1_, bf16[256,256]{1,0:T(8,128)(2,1)S(1)} %get-tuple-element.39.lo.refs_2_, bf16[1024,256]{1,0:T(8,128)(2,1)S(1)} %get-tuple-element.42.left, bf16[1024,15360]{1,0:T(8,128)(2,1)} %bitcast.32, ...), custom_call_target="tpu_custom_call" | custom-call | flops 268435456 | bytes 2621440 | tf_op jit(solution)/shard_map/send_part/pallas_call | solution.py:218
  181.3 4.6 %merge_part.18.rest_1_ = bf16[1024,7680]{1,0:T(8,128)(2,1)} custom-call(s32[1]{0:T(128)} %bitcast.place.refs_0_, bf16[256,256]{1,0:T(8,128)(2,1)S(1)} %get-tuple-element.38.hi.refs_1_, bf16[256,256]{1,0:T(8,128)(2,1)S(1)} %get-tuple-element.39.lo.refs_2_, bf16[1024,256]{1,0:T(8,128)(2,1)S(1)} %get-tuple-element.40.left.refs_3_, ...), custom_call_target="tpu_custom_call", output_to_operand_aliasing={{}: (8, {})} | custom-call | flops 1342177280 | bytes 4194304 | tf_op jit(solution)/shard_map/merge_part/pallas_call | solution.py:262
  186.0 4.6 %merge_part.19.rest_1_ = bf16[1024,7680]{1,0:T(8,128)(2,1)} custom-call(s32[1]{0:T(128)} %bitcast.place.refs_0_, bf16[256,256]{1,0:T(8,128)(2,1)S(1)} %get-tuple-element.38.hi.refs_1_, bf16[256,256]{1,0:T(8,128)(2,1)S(1)} %get-tuple-element.39.lo.refs_2_, bf16[1024,256]{1,0:T(8,128)(2,1)S(1)} %get-tuple-element.40.left.refs_3_, ...), custom_call_target="tpu_custom_call", output_to_operand_aliasing={{}: (8, {})} | custom-call | flops 1342177280 | bytes 4194304 | tf_op jit(solution)/shard_map/merge_part/pallas_call | solution.py:262
  190.6 6.9 %collective-permute-done.18.received = bf16[1024,512]{1,0:T(8,128)(2,1)S(1)} collective-permute-done((bf16[1024,512]{1,0:T(8,128)(2,1)}, bf16[1024,512]{1,0:T(8,128)(2,1)S(1)}, u32[]{:S(2)}, u32[]{:S(2)}) %collective-permute-start.18) | collective-permute-done | bytes 1048608 | tf_op jit(solution)/shard_map/ppermute | solution.py:24
  198.5 6.2 %reshape.97 = f32[9216,2]{1,0:T(8,128)} reshape(f32[16,1152]{1,0:T(8,128)S(1)} %slice_convert_fusion) | data formatting | bytes 147456 | tf_op jit(solution)/shard_map/convert_element_type | solution.py:453
  206.4 4.2 %send_part.23 = bf16[1024,512]{1,0:T(8,128)(2,1)} custom-call(s32[1]{0:T(128)} %bitcast.1.place, bf16[256,256]{1,0:T(8,128)(2,1)S(1)} %get-tuple-element.38.hi.refs_1_, bf16[256,256]{1,0:T(8,128)(2,1)S(1)} %get-tuple-element.39.lo.refs_2_, bf16[1024,256]{1,0:T(8,128)(2,1)S(1)} %get-tuple-element.42.left, bf16[1024,15360]{1,0:T(8,128)(2,1)} %bitcast.35, ...), custom_call_target="tpu_custom_call" | custom-call | flops 268435456 | bytes 2621440 | tf_op jit(solution)/shard_map/send_part/pallas_call | solution.py:218
  212.7 4.7 %merge_part.20.refs_10_ = bf16[1024,7680]{1,0:T(8,128)(2,1)} custom-call(s32[1]{0:T(128)} %bitcast.place.refs_0_, bf16[256,256]{1,0:T(8,128)(2,1)S(1)} %get-tuple-element.38.hi.refs_1_, bf16[256,256]{1,0:T(8,128)(2,1)S(1)} %get-tuple-element.39.lo.refs_2_, bf16[1024,256]{1,0:T(8,128)(2,1)S(1)} %get-tuple-element.40.left.refs_3_, ...), custom_call_target="tpu_custom_call", output_to_operand_aliasing={{}: (8, {})} | custom-call | flops 1342177280 | bytes 4194304 | tf_op jit(solution)/shard_map/merge_part/pallas_call | solution.py:262
  217.3 7.4 %all_gather.6 = bf16[1024,256]{1,0:T(8,128)(2,1)S(1)} all-gather(bf16[1024,128]{1,0:T(8,128)(2,1)} %collective-permute-done.10), channel_id=1, replica_groups=mesh['cube'=4,'row'=4,'col'=2] {'col'}, dimensions={1}, use_global_device_ids=true | all-gather | bytes 786432 | tf_op jit(solution)/shard_map/all_gather | solution.py:459
  226.0 7.6 %all_gather.7.refs_8_ = bf16[256,1152]{1,0:T(8,128)(2,1)S(1)} all-gather(bf16[64,1152]{1,0:T(8,128)(2,1)S(1)} %slice-done), channel_id=1, replica_groups=mesh['cube'=4,'row'=4,'col'=2] {'row'}, dimensions={0}, use_global_device_ids=true | all-gather | bytes 737280 | tf_op jit(solution)/shard_map/all_gather | solution.py:463
  233.5 4.2 %send_part.24 = bf16[1024,512]{1,0:T(8,128)(2,1)} custom-call(s32[1]{0:T(128)} %bitcast.1.place, bf16[256,256]{1,0:T(8,128)(2,1)S(1)} %get-tuple-element.38.hi.refs_1_, bf16[256,256]{1,0:T(8,128)(2,1)S(1)} %get-tuple-element.39.lo.refs_2_, bf16[1024,256]{1,0:T(8,128)(2,1)S(1)} %get-tuple-element.42.left, bf16[1024,15360]{1,0:T(8,128)(2,1)} %bitcast.37, ...), custom_call_target="tpu_custom_call" | custom-call | flops 268435456 | bytes 2621440 | tf_op jit(solution)/shard_map/send_part/pallas_call | solution.py:218
  238.2 5.3 %merge_part.21.refs_10_ = bf16[1024,7680]{1,0:T(8,128)(2,1)} custom-call(s32[1]{0:T(128)} %bitcast.place.refs_0_, bf16[256,256]{1,0:T(8,128)(2,1)S(1)} %get-tuple-element.38.hi.refs_1_, bf16[256,256]{1,0:T(8,128)(2,1)S(1)} %get-tuple-element.39.lo.refs_2_, bf16[1024,256]{1,0:T(8,128)(2,1)S(1)} %get-tuple-element.40.left.refs_3_, ...), custom_call_target="tpu_custom_call", output_to_operand_aliasing={{}: (10, {})} | custom-call | flops 1342177280 | bytes 4194304 | tf_op jit(solution)/shard_map/merge_part/pallas_call | solution.py:262
  243.5 5.3 %merge_part.22.refs_10_ = bf16[1024,7680]{1,0:T(8,128)(2,1)} custom-call(s32[1]{0:T(128)} %bitcast.place.refs_0_, bf16[256,256]{1,0:T(8,128)(2,1)S(1)} %get-tuple-element.38.hi.refs_1_, bf16[256,256]{1,0:T(8,128)(2,1)S(1)} %get-tuple-element.39.lo.refs_2_, bf16[1024,256]{1,0:T(8,128)(2,1)S(1)} %get-tuple-element.40.left.refs_3_, ...), custom_call_target="tpu_custom_call", output_to_operand_aliasing={{}: (10, {})} | custom-call | flops 1342177280 | bytes 4194304 | tf_op jit(solution)/shard_map/merge_part/pallas_call | solution.py:262
  248.8 4.1 %merge_part.23.rest_1_ = bf16[1024,7680]{1,0:T(8,128)(2,1)} custom-call(s32[1]{0:T(128)} %bitcast.place.refs_0_, bf16[256,256]{1,0:T(8,128)(2,1)S(1)} %get-tuple-element.38.hi.refs_1_, bf16[256,256]{1,0:T(8,128)(2,1)S(1)} %get-tuple-element.39.lo.refs_2_, bf16[1024,256]{1,0:T(8,128)(2,1)S(1)} %get-tuple-element.40.left.refs_3_, ...), custom_call_target="tpu_custom_call", output_to_operand_aliasing={{}: (10, {})} | custom-call | flops 335544320 | bytes 1048576 | tf_op jit(solution)/shard_map/merge_part/pallas_call | solution.py:262
  252.9 4.1 %send_part.25 = bf16[1024,512]{1,0:T(8,128)(2,1)} custom-call(s32[1]{0:T(128)} %bitcast.1.place, bf16[256,256]{1,0:T(8,128)(2,1)S(1)} %get-tuple-element.38.hi.refs_1_, bf16[256,256]{1,0:T(8,128)(2,1)S(1)} %get-tuple-element.39.lo.refs_2_, bf16[1024,256]{1,0:T(8,128)(2,1)S(1)} %get-tuple-element.42.left, bf16[1024,15360]{1,0:T(8,128)(2,1)} %bitcast.41, ...), custom_call_target="tpu_custom_call" | custom-call | flops 268435456 | bytes 2621440 | tf_op jit(solution)/shard_map/send_part/pallas_call | solution.py:218
  260.9 4.7 %merge_part.24.rest_1_ = bf16[1024,7680]{1,0:T(8,128)(2,1)} custom-call(s32[1]{0:T(128)} %bitcast.place.refs_0_, bf16[256,256]{1,0:T(8,128)(2,1)S(1)} %get-tuple-element.38.hi.refs_1_, bf16[256,256]{1,0:T(8,128)(2,1)S(1)} %get-tuple-element.39.lo.refs_2_, bf16[1024,256]{1,0:T(8,128)(2,1)S(1)} %get-tuple-element.40.left.refs_3_, ...), custom_call_target="tpu_custom_call", output_to_operand_aliasing={{}: (8, {})} | custom-call | flops 1342177280 | bytes 4194304 | tf_op jit(solution)/shard_map/merge_part/pallas_call | solution.py:262
  265.7 5.2 %merge_part.25.rest_1_ = bf16[1024,7680]{1,0:T(8,128)(2,1)} custom-call(s32[1]{0:T(128)} %bitcast.place.refs_0_, bf16[256,256]{1,0:T(8,128)(2,1)S(1)} %get-tuple-element.38.hi.refs_1_, bf16[256,256]{1,0:T(8,128)(2,1)S(1)} %get-tuple-element.39.lo.refs_2_, bf16[1024,256]{1,0:T(8,128)(2,1)S(1)} %get-tuple-element.40.left.refs_3_, ...), custom_call_target="tpu_custom_call", output_to_operand_aliasing={{}: (8, {})} | custom-call | flops 1342177280 | bytes 4194304 | tf_op jit(solution)/shard_map/merge_part/pallas_call | solution.py:262
  274.4 5.0 %merge_part.26.rest_1_ = bf16[1024,7680]{1,0:T(8,128)(2,1)} custom-call(s32[1]{0:T(128)} %bitcast.place.refs_0_, bf16[256,256]{1,0:T(8,128)(2,1)S(1)} %get-tuple-element.38.hi.refs_1_, bf16[256,256]{1,0:T(8,128)(2,1)S(1)} %get-tuple-element.39.lo.refs_2_, bf16[1024,256]{1,0:T(8,128)(2,1)S(1)} %get-tuple-element.40.left.refs_3_, ...), custom_call_target="tpu_custom_call", output_to_operand_aliasing={{}: (8, {})} | custom-call | flops 1342177280 | bytes 4194304 | tf_op jit(solution)/shard_map/merge_part/pallas_call | solution.py:262
  279.4 5.0 %merge_part.27.rest_1_ = bf16[1024,7680]{1,0:T(8,128)(2,1)} custom-call(s32[1]{0:T(128)} %bitcast.place.refs_0_, bf16[256,256]{1,0:T(8,128)(2,1)S(1)} %get-tuple-element.38.hi.refs_1_, bf16[256,256]{1,0:T(8,128)(2,1)S(1)} %get-tuple-element.39.lo.refs_2_, bf16[1024,256]{1,0:T(8,128)(2,1)S(1)} %get-tuple-element.40.left.refs_3_, ...), custom_call_target="tpu_custom_call", output_to_operand_aliasing={{}: (8, {})} | custom-call | flops 1342177280 | bytes 4194304 | tf_op jit(solution)/shard_map/merge_part/pallas_call | solution.py:262
  292.3 17.6 %collective-permute-done.28.received = bf16[1024,512]{1,0:T(8,128)(2,1)} collective-permute-done((bf16[1024,512]{1,0:T(8,128)(2,1)}, bf16[1024,512]{1,0:T(8,128)(2,1)}, u32[]{:S(2)}, u32[]{:S(2)}) %collective-permute-start.28) | collective-permute-done | bytes 1048608 | tf_op jit(solution)/shard_map/ppermute | solution.py:24
  315.6 5.0 %merge_part.28.rest_1_ = bf16[1024,7680]{1,0:T(8,128)(2,1)} custom-call(s32[1]{0:T(128)} %bitcast.place.refs_0_, bf16[256,256]{1,0:T(8,128)(2,1)S(1)} %get-tuple-element.38.hi.refs_1_, bf16[256,256]{1,0:T(8,128)(2,1)S(1)} %get-tuple-element.39.lo.refs_2_, bf16[1024,256]{1,0:T(8,128)(2,1)S(1)} %get-tuple-element.40.left.refs_3_, ...), custom_call_target="tpu_custom_call", output_to_operand_aliasing={{}: (8, {})} | custom-call | flops 1342177280 | bytes 4194304 | tf_op jit(solution)/shard_map/merge_part/pallas_call | solution.py:262
  320.6 5.0 %merge_part.29.rest_1_ = bf16[1024,7680]{1,0:T(8,128)(2,1)} custom-call(s32[1]{0:T(128)} %bitcast.place.refs_0_, bf16[256,256]{1,0:T(8,128)(2,1)S(1)} %get-tuple-element.38.hi.refs_1_, bf16[256,256]{1,0:T(8,128)(2,1)S(1)} %get-tuple-element.39.lo.refs_2_, bf16[1024,256]{1,0:T(8,128)(2,1)S(1)} %get-tuple-element.40.left.refs_3_, ...), custom_call_target="tpu_custom_call", output_to_operand_aliasing={{}: (8, {})} | custom-call | flops 1342177280 | bytes 4194304 | tf_op jit(solution)/shard_map/merge_part/pallas_call | solution.py:262
  325.6 6.7 %collective-permute-done.27.received = bf16[1024,512]{1,0:T(8,128)(2,1)S(1)} collective-permute-done((bf16[1024,512]{1,0:T(8,128)(2,1)S(1)}, bf16[1024,512]{1,0:T(8,128)(2,1)S(1)}, u32[]{:S(2)}, u32[]{:S(2)}) %collective-permute-start.27) | collective-permute-done | bytes 1048608 | tf_op jit(solution)/shard_map/ppermute | solution.py:24
  332.3 4.6 %merge_part.30.rest_1_ = bf16[1024,7680]{1,0:T(8,128)(2,1)} custom-call(s32[1]{0:T(128)} %bitcast.place.refs_0_, bf16[256,256]{1,0:T(8,128)(2,1)S(1)} %get-tuple-element.38.hi.refs_1_, bf16[256,256]{1,0:T(8,128)(2,1)S(1)} %get-tuple-element.39.lo.refs_2_, bf16[1024,256]{1,0:T(8,128)(2,1)S(1)} %get-tuple-element.40.left.refs_3_, ...), custom_call_target="tpu_custom_call", output_to_operand_aliasing={{}: (8, {})} | custom-call | flops 1342177280 | bytes 4194304 | tf_op jit(solution)/shard_map/merge_part/pallas_call | solution.py:262
  337.0 6.6 %collective-permute-done.26.received = bf16[1024,256]{1,0:T(8,128)(2,1)S(1)} collective-permute-done((bf16[1024,256]{1,0:T(8,128)(2,1)S(1)}, bf16[1024,256]{1,0:T(8,128)(2,1)S(1)}, u32[]{:S(2)}, u32[]{:S(2)}) %collective-permute-start.26) | collective-permute-done | bytes 524320 | tf_op jit(solution)/shard_map/ppermute | solution.py:24
  (191 shorter events, 110.9 us)
Async XLA Ops:
  3.4 65.0 %collective-permute-start.7 = (bf16[1024,1152]{1,0:T(8,128)(2,1)}, bf16[1024,1152]{1,0:T(8,128)(2,1)}, u32[]{:S(2)}, u32[]{:S(2)}) collective-permute-start(bf16[1024,1152]{1,0:T(8,128)(2,1)} %dynamic-slice_bitcast_fusion), channel_id=1, source_target_pairs={{0,8},{8,0},{16,24},{24,16},{1,9},{9,1},{17,25},{25,17},{2,10},{10... | collective-permute-start | bytes 7077896 | tf_op jit(solution)/shard_map/ppermute | solution.py:24
  6.4 7.7 %collective-permute-start = (f32[32,256]{1,0:T(8,128)S(1)}, f32[32,256]{1,0:T(8,128)S(1)}, u32[]{:S(2)}, u32[]{:S(2)}) collective-permute-start(f32[32,256]{1,0:T(8,128)S(1)} %bitcast.54), channel_id=1, source_target_pairs={{0,4},{1,5},{2,6},{3,7},{4,0},{5,1},{6,2},{7,3},{8,12},{9,13},{10,... | collective-permute-start | bytes 98312 | tf_op jit(solution)/shard_map/ppermute | solution.py:24
  8.0 13.7 %collective-permute-start.3 = (bf16[1024,128]{1,0:T(8,128)(2,1)S(1)}, bf16[1024,128]{1,0:T(8,128)(2,1)S(1)}, u32[]{:S(2)}, u32[]{:S(2)}) collective-permute-start(bf16[1024,128]{1,0:T(8,128)(2,1)S(1)} %bitcast.21), channel_id=1, source_target_pairs={{0,1},{1,0},{2,3},{3,2},{4,5},{5,4},{6,7},{7,6},{8,9},{9,8},{10,11... | collective-permute-start | bytes 786440 | tf_op jit(solution)/shard_map/ppermute | solution.py:24
  10.2 9.6 %collective-permute-start.4 = (bf16[64,2048]{1,0:T(8,128)(2,1)}, bf16[64,2048]{1,0:T(8,128)(2,1)}, u32[]{:S(2)}, u32[]{:S(2)}) collective-permute-start(bf16[64,2048]{1,0:T(8,128)(2,1)} %dynamic-slice_bitcast_fusion.3), channel_id=1, source_target_pairs={{0,4},{2,6},{4,0},{6,2},{1,5},{3,7},{5,1},{7,3},{8,12},{10,14},{12... | collective-permute-start | bytes 786440 | tf_op jit(solution)/shard_map/ppermute | solution.py:24
  12.3 50.5 %collective-permute-start.8 = (bf16[64,13312]{1,0:T(8,128)(2,1)}, bf16[64,13312]{1,0:T(8,128)(2,1)}, u32[]{:S(2)}, u32[]{:S(2)}) collective-permute-start(bf16[64,13312]{1,0:T(8,128)(2,1)} %pad_maximum_fusion), channel_id=1, source_target_pairs={{0,4},{2,6},{4,0},{6,2},{1,5},{3,7},{5,1},{7,3},{8,12},{10,14},{12... | collective-permute-start | bytes 5111816 | tf_op jit(solution)/shard_map/ppermute | solution.py:24
  14.2 4.3 %collective-permute-start.1 = (f32[64,256]{1,0:T(8,128)S(1)}, f32[64,256]{1,0:T(8,128)S(1)}, u32[]{:S(2)}, u32[]{:S(2)}) collective-permute-start(f32[64,256]{1,0:T(8,128)S(1)} %pad_maximum_fusion.7), channel_id=1, source_target_pairs={{0,1},{1,0},{2,3},{3,2},{4,5},{5,4},{6,7},{7,6},{8,9},{9,8},{10,11... | collective-permute-start | bytes 196616 | tf_op jit(solution)/shard_map/ppermute | solution.py:24
  18.5 3.1 collective-permute-start.2
  21.6 30.8 %collective-permute-start.5 = (bf16[128,2048]{1,0:T(8,128)(2,1)}, bf16[128,2048]{1,0:T(8,128)(2,1)}, u32[]{:S(2)}, u32[]{:S(2)}) collective-permute-start(bf16[128,2048]{1,0:T(8,128)(2,1)} %pad_maximum_fusion.3), channel_id=1, source_target_pairs={{0,2},{2,0},{4,6},{6,4},{1,3},{3,1},{5,7},{7,5},{8,10},{10,8},{12,... | collective-permute-start | bytes 1572872 | tf_op jit(solution)/shard_map/ppermute | solution.py:24
  51.4 21.9 %collective-permute-start.10 = (bf16[1024,128]{1,0:T(8,128)(2,1)}, bf16[1024,128]{1,0:T(8,128)(2,1)}, u32[]{:S(2)}, u32[]{:S(2)}) collective-permute-start(bf16[1024,128]{1,0:T(8,128)(2,1)} %constant_dynamic-slice_fusion), channel_id=1, source_target_pairs={{0,8},{8,0},{16,24},{24,16},{1,9},{9,1},{17,25},{25,17},{2,10},{10... | collective-permute-start | bytes 786440 | tf_op jit(solution)/shard_map/ppermute | solution.py:24
  57.6 23.6 %collective-permute-start.6 = (bf16[1024,384]{1,0:T(8,128)(2,1)S(1)}, bf16[1024,384]{1,0:T(8,128)(2,1)S(1)}, u32[]{:S(2)}, u32[]{:S(2)}) collective-permute-start(bf16[1024,384]{1,0:T(8,128)(2,1)S(1)} %send_part.15), channel_id=1, source_target_pairs={{0,8},{8,0},{16,24},{24,16},{1,9},{9,1},{17,25},{25,17},{2,10},{10... | collective-permute-start | bytes 2359304 | tf_op jit(solution)/shard_map/ppermute | solution.py:24
  62.2 41.4 %collective-permute-start.13 = (bf16[1024,512]{1,0:T(8,128)(2,1)S(1)}, bf16[1024,512]{1,0:T(8,128)(2,1)S(1)}, u32[]{:S(2)}, u32[]{:S(2)}) collective-permute-start(bf16[1024,512]{1,0:T(8,128)(2,1)S(1)} %send_part.16), channel_id=1, source_target_pairs={{0,8},{8,0},{16,24},{24,16},{1,9},{9,1},{17,25},{25,17},{2,10},{10... | collective-permute-start | bytes 3145736 | tf_op jit(solution)/shard_map/ppermute | solution.py:24
  64.0 4.4 %collective-permute-start.9 = (bf16[128,1024]{1,0:T(8,128)(2,1)S(1)}, bf16[128,1024]{1,0:T(8,128)(2,1)S(1)}, u32[]{:S(2)}, u32[]{:S(2)}) collective-permute-start(bf16[128,1024]{1,0:T(8,128)(2,1)S(1)} %pad_maximum_fusion.5), channel_id=1, source_target_pairs={{0,2},{2,0},{4,6},{6,4},{1,3},{3,1},{5,7},{7,5},{8,10},{10,8},{12,... | collective-permute-start | bytes 786440 | tf_op jit(solution)/shard_map/ppermute | solution.py:24
  72.7 37.9 %collective-permute-start.14 = (bf16[128,4608]{1,0:T(8,128)(2,1)}, bf16[128,4608]{1,0:T(8,128)(2,1)}, u32[]{:S(2)}, u32[]{:S(2)}) collective-permute-start(bf16[128,4608]{1,0:T(8,128)(2,1)} %pad_maximum_fusion.1), channel_id=1, source_target_pairs={{0,2},{2,0},{4,6},{6,4},{1,3},{3,1},{5,7},{7,5},{8,10},{10,8},{12,... | collective-permute-start | bytes 3538952 | tf_op jit(solution)/shard_map/ppermute | solution.py:24
  85.3 20.5 %collective-permute-start.16 = (bf16[128,2048]{1,0:T(8,128)(2,1)S(1)}, bf16[128,2048]{1,0:T(8,128)(2,1)S(1)}, u32[]{:S(2)}, u32[]{:S(2)}) collective-permute-start(bf16[128,2048]{1,0:T(8,128)(2,1)S(1)} %get-tuple-element.53), channel_id=1, source_target_pairs={{0,2},{2,0},{4,6},{6,4},{1,3},{3,1},{5,7},{7,5},{8,10},{10,8},{12,... | collective-permute-start | bytes 1572872 | tf_op jit(solution)/shard_map/ppermute | solution.py:24
  85.3 67.3 %collective-permute-start.12 = (bf16[1024,512]{1,0:T(8,128)(2,1)S(1)}, bf16[1024,512]{1,0:T(8,128)(2,1)S(1)}, u32[]{:S(2)}, u32[]{:S(2)}) collective-permute-start(bf16[1024,512]{1,0:T(8,128)(2,1)S(1)} %send_part.17), channel_id=1, source_target_pairs={{0,8},{8,0},{16,24},{24,16},{1,9},{9,1},{17,25},{25,17},{2,10},{10... | collective-permute-start | bytes 3145736 | tf_op jit(solution)/shard_map/ppermute | solution.py:24
  87.4 68.3 %collective-permute-start.11 = (bf16[1024,512]{1,0:T(8,128)(2,1)}, bf16[1024,512]{1,0:T(8,128)(2,1)S(1)}, u32[]{:S(2)}, u32[]{:S(2)}) collective-permute-start(bf16[1024,512]{1,0:T(8,128)(2,1)} %send_part.18), channel_id=1, source_target_pairs={{0,8},{8,0},{16,24},{24,16},{1,9},{9,1},{17,25},{25,17},{2,10},{10... | collective-permute-start | bytes 3145736 | tf_op jit(solution)/shard_map/ppermute | solution.py:24
  103.7 48.9 %collective-permute-start.15 = (bf16[80,1152]{1,0:T(8,128)(2,1)S(1)}, bf16[80,1152]{1,0:T(8,128)(2,1)S(1)}, u32[]{:S(2)}, u32[]{:S(2)}) collective-permute-start(bf16[80,1152]{1,0:T(8,128)(2,1)S(1)} %pad_maximum_fusion.6), channel_id=1, source_target_pairs={{0,8},{8,0},{16,24},{24,16},{1,9},{9,1},{17,25},{25,17},{2,10},{10... | collective-permute-start | bytes 552968 | tf_op jit(solution)/shard_map/ppermute | solution.py:24
  105.8 58.2 %copy-start.6 = (bf16[256,2048]{1,0:T(8,128)(2,1)}, bf16[256,2048]{1,0:T(8,128)(2,1)S(1)}, u32[]{:S(2)}) copy-start(bf16[256,2048]{1,0:T(8,128)(2,1)S(1)} %constant_dynamic-update-slice_fusion.7.rest_0_.refs_9_) | copy-start | bytes 3145732
  112.0 63.1 %copy-start.2 = (bf16[256,4608]{1,0:T(8,128)(2,1)}, bf16[256,4608]{1,0:T(8,128)(2,1)S(1)}, u32[]{:S(2)}) copy-start(bf16[256,4608]{1,0:T(8,128)(2,1)S(1)} %constant_dynamic-update-slice_fusion.5.rest_0_) | copy-start | bytes 7077892
  116.5 58.6 %collective-permute-start.19 = (bf16[1024,512]{1,0:T(8,128)(2,1)}, bf16[1024,512]{1,0:T(8,128)(2,1)S(1)}, u32[]{:S(2)}, u32[]{:S(2)}) collective-permute-start(bf16[1024,512]{1,0:T(8,128)(2,1)} %send_part.19), channel_id=1, source_target_pairs={{0,8},{8,0},{16,24},{24,16},{1,9},{9,1},{17,25},{25,17},{2,10},{10... | collective-permute-start | bytes 3145736 | tf_op jit(solution)/shard_map/ppermute | solution.py:24
  152.6 17.1 %collective-permute-start.20 = (bf16[128,2048]{1,0:T(8,128)(2,1)S(1)}, bf16[128,2048]{1,0:T(8,128)(2,1)}, u32[]{:S(2)}, u32[]{:S(2)}) collective-permute-start(bf16[128,2048]{1,0:T(8,128)(2,1)S(1)} %copy-done.30), channel_id=1, source_target_pairs={{0,2},{2,0},{4,6},{6,4},{1,3},{3,1},{5,7},{7,5},{8,10},{10,8},{12,... | collective-permute-start | bytes 1572872 | tf_op jit(solution)/shard_map/ppermute | solution.py:24
  160.2 8.4 %collective-permute-start.22 = (bf16[128,1536]{1,0:T(8,128)(2,1)}, bf16[128,1536]{1,0:T(8,128)(2,1)}, u32[]{:S(2)}, u32[]{:S(2)}) collective-permute-start(bf16[128,1536]{1,0:T(8,128)(2,1)} %pad_maximum_fusion.4), channel_id=1, source_target_pairs={{0,2},{2,0},{4,6},{6,4},{1,3},{3,1},{5,7},{7,5},{8,10},{10,8},{12,... | collective-permute-start | bytes 1179656 | tf_op jit(solution)/shard_map/ppermute | solution.py:24
  160.7 10.4 %collective-permute-start.21 = (bf16[128,2048]{1,0:T(8,128)(2,1)S(1)}, bf16[128,2048]{1,0:T(8,128)(2,1)}, u32[]{:S(2)}, u32[]{:S(2)}) collective-permute-start(bf16[128,2048]{1,0:T(8,128)(2,1)S(1)} %copy-done.29), channel_id=1, source_target_pairs={{0,2},{2,0},{4,6},{6,4},{1,3},{3,1},{5,7},{7,5},{8,10},{10,8},{12,... | collective-permute-start | bytes 1572872 | tf_op jit(solution)/shard_map/ppermute | solution.py:24
  160.8 36.7 %collective-permute-start.18 = (bf16[1024,512]{1,0:T(8,128)(2,1)}, bf16[1024,512]{1,0:T(8,128)(2,1)S(1)}, u32[]{:S(2)}, u32[]{:S(2)}) collective-permute-start(bf16[1024,512]{1,0:T(8,128)(2,1)} %copy-done.19), channel_id=1, source_target_pairs={{0,8},{8,0},{16,24},{24,16},{1,9},{9,1},{17,25},{25,17},{2,10},{10... | collective-permute-start | bytes 3145736 | tf_op jit(solution)/shard_map/ppermute | solution.py:24
  168.7 64.9 %collective-permute-start.17 = (bf16[1024,512]{1,0:T(8,128)(2,1)}, bf16[1024,512]{1,0:T(8,128)(2,1)}, u32[]{:S(2)}, u32[]{:S(2)}) collective-permute-start(bf16[1024,512]{1,0:T(8,128)(2,1)} %send_part.21), channel_id=1, source_target_pairs={{0,8},{8,0},{16,24},{24,16},{1,9},{9,1},{17,25},{25,17},{2,10},{10... | collective-permute-start | bytes 3145736 | tf_op jit(solution)/shard_map/ppermute | solution.py:24
  179.3 73.6 %collective-permute-start.25 = (bf16[1024,512]{1,0:T(8,128)(2,1)}, bf16[1024,512]{1,0:T(8,128)(2,1)}, u32[]{:S(2)}, u32[]{:S(2)}) collective-permute-start(bf16[1024,512]{1,0:T(8,128)(2,1)} %send_part.22), channel_id=1, source_target_pairs={{0,8},{8,0},{16,24},{24,16},{1,9},{9,1},{17,25},{25,17},{2,10},{10... | collective-permute-start | bytes 3145736 | tf_op jit(solution)/shard_map/ppermute | solution.py:24
  210.6 60.3 %collective-permute-start.24 = (bf16[1024,512]{1,0:T(8,128)(2,1)}, bf16[1024,512]{1,0:T(8,128)(2,1)}, u32[]{:S(2)}, u32[]{:S(2)}) collective-permute-start(bf16[1024,512]{1,0:T(8,128)(2,1)} %send_part.23), channel_id=1, source_target_pairs={{0,8},{8,0},{16,24},{24,16},{1,9},{9,1},{17,25},{25,17},{2,10},{10... | collective-permute-start | bytes 3145736 | tf_op jit(solution)/shard_map/ppermute | solution.py:24
  237.7 49.8 %collective-permute-start.23 = (bf16[1024,512]{1,0:T(8,128)(2,1)}, bf16[1024,512]{1,0:T(8,128)(2,1)}, u32[]{:S(2)}, u32[]{:S(2)}) collective-permute-start(bf16[1024,512]{1,0:T(8,128)(2,1)} %send_part.24), channel_id=1, source_target_pairs={{0,8},{8,0},{16,24},{24,16},{1,9},{9,1},{17,25},{25,17},{2,10},{10... | collective-permute-start | bytes 3145736 | tf_op jit(solution)/shard_map/ppermute | solution.py:24
  257.0 53.0 %collective-permute-start.28 = (bf16[1024,512]{1,0:T(8,128)(2,1)}, bf16[1024,512]{1,0:T(8,128)(2,1)}, u32[]{:S(2)}, u32[]{:S(2)}) collective-permute-start(bf16[1024,512]{1,0:T(8,128)(2,1)} %send_part.25), channel_id=1, source_target_pairs={{0,8},{8,0},{16,24},{24,16},{1,9},{9,1},{17,25},{25,17},{2,10},{10... | collective-permute-start | bytes 3145736 | tf_op jit(solution)/shard_map/ppermute | solution.py:24
  273.8 58.5 %collective-permute-start.27 = (bf16[1024,512]{1,0:T(8,128)(2,1)S(1)}, bf16[1024,512]{1,0:T(8,128)(2,1)S(1)}, u32[]{:S(2)}, u32[]{:S(2)}) collective-permute-start(bf16[1024,512]{1,0:T(8,128)(2,1)S(1)} %send_part.26), channel_id=1, source_target_pairs={{0,8},{8,0},{16,24},{24,16},{1,9},{9,1},{17,25},{25,17},{2,10},{10... | collective-permute-start | bytes 3145736 | tf_op jit(solution)/shard_map/ppermute | solution.py:24
  290.2 53.4 %collective-permute-start.26 = (bf16[1024,256]{1,0:T(8,128)(2,1)S(1)}, bf16[1024,256]{1,0:T(8,128)(2,1)S(1)}, u32[]{:S(2)}, u32[]{:S(2)}) collective-permute-start(bf16[1024,256]{1,0:T(8,128)(2,1)S(1)} %send_part.27), channel_id=1, source_target_pairs={{0,8},{8,0},{16,24},{24,16},{1,9},{9,1},{17,25},{25,17},{2,10},{10... | collective-permute-start | bytes 1572872 | tf_op jit(solution)/shard_map/ppermute | solution.py:24
  313.5 40.5 %collective-permute-start.29 = (bf16[1024,256]{1,0:T(8,128)(2,1)S(1)}, bf16[1024,256]{1,0:T(8,128)(2,1)S(1)}, u32[]{:S(2)}, u32[]{:S(2)}) collective-permute-start(bf16[1024,256]{1,0:T(8,128)(2,1)S(1)} %fusion.4), channel_id=1, source_target_pairs={{0,8},{8,0},{16,24},{24,16},{1,9},{9,1},{17,25},{25,17},{2,10},{10... | collective-permute-start | bytes 1572872 | tf_op jit(solution)/shard_map/ppermute | solution.py:24
  (35 other events, 291.2 us)
